TPU v7x, 32 devices: a whole 2x2x4 slice. The times are simulated.
32 devices in a mesh: row: 4 (over y, x), vec: 8 (over z, core).
Axes of the slice: x: 2, y: 2, z: 4, core: 2. Of those that a mesh axis runs over, the one named last changes fastest.
Arguments:
- filtered: bfloat16 [32768, 2048], P(('row', 'vec')), may hold values from -6 to 6
- ritz: bfloat16 [2048, 1024], P('row', 'vec'), may hold values from -0.125 to 0.125
- panel_cols: float32 [32768, 512], P(('row', 'vec')), may hold values from -0.25 to 0.25
- panel_inverse: float32 [2, 256, 256], replicated, may hold values from -0.15 to 2, as said below
Outputs:
- eigvecs: float32 [32768, 1024], P('row', 'vec')
Inputs may be any that keep to these rules, and one draw needn't show every extreme that they name: `panel_inverse`: each of the two blocks is upper triangular with a positive diagonal.
All inputs are finite; a program needn't handle non-finite values.
Results may differ from a plain program's by a relative error of at most 0.0003.
Values may be sent and summed in bfloat16 or wider, within the bound.
No kernel may reach another device: no remote copies, remote signals or barrier semaphores. Data moves between devices by JAX's collectives and lax.ppermute only.
A program may use at most 64 MiB of HBM per device.

v0:
```python
import jax
import jax.numpy as jnp
from jax import lax
from jax.sharding import PartitionSpec as P


def spread(value, axis, root):
    mine = lax.axis_index(axis) == root
    return lax.psum(jnp.where(mine, value, jnp.zeros_like(value)), axis)


def on_device(filtered, ritz, panel_cols, panel_inverse):
    highest = lax.Precision.HIGHEST
    local_rows = filtered.shape[0]
    width = panel_inverse.shape[1]
    ritz_full_rows = lax.all_gather(ritz, "row", axis=0, tiled=True)
    ritz_full = lax.all_gather(ritz_full_rows, "vec", axis=1, tiled=True)
    rotated = jnp.dot(filtered, ritz_full, preferred_element_type=jnp.float32)
    last_rank = lax.axis_size(("row", "vec")) - 1
    is_last = lax.axis_index(("row", "vec")) == last_rank
    lower = local_rows - 2 * width
    upper = local_rows - width
    last_x = jnp.dot(panel_inverse[1], rotated[upper:], precision=highest)
    middle = rotated[lower:upper] - jnp.dot(
        panel_cols[lower:upper, width:], last_x, precision=highest
    )
    next_x = jnp.dot(panel_inverse[0], middle, precision=highest)
    next_x, last_x = (
        spread(next_x, ("row", "vec"), last_rank),
        spread(last_x, ("row", "vec"), last_rank),
    )
    solved = jnp.concatenate([next_x, last_x], axis=0)
    rotated = rotated - jnp.dot(panel_cols, solved, precision=highest)
    solved_tail = jnp.concatenate([next_x, last_x], axis=0)
    tail = jnp.where(is_last, solved_tail, rotated[lower:])
    rotated = jnp.concatenate([rotated[:lower], tail], axis=0)
    return lax.all_to_all(rotated, "vec", split_axis=1, concat_axis=0, tiled=True)


def solution(mesh):
    in_specs = (P(("row", "vec"), None), P("row", "vec"), P(("row", "vec"), None), P())
    out_specs = P("row", "vec")
    return jax.shard_map(
        on_device, mesh=mesh, in_specs=in_specs, out_specs=out_specs, check_vma=False
    )
```

profile of v0, /device:TPU:9, one launch (start us, length us, event | category | flops | bytes accessed | tf_op | source)
XLA Modules:
  0.0 331.8 jit_solution(2411231544005953768)
XLA Ops:
  6.5 10.1 %all_gather.6 = bf16[2048,128]{1,0:T(8,128)(2,1)} all-gather(bf16[512,128]{1,0:T(8,128)(2,1)} %param.5), channel_id=1, replica_groups=mesh['row'=4,'vec'=8] {'row'}, dimensions={0}, use_global_device_ids=true | all-gather | bytes 655360 | tf_op jit(solution)/shard_map/all_gather | solution.py:16
  16.6 0.0 all-gather.2.cloned.1.call-update
  16.7 0.0 all-reduce.3.cloned.1.call-start
  16.7 0.0 copy-start.3
  16.7 48.8 %all-gather.2.cloned.1.call-done = bf16[2048,1024]{1,0:T(8,128)(2,1)} async-done(((bf16[2048,128]{1,0:T(8,128)(2,1)}), bf16[2048,1024]{1,0:T(8,128)(2,1)}) %all-gather.2.cloned.1.call-update) | async-done | bytes 4194320 | tf_op jit(solution)/shard_map/all_gather | solution.py:17
  65.5 7.5 %fusion.10 = f32[1024,1024]{1,0:T(8,128)S(1)} fusion(bf16[1024,2048]{1,0:T(8,128)(2,1)} %param.4, bf16[2048,1024]{1,0:T(8,128)(2,1)} %all-gather.2.cloned.1.call-done), kind=kOutput, calls=%fused_computation.19 | convolution fusion | flops 4294967296 | bytes 12582912 | tf_op jit(solution)/shard_map/dot_general | solution.py:18
  73.0 0.0 copy-start
  73.0 2.0 copy-done
  75.0 1.9 fusion.2
  76.9 0.3 copy.9
  77.3 2.4 fusion.1
  79.7 2.1 fusion
  81.7 1.1 select_bitcast_fusion
  82.8 0.0 all-reduce.3.cloned.1.call-update
  82.8 131.0 %all-reduce.3.cloned.1.call-done = (f32[256,1024]{1,0:T(8,128)}, f32[256,1024]{1,0:T(8,128)}) async-done(((f32[256,1024]{1,0:T(8,128)}, f32[256,1024]{1,0:T(8,128)}), (f32[256,1024]{1,0:T(8,128)}, f32[256,1024]{1,0:T(8,128)})) %all-reduce.3.cloned.1.call-update) | async-done | bytes 2097168 | tf_op jit(solution)/shard_map/psum | solution.py:9
  213.8 1.5 constant_dynamic-update-slice_fusion.1
  215.3 1.4 constant_dynamic-update-slice_fusion
  216.7 0.0 copy-done.2
  216.7 0.0 copy-done.1
  216.7 7.6 %bitcast_subtract_fusion = f32[1024,1024]{1,0:T(8,128)S(1)} fusion(f32[1024,1024]{1,0:T(8,128)S(1)} %copy-done.1, f32[512,1024]{1,0:T(8,128)S(1)} %constant_dynamic-update-slice_fusion, f32[1024,512]{1,0:T(8,128)S(1)} %copy-done.2), kind=kOutput, calls=%fused_computation.2 | convolution fusion | flops 6443499520 | bytes 12582912 | tf_op jit(solution)/shard_map/dot_general | solution.py:33
  224.3 1.0 fusion.9
  225.3 0.3 copy_bitcast_fusion
  225.6 97.4 %all_to_all.19 = f32[1024,8,128]{2,0,1:T(8,128)S(1)} all-to-all(f32[1024,8,128]{2,0,1:T(8,128)S(1)} %copy_bitcast_fusion), channel_id=1, replica_groups=mesh['row'=4,'vec'=8] {'vec'}, dimensions={1} | all-to-all | bytes 8388608 | tf_op jit(solution)/shard_map/all_to_all | solution.py:37
  323.0 2.0 copy.18
  (4 shorter events, 0.0 us)
Async XLA Ops:
  6.5 59.0 %all-gather.2.cloned.1.call-start = ((), (), s32[]{:S(2)}) async-start(), calls=%async_computation.1 | async-start | bytes 4718592 | tf_op jit(solution)/shard_map/all_gather | solution.py:17
  16.7 197.2 %all-reduce.3.cloned.1.call-start = ((), (), s32[]{:S(2)}) async-start(), calls=%async_computation.2 | async-start | bytes 4194304 | tf_op jit(solution)/shard_map/psum | solution.py:9
  16.7 58.3 %copy-start.3 = (f32[2,256,256]{2,1,0:T(8,128)S(1)}, f32[2,256,256]{2,1,0:T(8,128)}, u32[]{:S(2)}) copy-start(f32[2,256,256]{2,1,0:T(8,128)} %param.7) | copy-start | bytes 1572868
  73.0 2.0 copy-start
  81.7 135.0 %copy-start.2 = (f32[1024,512]{1,0:T(8,128)S(1)}, f32[1024,512]{1,0:T(8,128)}, u32[]{:S(2)}) copy-start(f32[1024,512]{1,0:T(8,128)} %param.6) | copy-start | bytes 6291460
  213.8 2.9 copy-start.1
Sparse Core Ops, SparseCore 0:
  16.8 48.6 all-gather.1
  82.9 130.8 all-reduce.2
where the time goes:
time: 336 us; the launch traced here: 332 us
  waiting for transfers between devices  180 us (54%)
  blocking collectives  107 us (32%)
  matrix products  21.4 us (6%)
  between operations  13.5 us (4%)
  local copies, waits for them, and re-layouts  7.25 us (2%)
    psum x1, waiting for transfers between devices, spread(): return lax.psum(jnp.where(mine, value, jnp.zeros_like(value)), axis)  131 us
    all_to_all x1, blocking collectives, on_device(): lax.all_to_all(rotated, 'vec', split_axis=1, concat_axis=0, tiled=True)  97.4 us
    all_gather x1, waiting for transfers between devices, on_device(): ritz_full = lax.all_gather(ritz_full_rows, 'vec', axis=1, tiled=True)  48.8 us
    all_gather x1, blocking collectives, on_device(): ritz_full_rows = lax.all_gather(ritz, 'row', axis=0, tiled=True)  10.1 us
    dot_general x1, matrix products, on_device(): rotated = rotated - jnp.dot(panel_cols, solved, precision=highest)  7.55 us
    dot_general x1, matrix products, on_device(): rotated = jnp.dot(filtered, ritz_full, preferred_element_type=jnp.float32)  7.5 us
  transfers between devices with their start and end apart: 2, of which 2 were waited for; matrix products, arithmetic and copies ran while one was open for 0% of the time, Pallas kernels for 0%

commit v1 on v0

v1 whole, which is shorter than its diff:
```python
import functools

import jax
import jax.numpy as jnp
from jax import lax
from jax.experimental import pallas as pl
from jax.experimental.pallas import tpu as pltpu
from jax.sharding import PartitionSpec as P

ROW, VEC = "row", "vec"


def swapped(value, axis, offset):
    return lax.ppermute(value, axis, [(i, i ^ offset) for i in range(lax.axis_size(axis))])


def split(value):
    high = value.astype(jnp.bfloat16)
    return high, (value - high.astype(jnp.float32)).astype(jnp.bfloat16)


def split_array(value):
    high = lax.reduce_precision(value, 8, 7)
    return high.astype(jnp.bfloat16), (value - high).astype(jnp.bfloat16)


def mul(a, b):
    return jnp.dot(a, b, preferred_element_type=jnp.float32)


def mul3(a, b):
    return mul(a[0], b[0]) + (mul(a[0], b[1]) + mul(a[1], b[0]))


def columns_kernel(
    width, depth,
    flags, filtered, cols_high, cols_low, tail_own, tail_other, cross, inverse, even, odd,
    out, power, solved, solved_high, solved_low, scale,
):
    step = pl.program_id(0)
    tile, half = out.shape[0], even.shape[1]

    @pl.when(step == 0)
    def _():
        own = pl.multiple_of(flags[1] * width, width)
        other = pl.multiple_of((1 - flags[1]) * width, width)
        for piece, ritz in enumerate((even, odd)):
            where = pl.ds(piece * half, half)
            solved[pl.ds(own, width), where] = mul(tail_own[...], ritz[...])
            solved[pl.ds(other, width), where] = mul(tail_other[...], ritz[...])
        last = mul3(split(inverse[1]), split(solved[width:, :]))
        middle = solved[:width, :] - mul3((cross[0], cross[1]), split(last))
        solved[width:, :] = last
        solved[:width, :] = mul3(split(inverse[0]), split(middle))
        high, low = split(solved[...])
        solved_high[...] = high
        solved_low[...] = low
        peak = jnp.concatenate(
            [jnp.max(jnp.abs(ritz[...].astype(jnp.float32)), axis=0, keepdims=True) for ritz in (even, odd)], axis=1
        )
        bound = 8.0 * depth * peak + 2.0 * width * jnp.max(jnp.abs(solved[...]), axis=0, keepdims=True)
        exponent = 14.0 - jnp.floor(jnp.log2(jnp.maximum(bound, 1e-30)))
        scale[...] = jnp.broadcast_to(jnp.exp2(exponent), scale.shape)
        power[...] = jnp.broadcast_to(jnp.exp2(-exponent), power.shape)

    for piece, ritz in enumerate((even, odd)):
        where = pl.ds(piece * half, half)
        total = mul(filtered[...], ritz[...])
        total -= mul(cols_high[...], solved_high[:, where])
        total -= mul(cols_high[...], solved_low[:, where]) + mul(cols_low[...], solved_high[:, where])
        out[:, where] = total * scale[0:1, where]

    @pl.when((flags[0] == 1) & (step >= pl.num_programs(0) - 2 * width // tile))
    def _():
        first = (step - (pl.num_programs(0) - 2 * width // tile)) * tile
        out[...] = solved[pl.ds(pl.multiple_of(first, tile), tile), :] * scale[0:1, :]


def columns(flags, filtered, cols, tails, cross, inverse, even, odd):
    rows, depth = filtered.shape
    width = inverse.shape[1]
    count = even.shape[1] + odd.shape[1]
    tile = 256
    whole = lambda a: pl.BlockSpec(a.shape, lambda i, f: (0,) * a.ndim)
    tiled = lambda a: pl.BlockSpec((tile, a.shape[1]), lambda i, f: (i, 0))
    return pl.pallas_call(
        functools.partial(columns_kernel, width, depth),
        grid_spec=pltpu.PrefetchScalarGridSpec(
            num_scalar_prefetch=1,
            grid=(rows // tile,),
            in_specs=[tiled(filtered), tiled(cols[0]), tiled(cols[1])]
            + [whole(a) for a in (tails[0], tails[1], cross, inverse, even, odd)],
            out_specs=[pl.BlockSpec((tile, count), lambda i, f: (i, 0)), pl.BlockSpec((8, count), lambda i, f: (0, 0))],
            scratch_shapes=[
                pltpu.VMEM((2 * width, count), jnp.float32),
                pltpu.VMEM((2 * width, count), jnp.bfloat16),
                pltpu.VMEM((2 * width, count), jnp.bfloat16),
                pltpu.VMEM((8, count), jnp.float32),
            ],
        ),
        out_shape=[jax.ShapeDtypeStruct((rows, count), jnp.float32), jax.ShapeDtypeStruct((8, count), jnp.float32)],
        compiler_params=pltpu.CompilerParams(vmem_limit_bytes=40 * 1024 * 1024),
        cost_estimate=pl.CostEstimate(
            flops=2 * (rows + 2 * width) * (depth + 6 * width) * count,
            bytes_accessed=filtered.nbytes * 2 + 4 * rows * count,
            transcendentals=0,
        ),
    )(flags, filtered, cols[0], cols[1], tails[0], tails[1], cross, inverse, even, odd)


def on_device(filtered, ritz, panel_cols, panel_inverse):
    rows, depth = filtered.shape
    width = panel_inverse.shape[1]
    n_row, n_vec = lax.axis_size(ROW), lax.axis_size(VEC)
    row, vec = lax.axis_index(ROW), lax.axis_index(VEC)
    core = vec % 2
    block, own_cols = ritz.shape
    is_last = (row == n_row - 1) & (vec == n_vec - 1)
    last = n_row * n_vec - 1
    lower = rows - 2 * width

    cross = jnp.concatenate(split_array(panel_cols[lower : lower + width, width:]), axis=0).reshape(-1, block)
    cross_rows = cross.shape[0] // n_row
    def part_of(r):
        return jnp.concatenate(
            [filtered[lower:, r * block : (r + 1) * block], cross[r * cross_rows : (r + 1) * cross_rows]], axis=0
        )
    part = jnp.where(is_last, part_of(n_row - 1), jnp.zeros((), filtered.dtype))
    for r in range(n_row - 1):
        part += lax.ppermute(part_of(r), (ROW, VEC), [(last, r * n_vec + n_vec - 1)])
    holders, step = [n_vec - 1], n_vec // 2
    while step > 1:
        part += lax.ppermute(part, VEC, [(i, i ^ step) for i in holders])
        holders += [i ^ step for i in holders]
        step //= 2
    half = cross_rows // 2
    def of_core(c):
        return jnp.concatenate([part[c * width : (c + 1) * width], part[2 * width + c * half : 2 * width + (c + 1) * half]])
    mine = jnp.where(core == 1, of_core(1), lax.ppermute(of_core(0), VEC, [(i, i ^ 1) for i in holders]))
    mine = jnp.stack([mine] + [swapped(mine, ROW, q) for q in range(1, n_row)])
    theirs = swapped(mine, VEC, 1)
    tails = [jnp.concatenate(list(t[:, :width]), axis=1) for t in (mine, theirs)]
    pieces = jnp.where(core == 1, jnp.stack([theirs, mine], 1), jnp.stack([mine, theirs], 1))[:, :, width:]
    pieces = jnp.concatenate([lax.dynamic_index_in_dim(pieces, row ^ q, 0) for q in range(n_row)])
    cross = pieces.reshape(2, width, width)

    evens = [ritz] + [swapped(ritz, VEC, k) for k in range(2, n_vec, 2)]
    cut = len(evens) // 2
    def gather(own):
        own = jnp.concatenate(own, axis=1)
        even = jnp.concatenate([own] + [swapped(own, ROW, q) for q in range(1, n_row)], axis=0)
        return even, swapped(even, VEC, 1)

    turned = jnp.concatenate(
        [lax.dynamic_slice_in_dim(filtered, (row ^ q) * block, block, 1) for q in range(n_row)], axis=1
    )
    cols = split_array(panel_cols)
    flags = jnp.stack([is_last.astype(jnp.int32), core])
    far, near = gather(evens[cut:]), gather(evens[:cut])
    far, _ = columns(flags, turned, cols, tails, cross, panel_inverse, *far)
    near, power = columns(flags, turned, cols, tails, cross, panel_inverse, *near)

    power = power[:1, :own_cols]
    out = jnp.zeros((n_vec * rows, own_cols), jnp.float32)
    put = lambda out, value, k: lax.dynamic_update_slice_in_dim(out, value * power, (vec ^ k) * rows, 0)
    offsets = [2 * j + odd for odd in range(2) for j in range(cut)]
    for values, base in ((far, 2 * cut), (near, 0)):
        for i, k in enumerate(offsets):
            value = values[:, i * own_cols : (i + 1) * own_cols]
            if base + k:
                value = swapped(value.astype(jnp.float16), VEC, base + k).astype(jnp.float32)
            out = put(out, value, base + k)
    return out


def solution(mesh):
    in_specs = (P((ROW, VEC), None), P(ROW, VEC), P((ROW, VEC), None), P())
    return jax.shard_map(on_device, mesh=mesh, in_specs=in_specs, out_specs=P(ROW, VEC), check_vma=False)
```

time: 336 us -> 146 us (0.43)
  waiting for transfers between devices: 180 us -> 57.6 us
  blocking collectives: 107 us -> 0 us
  starting transfers between devices: 0.04 us -> 41.5 us
  matrix products: 21.4 us -> 0 us
  Pallas kernels: 0 us -> 18.4 us
  between operations: 13.5 us -> 0.54 us
  local copies, waits for them, and re-layouts: 7.25 us -> 16 us
  other arithmetic: 2.38 us -> 11 us
    psum x1 -> x0, waiting for transfers between devices: 131 us -> none  [spread(): return lax.psum(jnp.where(mine, value, jnp.zeros_like(value)), axis)]
    all_to_all x1 -> x0, blocking collectives: 97.4 us -> none  [on_device(): lax.all_to_all(rotated, 'vec', split_axis=1, concat_axis=0, tiled=True)]
    ppermute x0 -> x28, waiting for transfers between devices: none -> 57.6 us  [the longest x22 53.1 us: swapped(): lax.ppermute(value, axis, [(i, i ^ offset) for i in range(lax.axis_size(a...]
    all_gather x1 -> x0, waiting for transfers between devices: 48.8 us -> none  [on_device(): ritz_full = lax.all_gather(ritz_full_rows, 'vec', axis=1, tiled=True)]
    ppermute x0 -> x28, starting transfers between devices: none -> 41.5 us  [the longest x22 33.7 us: swapped(): lax.ppermute(value, axis, [(i, i ^ offset) for i in range(lax.axis_size(a...]
    dot_general x5 -> x0, matrix products: 21.4 us -> none  [the longest x1 7.55 us: on_device(): rotated = rotated - jnp.dot(panel_cols, solved, precision=highest)]
    pallas_call x0 -> x2, Pallas kernels: none -> 18.4 us  [columns(): pl.pallas_call(functools.partial(columns_kernel, width, depth), grid_spec...]
    all_gather x1 -> x0, blocking collectives: 10.1 us -> none  [on_device(): ritz_full_rows = lax.all_gather(ritz, 'row', axis=0, tiled=True)]
  transfers between devices with their start and end apart: 2 -> 28, of which waited for: 2 -> 9; matrix products, arithmetic and copies ran while one was open for 0% -> 10% of each run, Pallas kernels for 0% -> 13%
where the time goes in v1:
time: 146 us; the launch traced here: 145 us
  waiting for transfers between devices  57.6 us (39%)
  starting transfers between devices  41.5 us (28%)
  Pallas kernels  18.4 us (13%)
  local copies, waits for them, and re-layouts  16 us (11%)
  other arithmetic  11 us (8%)
    ppermute x22, waiting for transfers between devices, swapped(): lax.ppermute(value, axis, [(i, i ^ offset) for i in range(lax.axis_size(a...  53.1 us
    ppermute x22, starting transfers between devices, swapped(): lax.ppermute(value, axis, [(i, i ^ offset) for i in range(lax.axis_size(a...  33.7 us
    pallas_call x2, Pallas kernels, columns(): pl.pallas_call(functools.partial(columns_kernel, width, depth), grid_spec...  18.4 us
    unnamed x20, local copies, waits for them, and re-layouts  8.02 us
    ppermute x2, waiting for transfers between devices, on_device(): part += lax.ppermute(part, VEC, [(i, i ^ step) for i in holders])  4.48 us
    ppermute x3, starting transfers between devices, on_device(): lax.ppermute(part_of(r), (ROW, VEC), [(last, r * n_vec + n_vec - 1)])  3.7 us
  transfers between devices with their start and end apart: 28, of which 9 were waited for; matrix products, arithmetic and copies ran while one was open for 10% of the time, Pallas kernels for 13%

profile of v1, /device:TPU:9, one launch (start us, length us, event | category | flops | bytes accessed | tf_op | source)
XLA Modules:
  0.0 145.0 jit_solution(7437853979576233612)
XLA Ops:
  7.6 1.7 %fusion.3 = bf16[576,512]{1,0:T(8,128)(2,1)S(1)} fusion(bf16[576,512]{1,0:T(8,128)(2,1)} %copy-done.6, bf16[576,512]{1,0:T(8,128)(2,1)} %collective-permute-done.1, bf16[576,512]{1,0:T(8,128)(2,1)} %collective-permute-done, bf16[64,512]{1,0:T(8,128)(2,1)S(1)} %slice.109, bf16[512,512]{1,0:T(8,128)(2,1)S(1)} %get-tuple-element.11, pred[]{:T(512)S(6)} %and.10), kind=kLoop, calls=%fused_computation.12 | loop fusion | flops 3833856 | bytes 2949121 | tf_op jit(solution)/shard_map/add | solution.py:130
  10.7 10.1 %collective-permute-start.10 = (bf16[512,128]{1,0:T(8,128)(2,1)S(1)}, bf16[512,128]{1,0:T(8,128)(2,1)S(1)}, u32[]{:S(2)}, u32[]{:S(2)}) collective-permute-start(bf16[512,128]{1,0:T(8,128)(2,1)S(1)} %copy-done.7), channel_id=1, source_target_pairs={{0,4},{1,5},{2,6},{3,7},{4,0},{5,1},{6,2},{7,3},{8,12},{9,13},{10,... | collective-permute-start | bytes 393224 | tf_op jit(solution)/shard_map/ppermute | solution.py:14
  21.0 2.5 %constant_dynamic-slice_fusion.7 = (bf16[1024,512]{1,0:T(8,128)(2,1)S(1)}, bf16[1024,512]{1,0:T(8,128)(2,1)S(1)}, bf16[1024,512]{1,0:T(8,128)(2,1)S(1)}, bf16[1024,512]{1,0:T(8,128)(2,1)S(1)}) fusion(bf16[1024,2048]{1,0:T(8,128)(2,1)} %param.4, s32[]{:T(128)S(6)} %select_n.81, s32[]{:T(128)S(6)} %select_n.84, s32[]{:T(128)S(6)} %select_n.83, s32[]{:T(128)S(6)} %select_n.82), kind=kLoop, calls=%fused_computation.52 | loop fusion | bytes 8388624 | tf_op jit(solution)/shard_map/dynamic_slice | solution.py:155
  23.5 4.5 %collective-permute-done.3 = bf16[576,512]{1,0:T(8,128)(2,1)S(1)} collective-permute-done((bf16[576,512]{1,0:T(8,128)(2,1)S(1)}, bf16[576,512]{1,0:T(8,128)(2,1)S(1)}, u32[]{:S(2)}, u32[]{:S(2)}) %collective-permute-start.3) | collective-permute-done | bytes 589856 | tf_op jit(solution)/shard_map/ppermute | solution.py:133
  29.4 2.3 %pad_maximum_fusion.filtered = bf16[1024,2048]{1,0:T(8,128)(2,1)} fusion(bf16[1024,512]{1,0:T(8,128)(2,1)S(1)} %get-tuple-element.16, bf16[1024,512]{1,0:T(8,128)(2,1)S(1)} %get-tuple-element.17, bf16[1024,512]{1,0:T(8,128)(2,1)S(1)} %get-tuple-element.18, bf16[1024,512]{1,0:T(8,128)(2,1)S(1)} %get-tuple-element.15), kind=kLoop, calls=%fused_computation | loop fusion | flops 16777216 | bytes 8388608 | tf_op jit(solution)/shard_map/concatenate | solution.py:154
  33.5 3.0 %collective-permute-start.18 = (bf16[512,256]{1,0:T(8,128)(2,1)S(1)}, bf16[512,256]{1,0:T(8,128)(2,1)S(1)}, u32[]{:S(2)}, u32[]{:S(2)}) collective-permute-start(bf16[512,256]{1,0:T(8,128)(2,1)S(1)} %constant_dynamic-update-slice_fusion.2), channel_id=1, source_target_pairs={{0,8},{8,0},{16,24},{24,16},{1,9},{9,1},{17,25},{25,17},{2,10},{10... | collective-permute-start | bytes 786440 | tf_op jit(solution)/shard_map/ppermute | solution.py:14
  36.5 3.6 %collective-permute-start.19 = (bf16[512,256]{1,0:T(8,128)(2,1)S(1)}, bf16[512,256]{1,0:T(8,128)(2,1)S(1)}, u32[]{:S(2)}, u32[]{:S(2)}) collective-permute-start(bf16[512,256]{1,0:T(8,128)(2,1)S(1)} %constant_dynamic-update-slice_fusion.2), channel_id=1, source_target_pairs={{0,16},{8,24},{16,0},{24,8},{1,17},{9,25},{17,1},{25,9},{2,18},{10... | collective-permute-start | bytes 786440 | tf_op jit(solution)/shard_map/ppermute | solution.py:14
  40.2 3.2 %collective-permute-start.20 = (bf16[512,256]{1,0:T(8,128)(2,1)S(1)}, bf16[512,256]{1,0:T(8,128)(2,1)S(1)}, u32[]{:S(2)}, u32[]{:S(2)}) collective-permute-start(bf16[512,256]{1,0:T(8,128)(2,1)S(1)} %constant_dynamic-update-slice_fusion.2), channel_id=1, source_target_pairs={{0,24},{8,16},{16,8},{24,0},{1,25},{9,17},{17,9},{25,1},{2,26},{10... | collective-permute-start | bytes 786440 | tf_op jit(solution)/shard_map/ppermute | solution.py:14
  46.7 2.0 %collective-permute-start.12 = (bf16[512,256]{1,0:T(8,128)(2,1)S(1)}, bf16[512,256]{1,0:T(8,128)(2,1)S(1)}, u32[]{:S(2)}, u32[]{:S(2)}) collective-permute-start(bf16[512,256]{1,0:T(8,128)(2,1)S(1)} %constant_dynamic-update-slice_fusion), channel_id=1, source_target_pairs={{0,8},{8,0},{16,24},{24,16},{1,9},{9,1},{17,25},{25,17},{2,10},{10... | collective-permute-start | bytes 786440 | tf_op jit(solution)/shard_map/ppermute | solution.py:14
  51.7 3.2 %collective-permute-done.12 = bf16[512,256]{1,0:T(8,128)(2,1)S(1)} collective-permute-done((bf16[512,256]{1,0:T(8,128)(2,1)S(1)}, bf16[512,256]{1,0:T(8,128)(2,1)S(1)}, u32[]{:S(2)}, u32[]{:S(2)}) %collective-permute-start.12) | collective-permute-done | bytes 262176 | tf_op jit(solution)/shard_map/ppermute | solution.py:14
  54.9 6.9 %collective-permute-done.13 = bf16[512,256]{1,0:T(8,128)(2,1)S(1)} collective-permute-done((bf16[512,256]{1,0:T(8,128)(2,1)S(1)}, bf16[512,256]{1,0:T(8,128)(2,1)S(1)}, u32[]{:S(2)}, u32[]{:S(2)}) %collective-permute-start.13) | collective-permute-done | bytes 262176 | tf_op jit(solution)/shard_map/ppermute | solution.py:14
  62.5 4.3 %collective-permute-done.6 = bf16[288,512]{1,0:T(8,128)(2,1)S(1)} collective-permute-done((bf16[288,512]{1,0:T(8,128)(2,1)S(1)}, bf16[288,512]{1,0:T(8,128)(2,1)S(1)}, u32[]{:S(2)}, u32[]{:S(2)}) %collective-permute-start.6) | collective-permute-done | bytes 294944 | tf_op jit(solution)/shard_map/ppermute | solution.py:14
  66.8 5.4 %collective-permute-done.7 = bf16[288,512]{1,0:T(8,128)(2,1)S(1)} collective-permute-done((bf16[288,512]{1,0:T(8,128)(2,1)S(1)}, bf16[288,512]{1,0:T(8,128)(2,1)S(1)}, u32[]{:S(2)}, u32[]{:S(2)}) %collective-permute-start.7) | collective-permute-done | bytes 294944 | tf_op jit(solution)/shard_map/ppermute | solution.py:14
  72.7 2.6 %collective-permute-done.9 = bf16[4,288,512]{2,1,0:T(8,128)(2,1)S(1)} collective-permute-done((bf16[4,288,512]{2,1,0:T(8,128)(2,1)S(1)}, bf16[4,288,512]{2,1,0:T(8,128)(2,1)S(1)}, u32[]{:S(2)}, u32[]{:S(2)}) %collective-permute-start.9) | collective-permute-done | bytes 1179680 | tf_op jit(solution)/shard_map/ppermute | solution.py:14
  80.1 2.2 %copy-done = bf16[1024,2048]{1,0:T(8,128)(2,1)S(1)} copy-done((bf16[1024,2048]{1,0:T(8,128)(2,1)S(1)}, bf16[1024,2048]{1,0:T(8,128)(2,1)}, u32[]{:S(2)}) %copy-start) | copy-done | bytes 4194328
  83.3 9.5 %shard_map.46 = (f32[1024,512]{1,0:T(8,128)S(1)}, f32[8,512]{1,0:T(8,128)}) custom-call(s32[2]{0:T(128)S(1)} %pad_add_fusion.flags, bf16[1024,2048]{1,0:T(8,128)(2,1)S(1)} %copy-done, bf16[1024,512]{1,0:T(8,128)(2,1)S(1)} %copy-done.2, bf16[1024,512]{1,0:T(8,128)(2,1)S(1)} %copy-done.1, bf16[256,2048]{1,0:T(8,128)(2,1)S(1)} %pad_maximum_fusion.2.tail_own, ...), custom_call_target="tpu_custom_call" | custom-call | flops 5637144576 | bytes 10485760 | tf_op jit(solution)/shard_map/pallas_call | solution.py:86
  93.7 8.9 %shard_map.47 = (f32[1024,512]{1,0:T(8,128)S(1)}, f32[8,512]{1,0:T(8,128)S(1)}) custom-call(s32[2]{0:T(128)S(1)} %pad_add_fusion.flags, bf16[1024,2048]{1,0:T(8,128)(2,1)S(1)} %copy-done, bf16[1024,512]{1,0:T(8,128)(2,1)S(1)} %copy-done.2, bf16[1024,512]{1,0:T(8,128)(2,1)S(1)} %copy-done.1, bf16[256,2048]{1,0:T(8,128)(2,1)S(1)} %pad_maximum_fusion.2.tail_own, ...), custom_call_target="tpu_custom_call" | custom-call | flops 5637144576 | bytes 10485760 | tf_op jit(solution)/shard_map/pallas_call | solution.py:86
  102.6 2.7 %collective-permute-start.22 = (f16[1024,128]{1,0:T(8,128)(2,1)S(1)}, f16[1024,128]{1,0:T(8,128)(2,1)S(1)}, u32[]{:S(2)}, u32[]{:S(2)}) collective-permute-start(f16[1024,128]{1,0:T(8,128)(2,1)S(1)} %get-tuple-element.34), channel_id=1, source_target_pairs={{0,6},{1,7},{2,4},{3,5},{4,2},{5,3},{6,0},{7,1},{8,14},{9,15},{10,... | collective-permute-start | bytes 786440 | tf_op jit(solution)/shard_map/ppermute | solution.py:14
  105.3 1.9 %collective-permute-start.23 = (f16[1024,128]{1,0:T(8,128)(2,1)S(1)}, f16[1024,128]{1,0:T(8,128)(2,1)S(1)}, u32[]{:S(2)}, u32[]{:S(2)}) collective-permute-start(f16[1024,128]{1,0:T(8,128)(2,1)S(1)} %get-tuple-element.33), channel_id=1, source_target_pairs={{0,5},{1,4},{2,7},{3,6},{4,1},{5,0},{6,3},{7,2},{8,13},{9,12},{10,... | collective-permute-start | bytes 786440 | tf_op jit(solution)/shard_map/ppermute | solution.py:14
  107.7 1.9 %collective-permute-start.25 = (f16[1024,128]{1,0:T(8,128)(2,1)S(1)}, f16[1024,128]{1,0:T(8,128)(2,1)S(1)}, u32[]{:S(2)}, u32[]{:S(2)}) collective-permute-start(f16[1024,128]{1,0:T(8,128)(2,1)S(1)} %get-tuple-element.31), channel_id=1, source_target_pairs={{0,2},{1,3},{2,0},{3,1},{4,6},{5,7},{6,4},{7,5},{8,10},{9,11},{10,... | collective-permute-start | bytes 786440 | tf_op jit(solution)/shard_map/ppermute | solution.py:14
  111.0 19.6 %collective-permute-done.22 = f16[1024,128]{1,0:T(8,128)(2,1)S(1)} collective-permute-done((f16[1024,128]{1,0:T(8,128)(2,1)S(1)}, f16[1024,128]{1,0:T(8,128)(2,1)S(1)}, u32[]{:S(2)}, u32[]{:S(2)}) %collective-permute-start.22) | collective-permute-done | bytes 262176 | tf_op jit(solution)/shard_map/ppermute | solution.py:14
  130.7 3.0 %collective-permute-done.23 = f16[1024,128]{1,0:T(8,128)(2,1)S(1)} collective-permute-done((f16[1024,128]{1,0:T(8,128)(2,1)S(1)}, f16[1024,128]{1,0:T(8,128)(2,1)S(1)}, u32[]{:S(2)}, u32[]{:S(2)}) %collective-permute-start.23) | collective-permute-done | bytes 262176 | tf_op jit(solution)/shard_map/ppermute | solution.py:14
  133.7 8.2 %collective-permute-done.24 = f16[1024,128]{1,0:T(8,128)(2,1)S(1)} collective-permute-done((f16[1024,128]{1,0:T(8,128)(2,1)S(1)}, f16[1024,128]{1,0:T(8,128)(2,1)S(1)}, u32[]{:S(2)}, u32[]{:S(2)}) %collective-permute-start.24) | collective-permute-done | bytes 262176 | tf_op jit(solution)/shard_map/ppermute | solution.py:14
  142.2 2.0 %copy-done.4 = f32[8192,128]{1,0:T(8,128)} copy-done((f32[8192,128]{1,0:T(8,128)}, f32[8192,128]{1,0:T(8,128)S(1)}, u32[]{:S(2)}) %copy-start.4) | copy-done | bytes 4194328
  (106 shorter events, 29.4 us)
Async XLA Ops:
  9.3 18.6 %collective-permute-start.3 = (bf16[576,512]{1,0:T(8,128)(2,1)S(1)}, bf16[576,512]{1,0:T(8,128)(2,1)S(1)}, u32[]{:S(2)}, u32[]{:S(2)}) collective-permute-start(bf16[576,512]{1,0:T(8,128)(2,1)S(1)} %fusion.3), channel_id=1, source_target_pairs={{7,3},{15,11},{23,19},{31,27}} | collective-permute-start | bytes 1769480 | tf_op jit(solution)/shard_map/ppermute | solution.py:133
  10.6 22.9 %collective-permute-start.17 = (bf16[512,128]{1,0:T(8,128)(2,1)S(1)}, bf16[512,128]{1,0:T(8,128)(2,1)S(1)}, u32[]{:S(2)}, u32[]{:S(2)}) collective-permute-start(bf16[512,128]{1,0:T(8,128)(2,1)S(1)} %copy-done.7), channel_id=1, source_target_pairs={{0,2},{1,3},{2,0},{3,1},{4,6},{5,7},{6,4},{7,5},{8,10},{9,11},{10,... | collective-permute-start | bytes 393224 | tf_op jit(solution)/shard_map/ppermute | solution.py:14
  10.7 32.9 %collective-permute-start.10 = (bf16[512,128]{1,0:T(8,128)(2,1)S(1)}, bf16[512,128]{1,0:T(8,128)(2,1)S(1)}, u32[]{:S(2)}, u32[]{:S(2)}) collective-permute-start(bf16[512,128]{1,0:T(8,128)(2,1)S(1)} %copy-done.7), channel_id=1, source_target_pairs={{0,4},{1,5},{2,6},{3,7},{4,0},{5,1},{6,2},{7,3},{8,12},{9,13},{10,... | collective-permute-start | bytes 393224 | tf_op jit(solution)/shard_map/ppermute | solution.py:14
  20.8 25.9 %collective-permute-start.11 = (bf16[512,128]{1,0:T(8,128)(2,1)S(1)}, bf16[512,128]{1,0:T(8,128)(2,1)S(1)}, u32[]{:S(2)}, u32[]{:S(2)}) collective-permute-start(bf16[512,128]{1,0:T(8,128)(2,1)S(1)} %copy-done.7), channel_id=1, source_target_pairs={{0,6},{1,7},{2,4},{3,5},{4,2},{5,3},{6,0},{7,1},{8,14},{9,15},{10,... | collective-permute-start | bytes 393224 | tf_op jit(solution)/shard_map/ppermute | solution.py:14
  28.1 12.1 %collective-permute-start.4 = (bf16[576,512]{1,0:T(8,128)(2,1)S(1)}, bf16[576,512]{1,0:T(8,128)(2,1)S(1)}, u32[]{:S(2)}, u32[]{:S(2)}) collective-permute-start(bf16[576,512]{1,0:T(8,128)(2,1)S(1)} %add.76), channel_id=1, source_target_pairs={{7,5},{3,1},{15,13},{11,9},{23,21},{19,17},{31,29},{27,25}} | collective-permute-start | bytes 1769480 | tf_op jit(solution)/shard_map/ppermute | solution.py:133
  33.5 15.3 %collective-permute-start.18 = (bf16[512,256]{1,0:T(8,128)(2,1)S(1)}, bf16[512,256]{1,0:T(8,128)(2,1)S(1)}, u32[]{:S(2)}, u32[]{:S(2)}) collective-permute-start(bf16[512,256]{1,0:T(8,128)(2,1)S(1)} %constant_dynamic-update-slice_fusion.2), channel_id=1, source_target_pairs={{0,8},{8,0},{16,24},{24,16},{1,9},{9,1},{17,25},{25,17},{2,10},{10... | collective-permute-start | bytes 786440 | tf_op jit(solution)/shard_map/ppermute | solution.py:14
  36.5 13.6 %collective-permute-start.19 = (bf16[512,256]{1,0:T(8,128)(2,1)S(1)}, bf16[512,256]{1,0:T(8,128)(2,1)S(1)}, u32[]{:S(2)}, u32[]{:S(2)}) collective-permute-start(bf16[512,256]{1,0:T(8,128)(2,1)S(1)} %constant_dynamic-update-slice_fusion.2), channel_id=1, source_target_pairs={{0,16},{8,24},{16,0},{24,8},{1,17},{9,25},{17,1},{25,9},{2,18},{10... | collective-permute-start | bytes 786440 | tf_op jit(solution)/shard_map/ppermute | solution.py:14
  40.2 11.4 %collective-permute-start.20 = (bf16[512,256]{1,0:T(8,128)(2,1)S(1)}, bf16[512,256]{1,0:T(8,128)(2,1)S(1)}, u32[]{:S(2)}, u32[]{:S(2)}) collective-permute-start(bf16[512,256]{1,0:T(8,128)(2,1)S(1)} %constant_dynamic-update-slice_fusion.2), channel_id=1, source_target_pairs={{0,24},{8,16},{16,8},{24,0},{1,25},{9,17},{17,9},{25,1},{2,26},{10... | collective-permute-start | bytes 786440 | tf_op jit(solution)/shard_map/ppermute | solution.py:14
  44.3 4.5 %collective-permute-start.5 = (bf16[288,512]{1,0:T(8,128)(2,1)S(1)}, bf16[288,512]{1,0:T(8,128)(2,1)S(1)}, u32[]{:S(2)}, u32[]{:S(2)}) collective-permute-start(bf16[288,512]{1,0:T(8,128)(2,1)S(1)} %pad_maximum_fusion.9), channel_id=1, source_target_pairs={{7,6},{3,2},{5,4},{1,0},{15,14},{11,10},{13,12},{9,8},{23,22},{19,... | collective-permute-start | bytes 884744 | tf_op jit(solution)/shard_map/ppermute | solution.py:139
  46.7 8.1 %collective-permute-start.12 = (bf16[512,256]{1,0:T(8,128)(2,1)S(1)}, bf16[512,256]{1,0:T(8,128)(2,1)S(1)}, u32[]{:S(2)}, u32[]{:S(2)}) collective-permute-start(bf16[512,256]{1,0:T(8,128)(2,1)S(1)} %constant_dynamic-update-slice_fusion), channel_id=1, source_target_pairs={{0,8},{8,0},{16,24},{24,16},{1,9},{9,1},{17,25},{25,17},{2,10},{10... | collective-permute-start | bytes 786440 | tf_op jit(solution)/shard_map/ppermute | solution.py:14
  48.8 13.0 %collective-permute-start.13 = (bf16[512,256]{1,0:T(8,128)(2,1)S(1)}, bf16[512,256]{1,0:T(8,128)(2,1)S(1)}, u32[]{:S(2)}, u32[]{:S(2)}) collective-permute-start(bf16[512,256]{1,0:T(8,128)(2,1)S(1)} %constant_dynamic-update-slice_fusion), channel_id=1, source_target_pairs={{0,16},{8,24},{16,0},{24,8},{1,17},{9,25},{17,1},{25,9},{2,18},{10... | collective-permute-start | bytes 786440 | tf_op jit(solution)/shard_map/ppermute | solution.py:14
  48.8 13.0 %collective-permute-start.14 = (bf16[512,256]{1,0:T(8,128)(2,1)S(1)}, bf16[512,256]{1,0:T(8,128)(2,1)S(1)}, u32[]{:S(2)}, u32[]{:S(2)}) collective-permute-start(bf16[512,256]{1,0:T(8,128)(2,1)S(1)} %constant_dynamic-update-slice_fusion), channel_id=1, source_target_pairs={{0,24},{8,16},{16,8},{24,0},{1,25},{9,17},{17,9},{25,1},{2,26},{10... | collective-permute-start | bytes 786440 | tf_op jit(solution)/shard_map/ppermute | solution.py:14
  50.2 16.6 %collective-permute-start.6 = (bf16[288,512]{1,0:T(8,128)(2,1)S(1)}, bf16[288,512]{1,0:T(8,128)(2,1)S(1)}, u32[]{:S(2)}, u32[]{:S(2)}) collective-permute-start(bf16[288,512]{1,0:T(8,128)(2,1)S(1)} %maximum_select_fusion.1), channel_id=1, source_target_pairs={{0,8},{8,0},{16,24},{24,16},{1,9},{9,1},{17,25},{25,17},{2,10},{10... | collective-permute-start | bytes 884744 | tf_op jit(solution)/shard_map/ppermute | solution.py:14
  51.6 20.5 %collective-permute-start.7 = (bf16[288,512]{1,0:T(8,128)(2,1)S(1)}, bf16[288,512]{1,0:T(8,128)(2,1)S(1)}, u32[]{:S(2)}, u32[]{:S(2)}) collective-permute-start(bf16[288,512]{1,0:T(8,128)(2,1)S(1)} %maximum_select_fusion.1), channel_id=1, source_target_pairs={{0,16},{8,24},{16,0},{24,8},{1,17},{9,25},{17,1},{25,9},{2,18},{10... | collective-permute-start | bytes 884744 | tf_op jit(solution)/shard_map/ppermute | solution.py:14
  54.9 17.3 %collective-permute-start.8 = (bf16[288,512]{1,0:T(8,128)(2,1)S(1)}, bf16[288,512]{1,0:T(8,128)(2,1)S(1)}, u32[]{:S(2)}, u32[]{:S(2)}) collective-permute-start(bf16[288,512]{1,0:T(8,128)(2,1)S(1)} %maximum_select_fusion.1), channel_id=1, source_target_pairs={{0,24},{8,16},{16,8},{24,0},{1,25},{9,17},{17,9},{25,1},{2,26},{10... | collective-permute-start | bytes 884744 | tf_op jit(solution)/shard_map/ppermute | solution.py:14
  61.8 31.9 %collective-permute-start.21 = (bf16[2048,256]{1,0:T(8,128)(2,1)S(1)}, bf16[2048,256]{1,0:T(8,128)(2,1)}, u32[]{:S(2)}, u32[]{:S(2)}) collective-permute-start(bf16[2048,256]{1,0:T(8,128)(2,1)S(1)} %pad_maximum_fusion.5.even), channel_id=1, source_target_pairs={{0,1},{1,0},{2,3},{3,2},{4,5},{5,4},{6,7},{7,6},{8,9},{9,8},{10,11... | collective-permute-start | bytes 3145736 | tf_op jit(solution)/shard_map/ppermute | solution.py:14
  61.9 17.8 %collective-permute-start.15 = (bf16[2048,256]{1,0:T(8,128)(2,1)S(1)}, bf16[2048,256]{1,0:T(8,128)(2,1)}, u32[]{:S(2)}, u32[]{:S(2)}) collective-permute-start(bf16[2048,256]{1,0:T(8,128)(2,1)S(1)} %pad_maximum_fusion.4.even), channel_id=1, source_target_pairs={{0,1},{1,0},{2,3},{3,2},{4,5},{5,4},{6,7},{7,6},{8,9},{9,8},{10,11... | collective-permute-start | bytes 3145736 | tf_op jit(solution)/shard_map/ppermute | solution.py:14
  93.2 16.4 %collective-permute-start.16 = (f16[1024,128]{1,0:T(8,128)(2,1)S(1)}, f16[1024,128]{1,0:T(8,128)(2,1)S(1)}, u32[]{:S(2)}, u32[]{:S(2)}) collective-permute-start(f16[1024,128]{1,0:T(8,128)(2,1)S(1)} %get-tuple-element.35), channel_id=1, source_target_pairs={{0,4},{1,5},{2,6},{3,7},{4,0},{5,1},{6,2},{7,3},{8,12},{9,13},{10,... | collective-permute-start | bytes 786440 | tf_op jit(solution)/shard_map/ppermute | solution.py:14
  102.6 28.0 %collective-permute-start.22 = (f16[1024,128]{1,0:T(8,128)(2,1)S(1)}, f16[1024,128]{1,0:T(8,128)(2,1)S(1)}, u32[]{:S(2)}, u32[]{:S(2)}) collective-permute-start(f16[1024,128]{1,0:T(8,128)(2,1)S(1)} %get-tuple-element.34), channel_id=1, source_target_pairs={{0,6},{1,7},{2,4},{3,5},{4,2},{5,3},{6,0},{7,1},{8,14},{9,15},{10,... | collective-permute-start | bytes 786440 | tf_op jit(solution)/shard_map/ppermute | solution.py:14
  105.3 28.3 %collective-permute-start.23 = (f16[1024,128]{1,0:T(8,128)(2,1)S(1)}, f16[1024,128]{1,0:T(8,128)(2,1)S(1)}, u32[]{:S(2)}, u32[]{:S(2)}) collective-permute-start(f16[1024,128]{1,0:T(8,128)(2,1)S(1)} %get-tuple-element.33), channel_id=1, source_target_pairs={{0,5},{1,4},{2,7},{3,6},{4,1},{5,0},{6,3},{7,2},{8,13},{9,12},{10,... | collective-permute-start | bytes 786440 | tf_op jit(solution)/shard_map/ppermute | solution.py:14
  107.2 34.7 %collective-permute-start.24 = (f16[1024,128]{1,0:T(8,128)(2,1)S(1)}, f16[1024,128]{1,0:T(8,128)(2,1)S(1)}, u32[]{:S(2)}, u32[]{:S(2)}) collective-permute-start(f16[1024,128]{1,0:T(8,128)(2,1)S(1)} %get-tuple-element.32), channel_id=1, source_target_pairs={{0,7},{1,6},{2,5},{3,4},{4,3},{5,2},{6,1},{7,0},{8,15},{9,14},{10,... | collective-permute-start | bytes 786440 | tf_op jit(solution)/shard_map/ppermute | solution.py:14
  107.7 34.3 %collective-permute-start.25 = (f16[1024,128]{1,0:T(8,128)(2,1)S(1)}, f16[1024,128]{1,0:T(8,128)(2,1)S(1)}, u32[]{:S(2)}, u32[]{:S(2)}) collective-permute-start(f16[1024,128]{1,0:T(8,128)(2,1)S(1)} %get-tuple-element.31), channel_id=1, source_target_pairs={{0,2},{1,3},{2,0},{3,1},{4,6},{5,7},{6,4},{7,5},{8,10},{9,11},{10,... | collective-permute-start | bytes 786440 | tf_op jit(solution)/shard_map/ppermute | solution.py:14
  109.6 32.5 %collective-permute-start.26 = (f16[1024,128]{1,0:T(8,128)(2,1)S(1)}, f16[1024,128]{1,0:T(8,128)(2,1)S(1)}, u32[]{:S(2)}, u32[]{:S(2)}) collective-permute-start(f16[1024,128]{1,0:T(8,128)(2,1)S(1)} %get-tuple-element.30), channel_id=1, source_target_pairs={{0,1},{1,0},{2,3},{3,2},{4,5},{5,4},{6,7},{7,6},{8,9},{9,8},{10,11... | collective-permute-start | bytes 786440 | tf_op jit(solution)/shard_map/ppermute | solution.py:14
  130.6 11.6 %collective-permute-start.27 = (f16[1024,128]{1,0:T(8,128)(2,1)S(1)}, f16[1024,128]{1,0:T(8,128)(2,1)S(1)}, u32[]{:S(2)}, u32[]{:S(2)}) collective-permute-start(f16[1024,128]{1,0:T(8,128)(2,1)S(1)} %get-tuple-element.29), channel_id=1, source_target_pairs={{0,3},{1,2},{2,1},{3,0},{4,7},{5,6},{6,5},{7,4},{8,11},{9,10},{10,... | collective-permute-start | bytes 786440 | tf_op jit(solution)/shard_map/ppermute | solution.py:14
  (13 other events, 27.2 us)

commit v2 on v0

v2 whole, which is shorter than its diff:
```python
import functools

import jax
import jax.numpy as jnp
from jax import lax
from jax.experimental import pallas as pl
from jax.experimental.pallas import tpu as pltpu
from jax.sharding import PartitionSpec as P

ROW, VEC = "row", "vec"
TILE = 256
VMEM_LIMIT = 48 * 1024 * 1024


def swapped(value, axis, offset):
    return lax.ppermute(value, axis, [(i, i ^ offset) for i in range(lax.axis_size(axis))])


def split(value):
    high = value.astype(jnp.bfloat16)
    return high, (value - high.astype(jnp.float32)).astype(jnp.bfloat16)


def split_array(value):
    high = lax.reduce_precision(value, 8, 7)
    return high.astype(jnp.bfloat16), (value - high).astype(jnp.bfloat16)


def mul(a, b):
    return jnp.dot(a, b, preferred_element_type=jnp.float32)


def mul3(a, b):
    return mul(a[0], b[0]) + (mul(a[0], b[1]) + mul(a[1], b[0]))


def rotate_kernel(n_row, flags, filtered, *refs):
    even, odd, out, peak = refs[:n_row], refs[n_row : 2 * n_row], refs[-2], refs[-1]
    block, half = even[0].shape
    for piece, ritz in enumerate((even, odd)):
        where = pl.ds(piece * half, half)

        @pl.loop(0, out.shape[0] // TILE)
        def _(i):
            rows = pl.ds(pl.multiple_of(i * TILE, TILE), TILE)
            total = None
            for q in range(n_row):
                start = pl.multiple_of((flags[2] ^ q) * block, block)
                term = mul(filtered[rows, pl.ds(start, block)], ritz[q][...])
                total = term if total is None else total + term
            out[rows, where] = total

        most = functools.reduce(
            jnp.maximum, [jnp.max(jnp.abs(r[...].astype(jnp.float32)), axis=0, keepdims=True) for r in ritz]
        )
        peak[:, where] = jnp.broadcast_to(most, (peak.shape[0], half))


def finish_kernel(n_row, width, depth, first, flags, rotated, peak, cols_high, cols_low, inverse, *refs):
    refs = list(refs)
    take = lambda: [refs.pop(0) for _ in range(n_row)]
    outer, inner, even, odd = take(), take(), take(), take()
    out, power, solved, cross, high_ref, low_ref = refs
    half = out.shape[1] // 2
    whole = even[0].shape[1]
    block = even[0].shape[0]
    cross_rows = cross.shape[0] // n_row

    def tail(parts):
        for piece, ritz in enumerate((even, odd)):
            total = None
            for q in range(n_row):
                term = mul(parts[q][: 2 * width, :], ritz[q][:, first : first + half])
                total = term if total is None else total + term
            solved[:, piece * half : (piece + 1) * half] = total
        for q in range(n_row):
            start = pl.multiple_of((flags[2] ^ q) * cross_rows, cross_rows)
            cross[pl.ds(start, cross_rows), :] = parts[q][2 * width :, :]

    pl.when(flags[1] == 1)(lambda: tail(outer))
    pl.when(flags[1] == 0)(lambda: tail(inner))

    if block == 2 * width:
        between = cross[:, :width], cross[:, width:]
    else:
        between = cross[:width, :], cross[width:, :]
    last = mul3(split(inverse[1]), split(solved[width:, :]))
    middle = solved[:width, :] - mul3(between, split(last))
    solved[width:, :] = last
    solved[:width, :] = mul3(split(inverse[0]), split(middle))
    high_ref[...], low_ref[...] = split(solved[...])
    most = jnp.concatenate([peak[0:1, first : first + half], peak[0:1, whole + first : whole + first + half]], axis=1)
    bound = 8.0 * depth * most + 2.0 * width * jnp.max(jnp.abs(solved[...]), axis=0, keepdims=True)
    exponent = 14.0 - jnp.floor(jnp.log2(jnp.maximum(bound, 1e-30)))
    scale = jnp.exp2(exponent)
    power[...] = jnp.broadcast_to(jnp.exp2(-exponent), power.shape)

    rows = out.shape[0]
    for piece in range(2):
        where = slice(piece * half, (piece + 1) * half)
        start = piece * whole + first

        @pl.loop(0, rows // TILE)
        def _(i):
            at = pl.ds(pl.multiple_of(i * TILE, TILE), TILE)
            total = mul(cols_high[at, :], high_ref[:, where])
            total += mul(cols_high[at, :], low_ref[:, where]) + mul(cols_low[at, :], high_ref[:, where])
            out[at, where] = (rotated[at, start : start + half] - total) * scale[:, where]

    @pl.when(flags[0] == 1)
    def _():
        out[rows - 2 * width :, :] = solved[...] * scale


def call(kernel, flags, inputs, out_shape, scratch, flops):
    return pl.pallas_call(
        kernel,
        in_specs=[pl.BlockSpec(memory_space=pltpu.SMEM)] + [pl.BlockSpec(memory_space=pltpu.VMEM)] * len(inputs),
        out_specs=[pl.BlockSpec(memory_space=pltpu.VMEM)] * len(out_shape),
        out_shape=out_shape,
        scratch_shapes=scratch,
        compiler_params=pltpu.CompilerParams(vmem_limit_bytes=VMEM_LIMIT),
        cost_estimate=pl.CostEstimate(
            flops=flops, bytes_accessed=sum(a.nbytes for a in inputs), transcendentals=0
        ),
    )(flags, *inputs)


def on_device(filtered, ritz, panel_cols, panel_inverse):
    rows, depth = filtered.shape
    width = panel_inverse.shape[1]
    n_row, n_vec = lax.axis_size(ROW), lax.axis_size(VEC)
    row, vec = lax.axis_index(ROW), lax.axis_index(VEC)
    core = vec % 2
    block, own_cols = ritz.shape
    is_last = (row == n_row - 1) & (vec == n_vec - 1)
    last = n_row * n_vec - 1
    lower = rows - 2 * width

    evens = [ritz] + [swapped(ritz, VEC, k) for k in range(2, n_vec, 2)]
    cut = len(evens) // 2

    cross = jnp.concatenate(split_array(panel_cols[lower : lower + width, width:]), axis=1 if block == 2 * width else 0)
    cross_rows = cross.shape[0] // n_row
    def part_of(r):
        return jnp.concatenate(
            [filtered[lower:, r * block : (r + 1) * block], cross[r * cross_rows : (r + 1) * cross_rows]], axis=0
        )
    part = jnp.where(is_last, part_of(n_row - 1), jnp.zeros((), filtered.dtype))
    for r in range(n_row - 1):
        part += lax.ppermute(part_of(r), (ROW, VEC), [(last, r * n_vec + n_vec - 1)])
    holders, step = [n_vec - 1], n_vec // 2
    while step > 1:
        part += lax.ppermute(part, VEC, [(i, i ^ step) for i in holders])
        holders += [i ^ step for i in holders]
        step //= 2
    outer = [part] + [
        lax.ppermute(part, (ROW, VEC), [(r * n_vec + i, (r ^ q) * n_vec + i) for r in range(n_row) for i in holders])
        for q in range(1, n_row)
    ]
    inner = [lax.ppermute(p, VEC, [(i, i ^ 1) for i in holders]) for p in outer]

    own = jnp.concatenate(evens, axis=1)
    even = [own] + [swapped(own, ROW, q) for q in range(1, n_row)]
    odd = [swapped(e, VEC, 1) for e in even]

    flags = jnp.stack([is_last.astype(jnp.int32), core, row])
    count = n_vec * own_cols
    rotated, peak = call(
        functools.partial(rotate_kernel, n_row), flags, [filtered, *even, *odd],
        [jax.ShapeDtypeStruct((rows, count), jnp.float32), jax.ShapeDtypeStruct((8, count), jnp.float32)],
        [], 2 * rows * depth * count,
    )
    cols = split_array(panel_cols)

    def finish(flags, first):
        return call(
            functools.partial(finish_kernel, n_row, width, depth, first), flags,
            [rotated, peak, *cols, panel_inverse, *outer, *inner, *even, *odd],
            [jax.ShapeDtypeStruct((rows, count // 2), jnp.float32), jax.ShapeDtypeStruct((8, count // 2), jnp.float32)],
            [pltpu.VMEM((2 * width, count // 2), jnp.float32), pltpu.VMEM(cross.shape, jnp.bfloat16)]
            + [pltpu.VMEM((2 * width, count // 2), jnp.bfloat16)] * 2,
            width * (depth + 6 * rows) * count,
        )

    offsets = [2 * j + side for side in range(2) for j in range(cut)]
    piece = lambda values, i: values[:, i * own_cols : (i + 1) * own_cols]
    far, _ = finish(flags, cut * own_cols)
    far = [piece(far, i).astype(jnp.float16) for i in range(2 * cut)]
    far, flags = lax.optimization_barrier((far, flags))
    sent = {2 * cut + k: swapped(f, VEC, 2 * cut + k) for f, k in zip(far, offsets)}
    near, power = finish(flags, 0)
    power = power[:1, :own_cols]
    for i, k in enumerate(offsets):
        sent[k] = swapped(piece(near, i).astype(jnp.float16), VEC, k) if k else piece(near, i)
    out = jnp.zeros((n_vec * rows, own_cols), jnp.float32)
    for k, value in sorted(sent.items()):
        out = lax.dynamic_update_slice_in_dim(out, value.astype(jnp.float32) * power, (vec ^ k) * rows, 0)
    return out


def solution(mesh):
    in_specs = (P((ROW, VEC), None), P(ROW, VEC), P((ROW, VEC), None), P())
    return jax.shard_map(on_device, mesh=mesh, in_specs=in_specs, out_specs=P(ROW, VEC), check_vma=False)
```

time: 336 us -> 163 us (0.49)
  waiting for transfers between devices: 180 us -> 60.1 us
  blocking collectives: 107 us -> 0 us
  starting transfers between devices: 0.04 us -> 51.7 us
  Pallas kernels: 0 us -> 31.6 us
  matrix products: 21.4 us -> 0 us
  between operations: 13.5 us -> 0.39 us
  other arithmetic: 2.38 us -> 10.2 us
    psum x1 -> x0, waiting for transfers between devices: 131 us -> none  [spread(): return lax.psum(jnp.where(mine, value, jnp.zeros_like(value)), axis)]
    all_to_all x1 -> x0, blocking collectives: 97.4 us -> none  [on_device(): lax.all_to_all(rotated, 'vec', split_axis=1, concat_axis=0, tiled=True)]
    ppermute x0 -> x29, waiting for transfers between devices: none -> 60.1 us  [the longest x17 58 us: swapped(): lax.ppermute(value, axis, [(i, i ^ offset) for i in range(lax.axis_size(a...]
    ppermute x0 -> x29, starting transfers between devices: none -> 51.7 us  [the longest x17 27.5 us: swapped(): lax.ppermute(value, axis, [(i, i ^ offset) for i in range(lax.axis_size(a...]
    all_gather x1 -> x0, waiting for transfers between devices: 48.8 us -> none  [on_device(): ritz_full = lax.all_gather(ritz_full_rows, 'vec', axis=1, tiled=True)]
    pallas_call x0 -> x3, Pallas kernels: none -> 31.6 us  [call(): pl.pallas_call(kernel, in_specs=[pl.BlockSpec(memory_space=pltpu.SMEM)] +...]
    dot_general x5 -> x0, matrix products: 21.4 us -> none  [the longest x1 7.55 us: on_device(): rotated = rotated - jnp.dot(panel_cols, solved, precision=highest)]
    all_gather x1 -> x0, blocking collectives: 10.1 us -> none  [on_device(): ritz_full_rows = lax.all_gather(ritz, 'row', axis=0, tiled=True)]
  transfers between devices with their start and end apart: 2 -> 29, of which waited for: 2 -> 11; matrix products, arithmetic and copies ran while one was open for 0% -> 3% of each run, Pallas kernels for 0% -> 6%
where the time goes in v2:
time: 163 us; the launch traced here: 162 us
  waiting for transfers between devices  60.1 us (37%)
  starting transfers between devices  51.7 us (32%)
  Pallas kernels  31.6 us (19%)
  other arithmetic  10.2 us (6%)
  local copies, waits for them, and re-layouts  8.04 us (5%)
    ppermute x17, waiting for transfers between devices, swapped(): lax.ppermute(value, axis, [(i, i ^ offset) for i in range(lax.axis_size(a...  58 us
    pallas_call x3, Pallas kernels, call(): pl.pallas_call(kernel, in_specs=[pl.BlockSpec(memory_space=pltpu.SMEM)] +...  31.6 us
    ppermute x17, starting transfers between devices, swapped(): lax.ppermute(value, axis, [(i, i ^ offset) for i in range(lax.axis_size(a...  27.5 us
    ppermute x3, starting transfers between devices, on_device(): lax.ppermute(part, (ROW, VEC), [(r * n_vec + i, (r ^ q) * n_vec + i) for...  10.2 us
    ppermute x4, starting transfers between devices, on_device(): inner = [lax.ppermute(p, VEC, [(i, i ^ 1) for i in holders]) for p in outer]  9.22 us
    unnamed x23, local copies, waits for them, and re-layouts  5.7 us
    another operation x2, other arithmetic  3.67 us
  transfers between devices with their start and end apart: 29, of which 11 were waited for; matrix products, arithmetic and copies ran while one was open for 3% of the time, Pallas kernels for 6%

profile of v2, /device:TPU:9, one launch (start us, length us, event | category | flops | bytes accessed | tf_op | source)
XLA Modules:
  0.0 162.0 jit_solution(17153196089664810735)
XLA Ops:
  7.5 11.2 %collective-permute-start.1 = (bf16[512,128]{1,0:T(8,128)(2,1)S(1)}, bf16[512,128]{1,0:T(8,128)(2,1)S(1)}, u32[]{:S(2)}, u32[]{:S(2)}) collective-permute-start(bf16[512,128]{1,0:T(8,128)(2,1)S(1)} %copy-done.9), channel_id=1, source_target_pairs={{0,4},{1,5},{2,6},{3,7},{4,0},{5,1},{6,2},{7,3},{8,12},{9,13},{10,... | collective-permute-start | bytes 393224 | tf_op jit(solution)/shard_map/ppermute | solution.py:16
  19.0 9.9 %collective-permute-done.1 = bf16[512,128]{1,0:T(8,128)(2,1)S(1)} collective-permute-done((bf16[512,128]{1,0:T(8,128)(2,1)S(1)}, bf16[512,128]{1,0:T(8,128)(2,1)S(1)}, u32[]{:S(2)}, u32[]{:S(2)}) %collective-permute-start.1) | collective-permute-done | bytes 131104 | tf_op jit(solution)/shard_map/ppermute | solution.py:16
  33.4 4.4 %collective-permute-start.4 = (bf16[512,512]{1,0:T(8,128)(2,1)S(1)}, bf16[512,512]{1,0:T(8,128)(2,1)S(1)}, u32[]{:S(2)}, u32[]{:S(2)}) collective-permute-start(bf16[512,512]{1,0:T(8,128)(2,1)S(1)} %constant_dynamic-update-slice_fusion.refs_0_.refs_8_), channel_id=1, source_target_pairs={{0,16},{8,24},{16,0},{24,8},{1,17},{9,25},{17,1},{25,9},{2,18},{10... | collective-permute-start | bytes 1572872 | tf_op jit(solution)/shard_map/ppermute | solution.py:16
  40.2 3.4 %collective-permute-start.15 = (bf16[576,512]{1,0:T(8,128)(2,1)S(1)}, bf16[576,512]{1,0:T(8,128)(2,1)S(1)}, u32[]{:S(2)}, u32[]{:S(2)}) collective-permute-start(bf16[576,512]{1,0:T(8,128)(2,1)S(1)} %add.48.refs_0_), channel_id=1, source_target_pairs={{7,15},{3,11},{5,13},{1,9},{15,7},{11,3},{13,5},{9,1},{23,31},{19,... | collective-permute-start | bytes 1769480 | tf_op jit(solution)/shard_map/ppermute | solution.py:158
  43.5 6.1 %collective-permute-done.4.refs_2_.refs_10_ = bf16[512,512]{1,0:T(8,128)(2,1)S(1)} collective-permute-done((bf16[512,512]{1,0:T(8,128)(2,1)S(1)}, bf16[512,512]{1,0:T(8,128)(2,1)S(1)}, u32[]{:S(2)}, u32[]{:S(2)}) %collective-permute-start.4) | collective-permute-done | bytes 524320 | tf_op jit(solution)/shard_map/ppermute | solution.py:16
  49.6 3.8 %collective-permute-start.16 = (bf16[576,512]{1,0:T(8,128)(2,1)S(1)}, bf16[576,512]{1,0:T(8,128)(2,1)}, u32[]{:S(2)}, u32[]{:S(2)}) collective-permute-start(bf16[576,512]{1,0:T(8,128)(2,1)S(1)} %add.48.refs_0_), channel_id=1, source_target_pairs={{7,23},{3,19},{5,21},{1,17},{15,31},{11,27},{13,29},{9,25},{23,7},... | collective-permute-start | bytes 1769480 | tf_op jit(solution)/shard_map/ppermute | solution.py:158
  53.4 3.0 %collective-permute-start.17 = (bf16[576,512]{1,0:T(8,128)(2,1)S(1)}, bf16[576,512]{1,0:T(8,128)(2,1)}, u32[]{:S(2)}, u32[]{:S(2)}) collective-permute-start(bf16[576,512]{1,0:T(8,128)(2,1)S(1)} %add.48.refs_0_), channel_id=1, source_target_pairs={{7,31},{3,27},{5,29},{1,25},{15,23},{11,19},{13,21},{9,17},{23,15}... | collective-permute-start | bytes 1769480 | tf_op jit(solution)/shard_map/ppermute | solution.py:158
  60.0 2.9 %collective-permute-start.18 = (bf16[576,512]{1,0:T(8,128)(2,1)S(1)}, bf16[576,512]{1,0:T(8,128)(2,1)}, u32[]{:S(2)}, u32[]{:S(2)}) collective-permute-start(bf16[576,512]{1,0:T(8,128)(2,1)S(1)} %add.48.refs_0_), channel_id=1, source_target_pairs={{7,6},{3,2},{5,4},{1,0},{15,14},{11,10},{13,12},{9,8},{23,22},{19,... | collective-permute-start | bytes 1769480 | tf_op jit(solution)/shard_map/ppermute | solution.py:161
  62.9 2.1 %collective-permute-start.19 = (bf16[576,512]{1,0:T(8,128)(2,1)S(1)}, bf16[576,512]{1,0:T(8,128)(2,1)}, u32[]{:S(2)}, u32[]{:S(2)}) collective-permute-start(bf16[576,512]{1,0:T(8,128)(2,1)S(1)} %collective-permute-done.15.refs_1_), channel_id=1, source_target_pairs={{7,6},{3,2},{5,4},{1,0},{15,14},{11,10},{13,12},{9,8},{23,22},{19,... | collective-permute-start | bytes 1769480 | tf_op jit(solution)/shard_map/ppermute | solution.py:161
  65.0 2.1 %collective-permute-done.16.refs_2_ = bf16[576,512]{1,0:T(8,128)(2,1)} collective-permute-done((bf16[576,512]{1,0:T(8,128)(2,1)S(1)}, bf16[576,512]{1,0:T(8,128)(2,1)}, u32[]{:S(2)}, u32[]{:S(2)}) %collective-permute-start.16) | collective-permute-done | bytes 589856 | tf_op jit(solution)/shard_map/ppermute | solution.py:158
  67.1 2.1 %collective-permute-start.20 = (bf16[576,512]{1,0:T(8,128)(2,1)}, bf16[576,512]{1,0:T(8,128)(2,1)}, u32[]{:S(2)}, u32[]{:S(2)}) collective-permute-start(bf16[576,512]{1,0:T(8,128)(2,1)} %collective-permute-done.16.refs_2_), channel_id=1, source_target_pairs={{7,6},{3,2},{5,4},{1,0},{15,14},{11,10},{13,12},{9,8},{23,22},{19,... | collective-permute-start | bytes 1769480 | tf_op jit(solution)/shard_map/ppermute | solution.py:161
  69.2 2.2 %collective-permute-start.21 = (bf16[576,512]{1,0:T(8,128)(2,1)}, bf16[576,512]{1,0:T(8,128)(2,1)}, u32[]{:S(2)}, u32[]{:S(2)}) collective-permute-start(bf16[576,512]{1,0:T(8,128)(2,1)} %collective-permute-done.17.refs_3_), channel_id=1, source_target_pairs={{7,6},{3,2},{5,4},{1,0},{15,14},{11,10},{13,12},{9,8},{23,22},{19,... | collective-permute-start | bytes 1769480 | tf_op jit(solution)/shard_map/ppermute | solution.py:161
  76.3 10.3 %shard_map.46 = (f32[1024,1024]{1,0:T(8,128)}, f32[8,1024]{1,0:T(8,128)S(1)}) custom-call(s32[3]{0:T(128)S(1)} %pad_add_fusion.flags, bf16[1024,2048]{1,0:T(8,128)(2,1)} %filtered.1, bf16[512,512]{1,0:T(8,128)(2,1)S(1)} %constant_dynamic-update-slice_fusion.refs_0_.refs_8_, bf16[512,512]{1,0:T(8,128)(2,1)S(1)} %collective-permute-done.3.refs_1_.refs_9_, ...), custom_call_target="tpu_custom_call" | custom-call | flops 4294967296 | bytes 8388608 | tf_op jit(solution)/shard_map/pallas_call | solution.py:116
  86.5 10.7 %shard_map.47 = (f32[1024,512]{1,0:T(8,128)}, f32[8,512]{1,0:T(8,128)}) custom-call(s32[3]{0:T(128)S(1)} %pad_add_fusion.flags, f32[1024,1024]{1,0:T(8,128)} %get-tuple-element.15.rotated, f32[8,1024]{1,0:T(8,128)S(1)} %get-tuple-element.16.peak, bf16[1024,512]{1,0:T(8,128)(2,1)} %get-tuple-element.32.cols_high, ...), custom_call_target="tpu_custom_call" | custom-call | flops 2147483648 | bytes 15761408 | tf_op jit(solution)/shard_map/pallas_call | solution.py:116
  97.2 1.8 %convert.12 = f16[1024,512]{1,0:T(8,128)(2,1)S(1)} convert(f32[1024,512]{1,0:T(8,128)} %get-tuple-element.17) | non-fusion elementwise | flops 524288 | bytes 3145728 | tf_op jit(solution)/shard_map/convert.7
  99.3 10.7 %shard_map.48 = (f32[1024,512]{1,0:T(8,128)}, f32[8,512]{1,0:T(8,128)S(1)}) custom-call(s32[3]{0:T(128)S(1)} %pad_add_fusion.flags, f32[1024,1024]{1,0:T(8,128)} %get-tuple-element.15.rotated, f32[8,1024]{1,0:T(8,128)S(1)} %get-tuple-element.16.peak, bf16[1024,512]{1,0:T(8,128)(2,1)} %get-tuple-element.32.cols_high, ...), custom_call_target="tpu_custom_call" | custom-call | flops 2147483648 | bytes 15761408 | tf_op jit(solution)/shard_map/pallas_call | solution.py:116
  112.1 2.0 %collective-permute-start.24 = (f16[1024,128]{1,0:T(8,128)(2,1)S(1)}, f16[1024,128]{1,0:T(8,128)(2,1)S(1)}, u32[]{:S(2)}, u32[]{:S(2)}) collective-permute-start(f16[1024,128]{1,0:T(8,128)(2,1)S(1)} %get-tuple-element.33), channel_id=1, source_target_pairs={{0,3},{1,2},{2,1},{3,0},{4,7},{5,6},{6,5},{7,4},{8,11},{9,10},{10,... | collective-permute-start | bytes 786440 | tf_op jit(solution)/shard_map/ppermute | solution.py:16
  114.2 2.3 %collective-permute-start.26 = (f16[1024,128]{1,0:T(8,128)(2,1)S(1)}, f16[1024,128]{1,0:T(8,128)(2,1)S(1)}, u32[]{:S(2)}, u32[]{:S(2)}) collective-permute-start(f16[1024,128]{1,0:T(8,128)(2,1)S(1)} %get-tuple-element.22), channel_id=1, source_target_pairs={{0,5},{1,4},{2,7},{3,6},{4,1},{5,0},{6,3},{7,2},{8,13},{9,12},{10,... | collective-permute-start | bytes 786440 | tf_op jit(solution)/shard_map/ppermute | solution.py:16
  118.0 8.3 %collective-permute-done.23 = f16[1024,128]{1,0:T(8,128)(2,1)S(1)} collective-permute-done((f16[1024,128]{1,0:T(8,128)(2,1)S(1)}, f16[1024,128]{1,0:T(8,128)(2,1)S(1)}, u32[]{:S(2)}, u32[]{:S(2)}) %collective-permute-start.23) | collective-permute-done | bytes 262176 | tf_op jit(solution)/shard_map/ppermute | solution.py:16
  126.3 3.7 %collective-permute-start.28 = (f16[1024,128]{1,0:T(8,128)(2,1)S(1)}, f16[1024,128]{1,0:T(8,128)(2,1)S(1)}, u32[]{:S(2)}, u32[]{:S(2)}) collective-permute-start(f16[1024,128]{1,0:T(8,128)(2,1)S(1)} %get-tuple-element.24), channel_id=1, source_target_pairs={{0,7},{1,6},{2,5},{3,4},{4,3},{5,2},{6,1},{7,0},{8,15},{9,14},{10,... | collective-permute-start | bytes 786440 | tf_op jit(solution)/shard_map/ppermute | solution.py:16
  130.1 1.8 %collective-permute-done.24 = f16[1024,128]{1,0:T(8,128)(2,1)S(1)} collective-permute-done((f16[1024,128]{1,0:T(8,128)(2,1)S(1)}, f16[1024,128]{1,0:T(8,128)(2,1)S(1)}, u32[]{:S(2)}, u32[]{:S(2)}) %collective-permute-start.24) | collective-permute-done | bytes 262176 | tf_op jit(solution)/shard_map/ppermute | solution.py:16
  132.1 16.0 %collective-permute-done.26 = f16[1024,128]{1,0:T(8,128)(2,1)S(1)} collective-permute-done((f16[1024,128]{1,0:T(8,128)(2,1)S(1)}, f16[1024,128]{1,0:T(8,128)(2,1)S(1)}, u32[]{:S(2)}, u32[]{:S(2)}) %collective-permute-start.26) | collective-permute-done | bytes 262176 | tf_op jit(solution)/shard_map/ppermute | solution.py:16
  148.1 7.2 %collective-permute-done.27 = f16[1024,128]{1,0:T(8,128)(2,1)S(1)} collective-permute-done((f16[1024,128]{1,0:T(8,128)(2,1)S(1)}, f16[1024,128]{1,0:T(8,128)(2,1)S(1)}, u32[]{:S(2)}, u32[]{:S(2)}) %collective-permute-start.27) | collective-permute-done | bytes 262176 | tf_op jit(solution)/shard_map/ppermute | solution.py:16
  155.4 5.9 %collective-permute-done.28 = f16[1024,128]{1,0:T(8,128)(2,1)S(1)} collective-permute-done((f16[1024,128]{1,0:T(8,128)(2,1)S(1)}, f16[1024,128]{1,0:T(8,128)(2,1)S(1)}, u32[]{:S(2)}, u32[]{:S(2)}) %collective-permute-start.28) | collective-permute-done | bytes 262176 | tf_op jit(solution)/shard_map/ppermute | solution.py:16
  (86 shorter events, 27.8 us)
Async XLA Ops:
  6.1 22.8 %collective-permute-start.13 = (bf16[576,512]{1,0:T(8,128)(2,1)S(1)}, bf16[576,512]{1,0:T(8,128)(2,1)S(1)}, u32[]{:S(2)}, u32[]{:S(2)}) collective-permute-start(bf16[576,512]{1,0:T(8,128)(2,1)S(1)} %fusion.7), channel_id=1, source_target_pairs={{7,3},{15,11},{23,19},{31,27}} | collective-permute-start | bytes 1769480 | tf_op jit(solution)/shard_map/ppermute | solution.py:154
  7.4 11.5 %collective-permute-start = (bf16[512,128]{1,0:T(8,128)(2,1)S(1)}, bf16[512,128]{1,0:T(8,128)(2,1)S(1)}, u32[]{:S(2)}, u32[]{:S(2)}) collective-permute-start(bf16[512,128]{1,0:T(8,128)(2,1)S(1)} %copy-done.9), channel_id=1, source_target_pairs={{0,2},{1,3},{2,0},{3,1},{4,6},{5,7},{6,4},{7,5},{8,10},{9,11},{10,... | collective-permute-start | bytes 393224 | tf_op jit(solution)/shard_map/ppermute | solution.py:16
  7.5 21.4 %collective-permute-start.1 = (bf16[512,128]{1,0:T(8,128)(2,1)S(1)}, bf16[512,128]{1,0:T(8,128)(2,1)S(1)}, u32[]{:S(2)}, u32[]{:S(2)}) collective-permute-start(bf16[512,128]{1,0:T(8,128)(2,1)S(1)} %copy-done.9), channel_id=1, source_target_pairs={{0,4},{1,5},{2,6},{3,7},{4,0},{5,1},{6,2},{7,3},{8,12},{9,13},{10,... | collective-permute-start | bytes 393224 | tf_op jit(solution)/shard_map/ppermute | solution.py:16
  18.7 13.0 %collective-permute-start.2 = (bf16[512,128]{1,0:T(8,128)(2,1)S(1)}, bf16[512,128]{1,0:T(8,128)(2,1)S(1)}, u32[]{:S(2)}, u32[]{:S(2)}) collective-permute-start(bf16[512,128]{1,0:T(8,128)(2,1)S(1)} %copy-done.9), channel_id=1, source_target_pairs={{0,6},{1,7},{2,4},{3,5},{4,2},{5,3},{6,0},{7,1},{8,14},{9,15},{10,... | collective-permute-start | bytes 393224 | tf_op jit(solution)/shard_map/ppermute | solution.py:16
  29.1 10.9 %collective-permute-start.14 = (bf16[576,512]{1,0:T(8,128)(2,1)S(1)}, bf16[576,512]{1,0:T(8,128)(2,1)S(1)}, u32[]{:S(2)}, u32[]{:S(2)}) collective-permute-start(bf16[576,512]{1,0:T(8,128)(2,1)S(1)} %add.47), channel_id=1, source_target_pairs={{7,5},{3,1},{15,13},{11,9},{23,21},{19,17},{31,29},{27,25}} | collective-permute-start | bytes 1769480 | tf_op jit(solution)/shard_map/ppermute | solution.py:154
  31.7 8.3 %collective-permute-start.3 = (bf16[512,512]{1,0:T(8,128)(2,1)S(1)}, bf16[512,512]{1,0:T(8,128)(2,1)S(1)}, u32[]{:S(2)}, u32[]{:S(2)}) collective-permute-start(bf16[512,512]{1,0:T(8,128)(2,1)S(1)} %constant_dynamic-update-slice_fusion.refs_0_.refs_8_), channel_id=1, source_target_pairs={{0,8},{8,0},{16,24},{24,16},{1,9},{9,1},{17,25},{25,17},{2,10},{10... | collective-permute-start | bytes 1572872 | tf_op jit(solution)/shard_map/ppermute | solution.py:16
  33.4 16.2 %collective-permute-start.4 = (bf16[512,512]{1,0:T(8,128)(2,1)S(1)}, bf16[512,512]{1,0:T(8,128)(2,1)S(1)}, u32[]{:S(2)}, u32[]{:S(2)}) collective-permute-start(bf16[512,512]{1,0:T(8,128)(2,1)S(1)} %constant_dynamic-update-slice_fusion.refs_0_.refs_8_), channel_id=1, source_target_pairs={{0,16},{8,24},{16,0},{24,8},{1,17},{9,25},{17,1},{25,9},{2,18},{10... | collective-permute-start | bytes 1572872 | tf_op jit(solution)/shard_map/ppermute | solution.py:16
  37.8 15.6 %collective-permute-start.5 = (bf16[512,512]{1,0:T(8,128)(2,1)S(1)}, bf16[512,512]{1,0:T(8,128)(2,1)S(1)}, u32[]{:S(2)}, u32[]{:S(2)}) collective-permute-start(bf16[512,512]{1,0:T(8,128)(2,1)S(1)} %constant_dynamic-update-slice_fusion.refs_0_.refs_8_), channel_id=1, source_target_pairs={{0,24},{8,16},{16,8},{24,0},{1,25},{9,17},{17,9},{25,1},{2,26},{10... | collective-permute-start | bytes 1572872 | tf_op jit(solution)/shard_map/ppermute | solution.py:16
  39.0 17.5 %collective-permute-start.6 = (bf16[512,512]{1,0:T(8,128)(2,1)S(1)}, bf16[512,512]{1,0:T(8,128)(2,1)S(1)}, u32[]{:S(2)}, u32[]{:S(2)}) collective-permute-start(bf16[512,512]{1,0:T(8,128)(2,1)S(1)} %constant_dynamic-update-slice_fusion.refs_0_.refs_8_), channel_id=1, source_target_pairs={{0,1},{1,0},{2,3},{3,2},{4,5},{5,4},{6,7},{7,6},{8,9},{9,8},{10,11... | collective-permute-start | bytes 1572872 | tf_op jit(solution)/shard_map/ppermute | solution.py:16
  40.0 17.3 %collective-permute-start.7 = (bf16[512,512]{1,0:T(8,128)(2,1)S(1)}, bf16[512,512]{1,0:T(8,128)(2,1)S(1)}, u32[]{:S(2)}, u32[]{:S(2)}) collective-permute-start(bf16[512,512]{1,0:T(8,128)(2,1)S(1)} %collective-permute-done.3.refs_1_.refs_9_), channel_id=1, source_target_pairs={{0,1},{1,0},{2,3},{3,2},{4,5},{5,4},{6,7},{7,6},{8,9},{9,8},{10,11... | collective-permute-start | bytes 1572872 | tf_op jit(solution)/shard_map/ppermute | solution.py:16
  40.2 22.7 %collective-permute-start.15 = (bf16[576,512]{1,0:T(8,128)(2,1)S(1)}, bf16[576,512]{1,0:T(8,128)(2,1)S(1)}, u32[]{:S(2)}, u32[]{:S(2)}) collective-permute-start(bf16[576,512]{1,0:T(8,128)(2,1)S(1)} %add.48.refs_0_), channel_id=1, source_target_pairs={{7,15},{3,11},{5,13},{1,9},{15,7},{11,3},{13,5},{9,1},{23,31},{19,... | collective-permute-start | bytes 1769480 | tf_op jit(solution)/shard_map/ppermute | solution.py:158
  49.6 17.5 %collective-permute-start.16 = (bf16[576,512]{1,0:T(8,128)(2,1)S(1)}, bf16[576,512]{1,0:T(8,128)(2,1)}, u32[]{:S(2)}, u32[]{:S(2)}) collective-permute-start(bf16[576,512]{1,0:T(8,128)(2,1)S(1)} %add.48.refs_0_), channel_id=1, source_target_pairs={{7,23},{3,19},{5,21},{1,17},{15,31},{11,27},{13,29},{9,25},{23,7},... | collective-permute-start | bytes 1769480 | tf_op jit(solution)/shard_map/ppermute | solution.py:158
  53.4 15.8 %collective-permute-start.17 = (bf16[576,512]{1,0:T(8,128)(2,1)S(1)}, bf16[576,512]{1,0:T(8,128)(2,1)}, u32[]{:S(2)}, u32[]{:S(2)}) collective-permute-start(bf16[576,512]{1,0:T(8,128)(2,1)S(1)} %add.48.refs_0_), channel_id=1, source_target_pairs={{7,31},{3,27},{5,29},{1,25},{15,23},{11,19},{13,21},{9,17},{23,15}... | collective-permute-start | bytes 1769480 | tf_op jit(solution)/shard_map/ppermute | solution.py:158
  58.1 15.0 %collective-permute-start.9 = (bf16[512,512]{1,0:T(8,128)(2,1)S(1)}, bf16[512,512]{1,0:T(8,128)(2,1)}, u32[]{:S(2)}, u32[]{:S(2)}) collective-permute-start(bf16[512,512]{1,0:T(8,128)(2,1)S(1)} %collective-permute-done.5.refs_3_.refs_11_), channel_id=1, source_target_pairs={{0,1},{1,0},{2,3},{3,2},{4,5},{5,4},{6,7},{7,6},{8,9},{9,8},{10,11... | collective-permute-start | bytes 1572872 | tf_op jit(solution)/shard_map/ppermute | solution.py:16
  60.0 26.5 %collective-permute-start.18 = (bf16[576,512]{1,0:T(8,128)(2,1)S(1)}, bf16[576,512]{1,0:T(8,128)(2,1)}, u32[]{:S(2)}, u32[]{:S(2)}) collective-permute-start(bf16[576,512]{1,0:T(8,128)(2,1)S(1)} %add.48.refs_0_), channel_id=1, source_target_pairs={{7,6},{3,2},{5,4},{1,0},{15,14},{11,10},{13,12},{9,8},{23,22},{19,... | collective-permute-start | bytes 1769480 | tf_op jit(solution)/shard_map/ppermute | solution.py:161
  62.9 23.7 %collective-permute-start.19 = (bf16[576,512]{1,0:T(8,128)(2,1)S(1)}, bf16[576,512]{1,0:T(8,128)(2,1)}, u32[]{:S(2)}, u32[]{:S(2)}) collective-permute-start(bf16[576,512]{1,0:T(8,128)(2,1)S(1)} %collective-permute-done.15.refs_1_), channel_id=1, source_target_pairs={{7,6},{3,2},{5,4},{1,0},{15,14},{11,10},{13,12},{9,8},{23,22},{19,... | collective-permute-start | bytes 1769480 | tf_op jit(solution)/shard_map/ppermute | solution.py:161
  67.1 19.4 %collective-permute-start.20 = (bf16[576,512]{1,0:T(8,128)(2,1)}, bf16[576,512]{1,0:T(8,128)(2,1)}, u32[]{:S(2)}, u32[]{:S(2)}) collective-permute-start(bf16[576,512]{1,0:T(8,128)(2,1)} %collective-permute-done.16.refs_2_), channel_id=1, source_target_pairs={{7,6},{3,2},{5,4},{1,0},{15,14},{11,10},{13,12},{9,8},{23,22},{19,... | collective-permute-start | bytes 1769480 | tf_op jit(solution)/shard_map/ppermute | solution.py:161
  69.2 17.3 %collective-permute-start.21 = (bf16[576,512]{1,0:T(8,128)(2,1)}, bf16[576,512]{1,0:T(8,128)(2,1)}, u32[]{:S(2)}, u32[]{:S(2)}) collective-permute-start(bf16[576,512]{1,0:T(8,128)(2,1)} %collective-permute-done.17.refs_3_), channel_id=1, source_target_pairs={{7,6},{3,2},{5,4},{1,0},{15,14},{11,10},{13,12},{9,8},{23,22},{19,... | collective-permute-start | bytes 1769480 | tf_op jit(solution)/shard_map/ppermute | solution.py:161
  112.0 14.3 %collective-permute-start.23 = (f16[1024,128]{1,0:T(8,128)(2,1)S(1)}, f16[1024,128]{1,0:T(8,128)(2,1)S(1)}, u32[]{:S(2)}, u32[]{:S(2)}) collective-permute-start(f16[1024,128]{1,0:T(8,128)(2,1)S(1)} %get-tuple-element.34), channel_id=1, source_target_pairs={{0,2},{1,3},{2,0},{3,1},{4,6},{5,7},{6,4},{7,5},{8,10},{9,11},{10,... | collective-permute-start | bytes 786440 | tf_op jit(solution)/shard_map/ppermute | solution.py:16
  112.1 19.8 %collective-permute-start.24 = (f16[1024,128]{1,0:T(8,128)(2,1)S(1)}, f16[1024,128]{1,0:T(8,128)(2,1)S(1)}, u32[]{:S(2)}, u32[]{:S(2)}) collective-permute-start(f16[1024,128]{1,0:T(8,128)(2,1)S(1)} %get-tuple-element.33), channel_id=1, source_target_pairs={{0,3},{1,2},{2,1},{3,0},{4,7},{5,6},{6,5},{7,4},{8,11},{9,10},{10,... | collective-permute-start | bytes 786440 | tf_op jit(solution)/shard_map/ppermute | solution.py:16
  114.2 17.8 %collective-permute-start.25 = (f16[1024,128]{1,0:T(8,128)(2,1)S(1)}, f16[1024,128]{1,0:T(8,128)(2,1)S(1)}, u32[]{:S(2)}, u32[]{:S(2)}) collective-permute-start(f16[1024,128]{1,0:T(8,128)(2,1)S(1)} %get-tuple-element.21), channel_id=1, source_target_pairs={{0,4},{1,5},{2,6},{3,7},{4,0},{5,1},{6,2},{7,3},{8,12},{9,13},{10,... | collective-permute-start | bytes 786440 | tf_op jit(solution)/shard_map/ppermute | solution.py:16
  114.2 33.9 %collective-permute-start.26 = (f16[1024,128]{1,0:T(8,128)(2,1)S(1)}, f16[1024,128]{1,0:T(8,128)(2,1)S(1)}, u32[]{:S(2)}, u32[]{:S(2)}) collective-permute-start(f16[1024,128]{1,0:T(8,128)(2,1)S(1)} %get-tuple-element.22), channel_id=1, source_target_pairs={{0,5},{1,4},{2,7},{3,6},{4,1},{5,0},{6,3},{7,2},{8,13},{9,12},{10,... | collective-permute-start | bytes 786440 | tf_op jit(solution)/shard_map/ppermute | solution.py:16
  117.9 37.4 %collective-permute-start.27 = (f16[1024,128]{1,0:T(8,128)(2,1)S(1)}, f16[1024,128]{1,0:T(8,128)(2,1)S(1)}, u32[]{:S(2)}, u32[]{:S(2)}) collective-permute-start(f16[1024,128]{1,0:T(8,128)(2,1)S(1)} %get-tuple-element.23), channel_id=1, source_target_pairs={{0,6},{1,7},{2,4},{3,5},{4,2},{5,3},{6,0},{7,1},{8,14},{9,15},{10,... | collective-permute-start | bytes 786440 | tf_op jit(solution)/shard_map/ppermute | solution.py:16
  126.3 34.9 %collective-permute-start.28 = (f16[1024,128]{1,0:T(8,128)(2,1)S(1)}, f16[1024,128]{1,0:T(8,128)(2,1)S(1)}, u32[]{:S(2)}, u32[]{:S(2)}) collective-permute-start(f16[1024,128]{1,0:T(8,128)(2,1)S(1)} %get-tuple-element.24), channel_id=1, source_target_pairs={{0,7},{1,6},{2,5},{3,4},{4,3},{5,2},{6,1},{7,0},{8,15},{9,14},{10,... | collective-permute-start | bytes 786440 | tf_op jit(solution)/shard_map/ppermute | solution.py:16
  (15 other events, 92.9 us)

commit v3 on v0

v3 whole, which is shorter than its diff:
```python
import functools

import jax
import jax.numpy as jnp
from jax import lax
from jax.experimental import pallas as pl
from jax.experimental.pallas import tpu as pltpu
from jax.sharding import PartitionSpec as P

ROW, VEC = "row", "vec"
VMEM_LIMIT = 16 * 1024 * 1024


def swapped(value, axis, offset):
    return lax.ppermute(value, axis, [(i, i ^ offset) for i in range(lax.axis_size(axis))])


def steps_of(size):
    return [1 << i for i in range(size.bit_length() - 1)]


def split(value):
    high = value.astype(jnp.bfloat16)
    return high, (value - high.astype(jnp.float32)).astype(jnp.bfloat16)


def split_array(value):
    high = lax.reduce_precision(value, 8, 7)
    return high.astype(jnp.bfloat16), (value - high).astype(jnp.bfloat16)


def mul(a, b):
    return jnp.dot(a, b, preferred_element_type=jnp.float32)


def mul3(a, b):
    left = jnp.concatenate([a[0], a[0], a[1]], axis=1)
    return mul(left, jnp.concatenate([b[0], b[1], b[0]], axis=0))


def side_kernel(*refs):
    *parts, first, second = refs
    cut, width = len(parts) // 2, parts[0].shape[1]
    for i, part in enumerate(parts):
        (first, second)[i // cut][:, i % cut * width : (i % cut + 1) * width] = part[...]


def rotate_kernel(places, flags, filtered, *refs):
    *parts, out, ritz, peak, rows, sems = refs
    n_row = len(places[0])
    block, half = ritz.shape[0] // n_row, ritz.shape[1] // 4
    copies = []
    for i, order in enumerate(places * 2):
        own = parts[i * len(parts) // 4 : (i + 1) * len(parts) // 4]
        for j, q in enumerate(order):
            part, place = own[j * len(own) // n_row], j % (n_row // len(own))
            into = ritz.at[pl.ds(q * block, block), pl.ds(i * half, half)]
            source = part.at[pl.ds(place * block, block), :]
            copies.append(pltpu.make_async_copy(source, into, sems.at[len(copies)]))
    chunk = rows.shape[0] // 4
    for i in range(4):
        at = pl.ds(i * chunk, chunk)
        copies.append(pltpu.make_async_copy(filtered.at[at, :], rows.at[at, :], sems.at[len(copies)]))
    for copy in copies:
        copy.start()
    for copy in copies[:-4]:
        copy.wait()
    for i in range(4):
        copies[4 * n_row + i].wait()
        at = slice(i * chunk, (i + 1) * chunk)
        left = jnp.concatenate(
            [rows[at, pl.ds(pl.multiple_of((flags[2] ^ q) * block, block), block)] for q in range(n_row)], axis=1
        )
        out[at, :] = mul(left, ritz[...])
    most = jnp.max(jnp.abs(ritz[...].astype(jnp.float32)), axis=0, keepdims=True)
    peak[...] = jnp.broadcast_to(most, peak.shape)


def solve_kernel(n_row, first, flags, inverse, ritz, *refs):
    tails, (out, rows, cross, solved, sems) = refs[:n_row], refs[n_row:]
    width = inverse.shape[1]
    half = out.shape[1] // 2
    block = ritz.shape[0] // n_row
    cross_rows = cross.shape[0] // n_row
    copies = []
    for q in range(n_row):
        into = rows.at[:, pl.ds(q * block, block)]
        copies.append(pltpu.make_async_copy(tails[q].at[pl.ds(0, 2 * width), :], into, sems.at[2 * q]))
        into = cross.at[pl.ds(pl.multiple_of((flags[2] ^ q) * cross_rows, cross_rows), cross_rows), :]
        copies.append(
            pltpu.make_async_copy(tails[q].at[pl.ds(2 * width, cross_rows), :], into, sems.at[2 * q + 1])
        )
    for copy in copies:
        copy.start()
    for copy in copies:
        copy.wait()
    for piece in range(2):
        start = first + 2 * piece * half
        solved[:, piece * half : (piece + 1) * half] = mul(rows[...], ritz[:, start : start + half])
    if block == 2 * width:
        between = cross[:, :width], cross[:, width:]
    else:
        between = cross[:width, :], cross[width:, :]
    last = mul3(split(inverse[1]), split(solved[width:, :]))
    middle = solved[:width, :] - mul3(between, split(last))
    after = mul3(split(inverse[0]), split(middle))
    out[width : 2 * width, :], out[3 * width :, :] = split(last)
    out[:width, :], out[2 * width : 3 * width, :] = split(after)


def correct_kernel(width, depth, first, flags, rotated, peak, cols_high, cols_low, own, other, out, power, solved):
    rows, count = out.shape
    half, size = count // 2, 2 * width

    @pl.when(flags[1] == 1)
    def _():
        solved[...] = own[...]

    @pl.when(flags[1] == 0)
    def _():
        solved[:, :half] = other[:, half:]
        solved[:, half:] = other[:, :half]

    panels = solved[:size, :].astype(jnp.float32) + solved[size:, :].astype(jnp.float32)
    most = jnp.concatenate([peak[0:1, i : i + half] for i in (first, first + 2 * half)], axis=1)
    bound = 8.0 * depth * most + size * jnp.max(jnp.abs(panels), axis=0, keepdims=True)
    exponent = 14.0 - jnp.floor(jnp.log2(jnp.maximum(bound, 1e-30)))
    scale = jnp.exp2(exponent)
    power[...] = jnp.broadcast_to(jnp.exp2(-exponent), power.shape)
    left = jnp.concatenate([cols_high[...], cols_high[...], cols_low[...]], axis=1)
    for piece in range(2):
        start = first + 2 * piece * half
        where = slice(piece * half, (piece + 1) * half)
        right = jnp.concatenate([solved[:, where], solved[:size, where]], axis=0)
        out[:, where] = (rotated[:, start : start + half] - mul(left, right)) * scale[:, where]

    @pl.when(flags[0] == 1)
    def _():
        out[rows - size :, :] = panels * scale


def place_kernel(ks, flags, power, *refs):
    out, ready, sems = refs[-3:]
    copies = []
    for i, k in enumerate(ks):
        size, width = refs[i].shape
        ready[i] = refs[i][...] * power[0:1, :width]
        into = out.at[pl.ds(pl.multiple_of((flags[3] ^ k) * size, size), size), :]
        copies.append(pltpu.make_async_copy(ready.at[i], into, sems.at[i]))
        copies[i].start()
    for copy in copies:
        copy.wait()


def call(kernel, flags, inputs, out_shape, scratch):
    spec = lambda space: pl.BlockSpec(memory_space=space)
    specs, arrays, scalars = [], [], [] if flags is None else [flags]
    for value in inputs:
        group = value if isinstance(value, list) else [value]
        specs += [spec(pltpu.HBM if isinstance(value, list) else pltpu.VMEM)] * len(group)
        arrays += group
    return pl.pallas_call(
        kernel,
        in_specs=[spec(pltpu.SMEM)] * len(scalars) + specs,
        out_specs=[spec(pltpu.VMEM)] * len(out_shape),
        out_shape=[jax.ShapeDtypeStruct(*s) for s in out_shape],
        scratch_shapes=scratch,
        compiler_params=pltpu.CompilerParams(vmem_limit_bytes=VMEM_LIMIT),
        cost_estimate=pl.CostEstimate(flops=1, bytes_accessed=1, transcendentals=0),
    )(*scalars, *arrays)


def on_device(filtered, ritz, panel_cols, panel_inverse):
    rows, depth = filtered.shape
    width = panel_inverse.shape[1]
    n_row, n_vec = lax.axis_size(ROW), lax.axis_size(VEC)
    row, vec = lax.axis_index(ROW), lax.axis_index(VEC)
    block, own_cols = ritz.shape
    is_last = (row == n_row - 1) & (vec == n_vec - 1)
    last = n_row * n_vec - 1
    lower = rows - 2 * width
    cut = n_vec // 4
    f32, bf16 = jnp.float32, jnp.bfloat16
    holders = range(1, n_vec, 2)

    flags = jnp.stack([is_last.astype(jnp.int32), vec & 1, row, vec])
    filtered, ritz, panel_cols, flags, is_last = lax.optimization_barrier((filtered, ritz, panel_cols, flags, is_last))
    cols = split_array(panel_cols)

    cross = jnp.concatenate(split_array(panel_cols[lower : lower + width, width:]), axis=1 if block == 2 * width else 0)
    cross_rows = cross.shape[0] // n_row
    def part_of(r):
        return jnp.concatenate(
            [filtered[lower:, r * block : (r + 1) * block], cross[r * cross_rows : (r + 1) * cross_rows]], axis=0
        )
    evens = [ritz] + [swapped(ritz, VEC, k) for k in range(2, n_vec, 2)]
    parts = [lax.ppermute(part_of(r), (ROW, VEC), [(last, r * n_vec + n_vec - 1)]) for r in range(n_row - 1)]
    evens, parts = lax.optimization_barrier((evens, parts))

    part = sum(parts, jnp.where(is_last, part_of(n_row - 1), jnp.zeros((), bf16)))
    halves = call(side_kernel, None, evens[cut:] + evens[:cut], [((block, cut * own_cols), bf16)] * 2, [])
    halves, places = [[h] for h in halves], [[0], [0]]
    steps, downs, sources = steps_of(n_row), steps_of(n_vec)[:0:-1], [n_vec - 1]
    for i in range(max(len(steps), len(downs))):
        if i < len(steps):
            for which, step in enumerate((steps[i], steps[-1 - i])):
                known = jnp.concatenate(halves[which], axis=0)
                halves[which] = [known, swapped(known, ROW, step)]
                places[which] = places[which] + [q ^ step for q in places[which]]
        if i < len(downs):
            part += lax.ppermute(part, VEC, [(v, v ^ downs[i]) for v in sources])
            sources += [v ^ downs[i] for v in sources]
        if i == 0:
            halves, part, cols = lax.optimization_barrier((halves, part, cols))
    odds = [[swapped(h, VEC, 1) for h in half] for half in halves]

    tails = [part] + [
        lax.ppermute(part, (ROW, VEC), [(r * n_vec + i, (r ^ q) * n_vec + i) for r in range(n_row) for i in holders])
        for q in range(1, n_row)
    ]
    count = n_vec * own_cols // 2

    rotated, gathered, peak = call(
        functools.partial(rotate_kernel, places), flags, [[filtered, *sum(halves + odds, [])]],
        [((rows, 2 * count), f32), ((depth, 2 * count), bf16), ((8, 2 * count), f32)],
        [pltpu.VMEM((rows, depth), bf16), pltpu.SemaphoreType.DMA((4 + 4 * n_row,))],
    )

    def solve(first):
        own, = call(
            functools.partial(solve_kernel, n_row, first), flags, [panel_inverse, gathered, tails],
            [((4 * width, count), bf16)],
            [
                pltpu.VMEM((2 * width, depth), bf16), pltpu.VMEM(cross.shape, bf16),
                pltpu.VMEM((2 * width, count), f32), pltpu.SemaphoreType.DMA((2 * n_row,)),
            ],
        )
        return own, lax.ppermute(own, VEC, [(i, i ^ 1) for i in holders])

    def correct(first, solved):
        return call(
            functools.partial(correct_kernel, width, depth, first), flags,
            [rotated, peak, *cols, *solved],
            [((rows, count), f32), ((8, count), f32)], [pltpu.VMEM((4 * width, count), bf16)],
        )

    tails, rotated, gathered, peak = lax.optimization_barrier((tails, rotated, gathered, peak))

    piece = lambda values, i: values[:, i * own_cols : (i + 1) * own_cols].astype(jnp.float16)
    solved = [solve(0), solve(count // 2)]
    values, _ = correct(0, solved[0])
    values = [piece(values, i) for i in range(2 * cut)]
    values, solved = lax.optimization_barrier((values, solved))
    sent = {}
    for i, k in enumerate(2 * cut + 2 * j + odd for odd in range(2) for j in range(cut)):
        sent[k] = swapped(values[i], VEC, k)
    values, power = correct(count // 2, solved[1])
    sent[0] = values[:, :own_cols]
    for i, k in enumerate(2 * j + odd for odd in range(2) for j in range(cut)):
        if k:
            sent[k] = swapped(piece(values, i), VEC, k)

    def place(out, ks):
        shape = jax.ShapeDtypeStruct((n_vec * rows, own_cols), f32)
        spec = lambda space: pl.BlockSpec(memory_space=space)
        return pl.pallas_call(
            functools.partial(place_kernel, ks),
            in_specs=[spec(pltpu.SMEM)] + [spec(pltpu.VMEM)] * (1 + len(ks)) + [spec(pl.ANY)] * len(out),
            out_specs=spec(pl.ANY), out_shape=shape,
            scratch_shapes=[pltpu.VMEM((len(ks), rows, own_cols), f32), pltpu.SemaphoreType.DMA((len(ks),))],
            input_output_aliases={2 + len(ks): 0} if out else {},
            compiler_params=pltpu.CompilerParams(vmem_limit_bytes=VMEM_LIMIT),
        )(flags, power, *(sent[k].astype(f32) for k in ks), *out)

    late = [k for k in sent if k >= 2 * cut or k == 2]
    return place([place([], [k for k in sent if k not in late])], late)


def solution(mesh):
    in_specs = (P((ROW, VEC), None), P(ROW, VEC), P((ROW, VEC), None), P())
    return jax.shard_map(on_device, mesh=mesh, in_specs=in_specs, out_specs=P(ROW, VEC), check_vma=False)
```

time: 336 us -> 133 us (0.40); the launches traced: 332 us -> 132 us
  waiting for transfers between devices: 180 us -> 63.3 us
  blocking collectives: 107 us -> 0 us
  starting transfers between devices: 0.04 us -> 39.6 us
  Pallas kernels: 0 us -> 23.5 us
  matrix products: 21.4 us -> 0 us
  between operations: 13.5 us -> 0.57 us
  local copies, waits for them, and re-layouts: 7.25 us -> 2.2 us
    psum x1 -> x0, waiting for transfers between devices: 131 us -> none  [spread(): return lax.psum(jnp.where(mine, value, jnp.zeros_like(value)), axis)]
    all_to_all x1 -> x0, blocking collectives: 97.4 us -> none  [on_device(): lax.all_to_all(rotated, 'vec', split_axis=1, concat_axis=0, tiled=True)]
    ppermute x0 -> x28, waiting for transfers between devices: none -> 63.3 us  [the longest x18 50.7 us: swapped(): lax.ppermute(value, axis, [(i, i ^ offset) for i in range(lax.axis_size(a...]
    all_gather x1 -> x0, waiting for transfers between devices: 48.8 us -> none  [on_device(): ritz_full = lax.all_gather(ritz_full_rows, 'vec', axis=1, tiled=True)]
    ppermute x0 -> x28, starting transfers between devices: none -> 39.6 us  [the longest x18 22.9 us: swapped(): lax.ppermute(value, axis, [(i, i ^ offset) for i in range(lax.axis_size(a...]
    pallas_call x0 -> x8, Pallas kernels: none -> 23.5 us  [the longest x6 19.7 us: call(): pl.pallas_call(kernel, in_specs=[spec(pltpu.SMEM)] * len(scalars) + specs...]
    dot_general x5 -> x0, matrix products: 21.4 us -> none  [the longest x1 7.55 us: on_device(): rotated = rotated - jnp.dot(panel_cols, solved, precision=highest)]
    all_gather x1 -> x0, blocking collectives: 10.1 us -> none  [on_device(): ritz_full_rows = lax.all_gather(ritz, 'row', axis=0, tiled=True)]
  transfers between devices with their start and end apart: 2 -> 28, of which waited for: 2 -> 15; matrix products, arithmetic and copies ran while one was open for 0% -> 1% of each run, Pallas kernels for 0% -> 12%
where the time goes in v3:
time: 133 us; the launch traced here: 132 us
  waiting for transfers between devices  63.3 us (48%)
  starting transfers between devices  39.6 us (30%)
  Pallas kernels  23.5 us (18%)
  other arithmetic  2.99 us (2%)
  local copies, waits for them, and re-layouts  2.2 us (2%)
    ppermute x18, waiting for transfers between devices, swapped(): lax.ppermute(value, axis, [(i, i ^ offset) for i in range(lax.axis_size(a...  50.7 us
    ppermute x18, starting transfers between devices, swapped(): lax.ppermute(value, axis, [(i, i ^ offset) for i in range(lax.axis_size(a...  22.9 us
    pallas_call x6, Pallas kernels, call(): pl.pallas_call(kernel, in_specs=[spec(pltpu.SMEM)] * len(scalars) + specs...  19.7 us
    ppermute x2, waiting for transfers between devices, on_device(): part += lax.ppermute(part, VEC, [(v, v ^ downs[i]) for v in sources])  11.1 us
    ppermute x3, starting transfers between devices, on_device(): lax.ppermute(part, (ROW, VEC), [(r * n_vec + i, (r ^ q) * n_vec + i) for...  9.14 us
    pallas_call x2, Pallas kernels, place(): pl.pallas_call(functools.partial(place_kernel, ks), in_specs=[spec(pltpu....  3.85 us
    ppermute x2, starting transfers between devices, on_device(): part += lax.ppermute(part, VEC, [(v, v ^ downs[i]) for v in sources])  2.74 us
    ppermute x2, starting transfers between devices, solve(): return (own, lax.ppermute(own, VEC, [(i, i ^ 1) for i in holders]))  2.71 us
  transfers between devices with their start and end apart: 28, of which 15 were waited for; matrix products, arithmetic and copies ran while one was open for 1% of the time, Pallas kernels for 12%

profile of v3, /device:TPU:9, one launch (start us, length us, event | category | flops | bytes accessed | tf_op | source)
XLA Modules:
  0.0 132.2 jit_solution(3617950347151520413)
XLA Ops:
  5.1 3.0 %collective-permute-start.1 = (bf16[512,128]{1,0:T(8,128)(2,1)S(1)}, bf16[512,128]{1,0:T(8,128)(2,1)S(1)}, u32[]{:S(2)}, u32[]{:S(2)}) collective-permute-start(bf16[512,128]{1,0:T(8,128)(2,1)S(1)} %copy-done.2), channel_id=1, source_target_pairs={{0,4},{1,5},{2,6},{3,7},{4,0},{5,1},{6,2},{7,3},{8,12},{9,13},{10,... | collective-permute-start | bytes 393224 | tf_op jit(solution)/shard_map/ppermute | solution.py:15
  9.5 2.9 %collective-permute-start.2 = (bf16[512,128]{1,0:T(8,128)(2,1)S(1)}, bf16[512,128]{1,0:T(8,128)(2,1)S(1)}, u32[]{:S(2)}, u32[]{:S(2)}) collective-permute-start(bf16[512,128]{1,0:T(8,128)(2,1)S(1)} %copy-done.2), channel_id=1, source_target_pairs={{0,6},{1,7},{2,4},{3,5},{4,2},{5,3},{6,0},{7,1},{8,14},{9,15},{10,... | collective-permute-start | bytes 393224 | tf_op jit(solution)/shard_map/ppermute | solution.py:15
  14.3 6.4 %collective-permute-done.2.refs_1_ = bf16[512,128]{1,0:T(8,128)(2,1)S(1)} collective-permute-done((bf16[512,128]{1,0:T(8,128)(2,1)S(1)}, bf16[512,128]{1,0:T(8,128)(2,1)S(1)}, u32[]{:S(2)}, u32[]{:S(2)}) %collective-permute-start.2) | collective-permute-done | bytes 131104 | tf_op jit(solution)/shard_map/ppermute | solution.py:15
  23.8 1.9 %collective-permute-start.7 = (bf16[512,256]{1,0:T(8,128)(2,1)S(1)}, bf16[512,256]{1,0:T(8,128)(2,1)S(1)}, u32[]{:S(2)}, u32[]{:S(2)}) collective-permute-start(bf16[512,256]{1,0:T(8,128)(2,1)S(1)} %get-tuple-element.62), channel_id=1, source_target_pairs={{0,16},{8,24},{16,0},{24,8},{1,17},{9,25},{17,1},{25,9},{2,18},{10... | collective-permute-start | bytes 786440 | tf_op jit(solution)/shard_map/ppermute | solution.py:15
  26.1 6.6 %collective-permute-done.8 = bf16[576,512]{1,0:T(8,128)(2,1)S(1)} collective-permute-done((bf16[576,512]{1,0:T(8,128)(2,1)S(1)}, bf16[576,512]{1,0:T(8,128)(2,1)S(1)}, u32[]{:S(2)}, u32[]{:S(2)}) %collective-permute-start.8) | collective-permute-done | bytes 589856 | tf_op jit(solution)/shard_map/ppermute | solution.py:211
  35.6 2.0 %collective-permute-start.13 = (bf16[1024,256]{1,0:T(8,128)(2,1)S(1)}, bf16[1024,256]{1,0:T(8,128)(2,1)S(1)}, u32[]{:S(2)}, u32[]{:S(2)}) collective-permute-start(bf16[1024,256]{1,0:T(8,128)(2,1)S(1)} %constant_dynamic-update-slice_fusion.refs_0_), channel_id=1, source_target_pairs={{0,16},{8,24},{16,0},{24,8},{1,17},{9,25},{17,1},{25,9},{2,18},{10... | collective-permute-start | bytes 1572872 | tf_op jit(solution)/shard_map/ppermute | solution.py:15
  37.8 4.6 %collective-permute-done.9 = bf16[576,512]{1,0:T(8,128)(2,1)S(1)} collective-permute-done((bf16[576,512]{1,0:T(8,128)(2,1)S(1)}, bf16[576,512]{1,0:T(8,128)(2,1)S(1)}, u32[]{:S(2)}, u32[]{:S(2)}) %collective-permute-start.9) | collective-permute-done | bytes 589856 | tf_op jit(solution)/shard_map/ppermute | solution.py:211
  42.5 2.9 %collective-permute-start.10 = (bf16[576,512]{1,0:T(8,128)(2,1)S(1)}, bf16[576,512]{1,0:T(8,128)(2,1)S(1)}, u32[]{:S(2)}, u32[]{:S(2)}) collective-permute-start(bf16[576,512]{1,0:T(8,128)(2,1)S(1)} %add.19.refs_0_), channel_id=1, source_target_pairs={{1,9},{3,11},{5,13},{7,15},{9,1},{11,3},{13,5},{15,7},{17,25},{19,... | collective-permute-start | bytes 1769480 | tf_op jit(solution)/shard_map/ppermute | solution.py:218
  46.4 3.9 %collective-permute-start.11 = (bf16[576,512]{1,0:T(8,128)(2,1)S(1)}, bf16[576,512]{1,0:T(8,128)(2,1)S(1)}, u32[]{:S(2)}, u32[]{:S(2)}) collective-permute-start(bf16[576,512]{1,0:T(8,128)(2,1)S(1)} %add.19.refs_0_), channel_id=1, source_target_pairs={{1,17},{3,19},{5,21},{7,23},{9,25},{11,27},{13,29},{15,31},{17,1},... | collective-permute-start | bytes 1769480 | tf_op jit(solution)/shard_map/ppermute | solution.py:218
  50.2 2.4 %collective-permute-start.12 = (bf16[576,512]{1,0:T(8,128)(2,1)S(1)}, bf16[576,512]{1,0:T(8,128)(2,1)S(1)}, u32[]{:S(2)}, u32[]{:S(2)}) collective-permute-start(bf16[576,512]{1,0:T(8,128)(2,1)S(1)} %add.19.refs_0_), channel_id=1, source_target_pairs={{1,25},{3,27},{5,29},{7,31},{9,17},{11,19},{13,21},{15,23},{17,9},... | collective-permute-start | bytes 1769480 | tf_op jit(solution)/shard_map/ppermute | solution.py:218
  55.4 7.0 %shard_map.47 = (f32[1024,1024]{1,0:T(8,128)S(1)}, bf16[2048,1024]{1,0:T(8,128)(2,1)S(1)}, f32[8,1024]{1,0:T(8,128)S(1)}) custom-call(s32[4]{0:T(128)S(1)} %pad_add_fusion.flags, bf16[1024,2048]{1,0:T(8,128)(2,1)S(1)} %copy-done, bf16[1024,256]{1,0:T(8,128)(2,1)S(1)} %constant_dynamic-update-slice_fusion.refs_0_, ...), custom_call_target="tpu_custom_call" | custom-call | flops 1 | bytes 1 | tf_op jit(solution)/shard_map/pallas_call | solution.py:162
  63.8 3.5 %shard_map.48.own = bf16[1024,512]{1,0:T(8,128)(2,1)S(1)} custom-call(s32[4]{0:T(128)S(1)} %pad_add_fusion.flags, f32[2,256,256]{2,1,0:T(8,128)S(1)} %copy-done.1, bf16[2048,1024]{1,0:T(8,128)(2,1)S(1)} %get-tuple-element.71.ritz, bf16[576,512]{1,0:T(8,128)(2,1)S(1)} %add.19.refs_0_, bf16[576,512]{1,0:T(8,128)(2,1)S(1)} %collective-permute-done.10.refs_1_, ...), custom_call_target="tpu_custom_call" | custom-call | flops 1 | bytes 1 | tf_op jit(solution)/shard_map/pallas_call | solution.py:162
  68.7 3.5 %shard_map.50.own = bf16[1024,512]{1,0:T(8,128)(2,1)S(1)} custom-call(s32[4]{0:T(128)S(1)} %pad_add_fusion.flags, f32[2,256,256]{2,1,0:T(8,128)S(1)} %copy-done.1, bf16[2048,1024]{1,0:T(8,128)(2,1)S(1)} %get-tuple-element.71.ritz, bf16[576,512]{1,0:T(8,128)(2,1)S(1)} %add.19.refs_0_, bf16[576,512]{1,0:T(8,128)(2,1)S(1)} %collective-permute-done.10.refs_1_, ...), custom_call_target="tpu_custom_call" | custom-call | flops 1 | bytes 1 | tf_op jit(solution)/shard_map/pallas_call | solution.py:162
  73.5 3.2 %shard_map.49 = (f32[1024,512]{1,0:T(8,128)S(1)}, f32[8,512]{1,0:T(8,128)}) custom-call(s32[4]{0:T(128)S(1)} %pad_add_fusion.flags, f32[1024,1024]{1,0:T(8,128)S(1)} %get-tuple-element.67.rotated, f32[8,1024]{1,0:T(8,128)S(1)} %get-tuple-element.68.peak, bf16[1024,512]{1,0:T(8,128)(2,1)S(1)} %get-tuple-element.69.cols_high, ...), custom_call_target="tpu_custom_call" | custom-call | flops 1 | bytes 1 | tf_op jit(solution)/shard_map/pallas_call | solution.py:162
  77.2 2.5 %shard_map.51 = (f32[1024,512]{1,0:T(8,128)S(1)}, f32[8,512]{1,0:T(8,128)S(1)}) custom-call(s32[4]{0:T(128)S(1)} %pad_add_fusion.flags, f32[1024,1024]{1,0:T(8,128)S(1)} %get-tuple-element.67.rotated, f32[8,1024]{1,0:T(8,128)S(1)} %get-tuple-element.68.peak, bf16[1024,512]{1,0:T(8,128)(2,1)S(1)} %get-tuple-element.69.cols_high, ...), custom_call_target="tpu_custom_call" | custom-call | flops 1 | bytes 1 | tf_op jit(solution)/shard_map/pallas_call | solution.py:162
  84.0 4.0 %collective-permute-start.23 = (f16[1024,128]{1,0:T(8,128)(2,1)S(1)}, f16[1024,128]{1,0:T(8,128)(2,1)S(1)}, u32[]{:S(2)}, u32[]{:S(2)}) collective-permute-start(f16[1024,128]{1,0:T(8,128)(2,1)S(1)} %get-tuple-element.82), channel_id=1, source_target_pairs={{0,5},{1,4},{2,7},{3,6},{4,1},{5,0},{6,3},{7,2},{8,13},{9,12},{10,... | collective-permute-start | bytes 786440 | tf_op jit(solution)/shard_map/ppermute | solution.py:15
  88.0 4.8 %collective-permute-done.27 = f16[1024,128]{1,0:T(8,128)(2,1)S(1)} collective-permute-done((f16[1024,128]{1,0:T(8,128)(2,1)S(1)}, f16[1024,128]{1,0:T(8,128)(2,1)S(1)}, u32[]{:S(2)}, u32[]{:S(2)}) %collective-permute-start.27) | collective-permute-done | bytes 262176 | tf_op jit(solution)/shard_map/ppermute | solution.py:15
  92.8 2.0 %collective-permute-start.24 = (f16[1024,128]{1,0:T(8,128)(2,1)S(1)}, f16[1024,128]{1,0:T(8,128)(2,1)S(1)}, u32[]{:S(2)}, u32[]{:S(2)}) collective-permute-start(f16[1024,128]{1,0:T(8,128)(2,1)S(1)} %get-tuple-element.83), channel_id=1, source_target_pairs={{0,7},{1,6},{2,5},{3,4},{4,3},{5,2},{6,1},{7,0},{8,15},{9,14},{10,... | collective-permute-start | bytes 786440 | tf_op jit(solution)/shard_map/ppermute | solution.py:15
  96.7 2.0 %collective-permute-done.25 = f16[1024,128]{1,0:T(8,128)(2,1)S(1)} collective-permute-done((f16[1024,128]{1,0:T(8,128)(2,1)S(1)}, f16[1024,128]{1,0:T(8,128)(2,1)S(1)}, u32[]{:S(2)}, u32[]{:S(2)}) %collective-permute-start.25) | collective-permute-done | bytes 262176 | tf_op jit(solution)/shard_map/ppermute | solution.py:15
  98.7 2.8 %collective-permute-done.21 = f16[1024,128]{1,0:T(8,128)(2,1)S(1)} collective-permute-done((f16[1024,128]{1,0:T(8,128)(2,1)S(1)}, f16[1024,128]{1,0:T(8,128)(2,1)S(1)}, u32[]{:S(2)}, u32[]{:S(2)}) %collective-permute-start.21) | collective-permute-done | bytes 262176 | tf_op jit(solution)/shard_map/ppermute | solution.py:15
  101.6 15.5 %collective-permute-done.22 = f16[1024,128]{1,0:T(8,128)(2,1)S(1)} collective-permute-done((f16[1024,128]{1,0:T(8,128)(2,1)S(1)}, f16[1024,128]{1,0:T(8,128)(2,1)S(1)}, u32[]{:S(2)}, u32[]{:S(2)}) %collective-permute-start.22) | collective-permute-done | bytes 262176 | tf_op jit(solution)/shard_map/ppermute | solution.py:15
  117.1 5.6 %collective-permute-done.23 = f16[1024,128]{1,0:T(8,128)(2,1)S(1)} collective-permute-done((f16[1024,128]{1,0:T(8,128)(2,1)S(1)}, f16[1024,128]{1,0:T(8,128)(2,1)S(1)}, u32[]{:S(2)}, u32[]{:S(2)}) %collective-permute-start.23) | collective-permute-done | bytes 262176 | tf_op jit(solution)/shard_map/ppermute | solution.py:15
  122.7 7.2 %collective-permute-done.24 = f16[1024,128]{1,0:T(8,128)(2,1)S(1)} collective-permute-done((f16[1024,128]{1,0:T(8,128)(2,1)S(1)}, f16[1024,128]{1,0:T(8,128)(2,1)S(1)}, u32[]{:S(2)}, u32[]{:S(2)}) %collective-permute-start.24) | collective-permute-done | bytes 262176 | tf_op jit(solution)/shard_map/ppermute | solution.py:15
  129.9 2.1 %shard_map.53 = f32[8192,128]{1,0:T(8,128)} custom-call(s32[4]{0:T(128)S(1)} %pad_add_fusion.flags, f32[8,512]{1,0:T(8,128)S(1)} %get-tuple-element.79.power, f32[1024,128]{1,0:T(8,128)S(1)} %convert_element_type.45.refs_0_, f32[1024,128]{1,0:T(8,128)S(1)} %convert_element_type.46.refs_1_, ...), custom_call_target="tpu_custom_call", output_to_operand_aliasing={{}: (7, {})} | custom-call | tf_op jit(solution)/shard_map/pallas_call | solution.py:266
  (75 shorter events, 29.7 us)
Async XLA Ops:
  2.8 17.9 %collective-permute-start.3 = (bf16[576,512]{1,0:T(8,128)(2,1)S(1)}, bf16[576,512]{1,0:T(8,128)(2,1)S(1)}, u32[]{:S(2)}, u32[]{:S(2)}) collective-permute-start(bf16[576,512]{1,0:T(8,128)(2,1)S(1)} %pad_maximum_fusion), channel_id=1, source_target_pairs={{31,7}} | collective-permute-start | bytes 1769480 | tf_op jit(solution)/shard_map/ppermute | solution.py:197
  3.6 17.1 %collective-permute-start.4 = (bf16[576,512]{1,0:T(8,128)(2,1)S(1)}, bf16[576,512]{1,0:T(8,128)(2,1)S(1)}, u32[]{:S(2)}, u32[]{:S(2)}) collective-permute-start(bf16[576,512]{1,0:T(8,128)(2,1)S(1)} %pad_maximum_fusion.1), channel_id=1, source_target_pairs={{31,15}} | collective-permute-start | bytes 1769480 | tf_op jit(solution)/shard_map/ppermute | solution.py:197
  4.3 16.3 %collective-permute-start.5 = (bf16[576,512]{1,0:T(8,128)(2,1)S(1)}, bf16[576,512]{1,0:T(8,128)(2,1)S(1)}, u32[]{:S(2)}, u32[]{:S(2)}) collective-permute-start(bf16[576,512]{1,0:T(8,128)(2,1)S(1)} %pad_maximum_fusion.2), channel_id=1, source_target_pairs={{31,23}} | collective-permute-start | bytes 1769480 | tf_op jit(solution)/shard_map/ppermute | solution.py:197
  5.1 9.1 %collective-permute-start.1 = (bf16[512,128]{1,0:T(8,128)(2,1)S(1)}, bf16[512,128]{1,0:T(8,128)(2,1)S(1)}, u32[]{:S(2)}, u32[]{:S(2)}) collective-permute-start(bf16[512,128]{1,0:T(8,128)(2,1)S(1)} %copy-done.2), channel_id=1, source_target_pairs={{0,4},{1,5},{2,6},{3,7},{4,0},{5,1},{6,2},{7,3},{8,12},{9,13},{10,... | collective-permute-start | bytes 393224 | tf_op jit(solution)/shard_map/ppermute | solution.py:15
  9.5 11.2 %collective-permute-start.2 = (bf16[512,128]{1,0:T(8,128)(2,1)S(1)}, bf16[512,128]{1,0:T(8,128)(2,1)S(1)}, u32[]{:S(2)}, u32[]{:S(2)}) collective-permute-start(bf16[512,128]{1,0:T(8,128)(2,1)S(1)} %copy-done.2), channel_id=1, source_target_pairs={{0,6},{1,7},{2,4},{3,5},{4,2},{5,3},{6,0},{7,1},{8,14},{9,15},{10,... | collective-permute-start | bytes 393224 | tf_op jit(solution)/shard_map/ppermute | solution.py:15
  21.0 11.7 %collective-permute-start.8 = (bf16[576,512]{1,0:T(8,128)(2,1)S(1)}, bf16[576,512]{1,0:T(8,128)(2,1)S(1)}, u32[]{:S(2)}, u32[]{:S(2)}) collective-permute-start(bf16[576,512]{1,0:T(8,128)(2,1)S(1)} %fusion.8), channel_id=1, source_target_pairs={{7,3},{15,11},{23,19},{31,27}} | collective-permute-start | bytes 1769480 | tf_op jit(solution)/shard_map/ppermute | solution.py:211
  22.6 10.3 %collective-permute-start.6 = (bf16[512,256]{1,0:T(8,128)(2,1)S(1)}, bf16[512,256]{1,0:T(8,128)(2,1)S(1)}, u32[]{:S(2)}, u32[]{:S(2)}) collective-permute-start(bf16[512,256]{1,0:T(8,128)(2,1)S(1)} %get-tuple-element.60), channel_id=1, source_target_pairs={{0,8},{8,0},{16,24},{24,16},{1,9},{9,1},{17,25},{25,17},{2,10},{10... | collective-permute-start | bytes 786440 | tf_op jit(solution)/shard_map/ppermute | solution.py:15
  23.8 9.0 %collective-permute-start.7 = (bf16[512,256]{1,0:T(8,128)(2,1)S(1)}, bf16[512,256]{1,0:T(8,128)(2,1)S(1)}, u32[]{:S(2)}, u32[]{:S(2)}) collective-permute-start(bf16[512,256]{1,0:T(8,128)(2,1)S(1)} %get-tuple-element.62), channel_id=1, source_target_pairs={{0,16},{8,24},{16,0},{24,8},{1,17},{9,25},{17,1},{25,9},{2,18},{10... | collective-permute-start | bytes 786440 | tf_op jit(solution)/shard_map/ppermute | solution.py:15
  32.9 13.4 %collective-permute-start.14 = (bf16[1024,256]{1,0:T(8,128)(2,1)S(1)}, bf16[1024,256]{1,0:T(8,128)(2,1)S(1)}, u32[]{:S(2)}, u32[]{:S(2)}) collective-permute-start(bf16[1024,256]{1,0:T(8,128)(2,1)S(1)} %constant_dynamic-update-slice_fusion.2.refs_2_), channel_id=1, source_target_pairs={{0,8},{8,0},{16,24},{24,16},{1,9},{9,1},{17,25},{25,17},{2,10},{10... | collective-permute-start | bytes 1572872 | tf_op jit(solution)/shard_map/ppermute | solution.py:15
  34.2 16.0 %collective-permute-start.17 = (bf16[1024,256]{1,0:T(8,128)(2,1)S(1)}, bf16[1024,256]{1,0:T(8,128)(2,1)S(1)}, u32[]{:S(2)}, u32[]{:S(2)}) collective-permute-start(bf16[1024,256]{1,0:T(8,128)(2,1)S(1)} %constant_dynamic-update-slice_fusion.2.refs_2_), channel_id=1, source_target_pairs={{0,1},{1,0},{2,3},{3,2},{4,5},{5,4},{6,7},{7,6},{8,9},{9,8},{10,11... | collective-permute-start | bytes 1572872 | tf_op jit(solution)/shard_map/ppermute | solution.py:15
  34.2 8.1 %collective-permute-start.9 = (bf16[576,512]{1,0:T(8,128)(2,1)S(1)}, bf16[576,512]{1,0:T(8,128)(2,1)S(1)}, u32[]{:S(2)}, u32[]{:S(2)}) collective-permute-start(bf16[576,512]{1,0:T(8,128)(2,1)S(1)} %add.18), channel_id=1, source_target_pairs={{7,5},{3,1},{15,13},{11,9},{23,21},{19,17},{31,29},{27,25}} | collective-permute-start | bytes 1769480 | tf_op jit(solution)/shard_map/ppermute | solution.py:211
  35.6 17.1 %collective-permute-start.13 = (bf16[1024,256]{1,0:T(8,128)(2,1)S(1)}, bf16[1024,256]{1,0:T(8,128)(2,1)S(1)}, u32[]{:S(2)}, u32[]{:S(2)}) collective-permute-start(bf16[1024,256]{1,0:T(8,128)(2,1)S(1)} %constant_dynamic-update-slice_fusion.refs_0_), channel_id=1, source_target_pairs={{0,16},{8,24},{16,0},{24,8},{1,17},{9,25},{17,1},{25,9},{2,18},{10... | collective-permute-start | bytes 1572872 | tf_op jit(solution)/shard_map/ppermute | solution.py:15
  37.6 15.2 %collective-permute-start.15 = (bf16[1024,256]{1,0:T(8,128)(2,1)S(1)}, bf16[1024,256]{1,0:T(8,128)(2,1)S(1)}, u32[]{:S(2)}, u32[]{:S(2)}) collective-permute-start(bf16[1024,256]{1,0:T(8,128)(2,1)S(1)} %constant_dynamic-update-slice_fusion.refs_0_), channel_id=1, source_target_pairs={{0,1},{1,0},{2,3},{3,2},{4,5},{5,4},{6,7},{7,6},{8,9},{9,8},{10,11... | collective-permute-start | bytes 1572872 | tf_op jit(solution)/shard_map/ppermute | solution.py:15
  42.5 19.9 %collective-permute-start.10 = (bf16[576,512]{1,0:T(8,128)(2,1)S(1)}, bf16[576,512]{1,0:T(8,128)(2,1)S(1)}, u32[]{:S(2)}, u32[]{:S(2)}) collective-permute-start(bf16[576,512]{1,0:T(8,128)(2,1)S(1)} %add.19.refs_0_), channel_id=1, source_target_pairs={{1,9},{3,11},{5,13},{7,15},{9,1},{11,3},{13,5},{15,7},{17,25},{19,... | collective-permute-start | bytes 1769480 | tf_op jit(solution)/shard_map/ppermute | solution.py:218
  46.4 17.4 %collective-permute-start.11 = (bf16[576,512]{1,0:T(8,128)(2,1)S(1)}, bf16[576,512]{1,0:T(8,128)(2,1)S(1)}, u32[]{:S(2)}, u32[]{:S(2)}) collective-permute-start(bf16[576,512]{1,0:T(8,128)(2,1)S(1)} %add.19.refs_0_), channel_id=1, source_target_pairs={{1,17},{3,19},{5,21},{7,23},{9,25},{11,27},{13,29},{15,31},{17,1},... | collective-permute-start | bytes 1769480 | tf_op jit(solution)/shard_map/ppermute | solution.py:218
  50.2 13.6 %collective-permute-start.12 = (bf16[576,512]{1,0:T(8,128)(2,1)S(1)}, bf16[576,512]{1,0:T(8,128)(2,1)S(1)}, u32[]{:S(2)}, u32[]{:S(2)}) collective-permute-start(bf16[576,512]{1,0:T(8,128)(2,1)S(1)} %add.19.refs_0_), channel_id=1, source_target_pairs={{1,25},{3,27},{5,29},{7,31},{9,17},{11,19},{13,21},{15,23},{17,9},... | collective-permute-start | bytes 1769480 | tf_op jit(solution)/shard_map/ppermute | solution.py:218
  67.3 6.2 %collective-permute-start.19 = (bf16[1024,512]{1,0:T(8,128)(2,1)S(1)}, bf16[1024,512]{1,0:T(8,128)(2,1)S(1)}, u32[]{:S(2)}, u32[]{:S(2)}) collective-permute-start(bf16[1024,512]{1,0:T(8,128)(2,1)S(1)} %shard_map.48.own), channel_id=1, source_target_pairs={{1,0},{3,2},{5,4},{7,6},{9,8},{11,10},{13,12},{15,14},{17,16},{19,... | collective-permute-start | bytes 3145736 | tf_op jit(solution)/shard_map/ppermute | solution.py:238
  72.1 5.1 %collective-permute-start.20 = (bf16[1024,512]{1,0:T(8,128)(2,1)S(1)}, bf16[1024,512]{1,0:T(8,128)(2,1)S(1)}, u32[]{:S(2)}, u32[]{:S(2)}) collective-permute-start(bf16[1024,512]{1,0:T(8,128)(2,1)S(1)} %shard_map.50.own), channel_id=1, source_target_pairs={{1,0},{3,2},{5,4},{7,6},{9,8},{11,10},{13,12},{15,14},{17,16},{19,... | collective-permute-start | bytes 3145736 | tf_op jit(solution)/shard_map/ppermute | solution.py:238
  80.2 12.6 %collective-permute-start.27 = (f16[1024,128]{1,0:T(8,128)(2,1)S(1)}, f16[1024,128]{1,0:T(8,128)(2,1)S(1)}, u32[]{:S(2)}, u32[]{:S(2)}) collective-permute-start(f16[1024,128]{1,0:T(8,128)(2,1)S(1)} %get-tuple-element.93), channel_id=1, source_target_pairs={{0,3},{1,2},{2,1},{3,0},{4,7},{5,6},{6,5},{7,4},{8,11},{9,10},{10,... | collective-permute-start | bytes 786440 | tf_op jit(solution)/shard_map/ppermute | solution.py:15
  81.3 17.4 %collective-permute-start.25 = (f16[1024,128]{1,0:T(8,128)(2,1)S(1)}, f16[1024,128]{1,0:T(8,128)(2,1)S(1)}, u32[]{:S(2)}, u32[]{:S(2)}) collective-permute-start(f16[1024,128]{1,0:T(8,128)(2,1)S(1)} %get-tuple-element.95), channel_id=1, source_target_pairs={{0,2},{1,3},{2,0},{3,1},{4,6},{5,7},{6,4},{7,5},{8,10},{9,11},{10,... | collective-permute-start | bytes 786440 | tf_op jit(solution)/shard_map/ppermute | solution.py:15
  82.1 19.5 %collective-permute-start.21 = (f16[1024,128]{1,0:T(8,128)(2,1)S(1)}, f16[1024,128]{1,0:T(8,128)(2,1)S(1)}, u32[]{:S(2)}, u32[]{:S(2)}) collective-permute-start(f16[1024,128]{1,0:T(8,128)(2,1)S(1)} %get-tuple-element.80), channel_id=1, source_target_pairs={{0,4},{1,5},{2,6},{3,7},{4,0},{5,1},{6,2},{7,3},{8,12},{9,13},{10,... | collective-permute-start | bytes 786440 | tf_op jit(solution)/shard_map/ppermute | solution.py:15
  83.7 33.4 %collective-permute-start.22 = (f16[1024,128]{1,0:T(8,128)(2,1)S(1)}, f16[1024,128]{1,0:T(8,128)(2,1)S(1)}, u32[]{:S(2)}, u32[]{:S(2)}) collective-permute-start(f16[1024,128]{1,0:T(8,128)(2,1)S(1)} %get-tuple-element.81), channel_id=1, source_target_pairs={{0,6},{1,7},{2,4},{3,5},{4,2},{5,3},{6,0},{7,1},{8,14},{9,15},{10,... | collective-permute-start | bytes 786440 | tf_op jit(solution)/shard_map/ppermute | solution.py:15
  84.0 38.7 %collective-permute-start.23 = (f16[1024,128]{1,0:T(8,128)(2,1)S(1)}, f16[1024,128]{1,0:T(8,128)(2,1)S(1)}, u32[]{:S(2)}, u32[]{:S(2)}) collective-permute-start(f16[1024,128]{1,0:T(8,128)(2,1)S(1)} %get-tuple-element.82), channel_id=1, source_target_pairs={{0,5},{1,4},{2,7},{3,6},{4,1},{5,0},{6,3},{7,2},{8,13},{9,12},{10,... | collective-permute-start | bytes 786440 | tf_op jit(solution)/shard_map/ppermute | solution.py:15
  92.8 37.1 %collective-permute-start.24 = (f16[1024,128]{1,0:T(8,128)(2,1)S(1)}, f16[1024,128]{1,0:T(8,128)(2,1)S(1)}, u32[]{:S(2)}, u32[]{:S(2)}) collective-permute-start(f16[1024,128]{1,0:T(8,128)(2,1)S(1)} %get-tuple-element.83), channel_id=1, source_target_pairs={{0,7},{1,6},{2,5},{3,4},{4,3},{5,2},{6,1},{7,0},{8,15},{9,14},{10,... | collective-permute-start | bytes 786440 | tf_op jit(solution)/shard_map/ppermute | solution.py:15
  (8 other events, 63.6 us)

commit v4 on v3

v4 whole, which is shorter than its diff:
```python
import functools

import jax
import jax.numpy as jnp
from jax import lax
from jax.experimental import pallas as pl
from jax.experimental.pallas import tpu as pltpu
from jax.sharding import PartitionSpec as P

ROW, VEC = "row", "vec"
VMEM_LIMIT = 16 * 1024 * 1024


def swapped(value, axis, offset):
    return lax.ppermute(value, axis, [(i, i ^ offset) for i in range(lax.axis_size(axis))])


def steps_of(size):
    return [1 << i for i in range(size.bit_length() - 1)]


def split(value):
    high = value.astype(jnp.bfloat16)
    return high, (value - high.astype(jnp.float32)).astype(jnp.bfloat16)


def split_array(value):
    high = lax.reduce_precision(value, 8, 7)
    return high.astype(jnp.bfloat16), (value - high).astype(jnp.bfloat16)


def mul(a, b):
    return jnp.dot(a, b, preferred_element_type=jnp.float32)


def mul3(a, b):
    left = jnp.concatenate([a[0], a[0], a[1]], axis=1)
    return mul(left, jnp.concatenate([b[0], b[1], b[0]], axis=0))


def side_kernel(*refs):
    *parts, first, second = refs
    cut, width = len(parts) // 2, parts[0].shape[1]
    for i, part in enumerate(parts):
        (first, second)[i // cut][:, i % cut * width : (i % cut + 1) * width] = part[...]


def gathered(parts, places, block):
    each = parts[0].shape[0] // block
    where = {q: (parts[j // each], j % each) for j, q in enumerate(places)}
    return jnp.concatenate([p[i * block : (i + 1) * block, :] for p, i in (where[q] for q in sorted(where))], axis=0)


def rotate_kernel(places, flags, own, other, *refs):
    *parts, out, peak = refs
    n_row, each, rows = len(places[0]), len(parts) // 2, own.shape[0]
    block = own.shape[1] // n_row
    for i, order in enumerate(places):
        ritz = gathered(parts[i * each : (i + 1) * each], order, block)
        where = slice(i * ritz.shape[1], (i + 1) * ritz.shape[1])
        for filtered, core in ((own, flags[1]), (other, 1 - flags[1])):
            left = jnp.concatenate(
                [filtered[:, pl.ds(pl.multiple_of((flags[2] ^ q) * block, block), block)] for q in range(n_row)], axis=1
            )
            out[pl.ds(pl.multiple_of(core * rows, rows), rows), where] = mul(left, ritz)
        most = jnp.max(jnp.abs(ritz.astype(jnp.float32)), axis=0, keepdims=True)
        peak[:, where] = jnp.broadcast_to(most, (peak.shape[0], most.shape[1]))


def solve_kernel(places, flags, inverse, *refs):
    n_row = len(places[0])
    outer, inner, parts, (out, cross, solved) = refs[:n_row], refs[n_row : 2 * n_row], refs[2 * n_row : -3], refs[-3:]
    width = inverse.shape[1]
    block = outer[0].shape[1]
    cross_rows = cross.shape[0] // n_row
    each = len(parts) // 2

    def tail(sent):
        rows = jnp.concatenate([t[: 2 * width, :] for t in sent], axis=1)
        for q in range(n_row):
            start = pl.multiple_of((flags[2] ^ q) * cross_rows, cross_rows)
            cross[pl.ds(start, cross_rows), :] = sent[q][2 * width :, :]
        for i, order in enumerate(places):
            ritz = gathered(parts[i * each : (i + 1) * each], order, block)
            solved[:, i * ritz.shape[1] : (i + 1) * ritz.shape[1]] = mul(rows, ritz)

    pl.when(flags[1] == 1)(lambda: tail(outer))
    pl.when(flags[1] == 0)(lambda: tail(inner))
    if block == 2 * width:
        between = cross[:, :width], cross[:, width:]
    else:
        between = cross[:width, :], cross[width:, :]
    last = mul3(split(inverse[1]), split(solved[width:, :]))
    middle = solved[:width, :] - mul3(between, split(last))
    after = mul3(split(inverse[0]), split(middle))
    out[width : 2 * width, :], out[3 * width :, :] = split(last)
    out[:width, :], out[2 * width : 3 * width, :] = split(after)


def correct_kernel(depth, which, flags, rotated, peak, own, other, solved, out, power):
    rows, size = own.shape[0], own.shape[1] // 2
    half = out.shape[1]
    where = slice(which * half, (which + 1) * half)
    panels = solved[:size, where].astype(jnp.float32) + solved[size:, where].astype(jnp.float32)
    bound = 8.0 * depth * peak[0:1, where] + size * jnp.max(jnp.abs(panels), axis=0, keepdims=True)
    exponent = 14.0 - jnp.floor(jnp.log2(jnp.maximum(bound, 1e-30)))
    scale = jnp.exp2(exponent)
    power[...] = jnp.broadcast_to(jnp.exp2(-exponent), power.shape)
    right = jnp.concatenate([solved[:, where], solved[:size, where]], axis=0)
    for cols, core in ((own, flags[1]), (other, 1 - flags[1])):
        at = pl.ds(pl.multiple_of(core * rows, rows), rows)
        left = jnp.concatenate([cols[:, :size], cols[...]], axis=1)
        out[at, :] = (rotated[at, where] - mul(left, right)) * scale

    @pl.when(flags[0] == 1)
    def _():
        out[2 * rows - size :, :] = panels * scale


def place_kernel(ks, flags, power, *refs):
    out, ready, sems = refs[-3:]
    size, width = ready.shape[1:]
    parts = list(refs)
    copies = []
    for i, (k, count) in enumerate(ks):
        for j in range(count):
            part = parts.pop(0)
            step = part.shape[0]
            ready[i, j * step : (j + 1) * step, :] = part[...] * power[0:1, :width]
        into = out.at[pl.ds(pl.multiple_of(((flags[3] ^ k) >> 1) * size, size), size), :]
        copies.append(pltpu.make_async_copy(ready.at[i], into, sems.at[i]))
        copies[i].start()
    for copy in copies:
        copy.wait()


def call(kernel, flags, inputs, out_shape, scratch):
    spec = lambda space: pl.BlockSpec(memory_space=space)
    specs, arrays, scalars = [], [], [] if flags is None else [flags]
    for value in inputs:
        group = value if isinstance(value, list) else [value]
        specs += [spec(pltpu.HBM if isinstance(value, list) else pltpu.VMEM)] * len(group)
        arrays += group
    return pl.pallas_call(
        kernel,
        in_specs=[spec(pltpu.SMEM)] * len(scalars) + specs,
        out_specs=[spec(pltpu.VMEM)] * len(out_shape),
        out_shape=[jax.ShapeDtypeStruct(*s) for s in out_shape],
        scratch_shapes=scratch,
        compiler_params=pltpu.CompilerParams(vmem_limit_bytes=VMEM_LIMIT),
        cost_estimate=pl.CostEstimate(flops=1, bytes_accessed=1, transcendentals=0),
    )(*scalars, *arrays)


def on_device(filtered, ritz, panel_cols, panel_inverse):
    rows, depth = filtered.shape
    width = panel_inverse.shape[1]
    n_row, n_vec = lax.axis_size(ROW), lax.axis_size(VEC)
    row, vec = lax.axis_index(ROW), lax.axis_index(VEC)
    block, own_cols = ritz.shape
    is_last = (row == n_row - 1) & (vec == n_vec - 1)
    last = n_row * n_vec - 1
    lower = rows - 2 * width
    cut = n_vec // 4
    f32, bf16 = jnp.float32, jnp.bfloat16
    holders = range(1, n_vec, 2)

    last_chip = (row == n_row - 1) & (vec >= n_vec - 2)
    flags = jnp.stack([last_chip.astype(jnp.int32), vec & 1, row, vec])
    filtered, ritz, panel_cols, flags, is_last = lax.optimization_barrier((filtered, ritz, panel_cols, flags, is_last))

    cross = jnp.concatenate(split_array(panel_cols[lower : lower + width, width:]), axis=1 if block == 2 * width else 0)
    cross_rows = cross.shape[0] // n_row
    def part_of(r):
        return jnp.concatenate(
            [filtered[lower:, r * block : (r + 1) * block], cross[r * cross_rows : (r + 1) * cross_rows]], axis=0
        )
    evens = {0: ritz}
    for step in steps_of(n_vec)[:0:-1]:
        evens.update({k | step: swapped(value, VEC, step) for k, value in evens.items()})
    evens = [evens[k] for k in sorted(evens)]
    parts = [lax.ppermute(part_of(r), (ROW, VEC), [(last, r * n_vec + n_vec - 1)]) for r in range(n_row - 1)]
    evens, parts, shared, cols = lax.optimization_barrier((evens, parts, filtered, panel_cols))
    shared = swapped(shared, VEC, 1)
    cols = jnp.concatenate(split_array(cols), axis=1)
    cols = [cols, swapped(cols, VEC, 1)]

    part = sum(parts, jnp.where(is_last, part_of(n_row - 1), jnp.zeros((), bf16)))
    halves = call(side_kernel, None, evens[cut:] + evens[:cut], [((block, cut * own_cols), bf16)] * 2, [])
    halves, places = [[h] for h in halves], [[0], [0]]
    steps, downs, sources = steps_of(n_row), steps_of(n_vec)[:0:-1], [n_vec - 1]
    for i in range(max(len(steps), len(downs))):
        if i < len(steps):
            for which, step in enumerate((steps[i], steps[-1 - i])):
                known = jnp.concatenate(halves[which], axis=0)
                halves[which] = [known, swapped(known, ROW, step)]
                places[which] = places[which] + [q ^ step for q in places[which]]
        if i < len(downs):
            part += lax.ppermute(part, VEC, [(v, v ^ downs[i]) for v in sources])
            sources += [v ^ downs[i] for v in sources]
        if i == 0:
            halves = lax.optimization_barrier(halves)
    across = lambda p: lax.ppermute(p, VEC, [(i, i ^ 1) for i in holders])
    outer = [part] + [
        lax.ppermute(part, (ROW, VEC), [(r * n_vec + i, (r ^ q) * n_vec + i) for r in range(n_row) for i in holders])
        for q in range(1, n_row)
    ]
    inner = [across(part)]
    count = n_vec * own_cols // 2
    parts = sum(halves, [])
    rotated, peak = call(
        functools.partial(rotate_kernel, places), flags, [filtered, shared, *parts],
        [((2 * rows, count), f32), ((8, count), f32)], [],
    )
    outer, rotated, peak, cols = lax.optimization_barrier((outer, rotated, peak, cols))
    inner += [across(p) for p in outer[1:]]

    solved, = call(
        functools.partial(solve_kernel, places), flags, [panel_inverse, *outer, *inner, *parts],
        [((4 * width, count), bf16)], [pltpu.VMEM(cross.shape, bf16), pltpu.VMEM((2 * width, count), f32)],
    )

    def correct(which, solved):
        return call(
            functools.partial(correct_kernel, depth, which), flags, [rotated, peak, *cols, solved],
            [((2 * rows, count // 2), f32), ((8, count // 2), f32)], [],
        )

    piece = lambda values, i: values[:, i * own_cols : (i + 1) * own_cols]
    values, _ = correct(0, solved)
    values = [piece(values, j).astype(jnp.float16) for j in range(cut)]
    values, solved = lax.optimization_barrier((values, solved))
    far = {2 * (cut + j): [swapped(values[j], VEC, 2 * (cut + j))] for j in range(cut)}
    values, power = correct(1, solved)
    near = {}
    for j in range(1, cut):
        value = piece(values, j).astype(jnp.float16)
        near[2 * j] = [swapped(v, VEC, 2 * j) for v in (value[:rows], value[rows:])]
    near[0] = [piece(values, 0)]

    shape = jax.ShapeDtypeStruct((n_vec * rows, own_cols), f32)
    spec = lambda space: pl.BlockSpec(memory_space=space)

    def place(blocks, out):
        parts = sum(blocks.values(), [])
        return pl.pallas_call(
            functools.partial(place_kernel, [(k, len(v)) for k, v in blocks.items()]),
            in_specs=[spec(pltpu.SMEM)] + [spec(pltpu.VMEM)] * (1 + len(parts)) + [spec(pl.ANY)] * len(out),
            out_specs=spec(pl.ANY), out_shape=shape,
            scratch_shapes=[
                pltpu.VMEM((len(blocks), 2 * rows, own_cols), f32), pltpu.SemaphoreType.DMA((len(blocks),))
            ],
            input_output_aliases={2 + len(parts): 0} if out else {},
            compiler_params=pltpu.CompilerParams(vmem_limit_bytes=VMEM_LIMIT),
            cost_estimate=pl.CostEstimate(flops=1, bytes_accessed=1, transcendentals=0),
        )(flags, power, *(v.astype(f32) for v in parts), *out)

    return place(far, [place(near, [])])


def solution(mesh):
    in_specs = (P((ROW, VEC), None), P(ROW, VEC), P((ROW, VEC), None), P())
    return jax.shard_map(on_device, mesh=mesh, in_specs=in_specs, out_specs=P(ROW, VEC), check_vma=False)
```

time: 133 us -> 127 us (0.955)
  starting transfers between devices: 39.6 us -> 33.1 us
  waiting for transfers between devices: 63.3 us -> 69.5 us
  Pallas kernels: 23.5 us -> 17.9 us
    ppermute x18 -> x13, starting transfers between devices: 22.9 us -> 14.3 us  [swapped(): lax.ppermute(value, axis, [(i, i ^ offset) for i in range(lax.axis_size(a...]
    pallas_call x6 -> x5, Pallas kernels: 19.7 us -> 14 us  [call(): pl.pallas_call(kernel, in_specs=[spec(pltpu.SMEM)] * len(scalars) + specs...]
    ppermute x2 -> x4, starting transfers between devices: 2.71 us -> 5.3 us  [on_device(): across = lambda p: lax.ppermute(p, VEC, [(i, i ^ 1) for i in holders])]
    ppermute x3, waiting for transfers between devices: 1.44 us -> 3.83 us  [on_device(): lax.ppermute(part, (ROW, VEC), [(r * n_vec + i, (r ^ q) * n_vec + i) for...]
    ppermute x2 -> x4, waiting for transfers between devices: 0.01 us -> 1.56 us  [on_device(): across = lambda p: lax.ppermute(p, VEC, [(i, i ^ 1) for i in holders])]
    ppermute x18 -> x13, waiting for transfers between devices: 50.7 us -> 52 us  [swapped(): lax.ppermute(value, axis, [(i, i ^ offset) for i in range(lax.axis_size(a...]
  transfers between devices with their start and end apart: 28 -> 25, of which waited for: 15 -> 13; matrix products, arithmetic and copies ran while one was open for 1% -> 2% of each run, Pallas kernels for 12% -> 8%
where the time goes in v4:
time: 127 us; the launch traced here: 126 us
  waiting for transfers between devices  69.5 us (55%)
  starting transfers between devices  33.1 us (26%)
  Pallas kernels  17.9 us (14%)
  other arithmetic  3.1 us (2%)
  local copies, waits for them, and re-layouts  2.3 us (2%)
    ppermute x13, waiting for transfers between devices, swapped(): lax.ppermute(value, axis, [(i, i ^ offset) for i in range(lax.axis_size(a...  52 us
    ppermute x13, starting transfers between devices, swapped(): lax.ppermute(value, axis, [(i, i ^ offset) for i in range(lax.axis_size(a...  14.3 us
    pallas_call x5, Pallas kernels, call(): pl.pallas_call(kernel, in_specs=[spec(pltpu.SMEM)] * len(scalars) + specs...  14 us
    ppermute x2, waiting for transfers between devices, on_device(): part += lax.ppermute(part, VEC, [(v, v ^ downs[i]) for v in sources])  12.1 us
    ppermute x3, starting transfers between devices, on_device(): lax.ppermute(part, (ROW, VEC), [(r * n_vec + i, (r ^ q) * n_vec + i) for...  8.5 us
    ppermute x4, starting transfers between devices, on_device(): across = lambda p: lax.ppermute(p, VEC, [(i, i ^ 1) for i in holders])  5.3 us
    pallas_call x2, Pallas kernels, place(): pl.pallas_call(functools.partial(place_kernel, [(k, len(v)) for k, v in b...  3.89 us
    ppermute x3, waiting for transfers between devices, on_device(): lax.ppermute(part, (ROW, VEC), [(r * n_vec + i, (r ^ q) * n_vec + i) for...  3.83 us
  transfers between devices with their start and end apart: 25, of which 13 were waited for; matrix products, arithmetic and copies ran while one was open for 2% of the time, Pallas kernels for 8%

profile of v4, /device:TPU:9, one launch (start us, length us, event | category | flops | bytes accessed | tf_op | source)
XLA Modules:
  0.0 126.4 jit_solution(10015416384061424613)
XLA Ops:
  1.1 1.8 %fusion.12 = (bf16[512,512]{1,0:T(8,128)(2,1)S(1)}, bf16[512,512]{1,0:T(8,128)(2,1)S(1)}, bf16[512,512]{1,0:T(8,128)(2,1)S(1)}, bf16[512,512]{1,0:T(8,128)(2,1)S(1)}) fusion(bf16[1024,2048]{1,0:T(8,128)(2,1)} %own), kind=kLoop, calls=%fused_computation.32 | loop fusion | bytes 4194304 | tf_op jit(solution)/shard_map/slice | solution.py:176
  5.5 3.0 %collective-permute-start.1 = (bf16[512,128]{1,0:T(8,128)(2,1)S(1)}, bf16[512,128]{1,0:T(8,128)(2,1)S(1)}, u32[]{:S(2)}, u32[]{:S(2)}) collective-permute-start(bf16[512,128]{1,0:T(8,128)(2,1)S(1)} %copy-done.2), channel_id=1, source_target_pairs={{0,4},{1,5},{2,6},{3,7},{4,0},{5,1},{6,2},{7,3},{8,12},{9,13},{10,... | collective-permute-start | bytes 393224 | tf_op jit(solution)/shard_map/ppermute | solution.py:15
  8.5 5.4 %collective-permute-done.1.refs_0_ = bf16[512,128]{1,0:T(8,128)(2,1)S(1)} collective-permute-done((bf16[512,128]{1,0:T(8,128)(2,1)S(1)}, bf16[512,128]{1,0:T(8,128)(2,1)S(1)}, u32[]{:S(2)}, u32[]{:S(2)}) %collective-permute-start.1) | collective-permute-done | bytes 131104 | tf_op jit(solution)/shard_map/ppermute | solution.py:15
  14.0 4.5 %collective-permute-done.2.refs_1_ = bf16[512,128]{1,0:T(8,128)(2,1)S(1)} collective-permute-done((bf16[512,128]{1,0:T(8,128)(2,1)S(1)}, bf16[512,128]{1,0:T(8,128)(2,1)S(1)}, u32[]{:S(2)}, u32[]{:S(2)}) %collective-permute-start.2) | collective-permute-done | bytes 131104 | tf_op jit(solution)/shard_map/ppermute | solution.py:15
  18.5 1.4 %collective-permute-start.11 = (bf16[1024,2048]{1,0:T(8,128)(2,1)S(1)}, bf16[1024,2048]{1,0:T(8,128)(2,1)S(1)}, u32[]{:S(2)}, u32[]{:S(2)}) collective-permute-start(bf16[1024,2048]{1,0:T(8,128)(2,1)S(1)} %copy-done), channel_id=1, source_target_pairs={{0,1},{1,0},{2,3},{3,2},{4,5},{5,4},{6,7},{7,6},{8,9},{9,8},{10,11... | collective-permute-start | bytes 12582920 | tf_op jit(solution)/shard_map/ppermute | solution.py:15
  21.2 1.7 %collective-permute-start.13 = (bf16[512,256]{1,0:T(8,128)(2,1)S(1)}, bf16[512,256]{1,0:T(8,128)(2,1)S(1)}, u32[]{:S(2)}, u32[]{:S(2)}) collective-permute-start(bf16[512,256]{1,0:T(8,128)(2,1)S(1)} %get-tuple-element.58), channel_id=1, source_target_pairs={{0,16},{8,24},{16,0},{24,8},{1,17},{9,25},{17,1},{25,9},{2,18},{10... | collective-permute-start | bytes 786440 | tf_op jit(solution)/shard_map/ppermute | solution.py:15
  25.8 2.1 %collective-permute-done.12 = bf16[512,256]{1,0:T(8,128)(2,1)S(1)} collective-permute-done((bf16[512,256]{1,0:T(8,128)(2,1)S(1)}, bf16[512,256]{1,0:T(8,128)(2,1)S(1)}, u32[]{:S(2)}, u32[]{:S(2)}) %collective-permute-start.12) | collective-permute-done | bytes 262176 | tf_op jit(solution)/shard_map/ppermute | solution.py:15
  27.9 1.3 %collective-permute-done.13 = bf16[512,256]{1,0:T(8,128)(2,1)S(1)} collective-permute-done((bf16[512,256]{1,0:T(8,128)(2,1)S(1)}, bf16[512,256]{1,0:T(8,128)(2,1)S(1)}, u32[]{:S(2)}, u32[]{:S(2)}) %collective-permute-start.13) | collective-permute-done | bytes 262176 | tf_op jit(solution)/shard_map/ppermute | solution.py:15
  30.6 5.4 %collective-permute-done.6 = bf16[576,512]{1,0:T(8,128)(2,1)S(1)} collective-permute-done((bf16[576,512]{1,0:T(8,128)(2,1)S(1)}, bf16[576,512]{1,0:T(8,128)(2,1)S(1)}, u32[]{:S(2)}, u32[]{:S(2)}) %collective-permute-start.6) | collective-permute-done | bytes 589856 | tf_op jit(solution)/shard_map/ppermute | solution.py:199
  37.6 6.7 %collective-permute-done.7 = bf16[576,512]{1,0:T(8,128)(2,1)S(1)} collective-permute-done((bf16[576,512]{1,0:T(8,128)(2,1)S(1)}, bf16[576,512]{1,0:T(8,128)(2,1)S(1)}, u32[]{:S(2)}, u32[]{:S(2)}) %collective-permute-start.7) | collective-permute-done | bytes 589856 | tf_op jit(solution)/shard_map/ppermute | solution.py:199
  44.5 2.1 %collective-permute-start.8 = (bf16[576,512]{1,0:T(8,128)(2,1)S(1)}, bf16[576,512]{1,0:T(8,128)(2,1)S(1)}, u32[]{:S(2)}, u32[]{:S(2)}) collective-permute-start(bf16[576,512]{1,0:T(8,128)(2,1)S(1)} %add.19.refs_0_), channel_id=1, source_target_pairs={{1,9},{3,11},{5,13},{7,15},{9,1},{11,3},{13,5},{15,7},{17,25},{19,... | collective-permute-start | bytes 1769480 | tf_op jit(solution)/shard_map/ppermute | solution.py:205
  46.5 2.1 %collective-permute-start.9 = (bf16[576,512]{1,0:T(8,128)(2,1)S(1)}, bf16[576,512]{1,0:T(8,128)(2,1)S(1)}, u32[]{:S(2)}, u32[]{:S(2)}) collective-permute-start(bf16[576,512]{1,0:T(8,128)(2,1)S(1)} %add.19.refs_0_), channel_id=1, source_target_pairs={{1,17},{3,19},{5,21},{7,23},{9,25},{11,27},{13,29},{15,31},{17,1},... | collective-permute-start | bytes 1769480 | tf_op jit(solution)/shard_map/ppermute | solution.py:205
  48.6 4.4 %collective-permute-start.10 = (bf16[576,512]{1,0:T(8,128)(2,1)S(1)}, bf16[576,512]{1,0:T(8,128)(2,1)S(1)}, u32[]{:S(2)}, u32[]{:S(2)}) collective-permute-start(bf16[576,512]{1,0:T(8,128)(2,1)S(1)} %add.19.refs_0_), channel_id=1, source_target_pairs={{1,25},{3,27},{5,29},{7,31},{9,17},{11,19},{13,21},{15,23},{17,9},... | collective-permute-start | bytes 1769480 | tf_op jit(solution)/shard_map/ppermute | solution.py:205
  54.4 5.3 %shard_map.47 = (f32[2048,512]{1,0:T(8,128)S(1)}, f32[8,512]{1,0:T(8,128)S(1)}) custom-call(s32[4]{0:T(128)S(1)} %pad_add_fusion.flags, bf16[1024,2048]{1,0:T(8,128)(2,1)S(1)} %copy-done, bf16[1024,2048]{1,0:T(8,128)(2,1)S(1)} %collective-permute-done.11.other, bf16[1024,256]{1,0:T(8,128)(2,1)S(1)} %constant_dynamic-update-slice_fusion.refs_0_.refs_8_, ...), custom_call_target="tpu_custom_call" | custom-call | flops 1 | bytes 1 | tf_op jit(solution)/shard_map/pallas_call | solution.py:144
  59.7 3.8 %collective-permute-done.9.refs_2_ = bf16[576,512]{1,0:T(8,128)(2,1)S(1)} collective-permute-done((bf16[576,512]{1,0:T(8,128)(2,1)S(1)}, bf16[576,512]{1,0:T(8,128)(2,1)S(1)}, u32[]{:S(2)}, u32[]{:S(2)}) %collective-permute-start.9) | collective-permute-done | bytes 589856 | tf_op jit(solution)/shard_map/ppermute | solution.py:205
  69.1 2.9 %shard_map.48.solved = bf16[1024,512]{1,0:T(8,128)(2,1)S(1)} custom-call(s32[4]{0:T(128)S(1)} %pad_add_fusion.flags, f32[2,256,256]{2,1,0:T(8,128)S(1)} %copy-done.1, bf16[576,512]{1,0:T(8,128)(2,1)S(1)} %add.19.refs_0_, bf16[576,512]{1,0:T(8,128)(2,1)S(1)} %collective-permute-done.8.refs_1_, bf16[576,512]{1,0:T(8,128)(2,1)S(1)} %collective-permute-done.9.refs_2_, ...), custom_call_target="tpu_custom_call" | custom-call | flops 1 | bytes 1 | tf_op jit(solution)/shard_map/pallas_call | solution.py:144
  72.0 3.3 %shard_map.49 = (f32[2048,256]{1,0:T(8,128)S(1)}, f32[8,256]{1,0:T(8,128)}) custom-call(s32[4]{0:T(128)S(1)} %pad_add_fusion.flags, f32[2048,512]{1,0:T(8,128)S(1)} %get-tuple-element.63.rotated, f32[8,512]{1,0:T(8,128)S(1)} %get-tuple-element.64.peak, bf16[1024,1024]{1,0:T(8,128)(2,1)S(1)} %pad_maximum_fusion.own, ...), custom_call_target="tpu_custom_call" | custom-call | flops 1 | bytes 1 | tf_op jit(solution)/shard_map/pallas_call | solution.py:144
  75.7 3.3 %collective-permute-start.22 = (f16[2048,128]{1,0:T(8,128)(2,1)S(1)}, f16[2048,128]{1,0:T(8,128)(2,1)S(1)}, u32[]{:S(2)}, u32[]{:S(2)}) collective-permute-start(f16[2048,128]{1,0:T(8,128)(2,1)S(1)} %get-tuple-element.75), channel_id=1, source_target_pairs={{0,6},{1,7},{2,4},{3,5},{4,2},{5,3},{6,0},{7,1},{8,14},{9,15},{10,... | collective-permute-start | bytes 1572872 | tf_op jit(solution)/shard_map/ppermute | solution.py:15
  79.1 2.5 %shard_map.50 = (f32[2048,256]{1,0:T(8,128)S(1)}, f32[8,256]{1,0:T(8,128)S(1)}) custom-call(s32[4]{0:T(128)S(1)} %pad_add_fusion.flags, f32[2048,512]{1,0:T(8,128)S(1)} %get-tuple-element.63.rotated, f32[8,512]{1,0:T(8,128)S(1)} %get-tuple-element.64.peak, bf16[1024,1024]{1,0:T(8,128)(2,1)S(1)} %pad_maximum_fusion.own, ...), custom_call_target="tpu_custom_call" | custom-call | flops 1 | bytes 1 | tf_op jit(solution)/shard_map/pallas_call | solution.py:144
  83.5 23.3 %collective-permute-done.23 = f16[1024,128]{1,0:T(8,128)(2,1)S(1)} collective-permute-done((f16[1024,128]{1,0:T(8,128)(2,1)S(1)}, f16[1024,128]{1,0:T(8,128)(2,1)S(1)}, u32[]{:S(2)}, u32[]{:S(2)}) %collective-permute-start.23) | collective-permute-done | bytes 262176 | tf_op jit(solution)/shard_map/ppermute | solution.py:15
  106.9 8.0 %collective-permute-done.24 = f16[1024,128]{1,0:T(8,128)(2,1)S(1)} collective-permute-done((f16[1024,128]{1,0:T(8,128)(2,1)S(1)}, f16[1024,128]{1,0:T(8,128)(2,1)S(1)}, u32[]{:S(2)}, u32[]{:S(2)}) %collective-permute-start.24) | collective-permute-done | bytes 262176 | tf_op jit(solution)/shard_map/ppermute | solution.py:15
  114.9 1.9 %shard_map.51.refs_2_ = f32[8192,128]{1,0:T(8,128)} custom-call(s32[4]{0:T(128)S(1)} %pad_add_fusion.flags, f32[8,256]{1,0:T(8,128)S(1)} %get-tuple-element.73.power, f32[1024,128]{1,0:T(8,128)S(1)} %convert_element_type.34.refs_0_, f32[1024,128]{1,0:T(8,128)S(1)} %convert_element_type.35.refs_1_, f32[2048,128]{1,0:T(8,128)S(1)} %slice.61.refs_2_), custom_call_target="tpu_custom_call" | custom-call | flops 1 | bytes 1 | tf_op jit(solution)/shard_map/pallas_call | solution.py:246
  116.9 7.3 %collective-permute-done.22 = f16[2048,128]{1,0:T(8,128)(2,1)S(1)} collective-permute-done((f16[2048,128]{1,0:T(8,128)(2,1)S(1)}, f16[2048,128]{1,0:T(8,128)(2,1)S(1)}, u32[]{:S(2)}, u32[]{:S(2)}) %collective-permute-start.22) | collective-permute-done | bytes 524320 | tf_op jit(solution)/shard_map/ppermute | solution.py:15
  124.3 1.9 %shard_map.52 = f32[8192,128]{1,0:T(8,128)} custom-call(s32[4]{0:T(128)S(1)} %pad_add_fusion.flags, f32[8,256]{1,0:T(8,128)S(1)} %get-tuple-element.73.power, f32[2048,128]{1,0:T(8,128)S(1)} %convert_element_type.32.refs_0_, f32[2048,128]{1,0:T(8,128)S(1)} %convert_element_type.33.refs_1_, f32[8192,128]{1,0:T(8,128)} %shard_map.51.refs_2_), custom_call_target="tpu_custom_call", output_to_operand_aliasing={{}: (4, {})} | custom-call | flops 1 | bytes 1 | tf_op jit(solution)/shard_map/pallas_call | solution.py:246
  (66 shorter events, 20.6 us)
Async XLA Ops:
  3.0 15.4 %collective-permute-start.3 = (bf16[576,512]{1,0:T(8,128)(2,1)S(1)}, bf16[576,512]{1,0:T(8,128)(2,1)S(1)}, u32[]{:S(2)}, u32[]{:S(2)}) collective-permute-start(bf16[576,512]{1,0:T(8,128)(2,1)S(1)} %pad_maximum_fusion.1), channel_id=1, source_target_pairs={{31,7}} | collective-permute-start | bytes 1769480 | tf_op jit(solution)/shard_map/ppermute | solution.py:182
  3.9 14.6 %collective-permute-start.4 = (bf16[576,512]{1,0:T(8,128)(2,1)S(1)}, bf16[576,512]{1,0:T(8,128)(2,1)S(1)}, u32[]{:S(2)}, u32[]{:S(2)}) collective-permute-start(bf16[576,512]{1,0:T(8,128)(2,1)S(1)} %pad_maximum_fusion.2), channel_id=1, source_target_pairs={{31,15}} | collective-permute-start | bytes 1769480 | tf_op jit(solution)/shard_map/ppermute | solution.py:182
  4.8 13.7 %collective-permute-start.5 = (bf16[576,512]{1,0:T(8,128)(2,1)S(1)}, bf16[576,512]{1,0:T(8,128)(2,1)S(1)}, u32[]{:S(2)}, u32[]{:S(2)}) collective-permute-start(bf16[576,512]{1,0:T(8,128)(2,1)S(1)} %fusion.4), channel_id=1, source_target_pairs={{31,23}} | collective-permute-start | bytes 1769480 | tf_op jit(solution)/shard_map/ppermute | solution.py:182
  5.5 8.3 %collective-permute-start.1 = (bf16[512,128]{1,0:T(8,128)(2,1)S(1)}, bf16[512,128]{1,0:T(8,128)(2,1)S(1)}, u32[]{:S(2)}, u32[]{:S(2)}) collective-permute-start(bf16[512,128]{1,0:T(8,128)(2,1)S(1)} %copy-done.2), channel_id=1, source_target_pairs={{0,4},{1,5},{2,6},{3,7},{4,0},{5,1},{6,2},{7,3},{8,12},{9,13},{10,... | collective-permute-start | bytes 393224 | tf_op jit(solution)/shard_map/ppermute | solution.py:15
  8.5 5.5 %collective-permute-start = (bf16[512,128]{1,0:T(8,128)(2,1)S(1)}, bf16[512,128]{1,0:T(8,128)(2,1)S(1)}, u32[]{:S(2)}, u32[]{:S(2)}) collective-permute-start(bf16[512,128]{1,0:T(8,128)(2,1)S(1)} %copy-done.2), channel_id=1, source_target_pairs={{0,2},{1,3},{2,0},{3,1},{4,6},{5,7},{6,4},{7,5},{8,10},{9,11},{10,... | collective-permute-start | bytes 393224 | tf_op jit(solution)/shard_map/ppermute | solution.py:15
  13.8 4.6 %collective-permute-start.2 = (bf16[512,128]{1,0:T(8,128)(2,1)S(1)}, bf16[512,128]{1,0:T(8,128)(2,1)S(1)}, u32[]{:S(2)}, u32[]{:S(2)}) collective-permute-start(bf16[512,128]{1,0:T(8,128)(2,1)S(1)} %collective-permute-done.1.refs_0_), channel_id=1, source_target_pairs={{0,2},{1,3},{2,0},{3,1},{4,6},{5,7},{6,4},{7,5},{8,10},{9,11},{10,... | collective-permute-start | bytes 393224 | tf_op jit(solution)/shard_map/ppermute | solution.py:15
  18.5 34.6 %collective-permute-start.11 = (bf16[1024,2048]{1,0:T(8,128)(2,1)S(1)}, bf16[1024,2048]{1,0:T(8,128)(2,1)S(1)}, u32[]{:S(2)}, u32[]{:S(2)}) collective-permute-start(bf16[1024,2048]{1,0:T(8,128)(2,1)S(1)} %copy-done), channel_id=1, source_target_pairs={{0,1},{1,0},{2,3},{3,2},{4,5},{5,4},{6,7},{7,6},{8,9},{9,8},{10,11... | collective-permute-start | bytes 12582920 | tf_op jit(solution)/shard_map/ppermute | solution.py:15
  19.9 8.0 %collective-permute-start.12 = (bf16[512,256]{1,0:T(8,128)(2,1)S(1)}, bf16[512,256]{1,0:T(8,128)(2,1)S(1)}, u32[]{:S(2)}, u32[]{:S(2)}) collective-permute-start(bf16[512,256]{1,0:T(8,128)(2,1)S(1)} %get-tuple-element.56), channel_id=1, source_target_pairs={{0,8},{8,0},{16,24},{24,16},{1,9},{9,1},{17,25},{25,17},{2,10},{10... | collective-permute-start | bytes 786440 | tf_op jit(solution)/shard_map/ppermute | solution.py:15
  21.2 8.1 %collective-permute-start.13 = (bf16[512,256]{1,0:T(8,128)(2,1)S(1)}, bf16[512,256]{1,0:T(8,128)(2,1)S(1)}, u32[]{:S(2)}, u32[]{:S(2)}) collective-permute-start(bf16[512,256]{1,0:T(8,128)(2,1)S(1)} %get-tuple-element.58), channel_id=1, source_target_pairs={{0,16},{8,24},{16,0},{24,8},{1,17},{9,25},{17,1},{25,9},{2,18},{10... | collective-permute-start | bytes 786440 | tf_op jit(solution)/shard_map/ppermute | solution.py:15
  23.5 40.0 %collective-permute-start.16 = (bf16[1024,1024]{1,0:T(8,128)(2,1)S(1)}, bf16[1024,1024]{1,0:T(8,128)(2,1)S(1)}, u32[]{:S(2)}, u32[]{:S(2)}) collective-permute-start(bf16[1024,1024]{1,0:T(8,128)(2,1)S(1)} %pad_maximum_fusion.own), channel_id=1, source_target_pairs={{0,1},{1,0},{2,3},{3,2},{4,5},{5,4},{6,7},{7,6},{8,9},{9,8},{10,11... | collective-permute-start | bytes 6291464 | tf_op jit(solution)/shard_map/ppermute | solution.py:15
  24.5 11.5 %collective-permute-start.6 = (bf16[576,512]{1,0:T(8,128)(2,1)S(1)}, bf16[576,512]{1,0:T(8,128)(2,1)S(1)}, u32[]{:S(2)}, u32[]{:S(2)}) collective-permute-start(bf16[576,512]{1,0:T(8,128)(2,1)S(1)} %fusion.7), channel_id=1, source_target_pairs={{7,3},{15,11},{23,19},{31,27}} | collective-permute-start | bytes 1769480 | tf_op jit(solution)/shard_map/ppermute | solution.py:199
  29.3 17.2 %collective-permute-start.14 = (bf16[1024,256]{1,0:T(8,128)(2,1)S(1)}, bf16[1024,256]{1,0:T(8,128)(2,1)S(1)}, u32[]{:S(2)}, u32[]{:S(2)}) collective-permute-start(bf16[1024,256]{1,0:T(8,128)(2,1)S(1)} %constant_dynamic-update-slice_fusion.refs_0_.refs_8_), channel_id=1, source_target_pairs={{0,16},{8,24},{16,0},{24,8},{1,17},{9,25},{17,1},{25,9},{2,18},{10... | collective-permute-start | bytes 1572872 | tf_op jit(solution)/shard_map/ppermute | solution.py:15
  36.2 8.1 %collective-permute-start.7 = (bf16[576,512]{1,0:T(8,128)(2,1)S(1)}, bf16[576,512]{1,0:T(8,128)(2,1)S(1)}, u32[]{:S(2)}, u32[]{:S(2)}) collective-permute-start(bf16[576,512]{1,0:T(8,128)(2,1)S(1)} %add.18), channel_id=1, source_target_pairs={{7,5},{3,1},{15,13},{11,9},{23,21},{19,17},{31,29},{27,25}} | collective-permute-start | bytes 1769480 | tf_op jit(solution)/shard_map/ppermute | solution.py:199
  37.5 11.1 %collective-permute-start.15 = (bf16[1024,256]{1,0:T(8,128)(2,1)S(1)}, bf16[1024,256]{1,0:T(8,128)(2,1)S(1)}, u32[]{:S(2)}, u32[]{:S(2)}) collective-permute-start(bf16[1024,256]{1,0:T(8,128)(2,1)S(1)} %constant_dynamic-update-slice_fusion.2.refs_2_.refs_10_), channel_id=1, source_target_pairs={{0,8},{8,0},{16,24},{24,16},{1,9},{9,1},{17,25},{25,17},{2,10},{10... | collective-permute-start | bytes 1572872 | tf_op jit(solution)/shard_map/ppermute | solution.py:15
  44.5 15.2 %collective-permute-start.8 = (bf16[576,512]{1,0:T(8,128)(2,1)S(1)}, bf16[576,512]{1,0:T(8,128)(2,1)S(1)}, u32[]{:S(2)}, u32[]{:S(2)}) collective-permute-start(bf16[576,512]{1,0:T(8,128)(2,1)S(1)} %add.19.refs_0_), channel_id=1, source_target_pairs={{1,9},{3,11},{5,13},{7,15},{9,1},{11,3},{13,5},{15,7},{17,25},{19,... | collective-permute-start | bytes 1769480 | tf_op jit(solution)/shard_map/ppermute | solution.py:205
  46.5 16.9 %collective-permute-start.9 = (bf16[576,512]{1,0:T(8,128)(2,1)S(1)}, bf16[576,512]{1,0:T(8,128)(2,1)S(1)}, u32[]{:S(2)}, u32[]{:S(2)}) collective-permute-start(bf16[576,512]{1,0:T(8,128)(2,1)S(1)} %add.19.refs_0_), channel_id=1, source_target_pairs={{1,17},{3,19},{5,21},{7,23},{9,25},{11,27},{13,29},{15,31},{17,1},... | collective-permute-start | bytes 1769480 | tf_op jit(solution)/shard_map/ppermute | solution.py:205
  48.6 14.9 %collective-permute-start.10 = (bf16[576,512]{1,0:T(8,128)(2,1)S(1)}, bf16[576,512]{1,0:T(8,128)(2,1)S(1)}, u32[]{:S(2)}, u32[]{:S(2)}) collective-permute-start(bf16[576,512]{1,0:T(8,128)(2,1)S(1)} %add.19.refs_0_), channel_id=1, source_target_pairs={{1,25},{3,27},{5,29},{7,31},{9,17},{11,19},{13,21},{15,23},{17,9},... | collective-permute-start | bytes 1769480 | tf_op jit(solution)/shard_map/ppermute | solution.py:205
  53.0 14.5 %collective-permute-start.17 = (bf16[576,512]{1,0:T(8,128)(2,1)S(1)}, bf16[576,512]{1,0:T(8,128)(2,1)S(1)}, u32[]{:S(2)}, u32[]{:S(2)}) collective-permute-start(bf16[576,512]{1,0:T(8,128)(2,1)S(1)} %add.19.refs_0_), channel_id=1, source_target_pairs={{1,0},{3,2},{5,4},{7,6},{9,8},{11,10},{13,12},{15,14},{17,16},{19,... | collective-permute-start | bytes 1769480 | tf_op jit(solution)/shard_map/ppermute | solution.py:203
  63.5 4.0 %collective-permute-start.18 = (bf16[576,512]{1,0:T(8,128)(2,1)S(1)}, bf16[576,512]{1,0:T(8,128)(2,1)S(1)}, u32[]{:S(2)}, u32[]{:S(2)}) collective-permute-start(bf16[576,512]{1,0:T(8,128)(2,1)S(1)} %collective-permute-done.8.refs_1_), channel_id=1, source_target_pairs={{1,0},{3,2},{5,4},{7,6},{9,8},{11,10},{13,12},{15,14},{17,16},{19,... | collective-permute-start | bytes 1769480 | tf_op jit(solution)/shard_map/ppermute | solution.py:203
  64.8 2.9 %collective-permute-start.19 = (bf16[576,512]{1,0:T(8,128)(2,1)S(1)}, bf16[576,512]{1,0:T(8,128)(2,1)S(1)}, u32[]{:S(2)}, u32[]{:S(2)}) collective-permute-start(bf16[576,512]{1,0:T(8,128)(2,1)S(1)} %collective-permute-done.9.refs_2_), channel_id=1, source_target_pairs={{1,0},{3,2},{5,4},{7,6},{9,8},{11,10},{13,12},{15,14},{17,16},{19,... | collective-permute-start | bytes 1769480 | tf_op jit(solution)/shard_map/ppermute | solution.py:203
  75.7 41.2 %collective-permute-start.21 = (f16[2048,128]{1,0:T(8,128)(2,1)S(1)}, f16[2048,128]{1,0:T(8,128)(2,1)S(1)}, u32[]{:S(2)}, u32[]{:S(2)}) collective-permute-start(f16[2048,128]{1,0:T(8,128)(2,1)S(1)} %get-tuple-element.74), channel_id=1, source_target_pairs={{0,4},{1,5},{2,6},{3,7},{4,0},{5,1},{6,2},{7,3},{8,12},{9,13},{10,... | collective-permute-start | bytes 1572872 | tf_op jit(solution)/shard_map/ppermute | solution.py:15
  75.7 48.5 %collective-permute-start.22 = (f16[2048,128]{1,0:T(8,128)(2,1)S(1)}, f16[2048,128]{1,0:T(8,128)(2,1)S(1)}, u32[]{:S(2)}, u32[]{:S(2)}) collective-permute-start(f16[2048,128]{1,0:T(8,128)(2,1)S(1)} %get-tuple-element.75), channel_id=1, source_target_pairs={{0,6},{1,7},{2,4},{3,5},{4,2},{5,3},{6,0},{7,1},{8,14},{9,15},{10,... | collective-permute-start | bytes 1572872 | tf_op jit(solution)/shard_map/ppermute | solution.py:15
  81.9 24.9 %collective-permute-start.23 = (f16[1024,128]{1,0:T(8,128)(2,1)S(1)}, f16[1024,128]{1,0:T(8,128)(2,1)S(1)}, u32[]{:S(2)}, u32[]{:S(2)}) collective-permute-start(f16[1024,128]{1,0:T(8,128)(2,1)S(1)} %get-tuple-element.86), channel_id=1, source_target_pairs={{0,2},{1,3},{2,0},{3,1},{4,6},{5,7},{6,4},{7,5},{8,10},{9,11},{10,... | collective-permute-start | bytes 786440 | tf_op jit(solution)/shard_map/ppermute | solution.py:15
  82.2 32.7 %collective-permute-start.24 = (f16[1024,128]{1,0:T(8,128)(2,1)S(1)}, f16[1024,128]{1,0:T(8,128)(2,1)S(1)}, u32[]{:S(2)}, u32[]{:S(2)}) collective-permute-start(f16[1024,128]{1,0:T(8,128)(2,1)S(1)} %get-tuple-element.85), channel_id=1, source_target_pairs={{0,2},{1,3},{2,0},{3,1},{4,6},{5,7},{6,4},{7,5},{8,10},{9,11},{10,... | collective-permute-start | bytes 786440 | tf_op jit(solution)/shard_map/ppermute | solution.py:15
  (5 other events, 69.3 us)

commit v5 on v4

--- a/solution.py
+++ b/solution.py
@@ -38,11 +38,10 @@
     return mul(left, jnp.concatenate([b[0], b[1], b[0]], axis=0))
 
 
-def side_kernel(*refs):
-    *parts, first, second = refs
-    cut, width = len(parts) // 2, parts[0].shape[1]
-    for i, part in enumerate(parts):
-        (first, second)[i // cut][:, i % cut * width : (i % cut + 1) * width] = part[...]
+def side_kernel(order, parts, first, second):
+    cut, width = len(order) // 2, parts.shape[2]
+    for i, j in enumerate(order):
+        (first, second)[i // cut][:, i % cut * width : (i % cut + 1) * width] = parts[j]
 
 
 def gathered(parts, places, block):
@@ -68,24 +67,23 @@
 
 
 def solve_kernel(places, flags, inverse, *refs):
-    n_row = len(places[0])
-    outer, inner, parts, (out, cross, solved) = refs[:n_row], refs[n_row : 2 * n_row], refs[2 * n_row : -3], refs[-3:]
+    n_row = len(places)
+    outer, inner, parts, (out, cross, solved) = refs[:n_row], refs[n_row], refs[n_row + 1 : -3], refs[-3:]
+    size = outer[0].shape[0]
     width = inverse.shape[1]
     block = outer[0].shape[1]
     cross_rows = cross.shape[0] // n_row
-    each = len(parts) // 2
 
     def tail(sent):
-        rows = jnp.concatenate([t[: 2 * width, :] for t in sent], axis=1)
+        rows = jnp.concatenate([t[start : start + 2 * width, :] for t, start in sent], axis=1)
         for q in range(n_row):
             start = pl.multiple_of((flags[2] ^ q) * cross_rows, cross_rows)
-            cross[pl.ds(start, cross_rows), :] = sent[q][2 * width :, :]
-        for i, order in enumerate(places):
-            ritz = gathered(parts[i * each : (i + 1) * each], order, block)
-            solved[:, i * ritz.shape[1] : (i + 1) * ritz.shape[1]] = mul(rows, ritz)
-
-    pl.when(flags[1] == 1)(lambda: tail(outer))
-    pl.when(flags[1] == 0)(lambda: tail(inner))
+            t, first = sent[q]
+            cross[pl.ds(start, cross_rows), :] = t[first + 2 * width : first + size, :]
+        solved[...] = mul(rows, gathered(parts, places, block))
+
+    pl.when(flags[1] == 1)(lambda: tail([(t, 0) for t in outer]))
+    pl.when(flags[1] == 0)(lambda: tail([(inner, q * size) for q in range(n_row)]))
     if block == 2 * width:
         between = cross[:, :width], cross[:, width:]
     else:
@@ -101,12 +99,12 @@
     rows, size = own.shape[0], own.shape[1] // 2
     half = out.shape[1]
     where = slice(which * half, (which + 1) * half)
-    panels = solved[:size, where].astype(jnp.float32) + solved[size:, where].astype(jnp.float32)
+    panels = solved[:size, :].astype(jnp.float32) + solved[size:, :].astype(jnp.float32)
     bound = 8.0 * depth * peak[0:1, where] + size * jnp.max(jnp.abs(panels), axis=0, keepdims=True)
     exponent = 14.0 - jnp.floor(jnp.log2(jnp.maximum(bound, 1e-30)))
     scale = jnp.exp2(exponent)
     power[...] = jnp.broadcast_to(jnp.exp2(-exponent), power.shape)
-    right = jnp.concatenate([solved[:, where], solved[:size, where]], axis=0)
+    right = jnp.concatenate([solved[...], solved[:size, :]], axis=0)
     for cols, core in ((own, flags[1]), (other, 1 - flags[1])):
         at = pl.ds(pl.multiple_of(core * rows, rows), rows)
         left = jnp.concatenate([cols[:, :size], cols[...]], axis=1)
@@ -134,7 +132,7 @@
         copy.wait()
 
 
-def call(kernel, flags, inputs, out_shape, scratch):
+def call(kernel, flags, inputs, out_shape, scratch, work=1):
     spec = lambda space: pl.BlockSpec(memory_space=space)
     specs, arrays, scalars = [], [], [] if flags is None else [flags]
     for value in inputs:
@@ -148,7 +146,7 @@
         out_shape=[jax.ShapeDtypeStruct(*s) for s in out_shape],
         scratch_shapes=scratch,
         compiler_params=pltpu.CompilerParams(vmem_limit_bytes=VMEM_LIMIT),
-        cost_estimate=pl.CostEstimate(flops=1, bytes_accessed=1, transcendentals=0),
+        cost_estimate=pl.CostEstimate(flops=work, bytes_accessed=1, transcendentals=0),
     )(*scalars, *arrays)
 
 
@@ -175,18 +173,20 @@
         return jnp.concatenate(
             [filtered[lower:, r * block : (r + 1) * block], cross[r * cross_rows : (r + 1) * cross_rows]], axis=0
         )
-    evens = {0: ritz}
+    own, evens = ritz[None], [0]
     for step in steps_of(n_vec)[:0:-1]:
-        evens.update({k | step: swapped(value, VEC, step) for k, value in evens.items()})
-    evens = [evens[k] for k in sorted(evens)]
+        own = jnp.concatenate([own, swapped(own, VEC, step)])
+        evens += [k ^ step for k in evens]
+    shared = swapped(filtered, VEC, 1)
     parts = [lax.ppermute(part_of(r), (ROW, VEC), [(last, r * n_vec + n_vec - 1)]) for r in range(n_row - 1)]
-    evens, parts, shared, cols = lax.optimization_barrier((evens, parts, filtered, panel_cols))
-    shared = swapped(shared, VEC, 1)
-    cols = jnp.concatenate(split_array(cols), axis=1)
-    cols = [cols, swapped(cols, VEC, 1)]
-
     part = sum(parts, jnp.where(is_last, part_of(n_row - 1), jnp.zeros((), bf16)))
-    halves = call(side_kernel, None, evens[cut:] + evens[:cut], [((block, cut * own_cols), bf16)] * 2, [])
+    cols = jnp.concatenate(split_array(panel_cols), axis=1)
+    own, part, shared, cols = lax.optimization_barrier((own, part, shared, cols))
+
+    order = [evens.index(2 * ((cut + i) % (2 * cut))) for i in range(2 * cut)]
+    halves = call(
+        functools.partial(side_kernel, order), None, [own], [((block, cut * own_cols), bf16)] * 2, []
+    )
     halves, places = [[h] for h in halves], [[0], [0]]
     steps, downs, sources = steps_of(n_row), steps_of(n_vec)[:0:-1], [n_vec - 1]
     for i in range(max(len(steps), len(downs))):
@@ -199,39 +199,44 @@
             part += lax.ppermute(part, VEC, [(v, v ^ downs[i]) for v in sources])
             sources += [v ^ downs[i] for v in sources]
         if i == 0:
-            halves = lax.optimization_barrier(halves)
+            halves, part, cols = lax.optimization_barrier((halves, part, cols))
+            other_cols = swapped(cols, VEC, 1)
+    part, other_cols = lax.optimization_barrier((part, other_cols))
+
     across = lambda p: lax.ppermute(p, VEC, [(i, i ^ 1) for i in holders])
     outer = [part] + [
         lax.ppermute(part, (ROW, VEC), [(r * n_vec + i, (r ^ q) * n_vec + i) for r in range(n_row) for i in holders])
         for q in range(1, n_row)
     ]
-    inner = [across(part)]
     count = n_vec * own_cols // 2
     parts = sum(halves, [])
     rotated, peak = call(
         functools.partial(rotate_kernel, places), flags, [filtered, shared, *parts],
-        [((2 * rows, count), f32), ((8, count), f32)], [],
+        [((2 * rows, count), f32), ((8, count), f32)], [], 1 << 36,
     )
-    outer, rotated, peak, cols = lax.optimization_barrier((outer, rotated, peak, cols))
-    inner += [across(p) for p in outer[1:]]
-
-    solved, = call(
-        functools.partial(solve_kernel, places), flags, [panel_inverse, *outer, *inner, *parts],
-        [((4 * width, count), bf16)], [pltpu.VMEM(cross.shape, bf16), pltpu.VMEM((2 * width, count), f32)],
-    )
+    outer, rotated, peak = lax.optimization_barrier((outer, rotated, peak))
+    inner = across(jnp.concatenate(outer, axis=0))
+
+    def solve(which):
+        solved, = call(
+            functools.partial(solve_kernel, places[which]), flags, [panel_inverse, *outer, inner, *halves[which]],
+            [((4 * width, count // 2), bf16)],
+            [pltpu.VMEM(cross.shape, bf16), pltpu.VMEM((2 * width, count // 2), f32)],
+        )
+        return solved
 
     def correct(which, solved):
         return call(
-            functools.partial(correct_kernel, depth, which), flags, [rotated, peak, *cols, solved],
+            functools.partial(correct_kernel, depth, which), flags, [rotated, peak, cols, other_cols, solved],
             [((2 * rows, count // 2), f32), ((8, count // 2), f32)], [],
         )
 
     piece = lambda values, i: values[:, i * own_cols : (i + 1) * own_cols]
-    values, _ = correct(0, solved)
+    values, _ = correct(0, solve(0))
     values = [piece(values, j).astype(jnp.float16) for j in range(cut)]
-    values, solved = lax.optimization_barrier((values, solved))
+    values, panel_inverse = lax.optimization_barrier((values, panel_inverse))
     far = {2 * (cut + j): [swapped(values[j], VEC, 2 * (cut + j))] for j in range(cut)}
-    values, power = correct(1, solved)
+    values, power = correct(1, solve(1))
     near = {}
     for j in range(1, cut):
         value = piece(values, j).astype(jnp.float16)

time: 127 us -> 122 us (0.961)
  waiting for transfers between devices: 69.5 us -> 64.9 us
  starting transfers between devices: 33.1 us -> 31.3 us
  Pallas kernels: 17.9 us -> 19.4 us
    ppermute x4 -> x1, starting transfers between devices: 5.3 us -> 1.52 us  [on_device(): across = lambda p: lax.ppermute(p, VEC, [(i, i ^ 1) for i in holders])]
    ppermute x13 -> x12, waiting for transfers between devices: 52 us -> 48.9 us  [swapped(): lax.ppermute(value, axis, [(i, i ^ offset) for i in range(lax.axis_size(a...]
    ppermute x3, waiting for transfers between devices: 3.83 us -> 0.96 us  [on_device(): lax.ppermute(part, (ROW, VEC), [(r * n_vec + i, (r ^ q) * n_vec + i) for...]
    ppermute x4 -> x1, waiting for transfers between devices: 1.56 us -> 3.99 us  [on_device(): across = lambda p: lax.ppermute(p, VEC, [(i, i ^ 1) for i in holders])]
    ppermute x3, starting transfers between devices: 8.5 us -> 10.2 us  [on_device(): lax.ppermute(part, (ROW, VEC), [(r * n_vec + i, (r ^ q) * n_vec + i) for...]
    pallas_call x5 -> x6, Pallas kernels: 14 us -> 15.5 us  [call(): pl.pallas_call(kernel, in_specs=[spec(pltpu.SMEM)] * len(scalars) + specs...]
    ppermute x13 -> x12, starting transfers between devices: 14.3 us -> 14.8 us  [swapped(): lax.ppermute(value, axis, [(i, i ^ offset) for i in range(lax.axis_size(a...]
  transfers between devices with their start and end apart: 25 -> 21, of which waited for: 13 -> 10; matrix products, arithmetic and copies ran while one was open for 2% -> 4% of each run, Pallas kernels for 8% -> 10%
where the time goes in v5:
time: 122 us
  waiting for transfers between devices  64.9 us (53%)
  starting transfers between devices  31.3 us (26%)
  Pallas kernels  19.4 us (16%)
  other arithmetic  3.37 us (3%)
  local copies, waits for them, and re-layouts  2.15 us (2%)
    ppermute x12, waiting for transfers between devices, swapped(): lax.ppermute(value, axis, [(i, i ^ offset) for i in range(lax.axis_size(a...  48.9 us
    pallas_call x6, Pallas kernels, call(): pl.pallas_call(kernel, in_specs=[spec(pltpu.SMEM)] * len(scalars) + specs...  15.5 us
    ppermute x12, starting transfers between devices, swapped(): lax.ppermute(value, axis, [(i, i ^ offset) for i in range(lax.axis_size(a...  14.8 us
    ppermute x2, waiting for transfers between devices, on_device(): part += lax.ppermute(part, VEC, [(v, v ^ downs[i]) for v in sources])  11 us
    ppermute x3, starting transfers between devices, on_device(): lax.ppermute(part, (ROW, VEC), [(r * n_vec + i, (r ^ q) * n_vec + i) for...  10.2 us
    ppermute x1, waiting for transfers between devices, on_device(): across = lambda p: lax.ppermute(p, VEC, [(i, i ^ 1) for i in holders])  3.99 us
    pallas_call x2, Pallas kernels, place(): pl.pallas_call(functools.partial(place_kernel, [(k, len(v)) for k, v in b...  3.89 us
    ppermute x2, starting transfers between devices, on_device(): part += lax.ppermute(part, VEC, [(v, v ^ downs[i]) for v in sources])  2.61 us
  transfers between devices with their start and end apart: 21, of which 10 were waited for; matrix products, arithmetic and copies ran while one was open for 4% of the time, Pallas kernels for 10%

profile of v5, /device:TPU:9, one launch (start us, length us, event | category | flops | bytes accessed | tf_op | source)
XLA Modules:
  0.0 121.7 jit_solution(7981908626963477289)
XLA Ops:
  0.8 2.3 %collective-permute-start = (bf16[1,512,128]{2,1,0:T(8,128)(2,1)}, bf16[1,512,128]{2,1,0:T(8,128)(2,1)S(1)}, u32[]{:S(2)}, u32[]{:S(2)}) collective-permute-start(bf16[1,512,128]{2,1,0:T(8,128)(2,1)} %bitcast.5), channel_id=1, source_target_pairs={{0,4},{1,5},{2,6},{3,7},{4,0},{5,1},{6,2},{7,3},{8,12},{9,13},{10,... | collective-permute-start | bytes 393224 | tf_op jit(solution)/shard_map/ppermute | solution.py:15
  4.1 1.7 %fusion.12 = (bf16[512,512]{1,0:T(8,128)(2,1)S(1)}, bf16[512,512]{1,0:T(8,128)(2,1)S(1)}, bf16[512,512]{1,0:T(8,128)(2,1)S(1)}, bf16[512,512]{1,0:T(8,128)(2,1)S(1)}) fusion(bf16[1024,2048]{1,0:T(8,128)(2,1)} %own), kind=kLoop, calls=%fused_computation.35 | loop fusion | bytes 4194304 | tf_op jit(solution)/shard_map/slice | solution.py:174
  10.8 6.1 %collective-permute-done.1 = bf16[2,512,128]{2,1,0:T(8,128)(2,1)S(1)} collective-permute-done((bf16[2,512,128]{2,1,0:T(8,128)(2,1)S(1)}, bf16[2,512,128]{2,1,0:T(8,128)(2,1)S(1)}, u32[]{:S(2)}, u32[]{:S(2)}) %collective-permute-start.1) | collective-permute-done | bytes 262176 | tf_op jit(solution)/shard_map/ppermute | solution.py:15
  21.3 7.6 %collective-permute-done.8 = bf16[576,512]{1,0:T(8,128)(2,1)S(1)} collective-permute-done((bf16[576,512]{1,0:T(8,128)(2,1)S(1)}, bf16[576,512]{1,0:T(8,128)(2,1)S(1)}, u32[]{:S(2)}, u32[]{:S(2)}) %collective-permute-start.8) | collective-permute-done | bytes 589856 | tf_op jit(solution)/shard_map/ppermute | solution.py:199
  31.9 3.3 %collective-permute-start.14 = (bf16[1024,256]{1,0:T(8,128)(2,1)S(1)}, bf16[1024,256]{1,0:T(8,128)(2,1)S(1)}, u32[]{:S(2)}, u32[]{:S(2)}) collective-permute-start(bf16[1024,256]{1,0:T(8,128)(2,1)S(1)} %constant_dynamic-update-slice_fusion.refs_0_.refs_5_), channel_id=1, source_target_pairs={{0,16},{8,24},{16,0},{24,8},{1,17},{9,25},{17,1},{25,9},{2,18},{10... | collective-permute-start | bytes 1572872 | tf_op jit(solution)/shard_map/ppermute | solution.py:15
  35.2 3.4 %collective-permute-done.9 = bf16[576,512]{1,0:T(8,128)(2,1)S(1)} collective-permute-done((bf16[576,512]{1,0:T(8,128)(2,1)S(1)}, bf16[576,512]{1,0:T(8,128)(2,1)S(1)}, u32[]{:S(2)}, u32[]{:S(2)}) %collective-permute-start.9) | collective-permute-done | bytes 589856 | tf_op jit(solution)/shard_map/ppermute | solution.py:199
  38.7 6.0 %collective-permute-start.13 = (bf16[576,512]{1,0:T(8,128)(2,1)S(1)}, bf16[576,512]{1,0:T(8,128)(2,1)S(1)}, u32[]{:S(2)}, u32[]{:S(2)}) collective-permute-start(bf16[576,512]{1,0:T(8,128)(2,1)S(1)} %add.19.refs_0_), channel_id=1, source_target_pairs={{1,25},{3,27},{5,29},{7,31},{9,17},{11,19},{13,21},{15,23},{17,9},... | collective-permute-start | bytes 1769480 | tf_op jit(solution)/shard_map/ppermute | solution.py:208
  44.8 1.9 %collective-permute-start.12 = (bf16[576,512]{1,0:T(8,128)(2,1)S(1)}, bf16[576,512]{1,0:T(8,128)(2,1)S(1)}, u32[]{:S(2)}, u32[]{:S(2)}) collective-permute-start(bf16[576,512]{1,0:T(8,128)(2,1)S(1)} %add.19.refs_0_), channel_id=1, source_target_pairs={{1,17},{3,19},{5,21},{7,23},{9,25},{11,27},{13,29},{15,31},{17,1},... | collective-permute-start | bytes 1769480 | tf_op jit(solution)/shard_map/ppermute | solution.py:208
  46.7 2.2 %collective-permute-start.11 = (bf16[576,512]{1,0:T(8,128)(2,1)S(1)}, bf16[576,512]{1,0:T(8,128)(2,1)S(1)}, u32[]{:S(2)}, u32[]{:S(2)}) collective-permute-start(bf16[576,512]{1,0:T(8,128)(2,1)S(1)} %add.19.refs_0_), channel_id=1, source_target_pairs={{1,9},{3,11},{5,13},{7,15},{9,1},{11,3},{13,5},{15,7},{17,25},{19,... | collective-permute-start | bytes 1769480 | tf_op jit(solution)/shard_map/ppermute | solution.py:208
  48.9 4.6 %collective-permute-done.14.refs_1_.refs_6_ = bf16[1024,256]{1,0:T(8,128)(2,1)S(1)} collective-permute-done((bf16[1024,256]{1,0:T(8,128)(2,1)S(1)}, bf16[1024,256]{1,0:T(8,128)(2,1)S(1)}, u32[]{:S(2)}, u32[]{:S(2)}) %collective-permute-start.14) | collective-permute-done | bytes 524320 | tf_op jit(solution)/shard_map/ppermute | solution.py:15
  53.5 5.3 %shard_map.47 = (f32[2048,512]{1,0:T(8,128)S(1)}, f32[8,512]{1,0:T(8,128)S(1)}) custom-call(s32[4]{0:T(128)S(1)} %pad_add_fusion.flags, bf16[1024,2048]{1,0:T(8,128)(2,1)S(1)} %copy-done.1, bf16[1024,2048]{1,0:T(8,128)(2,1)S(1)} %collective-permute-done.5.other, bf16[1024,256]{1,0:T(8,128)(2,1)S(1)} %constant_dynamic-update-slice_fusion.refs_0_.refs_5_, ...), custom_call_target="tpu_custom_call" | custom-call | flops 68719476736 | bytes 1 | tf_op jit(solution)/shard_map/pallas_call | solution.py:142
  59.9 1.5 %collective-permute-start.16 = (bf16[2304,512]{1,0:T(8,128)(2,1)S(1)}, bf16[2304,512]{1,0:T(8,128)(2,1)S(1)}, u32[]{:S(2)}, u32[]{:S(2)}) collective-permute-start(bf16[2304,512]{1,0:T(8,128)(2,1)S(1)} %pad_maximum_fusion), channel_id=1, source_target_pairs={{1,0},{3,2},{5,4},{7,6},{9,8},{11,10},{13,12},{15,14},{17,16},{19,... | collective-permute-start | bytes 7077896 | tf_op jit(solution)/shard_map/ppermute | solution.py:206
  61.5 4.0 %collective-permute-done.16.refs_4_ = bf16[2304,512]{1,0:T(8,128)(2,1)S(1)} collective-permute-done((bf16[2304,512]{1,0:T(8,128)(2,1)S(1)}, bf16[2304,512]{1,0:T(8,128)(2,1)S(1)}, u32[]{:S(2)}, u32[]{:S(2)}) %collective-permute-start.16) | collective-permute-done | bytes 2359328 | tf_op jit(solution)/shard_map/ppermute | solution.py:206
  65.5 2.2 %shard_map.48.solved = bf16[1024,256]{1,0:T(8,128)(2,1)S(1)} custom-call(s32[4]{0:T(128)S(1)} %pad_add_fusion.flags, f32[2,256,256]{2,1,0:T(8,128)S(1)} %copy-done, bf16[576,512]{1,0:T(8,128)(2,1)S(1)} %add.19.refs_0_, bf16[576,512]{1,0:T(8,128)(2,1)S(1)} %collective-permute-done.11.refs_1_, bf16[576,512]{1,0:T(8,128)(2,1)S(1)} %collective-permute-done.12.refs_2_, ...), custom_call_target="tpu_custom_call" | custom-call | flops 1 | bytes 1 | tf_op jit(solution)/shard_map/pallas_call | solution.py:142
  67.7 3.1 %shard_map.49 = (f32[2048,256]{1,0:T(8,128)S(1)}, f32[8,256]{1,0:T(8,128)}) custom-call(s32[4]{0:T(128)S(1)} %pad_add_fusion.flags, f32[2048,512]{1,0:T(8,128)S(1)} %get-tuple-element.58.rotated, f32[8,512]{1,0:T(8,128)S(1)} %get-tuple-element.59.peak, bf16[1024,1024]{1,0:T(8,128)(2,1)S(1)} %pad_maximum_fusion.1.own, ...), custom_call_target="tpu_custom_call" | custom-call | flops 1 | bytes 1 | tf_op jit(solution)/shard_map/pallas_call | solution.py:142
  71.2 1.6 %collective-permute-start.17 = (f16[2048,128]{1,0:T(8,128)(2,1)S(1)}, f16[2048,128]{1,0:T(8,128)(2,1)S(1)}, u32[]{:S(2)}, u32[]{:S(2)}) collective-permute-start(f16[2048,128]{1,0:T(8,128)(2,1)S(1)} %get-tuple-element.68), channel_id=1, source_target_pairs={{0,4},{1,5},{2,6},{3,7},{4,0},{5,1},{6,2},{7,3},{8,12},{9,13},{10,... | collective-permute-start | bytes 1572872 | tf_op jit(solution)/shard_map/ppermute | solution.py:15
  73.5 2.4 %shard_map.50.solved = bf16[1024,256]{1,0:T(8,128)(2,1)S(1)} custom-call(s32[4]{0:T(128)S(1)} %pad_add_fusion.flags, f32[2,256,256]{2,1,0:T(8,128)S(1)} %copy-done, bf16[576,512]{1,0:T(8,128)(2,1)S(1)} %add.19.refs_0_, bf16[576,512]{1,0:T(8,128)(2,1)S(1)} %collective-permute-done.11.refs_1_, bf16[576,512]{1,0:T(8,128)(2,1)S(1)} %collective-permute-done.12.refs_2_, ...), custom_call_target="tpu_custom_call" | custom-call | flops 1 | bytes 1 | tf_op jit(solution)/shard_map/pallas_call | solution.py:142
  75.9 2.5 %shard_map.51 = (f32[2048,256]{1,0:T(8,128)S(1)}, f32[8,256]{1,0:T(8,128)S(1)}) custom-call(s32[4]{0:T(128)S(1)} %pad_add_fusion.flags, f32[2048,512]{1,0:T(8,128)S(1)} %get-tuple-element.58.rotated, f32[8,512]{1,0:T(8,128)S(1)} %get-tuple-element.59.peak, bf16[1024,1024]{1,0:T(8,128)(2,1)S(1)} %pad_maximum_fusion.1.own, ...), custom_call_target="tpu_custom_call" | custom-call | flops 1 | bytes 1 | tf_op jit(solution)/shard_map/pallas_call | solution.py:142
  78.7 1.4 %collective-permute-start.20 = (f16[1024,128]{1,0:T(8,128)(2,1)S(1)}, f16[1024,128]{1,0:T(8,128)(2,1)S(1)}, u32[]{:S(2)}, u32[]{:S(2)}) collective-permute-start(f16[1024,128]{1,0:T(8,128)(2,1)S(1)} %get-tuple-element.79), channel_id=1, source_target_pairs={{0,2},{1,3},{2,0},{3,1},{4,6},{5,7},{6,4},{7,5},{8,10},{9,11},{10,... | collective-permute-start | bytes 786440 | tf_op jit(solution)/shard_map/ppermute | solution.py:15
  80.3 21.2 %collective-permute-done.20 = f16[1024,128]{1,0:T(8,128)(2,1)S(1)} collective-permute-done((f16[1024,128]{1,0:T(8,128)(2,1)S(1)}, f16[1024,128]{1,0:T(8,128)(2,1)S(1)}, u32[]{:S(2)}, u32[]{:S(2)}) %collective-permute-start.20) | collective-permute-done | bytes 262176 | tf_op jit(solution)/shard_map/ppermute | solution.py:15
  101.5 11.1 %collective-permute-done.19 = f16[1024,128]{1,0:T(8,128)(2,1)S(1)} collective-permute-done((f16[1024,128]{1,0:T(8,128)(2,1)S(1)}, f16[1024,128]{1,0:T(8,128)(2,1)S(1)}, u32[]{:S(2)}, u32[]{:S(2)}) %collective-permute-start.19) | collective-permute-done | bytes 262176 | tf_op jit(solution)/shard_map/ppermute | solution.py:15
  112.6 1.9 %shard_map.52.refs_2_ = f32[8192,128]{1,0:T(8,128)} custom-call(s32[4]{0:T(128)S(1)} %pad_add_fusion.flags, f32[8,256]{1,0:T(8,128)S(1)} %get-tuple-element.67.power, f32[1024,128]{1,0:T(8,128)S(1)} %convert_element_type.34.refs_0_, f32[1024,128]{1,0:T(8,128)S(1)} %convert_element_type.35.refs_1_, f32[2048,128]{1,0:T(8,128)S(1)} %slice.61.refs_2_), custom_call_target="tpu_custom_call" | custom-call | flops 1 | bytes 1 | tf_op jit(solution)/shard_map/pallas_call | solution.py:251
  114.7 4.8 %collective-permute-done.18 = f16[2048,128]{1,0:T(8,128)(2,1)S(1)} collective-permute-done((f16[2048,128]{1,0:T(8,128)(2,1)S(1)}, f16[2048,128]{1,0:T(8,128)(2,1)S(1)}, u32[]{:S(2)}, u32[]{:S(2)}) %collective-permute-start.18) | collective-permute-done | bytes 524320 | tf_op jit(solution)/shard_map/ppermute | solution.py:15
  119.5 1.9 %shard_map.53 = f32[8192,128]{1,0:T(8,128)} custom-call(s32[4]{0:T(128)S(1)} %pad_add_fusion.flags, f32[8,256]{1,0:T(8,128)S(1)} %get-tuple-element.67.power, f32[2048,128]{1,0:T(8,128)S(1)} %convert_element_type.32.refs_0_, f32[2048,128]{1,0:T(8,128)S(1)} %convert_element_type.33.refs_1_, f32[8192,128]{1,0:T(8,128)} %shard_map.52.refs_2_), custom_call_target="tpu_custom_call", output_to_operand_aliasing={{}: (4, {})} | custom-call | flops 1 | bytes 1 | tf_op jit(solution)/shard_map/pallas_call | solution.py:251
  (62 shorter events, 17.1 us)
Async XLA Ops:
  0.1 17.3 %collective-permute-start.5 = (bf16[1024,2048]{1,0:T(8,128)(2,1)}, bf16[1024,2048]{1,0:T(8,128)(2,1)S(1)}, u32[]{:S(2)}, u32[]{:S(2)}) collective-permute-start(bf16[1024,2048]{1,0:T(8,128)(2,1)} %own), channel_id=1, source_target_pairs={{0,1},{1,0},{2,3},{3,2},{4,5},{5,4},{6,7},{7,6},{8,9},{9,8},{10,11... | collective-permute-start | bytes 12582920 | tf_op jit(solution)/shard_map/ppermute | solution.py:15
  0.8 8.6 %collective-permute-start = (bf16[1,512,128]{2,1,0:T(8,128)(2,1)}, bf16[1,512,128]{2,1,0:T(8,128)(2,1)S(1)}, u32[]{:S(2)}, u32[]{:S(2)}) collective-permute-start(bf16[1,512,128]{2,1,0:T(8,128)(2,1)} %bitcast.5), channel_id=1, source_target_pairs={{0,4},{1,5},{2,6},{3,7},{4,0},{5,1},{6,2},{7,3},{8,12},{9,13},{10,... | collective-permute-start | bytes 393224 | tf_op jit(solution)/shard_map/ppermute | solution.py:15
  5.8 4.4 %copy-start.2 = (f32[1024,512]{1,0:T(8,128)S(1)}, f32[1024,512]{1,0:T(8,128)}, u32[]{:S(2)}) copy-start(f32[1024,512]{1,0:T(8,128)} %param.6) | copy-start | bytes 6291460
  5.8 11.1 %collective-permute-start.2 = (bf16[576,512]{1,0:T(8,128)(2,1)S(1)}, bf16[576,512]{1,0:T(8,128)(2,1)S(1)}, u32[]{:S(2)}, u32[]{:S(2)}) collective-permute-start(bf16[576,512]{1,0:T(8,128)(2,1)S(1)} %pad_maximum_fusion.2), channel_id=1, source_target_pairs={{31,7}} | collective-permute-start | bytes 1769480 | tf_op jit(solution)/shard_map/ppermute | solution.py:181
  6.7 10.2 %collective-permute-start.3 = (bf16[576,512]{1,0:T(8,128)(2,1)S(1)}, bf16[576,512]{1,0:T(8,128)(2,1)S(1)}, u32[]{:S(2)}, u32[]{:S(2)}) collective-permute-start(bf16[576,512]{1,0:T(8,128)(2,1)S(1)} %pad_maximum_fusion.3), channel_id=1, source_target_pairs={{31,15}} | collective-permute-start | bytes 1769480 | tf_op jit(solution)/shard_map/ppermute | solution.py:181
  7.5 9.5 %collective-permute-start.4 = (bf16[576,512]{1,0:T(8,128)(2,1)S(1)}, bf16[576,512]{1,0:T(8,128)(2,1)S(1)}, u32[]{:S(2)}, u32[]{:S(2)}) collective-permute-start(bf16[576,512]{1,0:T(8,128)(2,1)S(1)} %fusion.4), channel_id=1, source_target_pairs={{31,23}} | collective-permute-start | bytes 1769480 | tf_op jit(solution)/shard_map/ppermute | solution.py:181
  9.4 7.5 %collective-permute-start.1 = (bf16[2,512,128]{2,1,0:T(8,128)(2,1)S(1)}, bf16[2,512,128]{2,1,0:T(8,128)(2,1)S(1)}, u32[]{:S(2)}, u32[]{:S(2)}) collective-permute-start(bf16[2,512,128]{2,1,0:T(8,128)(2,1)S(1)} %pad_maximum_fusion.5), channel_id=1, source_target_pairs={{0,2},{1,3},{2,0},{3,1},{4,6},{5,7},{6,4},{7,5},{8,10},{9,11},{10,... | collective-permute-start | bytes 786440 | tf_op jit(solution)/shard_map/ppermute | solution.py:15
  17.3 11.5 %collective-permute-start.8 = (bf16[576,512]{1,0:T(8,128)(2,1)S(1)}, bf16[576,512]{1,0:T(8,128)(2,1)S(1)}, u32[]{:S(2)}, u32[]{:S(2)}) collective-permute-start(bf16[576,512]{1,0:T(8,128)(2,1)S(1)} %fusion.7), channel_id=1, source_target_pairs={{7,3},{15,11},{23,19},{31,27}} | collective-permute-start | bytes 1769480 | tf_op jit(solution)/shard_map/ppermute | solution.py:199
  18.7 10.3 %collective-permute-start.6 = (bf16[512,256]{1,0:T(8,128)(2,1)S(1)}, bf16[512,256]{1,0:T(8,128)(2,1)S(1)}, u32[]{:S(2)}, u32[]{:S(2)}) collective-permute-start(bf16[512,256]{1,0:T(8,128)(2,1)S(1)} %get-tuple-element.52), channel_id=1, source_target_pairs={{0,8},{8,0},{16,24},{24,16},{1,9},{9,1},{17,25},{25,17},{2,10},{10... | collective-permute-start | bytes 786440 | tf_op jit(solution)/shard_map/ppermute | solution.py:15
  20.0 9.0 %collective-permute-start.7 = (bf16[512,256]{1,0:T(8,128)(2,1)S(1)}, bf16[512,256]{1,0:T(8,128)(2,1)S(1)}, u32[]{:S(2)}, u32[]{:S(2)}) collective-permute-start(bf16[512,256]{1,0:T(8,128)(2,1)S(1)} %get-tuple-element.54), channel_id=1, source_target_pairs={{0,16},{8,24},{16,0},{24,8},{1,17},{9,25},{17,1},{25,9},{2,18},{10... | collective-permute-start | bytes 786440 | tf_op jit(solution)/shard_map/ppermute | solution.py:15
  28.9 24.6 %copy-start.1 = (bf16[1024,2048]{1,0:T(8,128)(2,1)S(1)}, bf16[1024,2048]{1,0:T(8,128)(2,1)}, u32[]{:S(2)}) copy-start(bf16[1024,2048]{1,0:T(8,128)(2,1)} %own) | copy-start | bytes 12582916
  29.1 9.7 %collective-permute-start.10 = (bf16[1024,1024]{1,0:T(8,128)(2,1)S(1)}, bf16[1024,1024]{1,0:T(8,128)(2,1)S(1)}, u32[]{:S(2)}, u32[]{:S(2)}) collective-permute-start(bf16[1024,1024]{1,0:T(8,128)(2,1)S(1)} %pad_maximum_fusion.1.own), channel_id=1, source_target_pairs={{0,1},{1,0},{2,3},{3,2},{4,5},{5,4},{6,7},{7,6},{8,9},{9,8},{10,11... | collective-permute-start | bytes 6291464 | tf_op jit(solution)/shard_map/ppermute | solution.py:15
  29.2 19.7 %collective-permute-start.15 = (bf16[1024,256]{1,0:T(8,128)(2,1)S(1)}, bf16[1024,256]{1,0:T(8,128)(2,1)S(1)}, u32[]{:S(2)}, u32[]{:S(2)}) collective-permute-start(bf16[1024,256]{1,0:T(8,128)(2,1)S(1)} %constant_dynamic-update-slice_fusion.2.refs_2_.refs_5_), channel_id=1, source_target_pairs={{0,8},{8,0},{16,24},{24,16},{1,9},{9,1},{17,25},{25,17},{2,10},{10... | collective-permute-start | bytes 1572872 | tf_op jit(solution)/shard_map/ppermute | solution.py:15
  30.5 8.1 %collective-permute-start.9 = (bf16[576,512]{1,0:T(8,128)(2,1)S(1)}, bf16[576,512]{1,0:T(8,128)(2,1)S(1)}, u32[]{:S(2)}, u32[]{:S(2)}) collective-permute-start(bf16[576,512]{1,0:T(8,128)(2,1)S(1)} %add.18), channel_id=1, source_target_pairs={{7,5},{3,1},{15,13},{11,9},{23,21},{19,17},{31,29},{27,25}} | collective-permute-start | bytes 1769480 | tf_op jit(solution)/shard_map/ppermute | solution.py:199
  31.9 21.7 %collective-permute-start.14 = (bf16[1024,256]{1,0:T(8,128)(2,1)S(1)}, bf16[1024,256]{1,0:T(8,128)(2,1)S(1)}, u32[]{:S(2)}, u32[]{:S(2)}) collective-permute-start(bf16[1024,256]{1,0:T(8,128)(2,1)S(1)} %constant_dynamic-update-slice_fusion.refs_0_.refs_5_), channel_id=1, source_target_pairs={{0,16},{8,24},{16,0},{24,8},{1,17},{9,25},{17,1},{25,9},{2,18},{10... | collective-permute-start | bytes 1572872 | tf_op jit(solution)/shard_map/ppermute | solution.py:15
  38.7 20.1 %collective-permute-start.13 = (bf16[576,512]{1,0:T(8,128)(2,1)S(1)}, bf16[576,512]{1,0:T(8,128)(2,1)S(1)}, u32[]{:S(2)}, u32[]{:S(2)}) collective-permute-start(bf16[576,512]{1,0:T(8,128)(2,1)S(1)} %add.19.refs_0_), channel_id=1, source_target_pairs={{1,25},{3,27},{5,29},{7,31},{9,17},{11,19},{13,21},{15,23},{17,9},... | collective-permute-start | bytes 1769480 | tf_op jit(solution)/shard_map/ppermute | solution.py:208
  44.8 15.0 %collective-permute-start.12 = (bf16[576,512]{1,0:T(8,128)(2,1)S(1)}, bf16[576,512]{1,0:T(8,128)(2,1)S(1)}, u32[]{:S(2)}, u32[]{:S(2)}) collective-permute-start(bf16[576,512]{1,0:T(8,128)(2,1)S(1)} %add.19.refs_0_), channel_id=1, source_target_pairs={{1,17},{3,19},{5,21},{7,23},{9,25},{11,27},{13,29},{15,31},{17,1},... | collective-permute-start | bytes 1769480 | tf_op jit(solution)/shard_map/ppermute | solution.py:208
  46.7 13.0 %collective-permute-start.11 = (bf16[576,512]{1,0:T(8,128)(2,1)S(1)}, bf16[576,512]{1,0:T(8,128)(2,1)S(1)}, u32[]{:S(2)}, u32[]{:S(2)}) collective-permute-start(bf16[576,512]{1,0:T(8,128)(2,1)S(1)} %add.19.refs_0_), channel_id=1, source_target_pairs={{1,9},{3,11},{5,13},{7,15},{9,1},{11,3},{13,5},{15,7},{17,25},{19,... | collective-permute-start | bytes 1769480 | tf_op jit(solution)/shard_map/ppermute | solution.py:208
  59.8 5.7 %copy-start = (f32[2,256,256]{2,1,0:T(8,128)S(1)}, f32[2,256,256]{2,1,0:T(8,128)}, u32[]{:S(2)}) copy-start(f32[2,256,256]{2,1,0:T(8,128)} %inverse.2) | copy-start | bytes 1572868
  59.9 5.5 %collective-permute-start.16 = (bf16[2304,512]{1,0:T(8,128)(2,1)S(1)}, bf16[2304,512]{1,0:T(8,128)(2,1)S(1)}, u32[]{:S(2)}, u32[]{:S(2)}) collective-permute-start(bf16[2304,512]{1,0:T(8,128)(2,1)S(1)} %pad_maximum_fusion), channel_id=1, source_target_pairs={{1,0},{3,2},{5,4},{7,6},{9,8},{11,10},{13,12},{15,14},{17,16},{19,... | collective-permute-start | bytes 7077896 | tf_op jit(solution)/shard_map/ppermute | solution.py:206
  71.2 43.4 %collective-permute-start.17 = (f16[2048,128]{1,0:T(8,128)(2,1)S(1)}, f16[2048,128]{1,0:T(8,128)(2,1)S(1)}, u32[]{:S(2)}, u32[]{:S(2)}) collective-permute-start(f16[2048,128]{1,0:T(8,128)(2,1)S(1)} %get-tuple-element.68), channel_id=1, source_target_pairs={{0,4},{1,5},{2,6},{3,7},{4,0},{5,1},{6,2},{7,3},{8,12},{9,13},{10,... | collective-permute-start | bytes 1572872 | tf_op jit(solution)/shard_map/ppermute | solution.py:15
  72.8 46.7 %collective-permute-start.18 = (f16[2048,128]{1,0:T(8,128)(2,1)S(1)}, f16[2048,128]{1,0:T(8,128)(2,1)S(1)}, u32[]{:S(2)}, u32[]{:S(2)}) collective-permute-start(f16[2048,128]{1,0:T(8,128)(2,1)S(1)} %get-tuple-element.69), channel_id=1, source_target_pairs={{0,6},{1,7},{2,4},{3,5},{4,2},{5,3},{6,0},{7,1},{8,14},{9,15},{10,... | collective-permute-start | bytes 1572872 | tf_op jit(solution)/shard_map/ppermute | solution.py:15
  78.7 22.8 %collective-permute-start.20 = (f16[1024,128]{1,0:T(8,128)(2,1)S(1)}, f16[1024,128]{1,0:T(8,128)(2,1)S(1)}, u32[]{:S(2)}, u32[]{:S(2)}) collective-permute-start(f16[1024,128]{1,0:T(8,128)(2,1)S(1)} %get-tuple-element.79), channel_id=1, source_target_pairs={{0,2},{1,3},{2,0},{3,1},{4,6},{5,7},{6,4},{7,5},{8,10},{9,11},{10,... | collective-permute-start | bytes 786440 | tf_op jit(solution)/shard_map/ppermute | solution.py:15
  80.0 32.5 %collective-permute-start.19 = (f16[1024,128]{1,0:T(8,128)(2,1)S(1)}, f16[1024,128]{1,0:T(8,128)(2,1)S(1)}, u32[]{:S(2)}, u32[]{:S(2)}) collective-permute-start(f16[1024,128]{1,0:T(8,128)(2,1)S(1)} %get-tuple-element.80), channel_id=1, source_target_pairs={{0,2},{1,3},{2,0},{3,1},{4,6},{5,7},{6,4},{7,5},{8,10},{9,11},{10,... | collective-permute-start | bytes 786440 | tf_op jit(solution)/shard_map/ppermute | solution.py:15
  (1 other events, 3.6 us)

commit v6 on v5

--- a/solution.py
+++ b/solution.py
@@ -68,10 +68,10 @@
 
 def solve_kernel(places, flags, inverse, *refs):
     n_row = len(places)
-    outer, inner, parts, (out, cross, solved) = refs[:n_row], refs[n_row], refs[n_row + 1 : -3], refs[-3:]
-    size = outer[0].shape[0]
+    here, there, parts, (out, cross, solved) = refs[0], refs[1], refs[2:-3], refs[-3:]
+    size = 2 * here.shape[0] // n_row
     width = inverse.shape[1]
-    block = outer[0].shape[1]
+    block = here.shape[1]
     cross_rows = cross.shape[0] // n_row
 
     def tail(sent):
@@ -82,8 +82,11 @@
             cross[pl.ds(start, cross_rows), :] = t[first + 2 * width : first + size, :]
         solved[...] = mul(rows, gathered(parts, places, block))
 
-    pl.when(flags[1] == 1)(lambda: tail([(t, 0) for t in outer]))
-    pl.when(flags[1] == 0)(lambda: tail([(inner, q * size) for q in range(n_row)]))
+    def pieces(first, second):
+        return [((first, second)[2 * q // n_row], q % (n_row // 2) * size) for q in range(n_row)]
+
+    pl.when(flags[1] == 1)(lambda: tail(pieces(here, there)))
+    pl.when(flags[1] == 0)(lambda: tail(pieces(there, here)))
     if block == 2 * width:
         between = cross[:, :width], cross[:, width:]
     else:
@@ -203,23 +206,24 @@
             other_cols = swapped(cols, VEC, 1)
     part, other_cols = lax.optimization_barrier((part, other_cols))
 
-    across = lambda p: lax.ppermute(p, VEC, [(i, i ^ 1) for i in holders])
-    outer = [part] + [
-        lax.ppermute(part, (ROW, VEC), [(r * n_vec + i, (r ^ q) * n_vec + i) for r in range(n_row) for i in holders])
-        for q in range(1, n_row)
-    ]
+    pieces = [part]
+    for q in range(1, n_row):
+        to = 0 if q < n_row // 2 else 1
+        pairs = [(r * n_vec + i, (r ^ q) * n_vec + (i ^ to)) for r in range(n_row) for i in holders]
+        pieces.append(lax.ppermute(part, (ROW, VEC), pairs))
     count = n_vec * own_cols // 2
     parts = sum(halves, [])
     rotated, peak = call(
         functools.partial(rotate_kernel, places), flags, [filtered, shared, *parts],
         [((2 * rows, count), f32), ((8, count), f32)], [], 1 << 36,
     )
-    outer, rotated, peak = lax.optimization_barrier((outer, rotated, peak))
-    inner = across(jnp.concatenate(outer, axis=0))
+    pieces, rotated, peak = lax.optimization_barrier((pieces, rotated, peak))
+    here = jnp.concatenate([pieces[q] + pieces[q + n_row // 2] for q in range(n_row // 2)], axis=0)
+    tails = [here, swapped(here, VEC, 1)]
 
     def solve(which):
         solved, = call(
-            functools.partial(solve_kernel, places[which]), flags, [panel_inverse, *outer, inner, *halves[which]],
+            functools.partial(solve_kernel, places[which]), flags, [panel_inverse, *tails, *halves[which]],
             [((4 * width, count // 2), bf16)],
             [pltpu.VMEM(cross.shape, bf16), pltpu.VMEM((2 * width, count // 2), f32)],
         )

time: 122 us -> 119 us (0.975)
  starting transfers between devices: 31.3 us -> 25.3 us
  waiting for transfers between devices: 64.9 us -> 67 us
    ppermute x4 -> x3, starting transfers between devices: 11.7 us -> 4.95 us  [on_device(): pieces.append(lax.ppermute(part, (ROW, VEC), pairs))]
    ppermute x12 -> x13, waiting for transfers between devices: 48.9 us -> 55.1 us  [swapped(): lax.ppermute(value, axis, [(i, i ^ offset) for i in range(lax.axis_size(a...]
    ppermute x4 -> x3, waiting for transfers between devices: 4.95 us -> 0.75 us  [on_device(): pieces.append(lax.ppermute(part, (ROW, VEC), pairs))]
    ppermute x12 -> x13, starting transfers between devices: 14.8 us -> 15.5 us  [swapped(): lax.ppermute(value, axis, [(i, i ^ offset) for i in range(lax.axis_size(a...]
where the time goes in v6:
time: 119 us; the launch traced here: 118 us
  waiting for transfers between devices  67 us (56%)
  starting transfers between devices  25.3 us (21%)
  Pallas kernels  19.4 us (16%)
  other arithmetic  3.63 us (3%)
  local copies, waits for them, and re-layouts  2.15 us (2%)
    ppermute x13, waiting for transfers between devices, swapped(): lax.ppermute(value, axis, [(i, i ^ offset) for i in range(lax.axis_size(a...  55.1 us
    pallas_call x6, Pallas kernels, call(): pl.pallas_call(kernel, in_specs=[spec(pltpu.SMEM)] * len(scalars) + specs...  15.5 us
    ppermute x13, starting transfers between devices, swapped(): lax.ppermute(value, axis, [(i, i ^ offset) for i in range(lax.axis_size(a...  15.5 us
    ppermute x2, waiting for transfers between devices, on_device(): part += lax.ppermute(part, VEC, [(v, v ^ downs[i]) for v in sources])  11.2 us
    ppermute x3, starting transfers between devices, on_device(): pieces.append(lax.ppermute(part, (ROW, VEC), pairs))  4.95 us
    pallas_call x2, Pallas kernels, place(): pl.pallas_call(functools.partial(place_kernel, [(k, len(v)) for k, v in b...  3.89 us
    ppermute x2, starting transfers between devices, on_device(): part += lax.ppermute(part, VEC, [(v, v ^ downs[i]) for v in sources])  2.61 us
  transfers between devices with their start and end apart: 21, of which 10 were waited for; matrix products, arithmetic and copies ran while one was open for 4% of the time, Pallas kernels for 10%

profile of v6, /device:TPU:9, one launch (start us, length us, event | category | flops | bytes accessed | tf_op | source)
XLA Modules:
  0.0 118.0 jit_solution(3215134867456270312)
XLA Ops:
  0.8 2.3 %collective-permute-start = (bf16[1,512,128]{2,1,0:T(8,128)(2,1)}, bf16[1,512,128]{2,1,0:T(8,128)(2,1)S(1)}, u32[]{:S(2)}, u32[]{:S(2)}) collective-permute-start(bf16[1,512,128]{2,1,0:T(8,128)(2,1)} %bitcast.5), channel_id=1, source_target_pairs={{0,4},{1,5},{2,6},{3,7},{4,0},{5,1},{6,2},{7,3},{8,12},{9,13},{10,... | collective-permute-start | bytes 393224 | tf_op jit(solution)/shard_map/ppermute | solution.py:15
  4.1 1.7 %fusion.12 = (bf16[512,512]{1,0:T(8,128)(2,1)S(1)}, bf16[512,512]{1,0:T(8,128)(2,1)S(1)}, bf16[512,512]{1,0:T(8,128)(2,1)S(1)}, bf16[512,512]{1,0:T(8,128)(2,1)S(1)}) fusion(bf16[1024,2048]{1,0:T(8,128)(2,1)} %own), kind=kLoop, calls=%fused_computation.35 | loop fusion | bytes 4194304 | tf_op jit(solution)/shard_map/slice | solution.py:177
  10.8 6.1 %collective-permute-done.1 = bf16[2,512,128]{2,1,0:T(8,128)(2,1)S(1)} collective-permute-done((bf16[2,512,128]{2,1,0:T(8,128)(2,1)S(1)}, bf16[2,512,128]{2,1,0:T(8,128)(2,1)S(1)}, u32[]{:S(2)}, u32[]{:S(2)}) %collective-permute-start.1) | collective-permute-done | bytes 262176 | tf_op jit(solution)/shard_map/ppermute | solution.py:15
  21.3 7.6 %collective-permute-done.8 = bf16[576,512]{1,0:T(8,128)(2,1)S(1)} collective-permute-done((bf16[576,512]{1,0:T(8,128)(2,1)S(1)}, bf16[576,512]{1,0:T(8,128)(2,1)S(1)}, u32[]{:S(2)}, u32[]{:S(2)}) %collective-permute-start.8) | collective-permute-done | bytes 589856 | tf_op jit(solution)/shard_map/ppermute | solution.py:202
  30.5 1.3 %collective-permute-start.9 = (bf16[576,512]{1,0:T(8,128)(2,1)S(1)}, bf16[576,512]{1,0:T(8,128)(2,1)S(1)}, u32[]{:S(2)}, u32[]{:S(2)}) collective-permute-start(bf16[576,512]{1,0:T(8,128)(2,1)S(1)} %add.24), channel_id=1, source_target_pairs={{7,5},{3,1},{15,13},{11,9},{23,21},{19,17},{31,29},{27,25}} | collective-permute-start | bytes 1769480 | tf_op jit(solution)/shard_map/ppermute | solution.py:202
  31.9 3.2 %collective-permute-start.14 = (bf16[1024,256]{1,0:T(8,128)(2,1)S(1)}, bf16[1024,256]{1,0:T(8,128)(2,1)S(1)}, u32[]{:S(2)}, u32[]{:S(2)}) collective-permute-start(bf16[1024,256]{1,0:T(8,128)(2,1)S(1)} %constant_dynamic-update-slice_fusion.refs_0_.refs_2_), channel_id=1, source_target_pairs={{0,16},{8,24},{16,0},{24,8},{1,17},{9,25},{17,1},{25,9},{2,18},{10... | collective-permute-start | bytes 1572872 | tf_op jit(solution)/shard_map/ppermute | solution.py:15
  35.0 3.6 %collective-permute-done.9 = bf16[576,512]{1,0:T(8,128)(2,1)S(1)} collective-permute-done((bf16[576,512]{1,0:T(8,128)(2,1)S(1)}, bf16[576,512]{1,0:T(8,128)(2,1)S(1)}, u32[]{:S(2)}, u32[]{:S(2)}) %collective-permute-start.9) | collective-permute-done | bytes 589856 | tf_op jit(solution)/shard_map/ppermute | solution.py:202
  38.7 1.3 %collective-permute-start.13 = (bf16[576,512]{1,0:T(8,128)(2,1)S(1)}, bf16[576,512]{1,0:T(8,128)(2,1)S(1)}, u32[]{:S(2)}, u32[]{:S(2)}) collective-permute-start(bf16[576,512]{1,0:T(8,128)(2,1)S(1)} %add.25), channel_id=1, source_target_pairs={{1,24},{3,26},{5,28},{7,30},{9,16},{11,18},{13,20},{15,22},{17,8},... | collective-permute-start | bytes 1769480 | tf_op jit(solution)/shard_map/ppermute | solution.py:213
  40.1 1.3 %collective-permute-start.12 = (bf16[576,512]{1,0:T(8,128)(2,1)S(1)}, bf16[576,512]{1,0:T(8,128)(2,1)S(1)}, u32[]{:S(2)}, u32[]{:S(2)}) collective-permute-start(bf16[576,512]{1,0:T(8,128)(2,1)S(1)} %add.25), channel_id=1, source_target_pairs={{1,16},{3,18},{5,20},{7,22},{9,24},{11,26},{13,28},{15,30},{17,0},... | collective-permute-start | bytes 1769480 | tf_op jit(solution)/shard_map/ppermute | solution.py:213
  41.4 2.3 %collective-permute-start.11 = (bf16[576,512]{1,0:T(8,128)(2,1)S(1)}, bf16[576,512]{1,0:T(8,128)(2,1)S(1)}, u32[]{:S(2)}, u32[]{:S(2)}) collective-permute-start(bf16[576,512]{1,0:T(8,128)(2,1)S(1)} %add.25), channel_id=1, source_target_pairs={{1,9},{3,11},{5,13},{7,15},{9,1},{11,3},{13,5},{15,7},{17,25},{19,... | collective-permute-start | bytes 1769480 | tf_op jit(solution)/shard_map/ppermute | solution.py:213
  43.7 9.6 %collective-permute-done.14.refs_1_.refs_3_ = bf16[1024,256]{1,0:T(8,128)(2,1)S(1)} collective-permute-done((bf16[1024,256]{1,0:T(8,128)(2,1)S(1)}, bf16[1024,256]{1,0:T(8,128)(2,1)S(1)}, u32[]{:S(2)}, u32[]{:S(2)}) %collective-permute-start.14) | collective-permute-done | bytes 524320 | tf_op jit(solution)/shard_map/ppermute | solution.py:15
  53.4 5.3 %shard_map.47 = (f32[2048,512]{1,0:T(8,128)S(1)}, f32[8,512]{1,0:T(8,128)S(1)}) custom-call(s32[4]{0:T(128)S(1)} %pad_add_fusion.flags, bf16[1024,2048]{1,0:T(8,128)(2,1)S(1)} %copy-done.1, bf16[1024,2048]{1,0:T(8,128)(2,1)S(1)} %collective-permute-done.5.other, bf16[1024,256]{1,0:T(8,128)(2,1)S(1)} %constant_dynamic-update-slice_fusion.refs_0_.refs_2_, ...), custom_call_target="tpu_custom_call" | custom-call | flops 68719476736 | bytes 1 | tf_op jit(solution)/shard_map/pallas_call | solution.py:145
  60.8 2.5 %collective-permute-done.16.refs_1_ = bf16[1152,512]{1,0:T(8,128)(2,1)S(1)} collective-permute-done((bf16[1152,512]{1,0:T(8,128)(2,1)S(1)}, bf16[1152,512]{1,0:T(8,128)(2,1)S(1)}, u32[]{:S(2)}, u32[]{:S(2)}) %collective-permute-start.16) | collective-permute-done | bytes 1179680 | tf_op jit(solution)/shard_map/ppermute | solution.py:15
  63.3 2.2 %shard_map.48.solved = bf16[1024,256]{1,0:T(8,128)(2,1)S(1)} custom-call(s32[4]{0:T(128)S(1)} %pad_add_fusion.flags, f32[2,256,256]{2,1,0:T(8,128)S(1)} %copy-done, bf16[1152,512]{1,0:T(8,128)(2,1)S(1)} %pad_maximum_fusion.1.refs_0_, bf16[1152,512]{1,0:T(8,128)(2,1)S(1)} %collective-permute-done.16.refs_1_, ...), custom_call_target="tpu_custom_call" | custom-call | flops 1 | bytes 1 | tf_op jit(solution)/shard_map/pallas_call | solution.py:145
  65.5 3.1 %shard_map.49 = (f32[2048,256]{1,0:T(8,128)S(1)}, f32[8,256]{1,0:T(8,128)}) custom-call(s32[4]{0:T(128)S(1)} %pad_add_fusion.flags, f32[2048,512]{1,0:T(8,128)S(1)} %get-tuple-element.58.rotated, f32[8,512]{1,0:T(8,128)S(1)} %get-tuple-element.59.peak, bf16[1024,1024]{1,0:T(8,128)(2,1)S(1)} %pad_maximum_fusion.own, ...), custom_call_target="tpu_custom_call" | custom-call | flops 1 | bytes 1 | tf_op jit(solution)/shard_map/pallas_call | solution.py:145
  69.0 1.4 %collective-permute-start.17 = (f16[2048,128]{1,0:T(8,128)(2,1)S(1)}, f16[2048,128]{1,0:T(8,128)(2,1)S(1)}, u32[]{:S(2)}, u32[]{:S(2)}) collective-permute-start(f16[2048,128]{1,0:T(8,128)(2,1)S(1)} %get-tuple-element.68), channel_id=1, source_target_pairs={{0,4},{1,5},{2,6},{3,7},{4,0},{5,1},{6,2},{7,3},{8,12},{9,13},{10,... | collective-permute-start | bytes 1572872 | tf_op jit(solution)/shard_map/ppermute | solution.py:15
  70.5 2.4 %shard_map.50.solved = bf16[1024,256]{1,0:T(8,128)(2,1)S(1)} custom-call(s32[4]{0:T(128)S(1)} %pad_add_fusion.flags, f32[2,256,256]{2,1,0:T(8,128)S(1)} %copy-done, bf16[1152,512]{1,0:T(8,128)(2,1)S(1)} %pad_maximum_fusion.1.refs_0_, bf16[1152,512]{1,0:T(8,128)(2,1)S(1)} %collective-permute-done.16.refs_1_, ...), custom_call_target="tpu_custom_call" | custom-call | flops 1 | bytes 1 | tf_op jit(solution)/shard_map/pallas_call | solution.py:145
  72.8 2.5 %shard_map.51 = (f32[2048,256]{1,0:T(8,128)S(1)}, f32[8,256]{1,0:T(8,128)S(1)}) custom-call(s32[4]{0:T(128)S(1)} %pad_add_fusion.flags, f32[2048,512]{1,0:T(8,128)S(1)} %get-tuple-element.58.rotated, f32[8,512]{1,0:T(8,128)S(1)} %get-tuple-element.59.peak, bf16[1024,1024]{1,0:T(8,128)(2,1)S(1)} %pad_maximum_fusion.own, ...), custom_call_target="tpu_custom_call" | custom-call | flops 1 | bytes 1 | tf_op jit(solution)/shard_map/pallas_call | solution.py:145
  75.7 2.2 %collective-permute-start.20 = (f16[1024,128]{1,0:T(8,128)(2,1)S(1)}, f16[1024,128]{1,0:T(8,128)(2,1)S(1)}, u32[]{:S(2)}, u32[]{:S(2)}) collective-permute-start(f16[1024,128]{1,0:T(8,128)(2,1)S(1)} %get-tuple-element.79), channel_id=1, source_target_pairs={{0,2},{1,3},{2,0},{3,1},{4,6},{5,7},{6,4},{7,5},{8,10},{9,11},{10,... | collective-permute-start | bytes 786440 | tf_op jit(solution)/shard_map/ppermute | solution.py:15
  78.1 20.8 %collective-permute-done.20 = f16[1024,128]{1,0:T(8,128)(2,1)S(1)} collective-permute-done((f16[1024,128]{1,0:T(8,128)(2,1)S(1)}, f16[1024,128]{1,0:T(8,128)(2,1)S(1)}, u32[]{:S(2)}, u32[]{:S(2)}) %collective-permute-start.20) | collective-permute-done | bytes 262176 | tf_op jit(solution)/shard_map/ppermute | solution.py:15
  98.9 10.7 %collective-permute-done.19 = f16[1024,128]{1,0:T(8,128)(2,1)S(1)} collective-permute-done((f16[1024,128]{1,0:T(8,128)(2,1)S(1)}, f16[1024,128]{1,0:T(8,128)(2,1)S(1)}, u32[]{:S(2)}, u32[]{:S(2)}) %collective-permute-start.19) | collective-permute-done | bytes 262176 | tf_op jit(solution)/shard_map/ppermute | solution.py:15
  109.6 1.9 %shard_map.52.refs_2_ = f32[8192,128]{1,0:T(8,128)} custom-call(s32[4]{0:T(128)S(1)} %pad_add_fusion.flags, f32[8,256]{1,0:T(8,128)S(1)} %get-tuple-element.67.power, f32[1024,128]{1,0:T(8,128)S(1)} %convert_element_type.34.refs_0_, f32[1024,128]{1,0:T(8,128)S(1)} %convert_element_type.35.refs_1_, f32[2048,128]{1,0:T(8,128)S(1)} %slice.61.refs_2_), custom_call_target="tpu_custom_call" | custom-call | flops 1 | bytes 1 | tf_op jit(solution)/shard_map/pallas_call | solution.py:255
  111.6 4.2 %collective-permute-done.18 = f16[2048,128]{1,0:T(8,128)(2,1)S(1)} collective-permute-done((f16[2048,128]{1,0:T(8,128)(2,1)S(1)}, f16[2048,128]{1,0:T(8,128)(2,1)S(1)}, u32[]{:S(2)}, u32[]{:S(2)}) %collective-permute-start.18) | collective-permute-done | bytes 524320 | tf_op jit(solution)/shard_map/ppermute | solution.py:15
  115.9 1.9 %shard_map.53 = f32[8192,128]{1,0:T(8,128)} custom-call(s32[4]{0:T(128)S(1)} %pad_add_fusion.flags, f32[8,256]{1,0:T(8,128)S(1)} %get-tuple-element.67.power, f32[2048,128]{1,0:T(8,128)S(1)} %convert_element_type.32.refs_0_, f32[2048,128]{1,0:T(8,128)S(1)} %convert_element_type.33.refs_1_, f32[8192,128]{1,0:T(8,128)} %shard_map.52.refs_2_), custom_call_target="tpu_custom_call", output_to_operand_aliasing={{}: (4, {})} | custom-call | flops 1 | bytes 1 | tf_op jit(solution)/shard_map/pallas_call | solution.py:255
  (64 shorter events, 16.0 us)
Async XLA Ops:
  0.1 17.3 %collective-permute-start.5 = (bf16[1024,2048]{1,0:T(8,128)(2,1)}, bf16[1024,2048]{1,0:T(8,128)(2,1)S(1)}, u32[]{:S(2)}, u32[]{:S(2)}) collective-permute-start(bf16[1024,2048]{1,0:T(8,128)(2,1)} %own), channel_id=1, source_target_pairs={{0,1},{1,0},{2,3},{3,2},{4,5},{5,4},{6,7},{7,6},{8,9},{9,8},{10,11... | collective-permute-start | bytes 12582920 | tf_op jit(solution)/shard_map/ppermute | solution.py:15
  0.8 8.6 %collective-permute-start = (bf16[1,512,128]{2,1,0:T(8,128)(2,1)}, bf16[1,512,128]{2,1,0:T(8,128)(2,1)S(1)}, u32[]{:S(2)}, u32[]{:S(2)}) collective-permute-start(bf16[1,512,128]{2,1,0:T(8,128)(2,1)} %bitcast.5), channel_id=1, source_target_pairs={{0,4},{1,5},{2,6},{3,7},{4,0},{5,1},{6,2},{7,3},{8,12},{9,13},{10,... | collective-permute-start | bytes 393224 | tf_op jit(solution)/shard_map/ppermute | solution.py:15
  5.8 11.1 %collective-permute-start.2 = (bf16[576,512]{1,0:T(8,128)(2,1)S(1)}, bf16[576,512]{1,0:T(8,128)(2,1)S(1)}, u32[]{:S(2)}, u32[]{:S(2)}) collective-permute-start(bf16[576,512]{1,0:T(8,128)(2,1)S(1)} %pad_maximum_fusion.2), channel_id=1, source_target_pairs={{31,7}} | collective-permute-start | bytes 1769480 | tf_op jit(solution)/shard_map/ppermute | solution.py:184
  6.5 3.6 %copy-start.2 = (f32[1024,512]{1,0:T(8,128)S(1)}, f32[1024,512]{1,0:T(8,128)}, u32[]{:S(2)}) copy-start(f32[1024,512]{1,0:T(8,128)} %param.6) | copy-start | bytes 6291460
  6.6 10.4 %collective-permute-start.3 = (bf16[576,512]{1,0:T(8,128)(2,1)S(1)}, bf16[576,512]{1,0:T(8,128)(2,1)S(1)}, u32[]{:S(2)}, u32[]{:S(2)}) collective-permute-start(bf16[576,512]{1,0:T(8,128)(2,1)S(1)} %pad_maximum_fusion.3), channel_id=1, source_target_pairs={{31,15}} | collective-permute-start | bytes 1769480 | tf_op jit(solution)/shard_map/ppermute | solution.py:184
  7.5 9.5 %collective-permute-start.4 = (bf16[576,512]{1,0:T(8,128)(2,1)S(1)}, bf16[576,512]{1,0:T(8,128)(2,1)S(1)}, u32[]{:S(2)}, u32[]{:S(2)}) collective-permute-start(bf16[576,512]{1,0:T(8,128)(2,1)S(1)} %fusion.4), channel_id=1, source_target_pairs={{31,23}} | collective-permute-start | bytes 1769480 | tf_op jit(solution)/shard_map/ppermute | solution.py:184
  9.4 7.5 %collective-permute-start.1 = (bf16[2,512,128]{2,1,0:T(8,128)(2,1)S(1)}, bf16[2,512,128]{2,1,0:T(8,128)(2,1)S(1)}, u32[]{:S(2)}, u32[]{:S(2)}) collective-permute-start(bf16[2,512,128]{2,1,0:T(8,128)(2,1)S(1)} %pad_maximum_fusion.5), channel_id=1, source_target_pairs={{0,2},{1,3},{2,0},{3,1},{4,6},{5,7},{6,4},{7,5},{8,10},{9,11},{10,... | collective-permute-start | bytes 786440 | tf_op jit(solution)/shard_map/ppermute | solution.py:15
  17.3 11.5 %collective-permute-start.8 = (bf16[576,512]{1,0:T(8,128)(2,1)S(1)}, bf16[576,512]{1,0:T(8,128)(2,1)S(1)}, u32[]{:S(2)}, u32[]{:S(2)}) collective-permute-start(bf16[576,512]{1,0:T(8,128)(2,1)S(1)} %fusion.7), channel_id=1, source_target_pairs={{7,3},{15,11},{23,19},{31,27}} | collective-permute-start | bytes 1769480 | tf_op jit(solution)/shard_map/ppermute | solution.py:202
  18.7 10.3 %collective-permute-start.6 = (bf16[512,256]{1,0:T(8,128)(2,1)S(1)}, bf16[512,256]{1,0:T(8,128)(2,1)S(1)}, u32[]{:S(2)}, u32[]{:S(2)}) collective-permute-start(bf16[512,256]{1,0:T(8,128)(2,1)S(1)} %get-tuple-element.52), channel_id=1, source_target_pairs={{0,8},{8,0},{16,24},{24,16},{1,9},{9,1},{17,25},{25,17},{2,10},{10... | collective-permute-start | bytes 786440 | tf_op jit(solution)/shard_map/ppermute | solution.py:15
  20.0 9.0 %collective-permute-start.7 = (bf16[512,256]{1,0:T(8,128)(2,1)S(1)}, bf16[512,256]{1,0:T(8,128)(2,1)S(1)}, u32[]{:S(2)}, u32[]{:S(2)}) collective-permute-start(bf16[512,256]{1,0:T(8,128)(2,1)S(1)} %get-tuple-element.54), channel_id=1, source_target_pairs={{0,16},{8,24},{16,0},{24,8},{1,17},{9,25},{17,1},{25,9},{2,18},{10... | collective-permute-start | bytes 786440 | tf_op jit(solution)/shard_map/ppermute | solution.py:15
  28.9 24.5 %copy-start.1 = (bf16[1024,2048]{1,0:T(8,128)(2,1)S(1)}, bf16[1024,2048]{1,0:T(8,128)(2,1)}, u32[]{:S(2)}) copy-start(bf16[1024,2048]{1,0:T(8,128)(2,1)} %own) | copy-start | bytes 12582916
  29.1 9.7 %collective-permute-start.10 = (bf16[1024,1024]{1,0:T(8,128)(2,1)S(1)}, bf16[1024,1024]{1,0:T(8,128)(2,1)S(1)}, u32[]{:S(2)}, u32[]{:S(2)}) collective-permute-start(bf16[1024,1024]{1,0:T(8,128)(2,1)S(1)} %pad_maximum_fusion.own), channel_id=1, source_target_pairs={{0,1},{1,0},{2,3},{3,2},{4,5},{5,4},{6,7},{7,6},{8,9},{9,8},{10,11... | collective-permute-start | bytes 6291464 | tf_op jit(solution)/shard_map/ppermute | solution.py:15
  29.2 14.5 %collective-permute-start.15 = (bf16[1024,256]{1,0:T(8,128)(2,1)S(1)}, bf16[1024,256]{1,0:T(8,128)(2,1)S(1)}, u32[]{:S(2)}, u32[]{:S(2)}) collective-permute-start(bf16[1024,256]{1,0:T(8,128)(2,1)S(1)} %constant_dynamic-update-slice_fusion.2.refs_2_), channel_id=1, source_target_pairs={{0,8},{8,0},{16,24},{24,16},{1,9},{9,1},{17,25},{25,17},{2,10},{10... | collective-permute-start | bytes 1572872 | tf_op jit(solution)/shard_map/ppermute | solution.py:15
  30.5 8.1 %collective-permute-start.9 = (bf16[576,512]{1,0:T(8,128)(2,1)S(1)}, bf16[576,512]{1,0:T(8,128)(2,1)S(1)}, u32[]{:S(2)}, u32[]{:S(2)}) collective-permute-start(bf16[576,512]{1,0:T(8,128)(2,1)S(1)} %add.24), channel_id=1, source_target_pairs={{7,5},{3,1},{15,13},{11,9},{23,21},{19,17},{31,29},{27,25}} | collective-permute-start | bytes 1769480 | tf_op jit(solution)/shard_map/ppermute | solution.py:202
  31.9 21.5 %collective-permute-start.14 = (bf16[1024,256]{1,0:T(8,128)(2,1)S(1)}, bf16[1024,256]{1,0:T(8,128)(2,1)S(1)}, u32[]{:S(2)}, u32[]{:S(2)}) collective-permute-start(bf16[1024,256]{1,0:T(8,128)(2,1)S(1)} %constant_dynamic-update-slice_fusion.refs_0_.refs_2_), channel_id=1, source_target_pairs={{0,16},{8,24},{16,0},{24,8},{1,17},{9,25},{17,1},{25,9},{2,18},{10... | collective-permute-start | bytes 1572872 | tf_op jit(solution)/shard_map/ppermute | solution.py:15
  38.7 19.9 %collective-permute-start.13 = (bf16[576,512]{1,0:T(8,128)(2,1)S(1)}, bf16[576,512]{1,0:T(8,128)(2,1)S(1)}, u32[]{:S(2)}, u32[]{:S(2)}) collective-permute-start(bf16[576,512]{1,0:T(8,128)(2,1)S(1)} %add.25), channel_id=1, source_target_pairs={{1,24},{3,26},{5,28},{7,30},{9,16},{11,18},{13,20},{15,22},{17,8},... | collective-permute-start | bytes 1769480 | tf_op jit(solution)/shard_map/ppermute | solution.py:213
  40.1 19.3 %collective-permute-start.12 = (bf16[576,512]{1,0:T(8,128)(2,1)S(1)}, bf16[576,512]{1,0:T(8,128)(2,1)S(1)}, u32[]{:S(2)}, u32[]{:S(2)}) collective-permute-start(bf16[576,512]{1,0:T(8,128)(2,1)S(1)} %add.25), channel_id=1, source_target_pairs={{1,16},{3,18},{5,20},{7,22},{9,24},{11,26},{13,28},{15,30},{17,0},... | collective-permute-start | bytes 1769480 | tf_op jit(solution)/shard_map/ppermute | solution.py:213
  41.4 18.0 %collective-permute-start.11 = (bf16[576,512]{1,0:T(8,128)(2,1)S(1)}, bf16[576,512]{1,0:T(8,128)(2,1)S(1)}, u32[]{:S(2)}, u32[]{:S(2)}) collective-permute-start(bf16[576,512]{1,0:T(8,128)(2,1)S(1)} %add.25), channel_id=1, source_target_pairs={{1,9},{3,11},{5,13},{7,15},{9,1},{11,3},{13,5},{15,7},{17,25},{19,... | collective-permute-start | bytes 1769480 | tf_op jit(solution)/shard_map/ppermute | solution.py:213
  59.7 3.6 %copy-start = (f32[2,256,256]{2,1,0:T(8,128)S(1)}, f32[2,256,256]{2,1,0:T(8,128)}, u32[]{:S(2)}) copy-start(f32[2,256,256]{2,1,0:T(8,128)} %inverse.2) | copy-start | bytes 1572868
  59.8 3.5 %collective-permute-start.16 = (bf16[1152,512]{1,0:T(8,128)(2,1)S(1)}, bf16[1152,512]{1,0:T(8,128)(2,1)S(1)}, u32[]{:S(2)}, u32[]{:S(2)}) collective-permute-start(bf16[1152,512]{1,0:T(8,128)(2,1)S(1)} %pad_maximum_fusion.1.refs_0_), channel_id=1, source_target_pairs={{0,1},{1,0},{2,3},{3,2},{4,5},{5,4},{6,7},{7,6},{8,9},{9,8},{10,11... | collective-permute-start | bytes 3538952 | tf_op jit(solution)/shard_map/ppermute | solution.py:15
  69.0 42.5 %collective-permute-start.17 = (f16[2048,128]{1,0:T(8,128)(2,1)S(1)}, f16[2048,128]{1,0:T(8,128)(2,1)S(1)}, u32[]{:S(2)}, u32[]{:S(2)}) collective-permute-start(f16[2048,128]{1,0:T(8,128)(2,1)S(1)} %get-tuple-element.68), channel_id=1, source_target_pairs={{0,4},{1,5},{2,6},{3,7},{4,0},{5,1},{6,2},{7,3},{8,12},{9,13},{10,... | collective-permute-start | bytes 1572872 | tf_op jit(solution)/shard_map/ppermute | solution.py:15
  70.5 45.4 %collective-permute-start.18 = (f16[2048,128]{1,0:T(8,128)(2,1)S(1)}, f16[2048,128]{1,0:T(8,128)(2,1)S(1)}, u32[]{:S(2)}, u32[]{:S(2)}) collective-permute-start(f16[2048,128]{1,0:T(8,128)(2,1)S(1)} %get-tuple-element.69), channel_id=1, source_target_pairs={{0,6},{1,7},{2,4},{3,5},{4,2},{5,3},{6,0},{7,1},{8,14},{9,15},{10,... | collective-permute-start | bytes 1572872 | tf_op jit(solution)/shard_map/ppermute | solution.py:15
  75.7 23.2 %collective-permute-start.20 = (f16[1024,128]{1,0:T(8,128)(2,1)S(1)}, f16[1024,128]{1,0:T(8,128)(2,1)S(1)}, u32[]{:S(2)}, u32[]{:S(2)}) collective-permute-start(f16[1024,128]{1,0:T(8,128)(2,1)S(1)} %get-tuple-element.79), channel_id=1, source_target_pairs={{0,2},{1,3},{2,0},{3,1},{4,6},{5,7},{6,4},{7,5},{8,10},{9,11},{10,... | collective-permute-start | bytes 786440 | tf_op jit(solution)/shard_map/ppermute | solution.py:15
  77.9 31.6 %collective-permute-start.19 = (f16[1024,128]{1,0:T(8,128)(2,1)S(1)}, f16[1024,128]{1,0:T(8,128)(2,1)S(1)}, u32[]{:S(2)}, u32[]{:S(2)}) collective-permute-start(f16[1024,128]{1,0:T(8,128)(2,1)S(1)} %get-tuple-element.80), channel_id=1, source_target_pairs={{0,2},{1,3},{2,0},{3,1},{4,6},{5,7},{6,4},{7,5},{8,10},{9,11},{10,... | collective-permute-start | bytes 786440 | tf_op jit(solution)/shard_map/ppermute | solution.py:15
  (1 other events, 2.8 us)

commit v7 on v6

--- a/solution.py
+++ b/solution.py
@@ -215,7 +215,7 @@
     parts = sum(halves, [])
     rotated, peak = call(
         functools.partial(rotate_kernel, places), flags, [filtered, shared, *parts],
-        [((2 * rows, count), f32), ((8, count), f32)], [], 1 << 36,
+        [((2 * rows, count), f32), ((8, count), f32)], [], 4 * rows * depth * count,
     )
     pieces, rotated, peak = lax.optimization_barrier((pieces, rotated, peak))
     here = jnp.concatenate([pieces[q] + pieces[q + n_row // 2] for q in range(n_row // 2)], axis=0)

time: 119 us -> 118 us (level)
  waiting for transfers between devices: 67 us -> 64.7 us
    ppermute x13, waiting for transfers between devices: 55.1 us -> 53.5 us  [swapped(): lax.ppermute(value, axis, [(i, i ^ offset) for i in range(lax.axis_size(a...]
  transfers between devices with their start and end apart: 21 -> 21, of which waited for: 10 -> 11; matrix products, arithmetic and copies ran while one was open for 4% -> 4% of each run, Pallas kernels for 10% -> 10%
where the time goes in v7:
time: 118 us; the launch traced here: 117 us
  waiting for transfers between devices  64.7 us (55%)
  starting transfers between devices  26.3 us (22%)
  Pallas kernels  19.4 us (16%)
  other arithmetic  3.63 us (3%)
  local copies, waits for them, and re-layouts  2.15 us (2%)
    ppermute x13, waiting for transfers between devices, swapped(): lax.ppermute(value, axis, [(i, i ^ offset) for i in range(lax.axis_size(a...  53.5 us
    pallas_call x6, Pallas kernels, call(): pl.pallas_call(kernel, in_specs=[spec(pltpu.SMEM)] * len(scalars) + specs...  15.5 us
    ppermute x13, starting transfers between devices, swapped(): lax.ppermute(value, axis, [(i, i ^ offset) for i in range(lax.axis_size(a...  15.2 us
    ppermute x2, waiting for transfers between devices, on_device(): part += lax.ppermute(part, VEC, [(v, v ^ downs[i]) for v in sources])  10.1 us
    ppermute x3, starting transfers between devices, on_device(): pieces.append(lax.ppermute(part, (ROW, VEC), pairs))  5.99 us
    pallas_call x2, Pallas kernels, place(): pl.pallas_call(functools.partial(place_kernel, [(k, len(v)) for k, v in b...  3.89 us
    ppermute x2, starting transfers between devices, on_device(): part += lax.ppermute(part, VEC, [(v, v ^ downs[i]) for v in sources])  2.88 us
  transfers between devices with their start and end apart: 21, of which 11 were waited for; matrix products, arithmetic and copies ran while one was open for 4% of the time, Pallas kernels for 10%

profile of v7, /device:TPU:9, one launch (start us, length us, event | category | flops | bytes accessed | tf_op | source)
XLA Modules:
  0.0 116.8 jit_solution(7661082374440620799)
XLA Ops:
  0.8 2.3 %collective-permute-start = (bf16[1,512,128]{2,1,0:T(8,128)(2,1)}, bf16[1,512,128]{2,1,0:T(8,128)(2,1)S(1)}, u32[]{:S(2)}, u32[]{:S(2)}) collective-permute-start(bf16[1,512,128]{2,1,0:T(8,128)(2,1)} %bitcast.5), channel_id=1, source_target_pairs={{0,4},{1,5},{2,6},{3,7},{4,0},{5,1},{6,2},{7,3},{8,12},{9,13},{10,... | collective-permute-start | bytes 393224 | tf_op jit(solution)/shard_map/ppermute | solution.py:15
  4.1 1.7 %fusion.12 = (bf16[512,512]{1,0:T(8,128)(2,1)S(1)}, bf16[512,512]{1,0:T(8,128)(2,1)S(1)}, bf16[512,512]{1,0:T(8,128)(2,1)S(1)}, bf16[512,512]{1,0:T(8,128)(2,1)S(1)}) fusion(bf16[1024,2048]{1,0:T(8,128)(2,1)} %own), kind=kLoop, calls=%fused_computation.35 | loop fusion | bytes 4194304 | tf_op jit(solution)/shard_map/slice | solution.py:177
  10.8 6.1 %collective-permute-done.1 = bf16[2,512,128]{2,1,0:T(8,128)(2,1)S(1)} collective-permute-done((bf16[2,512,128]{2,1,0:T(8,128)(2,1)S(1)}, bf16[2,512,128]{2,1,0:T(8,128)(2,1)S(1)}, u32[]{:S(2)}, u32[]{:S(2)}) %collective-permute-start.1) | collective-permute-done | bytes 262176 | tf_op jit(solution)/shard_map/ppermute | solution.py:15
  21.3 7.6 %collective-permute-done.8 = bf16[576,512]{1,0:T(8,128)(2,1)S(1)} collective-permute-done((bf16[576,512]{1,0:T(8,128)(2,1)S(1)}, bf16[576,512]{1,0:T(8,128)(2,1)S(1)}, u32[]{:S(2)}, u32[]{:S(2)}) %collective-permute-start.8) | collective-permute-done | bytes 589856 | tf_op jit(solution)/shard_map/ppermute | solution.py:202
  29.1 1.6 %collective-permute-start.9 = (bf16[576,512]{1,0:T(8,128)(2,1)S(1)}, bf16[576,512]{1,0:T(8,128)(2,1)S(1)}, u32[]{:S(2)}, u32[]{:S(2)}) collective-permute-start(bf16[576,512]{1,0:T(8,128)(2,1)S(1)} %add.24), channel_id=1, source_target_pairs={{7,5},{3,1},{15,13},{11,9},{23,21},{19,17},{31,29},{27,25}} | collective-permute-start | bytes 1769480 | tf_op jit(solution)/shard_map/ppermute | solution.py:202
  32.1 2.9 %collective-permute-start.14 = (bf16[1024,256]{1,0:T(8,128)(2,1)S(1)}, bf16[1024,256]{1,0:T(8,128)(2,1)S(1)}, u32[]{:S(2)}, u32[]{:S(2)}) collective-permute-start(bf16[1024,256]{1,0:T(8,128)(2,1)S(1)} %constant_dynamic-update-slice_fusion.refs_0_.refs_2_), channel_id=1, source_target_pairs={{0,16},{8,24},{16,0},{24,8},{1,17},{9,25},{17,1},{25,9},{2,18},{10... | collective-permute-start | bytes 1572872 | tf_op jit(solution)/shard_map/ppermute | solution.py:15
  35.0 2.5 %collective-permute-done.9 = bf16[576,512]{1,0:T(8,128)(2,1)S(1)} collective-permute-done((bf16[576,512]{1,0:T(8,128)(2,1)S(1)}, bf16[576,512]{1,0:T(8,128)(2,1)S(1)}, u32[]{:S(2)}, u32[]{:S(2)}) %collective-permute-start.9) | collective-permute-done | bytes 589856 | tf_op jit(solution)/shard_map/ppermute | solution.py:202
  37.7 1.3 %collective-permute-start.13 = (bf16[576,512]{1,0:T(8,128)(2,1)S(1)}, bf16[576,512]{1,0:T(8,128)(2,1)S(1)}, u32[]{:S(2)}, u32[]{:S(2)}) collective-permute-start(bf16[576,512]{1,0:T(8,128)(2,1)S(1)} %add.25), channel_id=1, source_target_pairs={{1,24},{3,26},{5,28},{7,30},{9,16},{11,18},{13,20},{15,22},{17,8},... | collective-permute-start | bytes 1769480 | tf_op jit(solution)/shard_map/ppermute | solution.py:213
  39.0 1.5 %collective-permute-start.12 = (bf16[576,512]{1,0:T(8,128)(2,1)S(1)}, bf16[576,512]{1,0:T(8,128)(2,1)S(1)}, u32[]{:S(2)}, u32[]{:S(2)}) collective-permute-start(bf16[576,512]{1,0:T(8,128)(2,1)S(1)} %add.25), channel_id=1, source_target_pairs={{1,16},{3,18},{5,20},{7,22},{9,24},{11,26},{13,28},{15,30},{17,0},... | collective-permute-start | bytes 1769480 | tf_op jit(solution)/shard_map/ppermute | solution.py:213
  40.6 3.1 %collective-permute-start.11 = (bf16[576,512]{1,0:T(8,128)(2,1)S(1)}, bf16[576,512]{1,0:T(8,128)(2,1)S(1)}, u32[]{:S(2)}, u32[]{:S(2)}) collective-permute-start(bf16[576,512]{1,0:T(8,128)(2,1)S(1)} %add.25), channel_id=1, source_target_pairs={{1,9},{3,11},{5,13},{7,15},{9,1},{11,3},{13,5},{15,7},{17,25},{19,... | collective-permute-start | bytes 1769480 | tf_op jit(solution)/shard_map/ppermute | solution.py:213
  44.8 8.3 %collective-permute-done.14.refs_1_.refs_3_ = bf16[1024,256]{1,0:T(8,128)(2,1)S(1)} collective-permute-done((bf16[1024,256]{1,0:T(8,128)(2,1)S(1)}, bf16[1024,256]{1,0:T(8,128)(2,1)S(1)}, u32[]{:S(2)}, u32[]{:S(2)}) %collective-permute-start.14) | collective-permute-done | bytes 524320 | tf_op jit(solution)/shard_map/ppermute | solution.py:15
  53.0 5.3 %shard_map.47 = (f32[2048,512]{1,0:T(8,128)S(1)}, f32[8,512]{1,0:T(8,128)S(1)}) custom-call(s32[4]{0:T(128)S(1)} %pad_add_fusion.flags, bf16[1024,2048]{1,0:T(8,128)(2,1)S(1)} %copy-done.1, bf16[1024,2048]{1,0:T(8,128)(2,1)S(1)} %collective-permute-done.5.other, bf16[1024,256]{1,0:T(8,128)(2,1)S(1)} %constant_dynamic-update-slice_fusion.refs_0_.refs_2_, ...), custom_call_target="tpu_custom_call" | custom-call | flops 4294967296 | bytes 1 | tf_op jit(solution)/shard_map/pallas_call | solution.py:145
  60.8 2.5 %collective-permute-done.16.refs_1_ = bf16[1152,512]{1,0:T(8,128)(2,1)S(1)} collective-permute-done((bf16[1152,512]{1,0:T(8,128)(2,1)S(1)}, bf16[1152,512]{1,0:T(8,128)(2,1)S(1)}, u32[]{:S(2)}, u32[]{:S(2)}) %collective-permute-start.16) | collective-permute-done | bytes 1179680 | tf_op jit(solution)/shard_map/ppermute | solution.py:15
  63.3 2.2 %shard_map.48.solved = bf16[1024,256]{1,0:T(8,128)(2,1)S(1)} custom-call(s32[4]{0:T(128)S(1)} %pad_add_fusion.flags, f32[2,256,256]{2,1,0:T(8,128)S(1)} %copy-done, bf16[1152,512]{1,0:T(8,128)(2,1)S(1)} %pad_maximum_fusion.1.refs_0_, bf16[1152,512]{1,0:T(8,128)(2,1)S(1)} %collective-permute-done.16.refs_1_, ...), custom_call_target="tpu_custom_call" | custom-call | flops 1 | bytes 1 | tf_op jit(solution)/shard_map/pallas_call | solution.py:145
  65.5 3.1 %shard_map.49 = (f32[2048,256]{1,0:T(8,128)S(1)}, f32[8,256]{1,0:T(8,128)}) custom-call(s32[4]{0:T(128)S(1)} %pad_add_fusion.flags, f32[2048,512]{1,0:T(8,128)S(1)} %get-tuple-element.58.rotated, f32[8,512]{1,0:T(8,128)S(1)} %get-tuple-element.59.peak, bf16[1024,1024]{1,0:T(8,128)(2,1)S(1)} %pad_maximum_fusion.own, ...), custom_call_target="tpu_custom_call" | custom-call | flops 1 | bytes 1 | tf_op jit(solution)/shard_map/pallas_call | solution.py:145
  69.0 1.4 %collective-permute-start.17 = (f16[2048,128]{1,0:T(8,128)(2,1)S(1)}, f16[2048,128]{1,0:T(8,128)(2,1)S(1)}, u32[]{:S(2)}, u32[]{:S(2)}) collective-permute-start(f16[2048,128]{1,0:T(8,128)(2,1)S(1)} %get-tuple-element.68), channel_id=1, source_target_pairs={{0,4},{1,5},{2,6},{3,7},{4,0},{5,1},{6,2},{7,3},{8,12},{9,13},{10,... | collective-permute-start | bytes 1572872 | tf_op jit(solution)/shard_map/ppermute | solution.py:15
  70.5 2.4 %shard_map.50.solved = bf16[1024,256]{1,0:T(8,128)(2,1)S(1)} custom-call(s32[4]{0:T(128)S(1)} %pad_add_fusion.flags, f32[2,256,256]{2,1,0:T(8,128)S(1)} %copy-done, bf16[1152,512]{1,0:T(8,128)(2,1)S(1)} %pad_maximum_fusion.1.refs_0_, bf16[1152,512]{1,0:T(8,128)(2,1)S(1)} %collective-permute-done.16.refs_1_, ...), custom_call_target="tpu_custom_call" | custom-call | flops 1 | bytes 1 | tf_op jit(solution)/shard_map/pallas_call | solution.py:145
  72.8 2.5 %shard_map.51 = (f32[2048,256]{1,0:T(8,128)S(1)}, f32[8,256]{1,0:T(8,128)S(1)}) custom-call(s32[4]{0:T(128)S(1)} %pad_add_fusion.flags, f32[2048,512]{1,0:T(8,128)S(1)} %get-tuple-element.58.rotated, f32[8,512]{1,0:T(8,128)S(1)} %get-tuple-element.59.peak, bf16[1024,1024]{1,0:T(8,128)(2,1)S(1)} %pad_maximum_fusion.own, ...), custom_call_target="tpu_custom_call" | custom-call | flops 1 | bytes 1 | tf_op jit(solution)/shard_map/pallas_call | solution.py:145
  75.7 2.2 %collective-permute-start.20 = (f16[1024,128]{1,0:T(8,128)(2,1)S(1)}, f16[1024,128]{1,0:T(8,128)(2,1)S(1)}, u32[]{:S(2)}, u32[]{:S(2)}) collective-permute-start(f16[1024,128]{1,0:T(8,128)(2,1)S(1)} %get-tuple-element.79), channel_id=1, source_target_pairs={{0,2},{1,3},{2,0},{3,1},{4,6},{5,7},{6,4},{7,5},{8,10},{9,11},{10,... | collective-permute-start | bytes 786440 | tf_op jit(solution)/shard_map/ppermute | solution.py:15
  78.0 20.0 %collective-permute-done.20 = f16[1024,128]{1,0:T(8,128)(2,1)S(1)} collective-permute-done((f16[1024,128]{1,0:T(8,128)(2,1)S(1)}, f16[1024,128]{1,0:T(8,128)(2,1)S(1)}, u32[]{:S(2)}, u32[]{:S(2)}) %collective-permute-start.20) | collective-permute-done | bytes 262176 | tf_op jit(solution)/shard_map/ppermute | solution.py:15
  98.1 9.7 %collective-permute-done.19 = f16[1024,128]{1,0:T(8,128)(2,1)S(1)} collective-permute-done((f16[1024,128]{1,0:T(8,128)(2,1)S(1)}, f16[1024,128]{1,0:T(8,128)(2,1)S(1)}, u32[]{:S(2)}, u32[]{:S(2)}) %collective-permute-start.19) | collective-permute-done | bytes 262176 | tf_op jit(solution)/shard_map/ppermute | solution.py:15
  107.8 1.9 %shard_map.52.refs_2_ = f32[8192,128]{1,0:T(8,128)} custom-call(s32[4]{0:T(128)S(1)} %pad_add_fusion.flags, f32[8,256]{1,0:T(8,128)S(1)} %get-tuple-element.67.power, f32[1024,128]{1,0:T(8,128)S(1)} %convert_element_type.34.refs_0_, f32[1024,128]{1,0:T(8,128)S(1)} %convert_element_type.35.refs_1_, f32[2048,128]{1,0:T(8,128)S(1)} %slice.61.refs_2_), custom_call_target="tpu_custom_call" | custom-call | flops 1 | bytes 1 | tf_op jit(solution)/shard_map/pallas_call | solution.py:255
  109.9 4.7 %collective-permute-done.18 = f16[2048,128]{1,0:T(8,128)(2,1)S(1)} collective-permute-done((f16[2048,128]{1,0:T(8,128)(2,1)S(1)}, f16[2048,128]{1,0:T(8,128)(2,1)S(1)}, u32[]{:S(2)}, u32[]{:S(2)}) %collective-permute-start.18) | collective-permute-done | bytes 524320 | tf_op jit(solution)/shard_map/ppermute | solution.py:15
  114.6 1.9 %shard_map.53 = f32[8192,128]{1,0:T(8,128)} custom-call(s32[4]{0:T(128)S(1)} %pad_add_fusion.flags, f32[8,256]{1,0:T(8,128)S(1)} %get-tuple-element.67.power, f32[2048,128]{1,0:T(8,128)S(1)} %convert_element_type.32.refs_0_, f32[2048,128]{1,0:T(8,128)S(1)} %convert_element_type.33.refs_1_, f32[8192,128]{1,0:T(8,128)} %shard_map.52.refs_2_), custom_call_target="tpu_custom_call", output_to_operand_aliasing={{}: (4, {})} | custom-call | flops 1 | bytes 1 | tf_op jit(solution)/shard_map/pallas_call | solution.py:255
  (64 shorter events, 17.4 us)
Async XLA Ops:
  0.1 17.3 %collective-permute-start.5 = (bf16[1024,2048]{1,0:T(8,128)(2,1)}, bf16[1024,2048]{1,0:T(8,128)(2,1)S(1)}, u32[]{:S(2)}, u32[]{:S(2)}) collective-permute-start(bf16[1024,2048]{1,0:T(8,128)(2,1)} %own), channel_id=1, source_target_pairs={{0,1},{1,0},{2,3},{3,2},{4,5},{5,4},{6,7},{7,6},{8,9},{9,8},{10,11... | collective-permute-start | bytes 12582920 | tf_op jit(solution)/shard_map/ppermute | solution.py:15
  0.8 8.6 %collective-permute-start = (bf16[1,512,128]{2,1,0:T(8,128)(2,1)}, bf16[1,512,128]{2,1,0:T(8,128)(2,1)S(1)}, u32[]{:S(2)}, u32[]{:S(2)}) collective-permute-start(bf16[1,512,128]{2,1,0:T(8,128)(2,1)} %bitcast.5), channel_id=1, source_target_pairs={{0,4},{1,5},{2,6},{3,7},{4,0},{5,1},{6,2},{7,3},{8,12},{9,13},{10,... | collective-permute-start | bytes 393224 | tf_op jit(solution)/shard_map/ppermute | solution.py:15
  5.8 11.1 %collective-permute-start.2 = (bf16[576,512]{1,0:T(8,128)(2,1)S(1)}, bf16[576,512]{1,0:T(8,128)(2,1)S(1)}, u32[]{:S(2)}, u32[]{:S(2)}) collective-permute-start(bf16[576,512]{1,0:T(8,128)(2,1)S(1)} %pad_maximum_fusion.2), channel_id=1, source_target_pairs={{31,7}} | collective-permute-start | bytes 1769480 | tf_op jit(solution)/shard_map/ppermute | solution.py:184
  6.5 3.6 %copy-start.2 = (f32[1024,512]{1,0:T(8,128)S(1)}, f32[1024,512]{1,0:T(8,128)}, u32[]{:S(2)}) copy-start(f32[1024,512]{1,0:T(8,128)} %param.6) | copy-start | bytes 6291460
  6.6 10.4 %collective-permute-start.3 = (bf16[576,512]{1,0:T(8,128)(2,1)S(1)}, bf16[576,512]{1,0:T(8,128)(2,1)S(1)}, u32[]{:S(2)}, u32[]{:S(2)}) collective-permute-start(bf16[576,512]{1,0:T(8,128)(2,1)S(1)} %pad_maximum_fusion.3), channel_id=1, source_target_pairs={{31,15}} | collective-permute-start | bytes 1769480 | tf_op jit(solution)/shard_map/ppermute | solution.py:184
  7.5 9.5 %collective-permute-start.4 = (bf16[576,512]{1,0:T(8,128)(2,1)S(1)}, bf16[576,512]{1,0:T(8,128)(2,1)S(1)}, u32[]{:S(2)}, u32[]{:S(2)}) collective-permute-start(bf16[576,512]{1,0:T(8,128)(2,1)S(1)} %fusion.4), channel_id=1, source_target_pairs={{31,23}} | collective-permute-start | bytes 1769480 | tf_op jit(solution)/shard_map/ppermute | solution.py:184
  9.4 7.5 %collective-permute-start.1 = (bf16[2,512,128]{2,1,0:T(8,128)(2,1)S(1)}, bf16[2,512,128]{2,1,0:T(8,128)(2,1)S(1)}, u32[]{:S(2)}, u32[]{:S(2)}) collective-permute-start(bf16[2,512,128]{2,1,0:T(8,128)(2,1)S(1)} %pad_maximum_fusion.5), channel_id=1, source_target_pairs={{0,2},{1,3},{2,0},{3,1},{4,6},{5,7},{6,4},{7,5},{8,10},{9,11},{10,... | collective-permute-start | bytes 786440 | tf_op jit(solution)/shard_map/ppermute | solution.py:15
  17.3 11.5 %collective-permute-start.8 = (bf16[576,512]{1,0:T(8,128)(2,1)S(1)}, bf16[576,512]{1,0:T(8,128)(2,1)S(1)}, u32[]{:S(2)}, u32[]{:S(2)}) collective-permute-start(bf16[576,512]{1,0:T(8,128)(2,1)S(1)} %fusion.7), channel_id=1, source_target_pairs={{7,3},{15,11},{23,19},{31,27}} | collective-permute-start | bytes 1769480 | tf_op jit(solution)/shard_map/ppermute | solution.py:202
  18.7 10.3 %collective-permute-start.6 = (bf16[512,256]{1,0:T(8,128)(2,1)S(1)}, bf16[512,256]{1,0:T(8,128)(2,1)S(1)}, u32[]{:S(2)}, u32[]{:S(2)}) collective-permute-start(bf16[512,256]{1,0:T(8,128)(2,1)S(1)} %get-tuple-element.52), channel_id=1, source_target_pairs={{0,8},{8,0},{16,24},{24,16},{1,9},{9,1},{17,25},{25,17},{2,10},{10... | collective-permute-start | bytes 786440 | tf_op jit(solution)/shard_map/ppermute | solution.py:15
  20.0 9.0 %collective-permute-start.7 = (bf16[512,256]{1,0:T(8,128)(2,1)S(1)}, bf16[512,256]{1,0:T(8,128)(2,1)S(1)}, u32[]{:S(2)}, u32[]{:S(2)}) collective-permute-start(bf16[512,256]{1,0:T(8,128)(2,1)S(1)} %get-tuple-element.54), channel_id=1, source_target_pairs={{0,16},{8,24},{16,0},{24,8},{1,17},{9,25},{17,1},{25,9},{2,18},{10... | collective-permute-start | bytes 786440 | tf_op jit(solution)/shard_map/ppermute | solution.py:15
  28.9 24.1 %copy-start.1 = (bf16[1024,2048]{1,0:T(8,128)(2,1)S(1)}, bf16[1024,2048]{1,0:T(8,128)(2,1)}, u32[]{:S(2)}) copy-start(bf16[1024,2048]{1,0:T(8,128)(2,1)} %own) | copy-start | bytes 12582916
  29.1 8.6 %collective-permute-start.10 = (bf16[1024,1024]{1,0:T(8,128)(2,1)S(1)}, bf16[1024,1024]{1,0:T(8,128)(2,1)S(1)}, u32[]{:S(2)}, u32[]{:S(2)}) collective-permute-start(bf16[1024,1024]{1,0:T(8,128)(2,1)S(1)} %pad_maximum_fusion.own), channel_id=1, source_target_pairs={{0,1},{1,0},{2,3},{3,2},{4,5},{5,4},{6,7},{7,6},{8,9},{9,8},{10,11... | collective-permute-start | bytes 6291464 | tf_op jit(solution)/shard_map/ppermute | solution.py:15
  29.1 8.4 %collective-permute-start.9 = (bf16[576,512]{1,0:T(8,128)(2,1)S(1)}, bf16[576,512]{1,0:T(8,128)(2,1)S(1)}, u32[]{:S(2)}, u32[]{:S(2)}) collective-permute-start(bf16[576,512]{1,0:T(8,128)(2,1)S(1)} %add.24), channel_id=1, source_target_pairs={{7,5},{3,1},{15,13},{11,9},{23,21},{19,17},{31,29},{27,25}} | collective-permute-start | bytes 1769480 | tf_op jit(solution)/shard_map/ppermute | solution.py:202
  30.8 14.0 %collective-permute-start.15 = (bf16[1024,256]{1,0:T(8,128)(2,1)S(1)}, bf16[1024,256]{1,0:T(8,128)(2,1)S(1)}, u32[]{:S(2)}, u32[]{:S(2)}) collective-permute-start(bf16[1024,256]{1,0:T(8,128)(2,1)S(1)} %constant_dynamic-update-slice_fusion.2.refs_2_), channel_id=1, source_target_pairs={{0,8},{8,0},{16,24},{24,16},{1,9},{9,1},{17,25},{25,17},{2,10},{10... | collective-permute-start | bytes 1572872 | tf_op jit(solution)/shard_map/ppermute | solution.py:15
  32.1 20.9 %collective-permute-start.14 = (bf16[1024,256]{1,0:T(8,128)(2,1)S(1)}, bf16[1024,256]{1,0:T(8,128)(2,1)S(1)}, u32[]{:S(2)}, u32[]{:S(2)}) collective-permute-start(bf16[1024,256]{1,0:T(8,128)(2,1)S(1)} %constant_dynamic-update-slice_fusion.refs_0_.refs_2_), channel_id=1, source_target_pairs={{0,16},{8,24},{16,0},{24,8},{1,17},{9,25},{17,1},{25,9},{2,18},{10... | collective-permute-start | bytes 1572872 | tf_op jit(solution)/shard_map/ppermute | solution.py:15
  37.7 20.6 %collective-permute-start.13 = (bf16[576,512]{1,0:T(8,128)(2,1)S(1)}, bf16[576,512]{1,0:T(8,128)(2,1)S(1)}, u32[]{:S(2)}, u32[]{:S(2)}) collective-permute-start(bf16[576,512]{1,0:T(8,128)(2,1)S(1)} %add.25), channel_id=1, source_target_pairs={{1,24},{3,26},{5,28},{7,30},{9,16},{11,18},{13,20},{15,22},{17,8},... | collective-permute-start | bytes 1769480 | tf_op jit(solution)/shard_map/ppermute | solution.py:213
  39.0 20.4 %collective-permute-start.12 = (bf16[576,512]{1,0:T(8,128)(2,1)S(1)}, bf16[576,512]{1,0:T(8,128)(2,1)S(1)}, u32[]{:S(2)}, u32[]{:S(2)}) collective-permute-start(bf16[576,512]{1,0:T(8,128)(2,1)S(1)} %add.25), channel_id=1, source_target_pairs={{1,16},{3,18},{5,20},{7,22},{9,24},{11,26},{13,28},{15,30},{17,0},... | collective-permute-start | bytes 1769480 | tf_op jit(solution)/shard_map/ppermute | solution.py:213
  40.6 18.8 %collective-permute-start.11 = (bf16[576,512]{1,0:T(8,128)(2,1)S(1)}, bf16[576,512]{1,0:T(8,128)(2,1)S(1)}, u32[]{:S(2)}, u32[]{:S(2)}) collective-permute-start(bf16[576,512]{1,0:T(8,128)(2,1)S(1)} %add.25), channel_id=1, source_target_pairs={{1,9},{3,11},{5,13},{7,15},{9,1},{11,3},{13,5},{15,7},{17,25},{19,... | collective-permute-start | bytes 1769480 | tf_op jit(solution)/shard_map/ppermute | solution.py:213
  59.7 3.5 %copy-start = (f32[2,256,256]{2,1,0:T(8,128)S(1)}, f32[2,256,256]{2,1,0:T(8,128)}, u32[]{:S(2)}) copy-start(f32[2,256,256]{2,1,0:T(8,128)} %inverse.2) | copy-start | bytes 1572868
  59.8 3.4 %collective-permute-start.16 = (bf16[1152,512]{1,0:T(8,128)(2,1)S(1)}, bf16[1152,512]{1,0:T(8,128)(2,1)S(1)}, u32[]{:S(2)}, u32[]{:S(2)}) collective-permute-start(bf16[1152,512]{1,0:T(8,128)(2,1)S(1)} %pad_maximum_fusion.1.refs_0_), channel_id=1, source_target_pairs={{0,1},{1,0},{2,3},{3,2},{4,5},{5,4},{6,7},{7,6},{8,9},{9,8},{10,11... | collective-permute-start | bytes 3538952 | tf_op jit(solution)/shard_map/ppermute | solution.py:15
  69.0 40.8 %collective-permute-start.17 = (f16[2048,128]{1,0:T(8,128)(2,1)S(1)}, f16[2048,128]{1,0:T(8,128)(2,1)S(1)}, u32[]{:S(2)}, u32[]{:S(2)}) collective-permute-start(f16[2048,128]{1,0:T(8,128)(2,1)S(1)} %get-tuple-element.68), channel_id=1, source_target_pairs={{0,4},{1,5},{2,6},{3,7},{4,0},{5,1},{6,2},{7,3},{8,12},{9,13},{10,... | collective-permute-start | bytes 1572872 | tf_op jit(solution)/shard_map/ppermute | solution.py:15
  70.5 44.1 %collective-permute-start.18 = (f16[2048,128]{1,0:T(8,128)(2,1)S(1)}, f16[2048,128]{1,0:T(8,128)(2,1)S(1)}, u32[]{:S(2)}, u32[]{:S(2)}) collective-permute-start(f16[2048,128]{1,0:T(8,128)(2,1)S(1)} %get-tuple-element.69), channel_id=1, source_target_pairs={{0,6},{1,7},{2,4},{3,5},{4,2},{5,3},{6,0},{7,1},{8,14},{9,15},{10,... | collective-permute-start | bytes 1572872 | tf_op jit(solution)/shard_map/ppermute | solution.py:15
  75.7 22.4 %collective-permute-start.20 = (f16[1024,128]{1,0:T(8,128)(2,1)S(1)}, f16[1024,128]{1,0:T(8,128)(2,1)S(1)}, u32[]{:S(2)}, u32[]{:S(2)}) collective-permute-start(f16[1024,128]{1,0:T(8,128)(2,1)S(1)} %get-tuple-element.79), channel_id=1, source_target_pairs={{0,2},{1,3},{2,0},{3,1},{4,6},{5,7},{6,4},{7,5},{8,10},{9,11},{10,... | collective-permute-start | bytes 786440 | tf_op jit(solution)/shard_map/ppermute | solution.py:15
  77.9 29.9 %collective-permute-start.19 = (f16[1024,128]{1,0:T(8,128)(2,1)S(1)}, f16[1024,128]{1,0:T(8,128)(2,1)S(1)}, u32[]{:S(2)}, u32[]{:S(2)}) collective-permute-start(f16[1024,128]{1,0:T(8,128)(2,1)S(1)} %get-tuple-element.80), channel_id=1, source_target_pairs={{0,2},{1,3},{2,0},{3,1},{4,6},{5,7},{6,4},{7,5},{8,10},{9,11},{10,... | collective-permute-start | bytes 786440 | tf_op jit(solution)/shard_map/ppermute | solution.py:15
  (1 other events, 2.8 us)

commit v8 on v7

--- a/solution.py
+++ b/solution.py
@@ -116,6 +116,12 @@
     @pl.when(flags[0] == 1)
     def _():
         out[2 * rows - size :, :] = panels * scale
+
+
+def finish_kernel(places, depth, which, flags, inverse, here, there, *refs):
+    *parts, rotated, peak, own, other, out, power, terms, cross, solved = refs
+    solve_kernel(places, flags, inverse, here, there, *parts, terms, cross, solved)
+    correct_kernel(depth, which, flags, rotated, peak, own, other, terms, out, power)
 
 
 def place_kernel(ks, flags, power, *refs):
@@ -194,7 +200,7 @@
     steps, downs, sources = steps_of(n_row), steps_of(n_vec)[:0:-1], [n_vec - 1]
     for i in range(max(len(steps), len(downs))):
         if i < len(steps):
-            for which, step in enumerate((steps[i], steps[-1 - i])):
+            for which, step in enumerate((steps[-1 - i], steps[i])):
                 known = jnp.concatenate(halves[which], axis=0)
                 halves[which] = [known, swapped(known, ROW, step)]
                 places[which] = places[which] + [q ^ step for q in places[which]]
@@ -221,26 +227,23 @@
     here = jnp.concatenate([pieces[q] + pieces[q + n_row // 2] for q in range(n_row // 2)], axis=0)
     tails = [here, swapped(here, VEC, 1)]
 
-    def solve(which):
-        solved, = call(
-            functools.partial(solve_kernel, places[which]), flags, [panel_inverse, *tails, *halves[which]],
-            [((4 * width, count // 2), bf16)],
-            [pltpu.VMEM(cross.shape, bf16), pltpu.VMEM((2 * width, count // 2), f32)],
+    def finish(which):
+        return call(
+            functools.partial(finish_kernel, places[which], depth, which), flags,
+            [panel_inverse, *tails, *halves[which], rotated, peak, cols, other_cols],
+            [((2 * rows, count // 2), f32), ((8, count // 2), f32)],
+            [
+                pltpu.VMEM((4 * width, count // 2), bf16), pltpu.VMEM(cross.shape, bf16),
+                pltpu.VMEM((2 * width, count // 2), f32),
+            ],
         )
-        return solved
-
-    def correct(which, solved):
-        return call(
-            functools.partial(correct_kernel, depth, which), flags, [rotated, peak, cols, other_cols, solved],
-            [((2 * rows, count // 2), f32), ((8, count // 2), f32)], [],
-        )
 
     piece = lambda values, i: values[:, i * own_cols : (i + 1) * own_cols]
-    values, _ = correct(0, solve(0))
+    values, _ = finish(0)
     values = [piece(values, j).astype(jnp.float16) for j in range(cut)]
     values, panel_inverse = lax.optimization_barrier((values, panel_inverse))
     far = {2 * (cut + j): [swapped(values[j], VEC, 2 * (cut + j))] for j in range(cut)}
-    values, power = correct(1, solve(1))
+    values, power = finish(1)
     near = {}
     for j in range(1, cut):
         value = piece(values, j).astype(jnp.float16)

time: 118 us -> 118 us (level)
    ppermute x3, waiting for transfers between devices: 1.1 us -> 7.44 us  [on_device(): pieces.append(lax.ppermute(part, (ROW, VEC), pairs))]
    ppermute x13, waiting for transfers between devices: 53.5 us -> 48.2 us  [swapped(): lax.ppermute(value, axis, [(i, i ^ offset) for i in range(lax.axis_size(a...]
    pallas_call x6 -> x4, Pallas kernels: 15.5 us -> 14.6 us  [call(): pl.pallas_call(kernel, in_specs=[spec(pltpu.SMEM)] * len(scalars) + specs...]
  transfers between devices with their start and end apart: 21 -> 21, of which waited for: 11 -> 12; matrix products, arithmetic and copies ran while one was open for 4% -> 4% of each run, Pallas kernels for 10% -> 10%
where the time goes in v8:
time: 118 us; the launch traced here: 116 us
  waiting for transfers between devices  65.8 us (56%)
  starting transfers between devices  25.4 us (22%)
  Pallas kernels  18.4 us (16%)
  other arithmetic  3.61 us (3%)
  local copies, waits for them, and re-layouts  2.15 us (2%)
    ppermute x13, waiting for transfers between devices, swapped(): lax.ppermute(value, axis, [(i, i ^ offset) for i in range(lax.axis_size(a...  48.2 us
    pallas_call x4, Pallas kernels, call(): pl.pallas_call(kernel, in_specs=[spec(pltpu.SMEM)] * len(scalars) + specs...  14.6 us
    ppermute x13, starting transfers between devices, swapped(): lax.ppermute(value, axis, [(i, i ^ offset) for i in range(lax.axis_size(a...  14.3 us
    ppermute x2, waiting for transfers between devices, on_device(): part += lax.ppermute(part, VEC, [(v, v ^ downs[i]) for v in sources])  10.1 us
    ppermute x3, waiting for transfers between devices, on_device(): pieces.append(lax.ppermute(part, (ROW, VEC), pairs))  7.44 us
    ppermute x3, starting transfers between devices, on_device(): pieces.append(lax.ppermute(part, (ROW, VEC), pairs))  5.99 us
    pallas_call x2, Pallas kernels, place(): pl.pallas_call(functools.partial(place_kernel, [(k, len(v)) for k, v in b...  3.89 us
    ppermute x2, starting transfers between devices, on_device(): part += lax.ppermute(part, VEC, [(v, v ^ downs[i]) for v in sources])  2.88 us
  transfers between devices with their start and end apart: 21, of which 12 were waited for; matrix products, arithmetic and copies ran while one was open for 4% of the time, Pallas kernels for 10%

profile of v8, /device:TPU:9, one launch (start us, length us, event | category | flops | bytes accessed | tf_op | source)
XLA Modules:
  0.0 116.0 jit_solution(8951738830807958918)
XLA Ops:
  0.8 2.3 %collective-permute-start = (bf16[1,512,128]{2,1,0:T(8,128)(2,1)}, bf16[1,512,128]{2,1,0:T(8,128)(2,1)S(1)}, u32[]{:S(2)}, u32[]{:S(2)}) collective-permute-start(bf16[1,512,128]{2,1,0:T(8,128)(2,1)} %bitcast.5), channel_id=1, source_target_pairs={{0,4},{1,5},{2,6},{3,7},{4,0},{5,1},{6,2},{7,3},{8,12},{9,13},{10,... | collective-permute-start | bytes 393224 | tf_op jit(solution)/shard_map/ppermute | solution.py:15
  4.1 1.7 %fusion.12 = (bf16[512,512]{1,0:T(8,128)(2,1)S(1)}, bf16[512,512]{1,0:T(8,128)(2,1)S(1)}, bf16[512,512]{1,0:T(8,128)(2,1)S(1)}, bf16[512,512]{1,0:T(8,128)(2,1)S(1)}) fusion(bf16[1024,2048]{1,0:T(8,128)(2,1)} %own), kind=kLoop, calls=%fused_computation.35 | loop fusion | bytes 4194304 | tf_op jit(solution)/shard_map/slice | solution.py:183
  10.8 6.1 %collective-permute-done.1 = bf16[2,512,128]{2,1,0:T(8,128)(2,1)S(1)} collective-permute-done((bf16[2,512,128]{2,1,0:T(8,128)(2,1)S(1)}, bf16[2,512,128]{2,1,0:T(8,128)(2,1)S(1)}, u32[]{:S(2)}, u32[]{:S(2)}) %collective-permute-start.1) | collective-permute-done | bytes 262176 | tf_op jit(solution)/shard_map/ppermute | solution.py:15
  21.3 7.6 %collective-permute-done.8 = bf16[576,512]{1,0:T(8,128)(2,1)S(1)} collective-permute-done((bf16[576,512]{1,0:T(8,128)(2,1)S(1)}, bf16[576,512]{1,0:T(8,128)(2,1)S(1)}, u32[]{:S(2)}, u32[]{:S(2)}) %collective-permute-start.8) | collective-permute-done | bytes 589856 | tf_op jit(solution)/shard_map/ppermute | solution.py:208
  29.1 1.6 %collective-permute-start.9 = (bf16[576,512]{1,0:T(8,128)(2,1)S(1)}, bf16[576,512]{1,0:T(8,128)(2,1)S(1)}, u32[]{:S(2)}, u32[]{:S(2)}) collective-permute-start(bf16[576,512]{1,0:T(8,128)(2,1)S(1)} %add.24), channel_id=1, source_target_pairs={{7,5},{3,1},{15,13},{11,9},{23,21},{19,17},{31,29},{27,25}} | collective-permute-start | bytes 1769480 | tf_op jit(solution)/shard_map/ppermute | solution.py:208
  30.8 4.1 %collective-permute-start.15 = (bf16[1024,256]{1,0:T(8,128)(2,1)S(1)}, bf16[1024,256]{1,0:T(8,128)(2,1)S(1)}, u32[]{:S(2)}, u32[]{:S(2)}) collective-permute-start(bf16[1024,256]{1,0:T(8,128)(2,1)S(1)} %constant_dynamic-update-slice_fusion.2.refs_2_.refs_0_), channel_id=1, source_target_pairs={{0,16},{8,24},{16,0},{24,8},{1,17},{9,25},{17,1},{25,9},{2,18},{10... | collective-permute-start | bytes 1572872 | tf_op jit(solution)/shard_map/ppermute | solution.py:15
  35.0 2.5 %collective-permute-done.9 = bf16[576,512]{1,0:T(8,128)(2,1)S(1)} collective-permute-done((bf16[576,512]{1,0:T(8,128)(2,1)S(1)}, bf16[576,512]{1,0:T(8,128)(2,1)S(1)}, u32[]{:S(2)}, u32[]{:S(2)}) %collective-permute-start.9) | collective-permute-done | bytes 589856 | tf_op jit(solution)/shard_map/ppermute | solution.py:208
  37.7 1.3 %collective-permute-start.13 = (bf16[576,512]{1,0:T(8,128)(2,1)S(1)}, bf16[576,512]{1,0:T(8,128)(2,1)S(1)}, u32[]{:S(2)}, u32[]{:S(2)}) collective-permute-start(bf16[576,512]{1,0:T(8,128)(2,1)S(1)} %add.25), channel_id=1, source_target_pairs={{1,24},{3,26},{5,28},{7,30},{9,16},{11,18},{13,20},{15,22},{17,8},... | collective-permute-start | bytes 1769480 | tf_op jit(solution)/shard_map/ppermute | solution.py:219
  39.0 1.5 %collective-permute-start.12 = (bf16[576,512]{1,0:T(8,128)(2,1)S(1)}, bf16[576,512]{1,0:T(8,128)(2,1)S(1)}, u32[]{:S(2)}, u32[]{:S(2)}) collective-permute-start(bf16[576,512]{1,0:T(8,128)(2,1)S(1)} %add.25), channel_id=1, source_target_pairs={{1,16},{3,18},{5,20},{7,22},{9,24},{11,26},{13,28},{15,30},{17,0},... | collective-permute-start | bytes 1769480 | tf_op jit(solution)/shard_map/ppermute | solution.py:219
  40.6 3.1 %collective-permute-start.11 = (bf16[576,512]{1,0:T(8,128)(2,1)S(1)}, bf16[576,512]{1,0:T(8,128)(2,1)S(1)}, u32[]{:S(2)}, u32[]{:S(2)}) collective-permute-start(bf16[576,512]{1,0:T(8,128)(2,1)S(1)} %add.25), channel_id=1, source_target_pairs={{1,9},{3,11},{5,13},{7,15},{9,1},{11,3},{13,5},{15,7},{17,25},{19,... | collective-permute-start | bytes 1769480 | tf_op jit(solution)/shard_map/ppermute | solution.py:219
  43.7 3.4 %collective-permute-done.15.refs_3_.refs_1_ = bf16[1024,256]{1,0:T(8,128)(2,1)S(1)} collective-permute-done((bf16[1024,256]{1,0:T(8,128)(2,1)S(1)}, bf16[1024,256]{1,0:T(8,128)(2,1)S(1)}, u32[]{:S(2)}, u32[]{:S(2)}) %collective-permute-start.15) | collective-permute-done | bytes 524320 | tf_op jit(solution)/shard_map/ppermute | solution.py:15
  47.1 1.5 %collective-permute-done.14.refs_1_ = bf16[1024,256]{1,0:T(8,128)(2,1)S(1)} collective-permute-done((bf16[1024,256]{1,0:T(8,128)(2,1)S(1)}, bf16[1024,256]{1,0:T(8,128)(2,1)S(1)}, u32[]{:S(2)}, u32[]{:S(2)}) %collective-permute-start.14) | collective-permute-done | bytes 524320 | tf_op jit(solution)/shard_map/ppermute | solution.py:15
  48.6 5.3 %shard_map.47 = (f32[2048,512]{1,0:T(8,128)S(1)}, f32[8,512]{1,0:T(8,128)S(1)}) custom-call(s32[4]{0:T(128)S(1)} %pad_add_fusion.flags, bf16[1024,2048]{1,0:T(8,128)(2,1)S(1)} %copy-done.1, bf16[1024,2048]{1,0:T(8,128)(2,1)S(1)} %collective-permute-done.5.other, bf16[1024,256]{1,0:T(8,128)(2,1)S(1)} %constant_dynamic-update-slice_fusion.refs_0_, ...), custom_call_target="tpu_custom_call" | custom-call | flops 4294967296 | bytes 1 | tf_op jit(solution)/shard_map/pallas_call | solution.py:151
  53.9 5.4 %collective-permute-done.12 = bf16[576,512]{1,0:T(8,128)(2,1)S(1)} collective-permute-done((bf16[576,512]{1,0:T(8,128)(2,1)S(1)}, bf16[576,512]{1,0:T(8,128)(2,1)S(1)}, u32[]{:S(2)}, u32[]{:S(2)}) %collective-permute-start.12) | collective-permute-done | bytes 589856 | tf_op jit(solution)/shard_map/ppermute | solution.py:219
  59.3 2.1 %collective-permute-done.11 = bf16[576,512]{1,0:T(8,128)(2,1)S(1)} collective-permute-done((bf16[576,512]{1,0:T(8,128)(2,1)S(1)}, bf16[576,512]{1,0:T(8,128)(2,1)S(1)}, u32[]{:S(2)}, u32[]{:S(2)}) %collective-permute-start.11) | collective-permute-done | bytes 589856 | tf_op jit(solution)/shard_map/ppermute | solution.py:219
  61.8 2.8 %collective-permute-done.16.there = bf16[1152,512]{1,0:T(8,128)(2,1)S(1)} collective-permute-done((bf16[1152,512]{1,0:T(8,128)(2,1)S(1)}, bf16[1152,512]{1,0:T(8,128)(2,1)S(1)}, u32[]{:S(2)}, u32[]{:S(2)}) %collective-permute-start.16) | collective-permute-done | bytes 1179680 | tf_op jit(solution)/shard_map/ppermute | solution.py:15
  64.7 4.8 %shard_map.48 = (f32[2048,256]{1,0:T(8,128)S(1)}, f32[8,256]{1,0:T(8,128)}) custom-call(s32[4]{0:T(128)S(1)} %pad_add_fusion.flags, f32[2,256,256]{2,1,0:T(8,128)S(1)} %copy-done, bf16[1152,512]{1,0:T(8,128)(2,1)S(1)} %pad_maximum_fusion.1.here, bf16[1152,512]{1,0:T(8,128)(2,1)S(1)} %collective-permute-done.16.there, ...), custom_call_target="tpu_custom_call" | custom-call | flops 1 | bytes 1 | tf_op jit(solution)/shard_map/pallas_call | solution.py:151
  70.0 4.4 %shard_map.49 = (f32[2048,256]{1,0:T(8,128)S(1)}, f32[8,256]{1,0:T(8,128)S(1)}) custom-call(s32[4]{0:T(128)S(1)} %pad_add_fusion.flags, f32[2,256,256]{2,1,0:T(8,128)S(1)} %copy-done, bf16[1152,512]{1,0:T(8,128)(2,1)S(1)} %pad_maximum_fusion.1.here, bf16[1152,512]{1,0:T(8,128)(2,1)S(1)} %collective-permute-done.16.there, ...), custom_call_target="tpu_custom_call" | custom-call | flops 1 | bytes 1 | tf_op jit(solution)/shard_map/pallas_call | solution.py:151
  74.8 3.5 %collective-permute-start.20 = (f16[1024,128]{1,0:T(8,128)(2,1)S(1)}, f16[1024,128]{1,0:T(8,128)(2,1)S(1)}, u32[]{:S(2)}, u32[]{:S(2)}) collective-permute-start(f16[1024,128]{1,0:T(8,128)(2,1)S(1)} %get-tuple-element.79), channel_id=1, source_target_pairs={{0,2},{1,3},{2,0},{3,1},{4,6},{5,7},{6,4},{7,5},{8,10},{9,11},{10,... | collective-permute-start | bytes 786440 | tf_op jit(solution)/shard_map/ppermute | solution.py:15
  78.4 18.8 %collective-permute-done.20 = f16[1024,128]{1,0:T(8,128)(2,1)S(1)} collective-permute-done((f16[1024,128]{1,0:T(8,128)(2,1)S(1)}, f16[1024,128]{1,0:T(8,128)(2,1)S(1)}, u32[]{:S(2)}, u32[]{:S(2)}) %collective-permute-start.20) | collective-permute-done | bytes 262176 | tf_op jit(solution)/shard_map/ppermute | solution.py:15
  97.2 9.8 %collective-permute-done.19 = f16[1024,128]{1,0:T(8,128)(2,1)S(1)} collective-permute-done((f16[1024,128]{1,0:T(8,128)(2,1)S(1)}, f16[1024,128]{1,0:T(8,128)(2,1)S(1)}, u32[]{:S(2)}, u32[]{:S(2)}) %collective-permute-start.19) | collective-permute-done | bytes 262176 | tf_op jit(solution)/shard_map/ppermute | solution.py:15
  107.1 1.9 %shard_map.50.refs_2_ = f32[8192,128]{1,0:T(8,128)} custom-call(s32[4]{0:T(128)S(1)} %pad_add_fusion.flags, f32[8,256]{1,0:T(8,128)S(1)} %get-tuple-element.67.power, f32[1024,128]{1,0:T(8,128)S(1)} %convert_element_type.34.refs_0_, f32[1024,128]{1,0:T(8,128)S(1)} %convert_element_type.35.refs_1_, f32[2048,128]{1,0:T(8,128)S(1)} %slice.61.refs_2_), custom_call_target="tpu_custom_call" | custom-call | flops 1 | bytes 1 | tf_op jit(solution)/shard_map/pallas_call | solution.py:258
  109.1 4.7 %collective-permute-done.18 = f16[2048,128]{1,0:T(8,128)(2,1)S(1)} collective-permute-done((f16[2048,128]{1,0:T(8,128)(2,1)S(1)}, f16[2048,128]{1,0:T(8,128)(2,1)S(1)}, u32[]{:S(2)}, u32[]{:S(2)}) %collective-permute-start.18) | collective-permute-done | bytes 524320 | tf_op jit(solution)/shard_map/ppermute | solution.py:15
  113.9 1.9 %shard_map.51 = f32[8192,128]{1,0:T(8,128)} custom-call(s32[4]{0:T(128)S(1)} %pad_add_fusion.flags, f32[8,256]{1,0:T(8,128)S(1)} %get-tuple-element.67.power, f32[2048,128]{1,0:T(8,128)S(1)} %convert_element_type.32.refs_0_, f32[2048,128]{1,0:T(8,128)S(1)} %convert_element_type.33.refs_1_, f32[8192,128]{1,0:T(8,128)} %shard_map.50.refs_2_), custom_call_target="tpu_custom_call", output_to_operand_aliasing={{}: (4, {})} | custom-call | flops 1 | bytes 1 | tf_op jit(solution)/shard_map/pallas_call | solution.py:258
  (62 shorter events, 13.3 us)
Async XLA Ops:
  0.1 17.3 %collective-permute-start.5 = (bf16[1024,2048]{1,0:T(8,128)(2,1)}, bf16[1024,2048]{1,0:T(8,128)(2,1)S(1)}, u32[]{:S(2)}, u32[]{:S(2)}) collective-permute-start(bf16[1024,2048]{1,0:T(8,128)(2,1)} %own), channel_id=1, source_target_pairs={{0,1},{1,0},{2,3},{3,2},{4,5},{5,4},{6,7},{7,6},{8,9},{9,8},{10,11... | collective-permute-start | bytes 12582920 | tf_op jit(solution)/shard_map/ppermute | solution.py:15
  0.8 8.6 %collective-permute-start = (bf16[1,512,128]{2,1,0:T(8,128)(2,1)}, bf16[1,512,128]{2,1,0:T(8,128)(2,1)S(1)}, u32[]{:S(2)}, u32[]{:S(2)}) collective-permute-start(bf16[1,512,128]{2,1,0:T(8,128)(2,1)} %bitcast.5), channel_id=1, source_target_pairs={{0,4},{1,5},{2,6},{3,7},{4,0},{5,1},{6,2},{7,3},{8,12},{9,13},{10,... | collective-permute-start | bytes 393224 | tf_op jit(solution)/shard_map/ppermute | solution.py:15
  5.8 11.1 %collective-permute-start.2 = (bf16[576,512]{1,0:T(8,128)(2,1)S(1)}, bf16[576,512]{1,0:T(8,128)(2,1)S(1)}, u32[]{:S(2)}, u32[]{:S(2)}) collective-permute-start(bf16[576,512]{1,0:T(8,128)(2,1)S(1)} %pad_maximum_fusion.2), channel_id=1, source_target_pairs={{31,7}} | collective-permute-start | bytes 1769480 | tf_op jit(solution)/shard_map/ppermute | solution.py:190
  6.5 3.6 %copy-start.2 = (f32[1024,512]{1,0:T(8,128)S(1)}, f32[1024,512]{1,0:T(8,128)}, u32[]{:S(2)}) copy-start(f32[1024,512]{1,0:T(8,128)} %param.6) | copy-start | bytes 6291460
  6.6 10.4 %collective-permute-start.3 = (bf16[576,512]{1,0:T(8,128)(2,1)S(1)}, bf16[576,512]{1,0:T(8,128)(2,1)S(1)}, u32[]{:S(2)}, u32[]{:S(2)}) collective-permute-start(bf16[576,512]{1,0:T(8,128)(2,1)S(1)} %pad_maximum_fusion.3), channel_id=1, source_target_pairs={{31,15}} | collective-permute-start | bytes 1769480 | tf_op jit(solution)/shard_map/ppermute | solution.py:190
  7.5 9.5 %collective-permute-start.4 = (bf16[576,512]{1,0:T(8,128)(2,1)S(1)}, bf16[576,512]{1,0:T(8,128)(2,1)S(1)}, u32[]{:S(2)}, u32[]{:S(2)}) collective-permute-start(bf16[576,512]{1,0:T(8,128)(2,1)S(1)} %fusion.4), channel_id=1, source_target_pairs={{31,23}} | collective-permute-start | bytes 1769480 | tf_op jit(solution)/shard_map/ppermute | solution.py:190
  9.4 7.5 %collective-permute-start.1 = (bf16[2,512,128]{2,1,0:T(8,128)(2,1)S(1)}, bf16[2,512,128]{2,1,0:T(8,128)(2,1)S(1)}, u32[]{:S(2)}, u32[]{:S(2)}) collective-permute-start(bf16[2,512,128]{2,1,0:T(8,128)(2,1)S(1)} %pad_maximum_fusion.5), channel_id=1, source_target_pairs={{0,2},{1,3},{2,0},{3,1},{4,6},{5,7},{6,4},{7,5},{8,10},{9,11},{10,... | collective-permute-start | bytes 786440 | tf_op jit(solution)/shard_map/ppermute | solution.py:15
  17.3 11.5 %collective-permute-start.8 = (bf16[576,512]{1,0:T(8,128)(2,1)S(1)}, bf16[576,512]{1,0:T(8,128)(2,1)S(1)}, u32[]{:S(2)}, u32[]{:S(2)}) collective-permute-start(bf16[576,512]{1,0:T(8,128)(2,1)S(1)} %fusion.7), channel_id=1, source_target_pairs={{7,3},{15,11},{23,19},{31,27}} | collective-permute-start | bytes 1769480 | tf_op jit(solution)/shard_map/ppermute | solution.py:208
  18.7 10.3 %collective-permute-start.6 = (bf16[512,256]{1,0:T(8,128)(2,1)S(1)}, bf16[512,256]{1,0:T(8,128)(2,1)S(1)}, u32[]{:S(2)}, u32[]{:S(2)}) collective-permute-start(bf16[512,256]{1,0:T(8,128)(2,1)S(1)} %get-tuple-element.52), channel_id=1, source_target_pairs={{0,16},{8,24},{16,0},{24,8},{1,17},{9,25},{17,1},{25,9},{2,18},{10... | collective-permute-start | bytes 786440 | tf_op jit(solution)/shard_map/ppermute | solution.py:15
  20.0 9.0 %collective-permute-start.7 = (bf16[512,256]{1,0:T(8,128)(2,1)S(1)}, bf16[512,256]{1,0:T(8,128)(2,1)S(1)}, u32[]{:S(2)}, u32[]{:S(2)}) collective-permute-start(bf16[512,256]{1,0:T(8,128)(2,1)S(1)} %get-tuple-element.54), channel_id=1, source_target_pairs={{0,8},{8,0},{16,24},{24,16},{1,9},{9,1},{17,25},{25,17},{2,10},{10... | collective-permute-start | bytes 786440 | tf_op jit(solution)/shard_map/ppermute | solution.py:15
  28.9 19.7 %copy-start.1 = (bf16[1024,2048]{1,0:T(8,128)(2,1)S(1)}, bf16[1024,2048]{1,0:T(8,128)(2,1)}, u32[]{:S(2)}) copy-start(bf16[1024,2048]{1,0:T(8,128)(2,1)} %own) | copy-start | bytes 12582916
  29.1 8.6 %collective-permute-start.10 = (bf16[1024,1024]{1,0:T(8,128)(2,1)S(1)}, bf16[1024,1024]{1,0:T(8,128)(2,1)S(1)}, u32[]{:S(2)}, u32[]{:S(2)}) collective-permute-start(bf16[1024,1024]{1,0:T(8,128)(2,1)S(1)} %pad_maximum_fusion.refs_4_), channel_id=1, source_target_pairs={{0,1},{1,0},{2,3},{3,2},{4,5},{5,4},{6,7},{7,6},{8,9},{9,8},{10,11... | collective-permute-start | bytes 6291464 | tf_op jit(solution)/shard_map/ppermute | solution.py:15
  29.1 8.4 %collective-permute-start.9 = (bf16[576,512]{1,0:T(8,128)(2,1)S(1)}, bf16[576,512]{1,0:T(8,128)(2,1)S(1)}, u32[]{:S(2)}, u32[]{:S(2)}) collective-permute-start(bf16[576,512]{1,0:T(8,128)(2,1)S(1)} %add.24), channel_id=1, source_target_pairs={{7,5},{3,1},{15,13},{11,9},{23,21},{19,17},{31,29},{27,25}} | collective-permute-start | bytes 1769480 | tf_op jit(solution)/shard_map/ppermute | solution.py:208
  30.8 16.3 %collective-permute-start.15 = (bf16[1024,256]{1,0:T(8,128)(2,1)S(1)}, bf16[1024,256]{1,0:T(8,128)(2,1)S(1)}, u32[]{:S(2)}, u32[]{:S(2)}) collective-permute-start(bf16[1024,256]{1,0:T(8,128)(2,1)S(1)} %constant_dynamic-update-slice_fusion.2.refs_2_.refs_0_), channel_id=1, source_target_pairs={{0,16},{8,24},{16,0},{24,8},{1,17},{9,25},{17,1},{25,9},{2,18},{10... | collective-permute-start | bytes 1572872 | tf_op jit(solution)/shard_map/ppermute | solution.py:15
  34.9 13.7 %collective-permute-start.14 = (bf16[1024,256]{1,0:T(8,128)(2,1)S(1)}, bf16[1024,256]{1,0:T(8,128)(2,1)S(1)}, u32[]{:S(2)}, u32[]{:S(2)}) collective-permute-start(bf16[1024,256]{1,0:T(8,128)(2,1)S(1)} %constant_dynamic-update-slice_fusion.refs_0_), channel_id=1, source_target_pairs={{0,8},{8,0},{16,24},{24,16},{1,9},{9,1},{17,25},{25,17},{2,10},{10... | collective-permute-start | bytes 1572872 | tf_op jit(solution)/shard_map/ppermute | solution.py:15
  37.7 16.2 %collective-permute-start.13 = (bf16[576,512]{1,0:T(8,128)(2,1)S(1)}, bf16[576,512]{1,0:T(8,128)(2,1)S(1)}, u32[]{:S(2)}, u32[]{:S(2)}) collective-permute-start(bf16[576,512]{1,0:T(8,128)(2,1)S(1)} %add.25), channel_id=1, source_target_pairs={{1,24},{3,26},{5,28},{7,30},{9,16},{11,18},{13,20},{15,22},{17,8},... | collective-permute-start | bytes 1769480 | tf_op jit(solution)/shard_map/ppermute | solution.py:219
  39.0 20.2 %collective-permute-start.12 = (bf16[576,512]{1,0:T(8,128)(2,1)S(1)}, bf16[576,512]{1,0:T(8,128)(2,1)S(1)}, u32[]{:S(2)}, u32[]{:S(2)}) collective-permute-start(bf16[576,512]{1,0:T(8,128)(2,1)S(1)} %add.25), channel_id=1, source_target_pairs={{1,16},{3,18},{5,20},{7,22},{9,24},{11,26},{13,28},{15,30},{17,0},... | collective-permute-start | bytes 1769480 | tf_op jit(solution)/shard_map/ppermute | solution.py:219
  40.6 20.8 %collective-permute-start.11 = (bf16[576,512]{1,0:T(8,128)(2,1)S(1)}, bf16[576,512]{1,0:T(8,128)(2,1)S(1)}, u32[]{:S(2)}, u32[]{:S(2)}) collective-permute-start(bf16[576,512]{1,0:T(8,128)(2,1)S(1)} %add.25), channel_id=1, source_target_pairs={{1,9},{3,11},{5,13},{7,15},{9,1},{11,3},{13,5},{15,7},{17,25},{19,... | collective-permute-start | bytes 1769480 | tf_op jit(solution)/shard_map/ppermute | solution.py:219
  61.6 3.0 %copy-start = (f32[2,256,256]{2,1,0:T(8,128)S(1)}, f32[2,256,256]{2,1,0:T(8,128)}, u32[]{:S(2)}) copy-start(f32[2,256,256]{2,1,0:T(8,128)} %inverse.2) | copy-start | bytes 1572868
  61.7 2.9 %collective-permute-start.16 = (bf16[1152,512]{1,0:T(8,128)(2,1)S(1)}, bf16[1152,512]{1,0:T(8,128)(2,1)S(1)}, u32[]{:S(2)}, u32[]{:S(2)}) collective-permute-start(bf16[1152,512]{1,0:T(8,128)(2,1)S(1)} %pad_maximum_fusion.1.here), channel_id=1, source_target_pairs={{0,1},{1,0},{2,3},{3,2},{4,5},{5,4},{6,7},{7,6},{8,9},{9,8},{10,11... | collective-permute-start | bytes 3538952 | tf_op jit(solution)/shard_map/ppermute | solution.py:15
  69.9 39.2 %collective-permute-start.17 = (f16[2048,128]{1,0:T(8,128)(2,1)S(1)}, f16[2048,128]{1,0:T(8,128)(2,1)S(1)}, u32[]{:S(2)}, u32[]{:S(2)}) collective-permute-start(f16[2048,128]{1,0:T(8,128)(2,1)S(1)} %get-tuple-element.68), channel_id=1, source_target_pairs={{0,4},{1,5},{2,6},{3,7},{4,0},{5,1},{6,2},{7,3},{8,12},{9,13},{10,... | collective-permute-start | bytes 1572872 | tf_op jit(solution)/shard_map/ppermute | solution.py:15
  70.0 43.8 %collective-permute-start.18 = (f16[2048,128]{1,0:T(8,128)(2,1)S(1)}, f16[2048,128]{1,0:T(8,128)(2,1)S(1)}, u32[]{:S(2)}, u32[]{:S(2)}) collective-permute-start(f16[2048,128]{1,0:T(8,128)(2,1)S(1)} %get-tuple-element.69), channel_id=1, source_target_pairs={{0,6},{1,7},{2,4},{3,5},{4,2},{5,3},{6,0},{7,1},{8,14},{9,15},{10,... | collective-permute-start | bytes 1572872 | tf_op jit(solution)/shard_map/ppermute | solution.py:15
  74.8 22.4 %collective-permute-start.20 = (f16[1024,128]{1,0:T(8,128)(2,1)S(1)}, f16[1024,128]{1,0:T(8,128)(2,1)S(1)}, u32[]{:S(2)}, u32[]{:S(2)}) collective-permute-start(f16[1024,128]{1,0:T(8,128)(2,1)S(1)} %get-tuple-element.79), channel_id=1, source_target_pairs={{0,2},{1,3},{2,0},{3,1},{4,6},{5,7},{6,4},{7,5},{8,10},{9,11},{10,... | collective-permute-start | bytes 786440 | tf_op jit(solution)/shard_map/ppermute | solution.py:15
  78.3 28.8 %collective-permute-start.19 = (f16[1024,128]{1,0:T(8,128)(2,1)S(1)}, f16[1024,128]{1,0:T(8,128)(2,1)S(1)}, u32[]{:S(2)}, u32[]{:S(2)}) collective-permute-start(f16[1024,128]{1,0:T(8,128)(2,1)S(1)} %get-tuple-element.80), channel_id=1, source_target_pairs={{0,2},{1,3},{2,0},{3,1},{4,6},{5,7},{6,4},{7,5},{8,10},{9,11},{10,... | collective-permute-start | bytes 786440 | tf_op jit(solution)/shard_map/ppermute | solution.py:15
  (1 other events, 2.8 us)

commit v9 on v8

--- a/solution.py
+++ b/solution.py
@@ -191,6 +191,7 @@
     part = sum(parts, jnp.where(is_last, part_of(n_row - 1), jnp.zeros((), bf16)))
     cols = jnp.concatenate(split_array(panel_cols), axis=1)
     own, part, shared, cols = lax.optimization_barrier((own, part, shared, cols))
+    other_cols = swapped(cols, VEC, 1)
 
     order = [evens.index(2 * ((cut + i) % (2 * cut))) for i in range(2 * cut)]
     halves = call(
@@ -208,9 +209,7 @@
             part += lax.ppermute(part, VEC, [(v, v ^ downs[i]) for v in sources])
             sources += [v ^ downs[i] for v in sources]
         if i == 0:
-            halves, part, cols = lax.optimization_barrier((halves, part, cols))
-            other_cols = swapped(cols, VEC, 1)
-    part, other_cols = lax.optimization_barrier((part, other_cols))
+            halves, part, other_cols = lax.optimization_barrier((halves, part, other_cols))
 
     pieces = [part]
     for q in range(1, n_row):
@@ -221,7 +220,7 @@
     parts = sum(halves, [])
     rotated, peak = call(
         functools.partial(rotate_kernel, places), flags, [filtered, shared, *parts],
-        [((2 * rows, count), f32), ((8, count), f32)], [], 4 * rows * depth * count,
+        [((2 * rows, count), f32), ((8, count), f32)], [], 1 << 31,
     )
     pieces, rotated, peak = lax.optimization_barrier((pieces, rotated, peak))
     here = jnp.concatenate([pieces[q] + pieces[q + n_row // 2] for q in range(n_row // 2)], axis=0)
@@ -267,7 +266,9 @@
             cost_estimate=pl.CostEstimate(flops=1, bytes_accessed=1, transcendentals=0),
         )(flags, power, *(v.astype(f32) for v in parts), *out)
 
-    return place(far, [place(near, [])])
+    last_far = max(far)
+    near.update({k: v for k, v in far.items() if k != last_far})
+    return place({last_far: far[last_far]}, [place(near, [])])
 
 
 def solution(mesh):

time: 118 us -> 117 us (level)
  starting transfers between devices: 25.4 us -> 26.9 us
  waiting for transfers between devices: 65.8 us -> 64.4 us
    ppermute x13, waiting for transfers between devices: 48.2 us -> 45.9 us  [swapped(): lax.ppermute(value, axis, [(i, i ^ offset) for i in range(lax.axis_size(a...]
    ppermute x13, starting transfers between devices: 14.3 us -> 16 us  [swapped(): lax.ppermute(value, axis, [(i, i ^ offset) for i in range(lax.axis_size(a...]
    ppermute x2, waiting for transfers between devices: 10.1 us -> 11.4 us  [on_device(): part += lax.ppermute(part, VEC, [(v, v ^ downs[i]) for v in sources])]
  transfers between devices with their start and end apart: 21 -> 21, of which waited for: 12 -> 13; matrix products, arithmetic and copies ran while one was open for 4% -> 4% of each run, Pallas kernels for 10% -> 10%
where the time goes in v9:
time: 117 us; the launch traced here: 116 us
  waiting for transfers between devices  64.4 us (55%)
  starting transfers between devices  26.9 us (23%)
  Pallas kernels  18.4 us (16%)
  other arithmetic  3.62 us (3%)
  local copies, waits for them, and re-layouts  2.15 us (2%)
    ppermute x13, waiting for transfers between devices, swapped(): lax.ppermute(value, axis, [(i, i ^ offset) for i in range(lax.axis_size(a...  45.9 us
    ppermute x13, starting transfers between devices, swapped(): lax.ppermute(value, axis, [(i, i ^ offset) for i in range(lax.axis_size(a...  16 us
    pallas_call x4, Pallas kernels, call(): pl.pallas_call(kernel, in_specs=[spec(pltpu.SMEM)] * len(scalars) + specs...  14.5 us
    ppermute x2, waiting for transfers between devices, on_device(): part += lax.ppermute(part, VEC, [(v, v ^ downs[i]) for v in sources])  11.4 us
    ppermute x3, waiting for transfers between devices, on_device(): pieces.append(lax.ppermute(part, (ROW, VEC), pairs))  7.12 us
    ppermute x3, starting transfers between devices, on_device(): pieces.append(lax.ppermute(part, (ROW, VEC), pairs))  5.77 us
    pallas_call x2, Pallas kernels, place(): pl.pallas_call(functools.partial(place_kernel, [(k, len(v)) for k, v in b...  3.89 us
    ppermute x2, starting transfers between devices, on_device(): part += lax.ppermute(part, VEC, [(v, v ^ downs[i]) for v in sources])  2.87 us
  transfers between devices with their start and end apart: 21, of which 13 were waited for; matrix products, arithmetic and copies ran while one was open for 4% of the time, Pallas kernels for 10%

profile of v9, /device:TPU:9, one launch (start us, length us, event | category | flops | bytes accessed | tf_op | source)
XLA Modules:
  0.0 116.0 jit_solution(9865346501846004645)
XLA Ops:
  0.8 2.3 %collective-permute-start = (bf16[1,512,128]{2,1,0:T(8,128)(2,1)}, bf16[1,512,128]{2,1,0:T(8,128)(2,1)S(1)}, u32[]{:S(2)}, u32[]{:S(2)}) collective-permute-start(bf16[1,512,128]{2,1,0:T(8,128)(2,1)} %bitcast.5), channel_id=1, source_target_pairs={{0,4},{1,5},{2,6},{3,7},{4,0},{5,1},{6,2},{7,3},{8,12},{9,13},{10,... | collective-permute-start | bytes 393224 | tf_op jit(solution)/shard_map/ppermute | solution.py:15
  4.1 1.7 %fusion.12 = (bf16[512,512]{1,0:T(8,128)(2,1)S(1)}, bf16[512,512]{1,0:T(8,128)(2,1)S(1)}, bf16[512,512]{1,0:T(8,128)(2,1)S(1)}, bf16[512,512]{1,0:T(8,128)(2,1)S(1)}) fusion(bf16[1024,2048]{1,0:T(8,128)(2,1)} %own), kind=kLoop, calls=%fused_computation.35 | loop fusion | bytes 4194304 | tf_op jit(solution)/shard_map/slice | solution.py:183
  10.8 6.1 %collective-permute-done.1 = bf16[2,512,128]{2,1,0:T(8,128)(2,1)S(1)} collective-permute-done((bf16[2,512,128]{2,1,0:T(8,128)(2,1)S(1)}, bf16[2,512,128]{2,1,0:T(8,128)(2,1)S(1)}, u32[]{:S(2)}, u32[]{:S(2)}) %collective-permute-start.1) | collective-permute-done | bytes 262176 | tf_op jit(solution)/shard_map/ppermute | solution.py:15
  17.3 1.3 %collective-permute-start.9 = (bf16[1024,1024]{1,0:T(8,128)(2,1)S(1)}, bf16[1024,1024]{1,0:T(8,128)(2,1)S(1)}, u32[]{:S(2)}, u32[]{:S(2)}) collective-permute-start(bf16[1024,1024]{1,0:T(8,128)(2,1)S(1)} %pad_maximum_fusion.refs_4_), channel_id=1, source_target_pairs={{0,1},{1,0},{2,3},{3,2},{4,5},{5,4},{6,7},{7,6},{8,9},{9,8},{10,11... | collective-permute-start | bytes 6291464 | tf_op jit(solution)/shard_map/ppermute | solution.py:15
  22.6 7.6 %collective-permute-done.8 = bf16[576,512]{1,0:T(8,128)(2,1)S(1)} collective-permute-done((bf16[576,512]{1,0:T(8,128)(2,1)S(1)}, bf16[576,512]{1,0:T(8,128)(2,1)S(1)}, u32[]{:S(2)}, u32[]{:S(2)}) %collective-permute-start.8) | collective-permute-done | bytes 589856 | tf_op jit(solution)/shard_map/ppermute | solution.py:209
  30.4 1.6 %collective-permute-start.10 = (bf16[576,512]{1,0:T(8,128)(2,1)S(1)}, bf16[576,512]{1,0:T(8,128)(2,1)S(1)}, u32[]{:S(2)}, u32[]{:S(2)}) collective-permute-start(bf16[576,512]{1,0:T(8,128)(2,1)S(1)} %add.24), channel_id=1, source_target_pairs={{7,5},{3,1},{15,13},{11,9},{23,21},{19,17},{31,29},{27,25}} | collective-permute-start | bytes 1769480 | tf_op jit(solution)/shard_map/ppermute | solution.py:209
  32.1 2.8 %collective-permute-start.15 = (bf16[1024,256]{1,0:T(8,128)(2,1)S(1)}, bf16[1024,256]{1,0:T(8,128)(2,1)S(1)}, u32[]{:S(2)}, u32[]{:S(2)}) collective-permute-start(bf16[1024,256]{1,0:T(8,128)(2,1)S(1)} %constant_dynamic-update-slice_fusion.2.refs_2_.refs_0_), channel_id=1, source_target_pairs={{0,16},{8,24},{16,0},{24,8},{1,17},{9,25},{17,1},{25,9},{2,18},{10... | collective-permute-start | bytes 1572872 | tf_op jit(solution)/shard_map/ppermute | solution.py:15
  35.0 3.8 %collective-permute-done.10 = bf16[576,512]{1,0:T(8,128)(2,1)S(1)} collective-permute-done((bf16[576,512]{1,0:T(8,128)(2,1)S(1)}, bf16[576,512]{1,0:T(8,128)(2,1)S(1)}, u32[]{:S(2)}, u32[]{:S(2)}) %collective-permute-start.10) | collective-permute-done | bytes 589856 | tf_op jit(solution)/shard_map/ppermute | solution.py:209
  38.9 1.3 %collective-permute-start.13 = (bf16[576,512]{1,0:T(8,128)(2,1)S(1)}, bf16[576,512]{1,0:T(8,128)(2,1)S(1)}, u32[]{:S(2)}, u32[]{:S(2)}) collective-permute-start(bf16[576,512]{1,0:T(8,128)(2,1)S(1)} %add.25), channel_id=1, source_target_pairs={{1,24},{3,26},{5,28},{7,30},{9,16},{11,18},{13,20},{15,22},{17,8},... | collective-permute-start | bytes 1769480 | tf_op jit(solution)/shard_map/ppermute | solution.py:218
  40.3 1.3 %collective-permute-start.12 = (bf16[576,512]{1,0:T(8,128)(2,1)S(1)}, bf16[576,512]{1,0:T(8,128)(2,1)S(1)}, u32[]{:S(2)}, u32[]{:S(2)}) collective-permute-start(bf16[576,512]{1,0:T(8,128)(2,1)S(1)} %add.25), channel_id=1, source_target_pairs={{1,16},{3,18},{5,20},{7,22},{9,24},{11,26},{13,28},{15,30},{17,0},... | collective-permute-start | bytes 1769480 | tf_op jit(solution)/shard_map/ppermute | solution.py:218
  41.6 3.1 %collective-permute-start.11 = (bf16[576,512]{1,0:T(8,128)(2,1)S(1)}, bf16[576,512]{1,0:T(8,128)(2,1)S(1)}, u32[]{:S(2)}, u32[]{:S(2)}) collective-permute-start(bf16[576,512]{1,0:T(8,128)(2,1)S(1)} %add.25), channel_id=1, source_target_pairs={{1,9},{3,11},{5,13},{7,15},{9,1},{11,3},{13,5},{15,7},{17,25},{19,... | collective-permute-start | bytes 1769480 | tf_op jit(solution)/shard_map/ppermute | solution.py:218
  45.9 5.3 %shard_map.47 = (f32[2048,512]{1,0:T(8,128)S(1)}, f32[8,512]{1,0:T(8,128)S(1)}) custom-call(s32[4]{0:T(128)S(1)} %pad_add_fusion.flags, bf16[1024,2048]{1,0:T(8,128)(2,1)S(1)} %copy-done, bf16[1024,2048]{1,0:T(8,128)(2,1)S(1)} %collective-permute-done.5.other, bf16[1024,256]{1,0:T(8,128)(2,1)S(1)} %constant_dynamic-update-slice_fusion.refs_0_, ...), custom_call_target="tpu_custom_call" | custom-call | flops 2147483648 | bytes 1 | tf_op jit(solution)/shard_map/pallas_call | solution.py:151
  51.3 4.7 %collective-permute-done.12 = bf16[576,512]{1,0:T(8,128)(2,1)S(1)} collective-permute-done((bf16[576,512]{1,0:T(8,128)(2,1)S(1)}, bf16[576,512]{1,0:T(8,128)(2,1)S(1)}, u32[]{:S(2)}, u32[]{:S(2)}) %collective-permute-start.12) | collective-permute-done | bytes 589856 | tf_op jit(solution)/shard_map/ppermute | solution.py:218
  56.0 2.3 %collective-permute-done.11 = bf16[576,512]{1,0:T(8,128)(2,1)S(1)} collective-permute-done((bf16[576,512]{1,0:T(8,128)(2,1)S(1)}, bf16[576,512]{1,0:T(8,128)(2,1)S(1)}, u32[]{:S(2)}, u32[]{:S(2)}) %collective-permute-start.11) | collective-permute-done | bytes 589856 | tf_op jit(solution)/shard_map/ppermute | solution.py:218
  59.1 2.6 %collective-permute-done.16.there = bf16[1152,512]{1,0:T(8,128)(2,1)S(1)} collective-permute-done((bf16[1152,512]{1,0:T(8,128)(2,1)S(1)}, bf16[1152,512]{1,0:T(8,128)(2,1)S(1)}, u32[]{:S(2)}, u32[]{:S(2)}) %collective-permute-start.16) | collective-permute-done | bytes 1179680 | tf_op jit(solution)/shard_map/ppermute | solution.py:15
  61.7 4.8 %shard_map.48 = (f32[2048,256]{1,0:T(8,128)S(1)}, f32[8,256]{1,0:T(8,128)}) custom-call(s32[4]{0:T(128)S(1)} %pad_add_fusion.flags, f32[2,256,256]{2,1,0:T(8,128)S(1)} %copy-done.1, bf16[1152,512]{1,0:T(8,128)(2,1)S(1)} %pad_maximum_fusion.1.here, bf16[1152,512]{1,0:T(8,128)(2,1)S(1)} %collective-permute-done.16.there, ...), custom_call_target="tpu_custom_call" | custom-call | flops 1 | bytes 1 | tf_op jit(solution)/shard_map/pallas_call | solution.py:151
  66.9 3.7 %collective-permute-start.20 = (f16[2048,128]{1,0:T(8,128)(2,1)S(1)}, f16[2048,128]{1,0:T(8,128)(2,1)S(1)}, u32[]{:S(2)}, u32[]{:S(2)}) collective-permute-start(f16[2048,128]{1,0:T(8,128)(2,1)S(1)} %get-tuple-element.66), channel_id=1, source_target_pairs={{0,4},{1,5},{2,6},{3,7},{4,0},{5,1},{6,2},{7,3},{8,12},{9,13},{10,... | collective-permute-start | bytes 1572872 | tf_op jit(solution)/shard_map/ppermute | solution.py:15
  70.6 4.4 %shard_map.49 = (f32[2048,256]{1,0:T(8,128)S(1)}, f32[8,256]{1,0:T(8,128)S(1)}) custom-call(s32[4]{0:T(128)S(1)} %pad_add_fusion.flags, f32[2,256,256]{2,1,0:T(8,128)S(1)} %copy-done.1, bf16[1152,512]{1,0:T(8,128)(2,1)S(1)} %pad_maximum_fusion.1.here, bf16[1152,512]{1,0:T(8,128)(2,1)S(1)} %collective-permute-done.16.there, ...), custom_call_target="tpu_custom_call" | custom-call | flops 1 | bytes 1 | tf_op jit(solution)/shard_map/pallas_call | solution.py:151
  75.3 1.3 %collective-permute-start.19 = (f16[1024,128]{1,0:T(8,128)(2,1)S(1)}, f16[1024,128]{1,0:T(8,128)(2,1)S(1)}, u32[]{:S(2)}, u32[]{:S(2)}) collective-permute-start(f16[1024,128]{1,0:T(8,128)(2,1)S(1)} %get-tuple-element.75), channel_id=1, source_target_pairs={{0,2},{1,3},{2,0},{3,1},{4,6},{5,7},{6,4},{7,5},{8,10},{9,11},{10,... | collective-permute-start | bytes 786440 | tf_op jit(solution)/shard_map/ppermute | solution.py:15
  76.9 20.7 %collective-permute-done.19 = f16[1024,128]{1,0:T(8,128)(2,1)S(1)} collective-permute-done((f16[1024,128]{1,0:T(8,128)(2,1)S(1)}, f16[1024,128]{1,0:T(8,128)(2,1)S(1)}, u32[]{:S(2)}, u32[]{:S(2)}) %collective-permute-start.19) | collective-permute-done | bytes 262176 | tf_op jit(solution)/shard_map/ppermute | solution.py:15
  97.6 9.9 %collective-permute-done.18 = f16[1024,128]{1,0:T(8,128)(2,1)S(1)} collective-permute-done((f16[1024,128]{1,0:T(8,128)(2,1)S(1)}, f16[1024,128]{1,0:T(8,128)(2,1)S(1)}, u32[]{:S(2)}, u32[]{:S(2)}) %collective-permute-start.18) | collective-permute-done | bytes 262176 | tf_op jit(solution)/shard_map/ppermute | solution.py:15
  107.6 2.3 %shard_map.50.refs_1_ = f32[8192,128]{1,0:T(8,128)} custom-call(s32[4]{0:T(128)S(1)} %pad_add_fusion.flags, f32[8,256]{1,0:T(8,128)S(1)} %get-tuple-element.63.power, f32[1024,128]{1,0:T(8,128)S(1)} %convert_element_type.33.refs_0_, f32[1024,128]{1,0:T(8,128)S(1)} %convert_element_type.34.refs_1_, f32[2048,128]{1,0:T(8,128)S(1)} %slice.61.refs_2_, ...), custom_call_target="tpu_custom_call" | custom-call | flops 1 | bytes 1 | tf_op jit(solution)/shard_map/pallas_call | solution.py:257
  109.9 4.2 %collective-permute-done.17 = f16[2048,128]{1,0:T(8,128)(2,1)S(1)} collective-permute-done((f16[2048,128]{1,0:T(8,128)(2,1)S(1)}, f16[2048,128]{1,0:T(8,128)(2,1)S(1)}, u32[]{:S(2)}, u32[]{:S(2)}) %collective-permute-start.17) | collective-permute-done | bytes 524320 | tf_op jit(solution)/shard_map/ppermute | solution.py:15
  114.2 1.6 %shard_map.51 = f32[8192,128]{1,0:T(8,128)} custom-call(s32[4]{0:T(128)S(1)} %pad_add_fusion.flags, f32[8,256]{1,0:T(8,128)S(1)} %get-tuple-element.63.power, f32[2048,128]{1,0:T(8,128)S(1)} %convert_element_type.32.refs_0_, f32[8192,128]{1,0:T(8,128)} %shard_map.50.refs_1_), custom_call_target="tpu_custom_call", output_to_operand_aliasing={{}: (3, {})} | custom-call | flops 1 | bytes 1 | tf_op jit(solution)/shard_map/pallas_call | solution.py:257
  (62 shorter events, 14.7 us)
Async XLA Ops:
  0.1 17.2 %collective-permute-start.5 = (bf16[1024,2048]{1,0:T(8,128)(2,1)}, bf16[1024,2048]{1,0:T(8,128)(2,1)S(1)}, u32[]{:S(2)}, u32[]{:S(2)}) collective-permute-start(bf16[1024,2048]{1,0:T(8,128)(2,1)} %own), channel_id=1, source_target_pairs={{0,1},{1,0},{2,3},{3,2},{4,5},{5,4},{6,7},{7,6},{8,9},{9,8},{10,11... | collective-permute-start | bytes 12582920 | tf_op jit(solution)/shard_map/ppermute | solution.py:15
  0.8 8.6 %collective-permute-start = (bf16[1,512,128]{2,1,0:T(8,128)(2,1)}, bf16[1,512,128]{2,1,0:T(8,128)(2,1)S(1)}, u32[]{:S(2)}, u32[]{:S(2)}) collective-permute-start(bf16[1,512,128]{2,1,0:T(8,128)(2,1)} %bitcast.5), channel_id=1, source_target_pairs={{0,4},{1,5},{2,6},{3,7},{4,0},{5,1},{6,2},{7,3},{8,12},{9,13},{10,... | collective-permute-start | bytes 393224 | tf_op jit(solution)/shard_map/ppermute | solution.py:15
  5.8 11.1 %collective-permute-start.2 = (bf16[576,512]{1,0:T(8,128)(2,1)S(1)}, bf16[576,512]{1,0:T(8,128)(2,1)S(1)}, u32[]{:S(2)}, u32[]{:S(2)}) collective-permute-start(bf16[576,512]{1,0:T(8,128)(2,1)S(1)} %pad_maximum_fusion.2), channel_id=1, source_target_pairs={{31,7}} | collective-permute-start | bytes 1769480 | tf_op jit(solution)/shard_map/ppermute | solution.py:190
  6.5 3.6 %copy-start.2 = (f32[1024,512]{1,0:T(8,128)S(1)}, f32[1024,512]{1,0:T(8,128)}, u32[]{:S(2)}) copy-start(f32[1024,512]{1,0:T(8,128)} %param.6) | copy-start | bytes 6291460
  6.6 10.4 %collective-permute-start.3 = (bf16[576,512]{1,0:T(8,128)(2,1)S(1)}, bf16[576,512]{1,0:T(8,128)(2,1)S(1)}, u32[]{:S(2)}, u32[]{:S(2)}) collective-permute-start(bf16[576,512]{1,0:T(8,128)(2,1)S(1)} %pad_maximum_fusion.3), channel_id=1, source_target_pairs={{31,15}} | collective-permute-start | bytes 1769480 | tf_op jit(solution)/shard_map/ppermute | solution.py:190
  7.5 9.5 %collective-permute-start.4 = (bf16[576,512]{1,0:T(8,128)(2,1)S(1)}, bf16[576,512]{1,0:T(8,128)(2,1)S(1)}, u32[]{:S(2)}, u32[]{:S(2)}) collective-permute-start(bf16[576,512]{1,0:T(8,128)(2,1)S(1)} %fusion.4), channel_id=1, source_target_pairs={{31,23}} | collective-permute-start | bytes 1769480 | tf_op jit(solution)/shard_map/ppermute | solution.py:190
  9.4 7.5 %collective-permute-start.1 = (bf16[2,512,128]{2,1,0:T(8,128)(2,1)S(1)}, bf16[2,512,128]{2,1,0:T(8,128)(2,1)S(1)}, u32[]{:S(2)}, u32[]{:S(2)}) collective-permute-start(bf16[2,512,128]{2,1,0:T(8,128)(2,1)S(1)} %pad_maximum_fusion.5), channel_id=1, source_target_pairs={{0,2},{1,3},{2,0},{3,1},{4,6},{5,7},{6,4},{7,5},{8,10},{9,11},{10,... | collective-permute-start | bytes 786440 | tf_op jit(solution)/shard_map/ppermute | solution.py:15
  17.3 13.1 %collective-permute-start.9 = (bf16[1024,1024]{1,0:T(8,128)(2,1)S(1)}, bf16[1024,1024]{1,0:T(8,128)(2,1)S(1)}, u32[]{:S(2)}, u32[]{:S(2)}) collective-permute-start(bf16[1024,1024]{1,0:T(8,128)(2,1)S(1)} %pad_maximum_fusion.refs_4_), channel_id=1, source_target_pairs={{0,1},{1,0},{2,3},{3,2},{4,5},{5,4},{6,7},{7,6},{8,9},{9,8},{10,11... | collective-permute-start | bytes 6291464 | tf_op jit(solution)/shard_map/ppermute | solution.py:15
  18.7 11.5 %collective-permute-start.8 = (bf16[576,512]{1,0:T(8,128)(2,1)S(1)}, bf16[576,512]{1,0:T(8,128)(2,1)S(1)}, u32[]{:S(2)}, u32[]{:S(2)}) collective-permute-start(bf16[576,512]{1,0:T(8,128)(2,1)S(1)} %fusion.7), channel_id=1, source_target_pairs={{7,3},{15,11},{23,19},{31,27}} | collective-permute-start | bytes 1769480 | tf_op jit(solution)/shard_map/ppermute | solution.py:209
  20.1 10.3 %collective-permute-start.6 = (bf16[512,256]{1,0:T(8,128)(2,1)S(1)}, bf16[512,256]{1,0:T(8,128)(2,1)S(1)}, u32[]{:S(2)}, u32[]{:S(2)}) collective-permute-start(bf16[512,256]{1,0:T(8,128)(2,1)S(1)} %get-tuple-element.48), channel_id=1, source_target_pairs={{0,16},{8,24},{16,0},{24,8},{1,17},{9,25},{17,1},{25,9},{2,18},{10... | collective-permute-start | bytes 786440 | tf_op jit(solution)/shard_map/ppermute | solution.py:15
  21.4 9.0 %collective-permute-start.7 = (bf16[512,256]{1,0:T(8,128)(2,1)S(1)}, bf16[512,256]{1,0:T(8,128)(2,1)S(1)}, u32[]{:S(2)}, u32[]{:S(2)}) collective-permute-start(bf16[512,256]{1,0:T(8,128)(2,1)S(1)} %get-tuple-element.50), channel_id=1, source_target_pairs={{0,8},{8,0},{16,24},{24,16},{1,9},{9,1},{17,25},{25,17},{2,10},{10... | collective-permute-start | bytes 786440 | tf_op jit(solution)/shard_map/ppermute | solution.py:15
  30.2 15.7 %copy-start = (bf16[1024,2048]{1,0:T(8,128)(2,1)S(1)}, bf16[1024,2048]{1,0:T(8,128)(2,1)}, u32[]{:S(2)}) copy-start(bf16[1024,2048]{1,0:T(8,128)(2,1)} %own) | copy-start | bytes 12582916
  30.4 8.4 %collective-permute-start.10 = (bf16[576,512]{1,0:T(8,128)(2,1)S(1)}, bf16[576,512]{1,0:T(8,128)(2,1)S(1)}, u32[]{:S(2)}, u32[]{:S(2)}) collective-permute-start(bf16[576,512]{1,0:T(8,128)(2,1)S(1)} %add.24), channel_id=1, source_target_pairs={{7,5},{3,1},{15,13},{11,9},{23,21},{19,17},{31,29},{27,25}} | collective-permute-start | bytes 1769480 | tf_op jit(solution)/shard_map/ppermute | solution.py:209
  32.1 13.0 %collective-permute-start.15 = (bf16[1024,256]{1,0:T(8,128)(2,1)S(1)}, bf16[1024,256]{1,0:T(8,128)(2,1)S(1)}, u32[]{:S(2)}, u32[]{:S(2)}) collective-permute-start(bf16[1024,256]{1,0:T(8,128)(2,1)S(1)} %constant_dynamic-update-slice_fusion.2.refs_2_.refs_0_), channel_id=1, source_target_pairs={{0,16},{8,24},{16,0},{24,8},{1,17},{9,25},{17,1},{25,9},{2,18},{10... | collective-permute-start | bytes 1572872 | tf_op jit(solution)/shard_map/ppermute | solution.py:15
  34.9 11.0 %collective-permute-start.14 = (bf16[1024,256]{1,0:T(8,128)(2,1)S(1)}, bf16[1024,256]{1,0:T(8,128)(2,1)S(1)}, u32[]{:S(2)}, u32[]{:S(2)}) collective-permute-start(bf16[1024,256]{1,0:T(8,128)(2,1)S(1)} %constant_dynamic-update-slice_fusion.refs_0_), channel_id=1, source_target_pairs={{0,8},{8,0},{16,24},{24,16},{1,9},{9,1},{17,25},{25,17},{2,10},{10... | collective-permute-start | bytes 1572872 | tf_op jit(solution)/shard_map/ppermute | solution.py:15
  38.9 12.4 %collective-permute-start.13 = (bf16[576,512]{1,0:T(8,128)(2,1)S(1)}, bf16[576,512]{1,0:T(8,128)(2,1)S(1)}, u32[]{:S(2)}, u32[]{:S(2)}) collective-permute-start(bf16[576,512]{1,0:T(8,128)(2,1)S(1)} %add.25), channel_id=1, source_target_pairs={{1,24},{3,26},{5,28},{7,30},{9,16},{11,18},{13,20},{15,22},{17,8},... | collective-permute-start | bytes 1769480 | tf_op jit(solution)/shard_map/ppermute | solution.py:218
  40.3 15.7 %collective-permute-start.12 = (bf16[576,512]{1,0:T(8,128)(2,1)S(1)}, bf16[576,512]{1,0:T(8,128)(2,1)S(1)}, u32[]{:S(2)}, u32[]{:S(2)}) collective-permute-start(bf16[576,512]{1,0:T(8,128)(2,1)S(1)} %add.25), channel_id=1, source_target_pairs={{1,16},{3,18},{5,20},{7,22},{9,24},{11,26},{13,28},{15,30},{17,0},... | collective-permute-start | bytes 1769480 | tf_op jit(solution)/shard_map/ppermute | solution.py:218
  41.6 16.7 %collective-permute-start.11 = (bf16[576,512]{1,0:T(8,128)(2,1)S(1)}, bf16[576,512]{1,0:T(8,128)(2,1)S(1)}, u32[]{:S(2)}, u32[]{:S(2)}) collective-permute-start(bf16[576,512]{1,0:T(8,128)(2,1)S(1)} %add.25), channel_id=1, source_target_pairs={{1,9},{3,11},{5,13},{7,15},{9,1},{11,3},{13,5},{15,7},{17,25},{19,... | collective-permute-start | bytes 1769480 | tf_op jit(solution)/shard_map/ppermute | solution.py:218
  58.7 3.0 %copy-start.1 = (f32[2,256,256]{2,1,0:T(8,128)S(1)}, f32[2,256,256]{2,1,0:T(8,128)}, u32[]{:S(2)}) copy-start(f32[2,256,256]{2,1,0:T(8,128)} %inverse.2) | copy-start | bytes 1572868
  58.8 2.9 %collective-permute-start.16 = (bf16[1152,512]{1,0:T(8,128)(2,1)S(1)}, bf16[1152,512]{1,0:T(8,128)(2,1)S(1)}, u32[]{:S(2)}, u32[]{:S(2)}) collective-permute-start(bf16[1152,512]{1,0:T(8,128)(2,1)S(1)} %pad_maximum_fusion.1.here), channel_id=1, source_target_pairs={{0,1},{1,0},{2,3},{3,2},{4,5},{5,4},{6,7},{7,6},{8,9},{9,8},{10,11... | collective-permute-start | bytes 3538952 | tf_op jit(solution)/shard_map/ppermute | solution.py:15
  66.9 40.7 %collective-permute-start.20 = (f16[2048,128]{1,0:T(8,128)(2,1)S(1)}, f16[2048,128]{1,0:T(8,128)(2,1)S(1)}, u32[]{:S(2)}, u32[]{:S(2)}) collective-permute-start(f16[2048,128]{1,0:T(8,128)(2,1)S(1)} %get-tuple-element.66), channel_id=1, source_target_pairs={{0,4},{1,5},{2,6},{3,7},{4,0},{5,1},{6,2},{7,3},{8,12},{9,13},{10,... | collective-permute-start | bytes 1572872 | tf_op jit(solution)/shard_map/ppermute | solution.py:15
  70.6 43.6 %collective-permute-start.17 = (f16[2048,128]{1,0:T(8,128)(2,1)S(1)}, f16[2048,128]{1,0:T(8,128)(2,1)S(1)}, u32[]{:S(2)}, u32[]{:S(2)}) collective-permute-start(f16[2048,128]{1,0:T(8,128)(2,1)S(1)} %get-tuple-element.64), channel_id=1, source_target_pairs={{0,6},{1,7},{2,4},{3,5},{4,2},{5,3},{6,0},{7,1},{8,14},{9,15},{10,... | collective-permute-start | bytes 1572872 | tf_op jit(solution)/shard_map/ppermute | solution.py:15
  75.3 22.3 %collective-permute-start.19 = (f16[1024,128]{1,0:T(8,128)(2,1)S(1)}, f16[1024,128]{1,0:T(8,128)(2,1)S(1)}, u32[]{:S(2)}, u32[]{:S(2)}) collective-permute-start(f16[1024,128]{1,0:T(8,128)(2,1)S(1)} %get-tuple-element.75), channel_id=1, source_target_pairs={{0,2},{1,3},{2,0},{3,1},{4,6},{5,7},{6,4},{7,5},{8,10},{9,11},{10,... | collective-permute-start | bytes 786440 | tf_op jit(solution)/shard_map/ppermute | solution.py:15
  76.6 30.9 %collective-permute-start.18 = (f16[1024,128]{1,0:T(8,128)(2,1)S(1)}, f16[1024,128]{1,0:T(8,128)(2,1)S(1)}, u32[]{:S(2)}, u32[]{:S(2)}) collective-permute-start(f16[1024,128]{1,0:T(8,128)(2,1)S(1)} %get-tuple-element.76), channel_id=1, source_target_pairs={{0,2},{1,3},{2,0},{3,1},{4,6},{5,7},{6,4},{7,5},{8,10},{9,11},{10,... | collective-permute-start | bytes 786440 | tf_op jit(solution)/shard_map/ppermute | solution.py:15
  (1 other events, 2.8 us)

commit v10 on v9

--- a/solution.py
+++ b/solution.py
@@ -132,11 +132,13 @@
     for i, (k, count) in enumerate(ks):
         for j in range(count):
             part = parts.pop(0)
-            step = part.shape[0]
-            ready[i, j * step : (j + 1) * step, :] = part[...] * power[0:1, :width]
-        into = out.at[pl.ds(pl.multiple_of(((flags[3] ^ k) >> 1) * size, size), size), :]
-        copies.append(pltpu.make_async_copy(ready.at[i], into, sems.at[i]))
-        copies[i].start()
+            step = size // 4
+            for start in range(0, part.shape[0], step):
+                at = j * part.shape[0] + start
+                ready[i, at : at + step, :] = part[start : start + step, :] * power[0:1, :width]
+                into = out.at[pl.ds(pl.multiple_of(((flags[3] ^ k) >> 1) * size + at, step), step), :]
+                copies.append(pltpu.make_async_copy(ready.at[i, pl.ds(at, step), :], into, sems.at[len(copies)]))
+                copies[-1].start()
     for copy in copies:
         copy.wait()
 
@@ -259,7 +261,7 @@
             in_specs=[spec(pltpu.SMEM)] + [spec(pltpu.VMEM)] * (1 + len(parts)) + [spec(pl.ANY)] * len(out),
             out_specs=spec(pl.ANY), out_shape=shape,
             scratch_shapes=[
-                pltpu.VMEM((len(blocks), 2 * rows, own_cols), f32), pltpu.SemaphoreType.DMA((len(blocks),))
+                pltpu.VMEM((len(blocks), 2 * rows, own_cols), f32), pltpu.SemaphoreType.DMA((4 * len(blocks),))
             ],
             input_output_aliases={2 + len(parts): 0} if out else {},
             compiler_params=pltpu.CompilerParams(vmem_limit_bytes=VMEM_LIMIT),

time: 117 us -> 117 us (level)
  no operation moved by 1% of the time
where the time goes in v10:
time: 117 us; the launch traced here: 116 us
  waiting for transfers between devices  64.4 us (55%)
  starting transfers between devices  26.9 us (23%)
  Pallas kernels  18.4 us (16%)
  other arithmetic  3.62 us (3%)
  local copies, waits for them, and re-layouts  2.15 us (2%)
    ppermute x13, waiting for transfers between devices, swapped(): lax.ppermute(value, axis, [(i, i ^ offset) for i in range(lax.axis_size(a...  45.9 us
    ppermute x13, starting transfers between devices, swapped(): lax.ppermute(value, axis, [(i, i ^ offset) for i in range(lax.axis_size(a...  16 us
    pallas_call x4, Pallas kernels, call(): pl.pallas_call(kernel, in_specs=[spec(pltpu.SMEM)] * len(scalars) + specs...  14.5 us
    ppermute x2, waiting for transfers between devices, on_device(): part += lax.ppermute(part, VEC, [(v, v ^ downs[i]) for v in sources])  11.4 us
    ppermute x3, waiting for transfers between devices, on_device(): pieces.append(lax.ppermute(part, (ROW, VEC), pairs))  7.12 us
    ppermute x3, starting transfers between devices, on_device(): pieces.append(lax.ppermute(part, (ROW, VEC), pairs))  5.77 us
    pallas_call x2, Pallas kernels, place(): pl.pallas_call(functools.partial(place_kernel, [(k, len(v)) for k, v in b...  3.87 us
    ppermute x2, starting transfers between devices, on_device(): part += lax.ppermute(part, VEC, [(v, v ^ downs[i]) for v in sources])  2.87 us
  transfers between devices with their start and end apart: 21, of which 13 were waited for; matrix products, arithmetic and copies ran while one was open for 4% of the time, Pallas kernels for 10%

profile of v10, /device:TPU:9, one launch (start us, length us, event | category | flops | bytes accessed | tf_op | source)
XLA Modules:
  0.0 115.9 jit_solution(3343360642489088653)
XLA Ops:
  0.8 2.3 %collective-permute-start = (bf16[1,512,128]{2,1,0:T(8,128)(2,1)}, bf16[1,512,128]{2,1,0:T(8,128)(2,1)S(1)}, u32[]{:S(2)}, u32[]{:S(2)}) collective-permute-start(bf16[1,512,128]{2,1,0:T(8,128)(2,1)} %bitcast.5), channel_id=1, source_target_pairs={{0,4},{1,5},{2,6},{3,7},{4,0},{5,1},{6,2},{7,3},{8,12},{9,13},{10,... | collective-permute-start | bytes 393224 | tf_op jit(solution)/shard_map/ppermute | solution.py:15
  4.1 1.7 %fusion.12 = (bf16[512,512]{1,0:T(8,128)(2,1)S(1)}, bf16[512,512]{1,0:T(8,128)(2,1)S(1)}, bf16[512,512]{1,0:T(8,128)(2,1)S(1)}, bf16[512,512]{1,0:T(8,128)(2,1)S(1)}) fusion(bf16[1024,2048]{1,0:T(8,128)(2,1)} %own), kind=kLoop, calls=%fused_computation.35 | loop fusion | bytes 4194304 | tf_op jit(solution)/shard_map/slice | solution.py:185
  10.8 6.1 %collective-permute-done.1 = bf16[2,512,128]{2,1,0:T(8,128)(2,1)S(1)} collective-permute-done((bf16[2,512,128]{2,1,0:T(8,128)(2,1)S(1)}, bf16[2,512,128]{2,1,0:T(8,128)(2,1)S(1)}, u32[]{:S(2)}, u32[]{:S(2)}) %collective-permute-start.1) | collective-permute-done | bytes 262176 | tf_op jit(solution)/shard_map/ppermute | solution.py:15
  17.3 1.3 %collective-permute-start.9 = (bf16[1024,1024]{1,0:T(8,128)(2,1)S(1)}, bf16[1024,1024]{1,0:T(8,128)(2,1)S(1)}, u32[]{:S(2)}, u32[]{:S(2)}) collective-permute-start(bf16[1024,1024]{1,0:T(8,128)(2,1)S(1)} %pad_maximum_fusion.refs_4_), channel_id=1, source_target_pairs={{0,1},{1,0},{2,3},{3,2},{4,5},{5,4},{6,7},{7,6},{8,9},{9,8},{10,11... | collective-permute-start | bytes 6291464 | tf_op jit(solution)/shard_map/ppermute | solution.py:15
  22.6 7.6 %collective-permute-done.8 = bf16[576,512]{1,0:T(8,128)(2,1)S(1)} collective-permute-done((bf16[576,512]{1,0:T(8,128)(2,1)S(1)}, bf16[576,512]{1,0:T(8,128)(2,1)S(1)}, u32[]{:S(2)}, u32[]{:S(2)}) %collective-permute-start.8) | collective-permute-done | bytes 589856 | tf_op jit(solution)/shard_map/ppermute | solution.py:211
  30.4 1.6 %collective-permute-start.10 = (bf16[576,512]{1,0:T(8,128)(2,1)S(1)}, bf16[576,512]{1,0:T(8,128)(2,1)S(1)}, u32[]{:S(2)}, u32[]{:S(2)}) collective-permute-start(bf16[576,512]{1,0:T(8,128)(2,1)S(1)} %add.24), channel_id=1, source_target_pairs={{7,5},{3,1},{15,13},{11,9},{23,21},{19,17},{31,29},{27,25}} | collective-permute-start | bytes 1769480 | tf_op jit(solution)/shard_map/ppermute | solution.py:211
  32.1 2.8 %collective-permute-start.15 = (bf16[1024,256]{1,0:T(8,128)(2,1)S(1)}, bf16[1024,256]{1,0:T(8,128)(2,1)S(1)}, u32[]{:S(2)}, u32[]{:S(2)}) collective-permute-start(bf16[1024,256]{1,0:T(8,128)(2,1)S(1)} %constant_dynamic-update-slice_fusion.2.refs_2_.refs_0_), channel_id=1, source_target_pairs={{0,16},{8,24},{16,0},{24,8},{1,17},{9,25},{17,1},{25,9},{2,18},{10... | collective-permute-start | bytes 1572872 | tf_op jit(solution)/shard_map/ppermute | solution.py:15
  35.0 3.8 %collective-permute-done.10 = bf16[576,512]{1,0:T(8,128)(2,1)S(1)} collective-permute-done((bf16[576,512]{1,0:T(8,128)(2,1)S(1)}, bf16[576,512]{1,0:T(8,128)(2,1)S(1)}, u32[]{:S(2)}, u32[]{:S(2)}) %collective-permute-start.10) | collective-permute-done | bytes 589856 | tf_op jit(solution)/shard_map/ppermute | solution.py:211
  38.9 1.3 %collective-permute-start.13 = (bf16[576,512]{1,0:T(8,128)(2,1)S(1)}, bf16[576,512]{1,0:T(8,128)(2,1)S(1)}, u32[]{:S(2)}, u32[]{:S(2)}) collective-permute-start(bf16[576,512]{1,0:T(8,128)(2,1)S(1)} %add.25), channel_id=1, source_target_pairs={{1,24},{3,26},{5,28},{7,30},{9,16},{11,18},{13,20},{15,22},{17,8},... | collective-permute-start | bytes 1769480 | tf_op jit(solution)/shard_map/ppermute | solution.py:220
  40.3 1.3 %collective-permute-start.12 = (bf16[576,512]{1,0:T(8,128)(2,1)S(1)}, bf16[576,512]{1,0:T(8,128)(2,1)S(1)}, u32[]{:S(2)}, u32[]{:S(2)}) collective-permute-start(bf16[576,512]{1,0:T(8,128)(2,1)S(1)} %add.25), channel_id=1, source_target_pairs={{1,16},{3,18},{5,20},{7,22},{9,24},{11,26},{13,28},{15,30},{17,0},... | collective-permute-start | bytes 1769480 | tf_op jit(solution)/shard_map/ppermute | solution.py:220
  41.6 3.1 %collective-permute-start.11 = (bf16[576,512]{1,0:T(8,128)(2,1)S(1)}, bf16[576,512]{1,0:T(8,128)(2,1)S(1)}, u32[]{:S(2)}, u32[]{:S(2)}) collective-permute-start(bf16[576,512]{1,0:T(8,128)(2,1)S(1)} %add.25), channel_id=1, source_target_pairs={{1,9},{3,11},{5,13},{7,15},{9,1},{11,3},{13,5},{15,7},{17,25},{19,... | collective-permute-start | bytes 1769480 | tf_op jit(solution)/shard_map/ppermute | solution.py:220
  45.9 5.3 %shard_map.47 = (f32[2048,512]{1,0:T(8,128)S(1)}, f32[8,512]{1,0:T(8,128)S(1)}) custom-call(s32[4]{0:T(128)S(1)} %pad_add_fusion.flags, bf16[1024,2048]{1,0:T(8,128)(2,1)S(1)} %copy-done, bf16[1024,2048]{1,0:T(8,128)(2,1)S(1)} %collective-permute-done.5.other, bf16[1024,256]{1,0:T(8,128)(2,1)S(1)} %constant_dynamic-update-slice_fusion.refs_0_, ...), custom_call_target="tpu_custom_call" | custom-call | flops 2147483648 | bytes 1 | tf_op jit(solution)/shard_map/pallas_call | solution.py:153
  51.3 4.7 %collective-permute-done.12 = bf16[576,512]{1,0:T(8,128)(2,1)S(1)} collective-permute-done((bf16[576,512]{1,0:T(8,128)(2,1)S(1)}, bf16[576,512]{1,0:T(8,128)(2,1)S(1)}, u32[]{:S(2)}, u32[]{:S(2)}) %collective-permute-start.12) | collective-permute-done | bytes 589856 | tf_op jit(solution)/shard_map/ppermute | solution.py:220
  56.0 2.3 %collective-permute-done.11 = bf16[576,512]{1,0:T(8,128)(2,1)S(1)} collective-permute-done((bf16[576,512]{1,0:T(8,128)(2,1)S(1)}, bf16[576,512]{1,0:T(8,128)(2,1)S(1)}, u32[]{:S(2)}, u32[]{:S(2)}) %collective-permute-start.11) | collective-permute-done | bytes 589856 | tf_op jit(solution)/shard_map/ppermute | solution.py:220
  59.1 2.6 %collective-permute-done.16.there = bf16[1152,512]{1,0:T(8,128)(2,1)S(1)} collective-permute-done((bf16[1152,512]{1,0:T(8,128)(2,1)S(1)}, bf16[1152,512]{1,0:T(8,128)(2,1)S(1)}, u32[]{:S(2)}, u32[]{:S(2)}) %collective-permute-start.16) | collective-permute-done | bytes 1179680 | tf_op jit(solution)/shard_map/ppermute | solution.py:15
  61.7 4.8 %shard_map.48 = (f32[2048,256]{1,0:T(8,128)S(1)}, f32[8,256]{1,0:T(8,128)}) custom-call(s32[4]{0:T(128)S(1)} %pad_add_fusion.flags, f32[2,256,256]{2,1,0:T(8,128)S(1)} %copy-done.1, bf16[1152,512]{1,0:T(8,128)(2,1)S(1)} %pad_maximum_fusion.1.here, bf16[1152,512]{1,0:T(8,128)(2,1)S(1)} %collective-permute-done.16.there, ...), custom_call_target="tpu_custom_call" | custom-call | flops 1 | bytes 1 | tf_op jit(solution)/shard_map/pallas_call | solution.py:153
  66.9 3.7 %collective-permute-start.20 = (f16[2048,128]{1,0:T(8,128)(2,1)S(1)}, f16[2048,128]{1,0:T(8,128)(2,1)S(1)}, u32[]{:S(2)}, u32[]{:S(2)}) collective-permute-start(f16[2048,128]{1,0:T(8,128)(2,1)S(1)} %get-tuple-element.66), channel_id=1, source_target_pairs={{0,4},{1,5},{2,6},{3,7},{4,0},{5,1},{6,2},{7,3},{8,12},{9,13},{10,... | collective-permute-start | bytes 1572872 | tf_op jit(solution)/shard_map/ppermute | solution.py:15
  70.6 4.4 %shard_map.49 = (f32[2048,256]{1,0:T(8,128)S(1)}, f32[8,256]{1,0:T(8,128)S(1)}) custom-call(s32[4]{0:T(128)S(1)} %pad_add_fusion.flags, f32[2,256,256]{2,1,0:T(8,128)S(1)} %copy-done.1, bf16[1152,512]{1,0:T(8,128)(2,1)S(1)} %pad_maximum_fusion.1.here, bf16[1152,512]{1,0:T(8,128)(2,1)S(1)} %collective-permute-done.16.there, ...), custom_call_target="tpu_custom_call" | custom-call | flops 1 | bytes 1 | tf_op jit(solution)/shard_map/pallas_call | solution.py:153
  75.3 1.3 %collective-permute-start.19 = (f16[1024,128]{1,0:T(8,128)(2,1)S(1)}, f16[1024,128]{1,0:T(8,128)(2,1)S(1)}, u32[]{:S(2)}, u32[]{:S(2)}) collective-permute-start(f16[1024,128]{1,0:T(8,128)(2,1)S(1)} %get-tuple-element.75), channel_id=1, source_target_pairs={{0,2},{1,3},{2,0},{3,1},{4,6},{5,7},{6,4},{7,5},{8,10},{9,11},{10,... | collective-permute-start | bytes 786440 | tf_op jit(solution)/shard_map/ppermute | solution.py:15
  76.9 20.7 %collective-permute-done.19 = f16[1024,128]{1,0:T(8,128)(2,1)S(1)} collective-permute-done((f16[1024,128]{1,0:T(8,128)(2,1)S(1)}, f16[1024,128]{1,0:T(8,128)(2,1)S(1)}, u32[]{:S(2)}, u32[]{:S(2)}) %collective-permute-start.19) | collective-permute-done | bytes 262176 | tf_op jit(solution)/shard_map/ppermute | solution.py:15
  97.6 9.9 %collective-permute-done.18 = f16[1024,128]{1,0:T(8,128)(2,1)S(1)} collective-permute-done((f16[1024,128]{1,0:T(8,128)(2,1)S(1)}, f16[1024,128]{1,0:T(8,128)(2,1)S(1)}, u32[]{:S(2)}, u32[]{:S(2)}) %collective-permute-start.18) | collective-permute-done | bytes 262176 | tf_op jit(solution)/shard_map/ppermute | solution.py:15
  107.6 2.3 %shard_map.50.refs_1_ = f32[8192,128]{1,0:T(8,128)} custom-call(s32[4]{0:T(128)S(1)} %pad_add_fusion.flags, f32[8,256]{1,0:T(8,128)S(1)} %get-tuple-element.63.power, f32[1024,128]{1,0:T(8,128)S(1)} %convert_element_type.33.refs_0_, f32[1024,128]{1,0:T(8,128)S(1)} %convert_element_type.34.refs_1_, f32[2048,128]{1,0:T(8,128)S(1)} %slice.61.refs_2_, ...), custom_call_target="tpu_custom_call" | custom-call | flops 1 | bytes 1 | tf_op jit(solution)/shard_map/pallas_call | solution.py:259
  110.0 4.2 %collective-permute-done.17 = f16[2048,128]{1,0:T(8,128)(2,1)S(1)} collective-permute-done((f16[2048,128]{1,0:T(8,128)(2,1)S(1)}, f16[2048,128]{1,0:T(8,128)(2,1)S(1)}, u32[]{:S(2)}, u32[]{:S(2)}) %collective-permute-start.17) | collective-permute-done | bytes 524320 | tf_op jit(solution)/shard_map/ppermute | solution.py:15
  114.2 1.6 %shard_map.51 = f32[8192,128]{1,0:T(8,128)} custom-call(s32[4]{0:T(128)S(1)} %pad_add_fusion.flags, f32[8,256]{1,0:T(8,128)S(1)} %get-tuple-element.63.power, f32[2048,128]{1,0:T(8,128)S(1)} %convert_element_type.32.refs_0_, f32[8192,128]{1,0:T(8,128)} %shard_map.50.refs_1_), custom_call_target="tpu_custom_call", output_to_operand_aliasing={{}: (3, {})} | custom-call | flops 1 | bytes 1 | tf_op jit(solution)/shard_map/pallas_call | solution.py:259
  (62 shorter events, 14.7 us)
Async XLA Ops:
  0.1 17.2 %collective-permute-start.5 = (bf16[1024,2048]{1,0:T(8,128)(2,1)}, bf16[1024,2048]{1,0:T(8,128)(2,1)S(1)}, u32[]{:S(2)}, u32[]{:S(2)}) collective-permute-start(bf16[1024,2048]{1,0:T(8,128)(2,1)} %own), channel_id=1, source_target_pairs={{0,1},{1,0},{2,3},{3,2},{4,5},{5,4},{6,7},{7,6},{8,9},{9,8},{10,11... | collective-permute-start | bytes 12582920 | tf_op jit(solution)/shard_map/ppermute | solution.py:15
  0.8 8.6 %collective-permute-start = (bf16[1,512,128]{2,1,0:T(8,128)(2,1)}, bf16[1,512,128]{2,1,0:T(8,128)(2,1)S(1)}, u32[]{:S(2)}, u32[]{:S(2)}) collective-permute-start(bf16[1,512,128]{2,1,0:T(8,128)(2,1)} %bitcast.5), channel_id=1, source_target_pairs={{0,4},{1,5},{2,6},{3,7},{4,0},{5,1},{6,2},{7,3},{8,12},{9,13},{10,... | collective-permute-start | bytes 393224 | tf_op jit(solution)/shard_map/ppermute | solution.py:15
  5.8 11.1 %collective-permute-start.2 = (bf16[576,512]{1,0:T(8,128)(2,1)S(1)}, bf16[576,512]{1,0:T(8,128)(2,1)S(1)}, u32[]{:S(2)}, u32[]{:S(2)}) collective-permute-start(bf16[576,512]{1,0:T(8,128)(2,1)S(1)} %pad_maximum_fusion.2), channel_id=1, source_target_pairs={{31,7}} | collective-permute-start | bytes 1769480 | tf_op jit(solution)/shard_map/ppermute | solution.py:192
  6.5 3.6 %copy-start.2 = (f32[1024,512]{1,0:T(8,128)S(1)}, f32[1024,512]{1,0:T(8,128)}, u32[]{:S(2)}) copy-start(f32[1024,512]{1,0:T(8,128)} %param.6) | copy-start | bytes 6291460
  6.6 10.4 %collective-permute-start.3 = (bf16[576,512]{1,0:T(8,128)(2,1)S(1)}, bf16[576,512]{1,0:T(8,128)(2,1)S(1)}, u32[]{:S(2)}, u32[]{:S(2)}) collective-permute-start(bf16[576,512]{1,0:T(8,128)(2,1)S(1)} %pad_maximum_fusion.3), channel_id=1, source_target_pairs={{31,15}} | collective-permute-start | bytes 1769480 | tf_op jit(solution)/shard_map/ppermute | solution.py:192
  7.5 9.5 %collective-permute-start.4 = (bf16[576,512]{1,0:T(8,128)(2,1)S(1)}, bf16[576,512]{1,0:T(8,128)(2,1)S(1)}, u32[]{:S(2)}, u32[]{:S(2)}) collective-permute-start(bf16[576,512]{1,0:T(8,128)(2,1)S(1)} %fusion.4), channel_id=1, source_target_pairs={{31,23}} | collective-permute-start | bytes 1769480 | tf_op jit(solution)/shard_map/ppermute | solution.py:192
  9.4 7.5 %collective-permute-start.1 = (bf16[2,512,128]{2,1,0:T(8,128)(2,1)S(1)}, bf16[2,512,128]{2,1,0:T(8,128)(2,1)S(1)}, u32[]{:S(2)}, u32[]{:S(2)}) collective-permute-start(bf16[2,512,128]{2,1,0:T(8,128)(2,1)S(1)} %pad_maximum_fusion.5), channel_id=1, source_target_pairs={{0,2},{1,3},{2,0},{3,1},{4,6},{5,7},{6,4},{7,5},{8,10},{9,11},{10,... | collective-permute-start | bytes 786440 | tf_op jit(solution)/shard_map/ppermute | solution.py:15
  17.3 13.1 %collective-permute-start.9 = (bf16[1024,1024]{1,0:T(8,128)(2,1)S(1)}, bf16[1024,1024]{1,0:T(8,128)(2,1)S(1)}, u32[]{:S(2)}, u32[]{:S(2)}) collective-permute-start(bf16[1024,1024]{1,0:T(8,128)(2,1)S(1)} %pad_maximum_fusion.refs_4_), channel_id=1, source_target_pairs={{0,1},{1,0},{2,3},{3,2},{4,5},{5,4},{6,7},{7,6},{8,9},{9,8},{10,11... | collective-permute-start | bytes 6291464 | tf_op jit(solution)/shard_map/ppermute | solution.py:15
  18.7 11.5 %collective-permute-start.8 = (bf16[576,512]{1,0:T(8,128)(2,1)S(1)}, bf16[576,512]{1,0:T(8,128)(2,1)S(1)}, u32[]{:S(2)}, u32[]{:S(2)}) collective-permute-start(bf16[576,512]{1,0:T(8,128)(2,1)S(1)} %fusion.7), channel_id=1, source_target_pairs={{7,3},{15,11},{23,19},{31,27}} | collective-permute-start | bytes 1769480 | tf_op jit(solution)/shard_map/ppermute | solution.py:211
  20.1 10.3 %collective-permute-start.6 = (bf16[512,256]{1,0:T(8,128)(2,1)S(1)}, bf16[512,256]{1,0:T(8,128)(2,1)S(1)}, u32[]{:S(2)}, u32[]{:S(2)}) collective-permute-start(bf16[512,256]{1,0:T(8,128)(2,1)S(1)} %get-tuple-element.48), channel_id=1, source_target_pairs={{0,16},{8,24},{16,0},{24,8},{1,17},{9,25},{17,1},{25,9},{2,18},{10... | collective-permute-start | bytes 786440 | tf_op jit(solution)/shard_map/ppermute | solution.py:15
  21.4 9.0 %collective-permute-start.7 = (bf16[512,256]{1,0:T(8,128)(2,1)S(1)}, bf16[512,256]{1,0:T(8,128)(2,1)S(1)}, u32[]{:S(2)}, u32[]{:S(2)}) collective-permute-start(bf16[512,256]{1,0:T(8,128)(2,1)S(1)} %get-tuple-element.50), channel_id=1, source_target_pairs={{0,8},{8,0},{16,24},{24,16},{1,9},{9,1},{17,25},{25,17},{2,10},{10... | collective-permute-start | bytes 786440 | tf_op jit(solution)/shard_map/ppermute | solution.py:15
  30.2 15.7 %copy-start = (bf16[1024,2048]{1,0:T(8,128)(2,1)S(1)}, bf16[1024,2048]{1,0:T(8,128)(2,1)}, u32[]{:S(2)}) copy-start(bf16[1024,2048]{1,0:T(8,128)(2,1)} %own) | copy-start | bytes 12582916
  30.4 8.4 %collective-permute-start.10 = (bf16[576,512]{1,0:T(8,128)(2,1)S(1)}, bf16[576,512]{1,0:T(8,128)(2,1)S(1)}, u32[]{:S(2)}, u32[]{:S(2)}) collective-permute-start(bf16[576,512]{1,0:T(8,128)(2,1)S(1)} %add.24), channel_id=1, source_target_pairs={{7,5},{3,1},{15,13},{11,9},{23,21},{19,17},{31,29},{27,25}} | collective-permute-start | bytes 1769480 | tf_op jit(solution)/shard_map/ppermute | solution.py:211
  32.1 13.0 %collective-permute-start.15 = (bf16[1024,256]{1,0:T(8,128)(2,1)S(1)}, bf16[1024,256]{1,0:T(8,128)(2,1)S(1)}, u32[]{:S(2)}, u32[]{:S(2)}) collective-permute-start(bf16[1024,256]{1,0:T(8,128)(2,1)S(1)} %constant_dynamic-update-slice_fusion.2.refs_2_.refs_0_), channel_id=1, source_target_pairs={{0,16},{8,24},{16,0},{24,8},{1,17},{9,25},{17,1},{25,9},{2,18},{10... | collective-permute-start | bytes 1572872 | tf_op jit(solution)/shard_map/ppermute | solution.py:15
  34.9 11.0 %collective-permute-start.14 = (bf16[1024,256]{1,0:T(8,128)(2,1)S(1)}, bf16[1024,256]{1,0:T(8,128)(2,1)S(1)}, u32[]{:S(2)}, u32[]{:S(2)}) collective-permute-start(bf16[1024,256]{1,0:T(8,128)(2,1)S(1)} %constant_dynamic-update-slice_fusion.refs_0_), channel_id=1, source_target_pairs={{0,8},{8,0},{16,24},{24,16},{1,9},{9,1},{17,25},{25,17},{2,10},{10... | collective-permute-start | bytes 1572872 | tf_op jit(solution)/shard_map/ppermute | solution.py:15
  38.9 12.4 %collective-permute-start.13 = (bf16[576,512]{1,0:T(8,128)(2,1)S(1)}, bf16[576,512]{1,0:T(8,128)(2,1)S(1)}, u32[]{:S(2)}, u32[]{:S(2)}) collective-permute-start(bf16[576,512]{1,0:T(8,128)(2,1)S(1)} %add.25), channel_id=1, source_target_pairs={{1,24},{3,26},{5,28},{7,30},{9,16},{11,18},{13,20},{15,22},{17,8},... | collective-permute-start | bytes 1769480 | tf_op jit(solution)/shard_map/ppermute | solution.py:220
  40.3 15.7 %collective-permute-start.12 = (bf16[576,512]{1,0:T(8,128)(2,1)S(1)}, bf16[576,512]{1,0:T(8,128)(2,1)S(1)}, u32[]{:S(2)}, u32[]{:S(2)}) collective-permute-start(bf16[576,512]{1,0:T(8,128)(2,1)S(1)} %add.25), channel_id=1, source_target_pairs={{1,16},{3,18},{5,20},{7,22},{9,24},{11,26},{13,28},{15,30},{17,0},... | collective-permute-start | bytes 1769480 | tf_op jit(solution)/shard_map/ppermute | solution.py:220
  41.6 16.7 %collective-permute-start.11 = (bf16[576,512]{1,0:T(8,128)(2,1)S(1)}, bf16[576,512]{1,0:T(8,128)(2,1)S(1)}, u32[]{:S(2)}, u32[]{:S(2)}) collective-permute-start(bf16[576,512]{1,0:T(8,128)(2,1)S(1)} %add.25), channel_id=1, source_target_pairs={{1,9},{3,11},{5,13},{7,15},{9,1},{11,3},{13,5},{15,7},{17,25},{19,... | collective-permute-start | bytes 1769480 | tf_op jit(solution)/shard_map/ppermute | solution.py:220
  58.7 3.0 %copy-start.1 = (f32[2,256,256]{2,1,0:T(8,128)S(1)}, f32[2,256,256]{2,1,0:T(8,128)}, u32[]{:S(2)}) copy-start(f32[2,256,256]{2,1,0:T(8,128)} %inverse.2) | copy-start | bytes 1572868
  58.8 2.9 %collective-permute-start.16 = (bf16[1152,512]{1,0:T(8,128)(2,1)S(1)}, bf16[1152,512]{1,0:T(8,128)(2,1)S(1)}, u32[]{:S(2)}, u32[]{:S(2)}) collective-permute-start(bf16[1152,512]{1,0:T(8,128)(2,1)S(1)} %pad_maximum_fusion.1.here), channel_id=1, source_target_pairs={{0,1},{1,0},{2,3},{3,2},{4,5},{5,4},{6,7},{7,6},{8,9},{9,8},{10,11... | collective-permute-start | bytes 3538952 | tf_op jit(solution)/shard_map/ppermute | solution.py:15
  66.9 40.7 %collective-permute-start.20 = (f16[2048,128]{1,0:T(8,128)(2,1)S(1)}, f16[2048,128]{1,0:T(8,128)(2,1)S(1)}, u32[]{:S(2)}, u32[]{:S(2)}) collective-permute-start(f16[2048,128]{1,0:T(8,128)(2,1)S(1)} %get-tuple-element.66), channel_id=1, source_target_pairs={{0,4},{1,5},{2,6},{3,7},{4,0},{5,1},{6,2},{7,3},{8,12},{9,13},{10,... | collective-permute-start | bytes 1572872 | tf_op jit(solution)/shard_map/ppermute | solution.py:15
  70.6 43.6 %collective-permute-start.17 = (f16[2048,128]{1,0:T(8,128)(2,1)S(1)}, f16[2048,128]{1,0:T(8,128)(2,1)S(1)}, u32[]{:S(2)}, u32[]{:S(2)}) collective-permute-start(f16[2048,128]{1,0:T(8,128)(2,1)S(1)} %get-tuple-element.64), channel_id=1, source_target_pairs={{0,6},{1,7},{2,4},{3,5},{4,2},{5,3},{6,0},{7,1},{8,14},{9,15},{10,... | collective-permute-start | bytes 1572872 | tf_op jit(solution)/shard_map/ppermute | solution.py:15
  75.3 22.3 %collective-permute-start.19 = (f16[1024,128]{1,0:T(8,128)(2,1)S(1)}, f16[1024,128]{1,0:T(8,128)(2,1)S(1)}, u32[]{:S(2)}, u32[]{:S(2)}) collective-permute-start(f16[1024,128]{1,0:T(8,128)(2,1)S(1)} %get-tuple-element.75), channel_id=1, source_target_pairs={{0,2},{1,3},{2,0},{3,1},{4,6},{5,7},{6,4},{7,5},{8,10},{9,11},{10,... | collective-permute-start | bytes 786440 | tf_op jit(solution)/shard_map/ppermute | solution.py:15
  76.6 30.9 %collective-permute-start.18 = (f16[1024,128]{1,0:T(8,128)(2,1)S(1)}, f16[1024,128]{1,0:T(8,128)(2,1)S(1)}, u32[]{:S(2)}, u32[]{:S(2)}) collective-permute-start(f16[1024,128]{1,0:T(8,128)(2,1)S(1)} %get-tuple-element.76), channel_id=1, source_target_pairs={{0,2},{1,3},{2,0},{3,1},{4,6},{5,7},{6,4},{7,5},{8,10},{9,11},{10,... | collective-permute-start | bytes 786440 | tf_op jit(solution)/shard_map/ppermute | solution.py:15
  (1 other events, 2.8 us)

commit v11 on v10

--- a/solution.py
+++ b/solution.py
@@ -107,11 +107,11 @@
     exponent = 14.0 - jnp.floor(jnp.log2(jnp.maximum(bound, 1e-30)))
     scale = jnp.exp2(exponent)
     power[...] = jnp.broadcast_to(jnp.exp2(-exponent), power.shape)
-    right = jnp.concatenate([solved[...], solved[:size, :]], axis=0)
+    twice = jnp.concatenate([solved[:size, :], solved[:size, :]], axis=0)
     for cols, core in ((own, flags[1]), (other, 1 - flags[1])):
         at = pl.ds(pl.multiple_of(core * rows, rows), rows)
-        left = jnp.concatenate([cols[:, :size], cols[...]], axis=1)
-        out[at, :] = (rotated[at, where] - mul(left, right)) * scale
+        total = mul(cols[...], twice) + mul(cols[:, :size], solved[size:, :])
+        out[at, :] = (rotated[at, where] - total) * scale
 
     @pl.when(flags[0] == 1)
     def _():

time: 117 us -> 117 us (level)
  no operation moved by 1% of the time
where the time goes in v11:
time: 117 us; the launch traced here: 116 us
  waiting for transfers between devices  64.4 us (55%)
  starting transfers between devices  26.9 us (23%)
  Pallas kernels  18.4 us (16%)
  other arithmetic  3.62 us (3%)
  local copies, waits for them, and re-layouts  2.15 us (2%)
    ppermute x13, waiting for transfers between devices, swapped(): lax.ppermute(value, axis, [(i, i ^ offset) for i in range(lax.axis_size(a...  45.9 us
    ppermute x13, starting transfers between devices, swapped(): lax.ppermute(value, axis, [(i, i ^ offset) for i in range(lax.axis_size(a...  16 us
    pallas_call x4, Pallas kernels, call(): pl.pallas_call(kernel, in_specs=[spec(pltpu.SMEM)] * len(scalars) + specs...  14.5 us
    ppermute x2, waiting for transfers between devices, on_device(): part += lax.ppermute(part, VEC, [(v, v ^ downs[i]) for v in sources])  11.4 us
    ppermute x3, waiting for transfers between devices, on_device(): pieces.append(lax.ppermute(part, (ROW, VEC), pairs))  7.12 us
    ppermute x3, starting transfers between devices, on_device(): pieces.append(lax.ppermute(part, (ROW, VEC), pairs))  5.77 us
    pallas_call x2, Pallas kernels, place(): pl.pallas_call(functools.partial(place_kernel, [(k, len(v)) for k, v in b...  3.87 us
    ppermute x2, starting transfers between devices, on_device(): part += lax.ppermute(part, VEC, [(v, v ^ downs[i]) for v in sources])  2.87 us
  transfers between devices with their start and end apart: 21, of which 13 were waited for; matrix products, arithmetic and copies ran while one was open for 4% of the time, Pallas kernels for 10%

profile of v11, /device:TPU:9, one launch (start us, length us, event | category | flops | bytes accessed | tf_op | source)
XLA Modules:
  0.0 115.9 jit_solution(7783517466682182716)
XLA Ops:
  0.8 2.3 %collective-permute-start = (bf16[1,512,128]{2,1,0:T(8,128)(2,1)}, bf16[1,512,128]{2,1,0:T(8,128)(2,1)S(1)}, u32[]{:S(2)}, u32[]{:S(2)}) collective-permute-start(bf16[1,512,128]{2,1,0:T(8,128)(2,1)} %bitcast.5), channel_id=1, source_target_pairs={{0,4},{1,5},{2,6},{3,7},{4,0},{5,1},{6,2},{7,3},{8,12},{9,13},{10,... | collective-permute-start | bytes 393224 | tf_op jit(solution)/shard_map/ppermute | solution.py:15
  4.1 1.7 %fusion.12 = (bf16[512,512]{1,0:T(8,128)(2,1)S(1)}, bf16[512,512]{1,0:T(8,128)(2,1)S(1)}, bf16[512,512]{1,0:T(8,128)(2,1)S(1)}, bf16[512,512]{1,0:T(8,128)(2,1)S(1)}) fusion(bf16[1024,2048]{1,0:T(8,128)(2,1)} %own), kind=kLoop, calls=%fused_computation.35 | loop fusion | bytes 4194304 | tf_op jit(solution)/shard_map/slice | solution.py:185
  10.8 6.1 %collective-permute-done.1 = bf16[2,512,128]{2,1,0:T(8,128)(2,1)S(1)} collective-permute-done((bf16[2,512,128]{2,1,0:T(8,128)(2,1)S(1)}, bf16[2,512,128]{2,1,0:T(8,128)(2,1)S(1)}, u32[]{:S(2)}, u32[]{:S(2)}) %collective-permute-start.1) | collective-permute-done | bytes 262176 | tf_op jit(solution)/shard_map/ppermute | solution.py:15
  17.3 1.3 %collective-permute-start.9 = (bf16[1024,1024]{1,0:T(8,128)(2,1)S(1)}, bf16[1024,1024]{1,0:T(8,128)(2,1)S(1)}, u32[]{:S(2)}, u32[]{:S(2)}) collective-permute-start(bf16[1024,1024]{1,0:T(8,128)(2,1)S(1)} %pad_maximum_fusion.refs_4_), channel_id=1, source_target_pairs={{0,1},{1,0},{2,3},{3,2},{4,5},{5,4},{6,7},{7,6},{8,9},{9,8},{10,11... | collective-permute-start | bytes 6291464 | tf_op jit(solution)/shard_map/ppermute | solution.py:15
  22.6 7.6 %collective-permute-done.8 = bf16[576,512]{1,0:T(8,128)(2,1)S(1)} collective-permute-done((bf16[576,512]{1,0:T(8,128)(2,1)S(1)}, bf16[576,512]{1,0:T(8,128)(2,1)S(1)}, u32[]{:S(2)}, u32[]{:S(2)}) %collective-permute-start.8) | collective-permute-done | bytes 589856 | tf_op jit(solution)/shard_map/ppermute | solution.py:211
  30.4 1.6 %collective-permute-start.10 = (bf16[576,512]{1,0:T(8,128)(2,1)S(1)}, bf16[576,512]{1,0:T(8,128)(2,1)S(1)}, u32[]{:S(2)}, u32[]{:S(2)}) collective-permute-start(bf16[576,512]{1,0:T(8,128)(2,1)S(1)} %add.24), channel_id=1, source_target_pairs={{7,5},{3,1},{15,13},{11,9},{23,21},{19,17},{31,29},{27,25}} | collective-permute-start | bytes 1769480 | tf_op jit(solution)/shard_map/ppermute | solution.py:211
  32.1 2.8 %collective-permute-start.15 = (bf16[1024,256]{1,0:T(8,128)(2,1)S(1)}, bf16[1024,256]{1,0:T(8,128)(2,1)S(1)}, u32[]{:S(2)}, u32[]{:S(2)}) collective-permute-start(bf16[1024,256]{1,0:T(8,128)(2,1)S(1)} %constant_dynamic-update-slice_fusion.2.refs_2_.refs_0_), channel_id=1, source_target_pairs={{0,16},{8,24},{16,0},{24,8},{1,17},{9,25},{17,1},{25,9},{2,18},{10... | collective-permute-start | bytes 1572872 | tf_op jit(solution)/shard_map/ppermute | solution.py:15
  35.0 3.8 %collective-permute-done.10 = bf16[576,512]{1,0:T(8,128)(2,1)S(1)} collective-permute-done((bf16[576,512]{1,0:T(8,128)(2,1)S(1)}, bf16[576,512]{1,0:T(8,128)(2,1)S(1)}, u32[]{:S(2)}, u32[]{:S(2)}) %collective-permute-start.10) | collective-permute-done | bytes 589856 | tf_op jit(solution)/shard_map/ppermute | solution.py:211
  38.9 1.3 %collective-permute-start.13 = (bf16[576,512]{1,0:T(8,128)(2,1)S(1)}, bf16[576,512]{1,0:T(8,128)(2,1)S(1)}, u32[]{:S(2)}, u32[]{:S(2)}) collective-permute-start(bf16[576,512]{1,0:T(8,128)(2,1)S(1)} %add.25), channel_id=1, source_target_pairs={{1,24},{3,26},{5,28},{7,30},{9,16},{11,18},{13,20},{15,22},{17,8},... | collective-permute-start | bytes 1769480 | tf_op jit(solution)/shard_map/ppermute | solution.py:220
  40.3 1.3 %collective-permute-start.12 = (bf16[576,512]{1,0:T(8,128)(2,1)S(1)}, bf16[576,512]{1,0:T(8,128)(2,1)S(1)}, u32[]{:S(2)}, u32[]{:S(2)}) collective-permute-start(bf16[576,512]{1,0:T(8,128)(2,1)S(1)} %add.25), channel_id=1, source_target_pairs={{1,16},{3,18},{5,20},{7,22},{9,24},{11,26},{13,28},{15,30},{17,0},... | collective-permute-start | bytes 1769480 | tf_op jit(solution)/shard_map/ppermute | solution.py:220
  41.6 3.1 %collective-permute-start.11 = (bf16[576,512]{1,0:T(8,128)(2,1)S(1)}, bf16[576,512]{1,0:T(8,128)(2,1)S(1)}, u32[]{:S(2)}, u32[]{:S(2)}) collective-permute-start(bf16[576,512]{1,0:T(8,128)(2,1)S(1)} %add.25), channel_id=1, source_target_pairs={{1,9},{3,11},{5,13},{7,15},{9,1},{11,3},{13,5},{15,7},{17,25},{19,... | collective-permute-start | bytes 1769480 | tf_op jit(solution)/shard_map/ppermute | solution.py:220
  45.9 5.3 %shard_map.47 = (f32[2048,512]{1,0:T(8,128)S(1)}, f32[8,512]{1,0:T(8,128)S(1)}) custom-call(s32[4]{0:T(128)S(1)} %pad_add_fusion.flags, bf16[1024,2048]{1,0:T(8,128)(2,1)S(1)} %copy-done, bf16[1024,2048]{1,0:T(8,128)(2,1)S(1)} %collective-permute-done.5.other, bf16[1024,256]{1,0:T(8,128)(2,1)S(1)} %constant_dynamic-update-slice_fusion.refs_0_, ...), custom_call_target="tpu_custom_call" | custom-call | flops 2147483648 | bytes 1 | tf_op jit(solution)/shard_map/pallas_call | solution.py:153
  51.3 4.7 %collective-permute-done.12 = bf16[576,512]{1,0:T(8,128)(2,1)S(1)} collective-permute-done((bf16[576,512]{1,0:T(8,128)(2,1)S(1)}, bf16[576,512]{1,0:T(8,128)(2,1)S(1)}, u32[]{:S(2)}, u32[]{:S(2)}) %collective-permute-start.12) | collective-permute-done | bytes 589856 | tf_op jit(solution)/shard_map/ppermute | solution.py:220
  56.0 2.3 %collective-permute-done.11 = bf16[576,512]{1,0:T(8,128)(2,1)S(1)} collective-permute-done((bf16[576,512]{1,0:T(8,128)(2,1)S(1)}, bf16[576,512]{1,0:T(8,128)(2,1)S(1)}, u32[]{:S(2)}, u32[]{:S(2)}) %collective-permute-start.11) | collective-permute-done | bytes 589856 | tf_op jit(solution)/shard_map/ppermute | solution.py:220
  59.1 2.6 %collective-permute-done.16.there = bf16[1152,512]{1,0:T(8,128)(2,1)S(1)} collective-permute-done((bf16[1152,512]{1,0:T(8,128)(2,1)S(1)}, bf16[1152,512]{1,0:T(8,128)(2,1)S(1)}, u32[]{:S(2)}, u32[]{:S(2)}) %collective-permute-start.16) | collective-permute-done | bytes 1179680 | tf_op jit(solution)/shard_map/ppermute | solution.py:15
  61.7 4.8 %shard_map.48 = (f32[2048,256]{1,0:T(8,128)S(1)}, f32[8,256]{1,0:T(8,128)}) custom-call(s32[4]{0:T(128)S(1)} %pad_add_fusion.flags, f32[2,256,256]{2,1,0:T(8,128)S(1)} %copy-done.1, bf16[1152,512]{1,0:T(8,128)(2,1)S(1)} %pad_maximum_fusion.1.here, bf16[1152,512]{1,0:T(8,128)(2,1)S(1)} %collective-permute-done.16.there, ...), custom_call_target="tpu_custom_call" | custom-call | flops 1 | bytes 1 | tf_op jit(solution)/shard_map/pallas_call | solution.py:153
  66.9 3.6 %collective-permute-start.20 = (f16[2048,128]{1,0:T(8,128)(2,1)S(1)}, f16[2048,128]{1,0:T(8,128)(2,1)S(1)}, u32[]{:S(2)}, u32[]{:S(2)}) collective-permute-start(f16[2048,128]{1,0:T(8,128)(2,1)S(1)} %get-tuple-element.66), channel_id=1, source_target_pairs={{0,4},{1,5},{2,6},{3,7},{4,0},{5,1},{6,2},{7,3},{8,12},{9,13},{10,... | collective-permute-start | bytes 1572872 | tf_op jit(solution)/shard_map/ppermute | solution.py:15
  70.6 4.4 %shard_map.49 = (f32[2048,256]{1,0:T(8,128)S(1)}, f32[8,256]{1,0:T(8,128)S(1)}) custom-call(s32[4]{0:T(128)S(1)} %pad_add_fusion.flags, f32[2,256,256]{2,1,0:T(8,128)S(1)} %copy-done.1, bf16[1152,512]{1,0:T(8,128)(2,1)S(1)} %pad_maximum_fusion.1.here, bf16[1152,512]{1,0:T(8,128)(2,1)S(1)} %collective-permute-done.16.there, ...), custom_call_target="tpu_custom_call" | custom-call | flops 1 | bytes 1 | tf_op jit(solution)/shard_map/pallas_call | solution.py:153
  75.3 1.3 %collective-permute-start.19 = (f16[1024,128]{1,0:T(8,128)(2,1)S(1)}, f16[1024,128]{1,0:T(8,128)(2,1)S(1)}, u32[]{:S(2)}, u32[]{:S(2)}) collective-permute-start(f16[1024,128]{1,0:T(8,128)(2,1)S(1)} %get-tuple-element.75), channel_id=1, source_target_pairs={{0,2},{1,3},{2,0},{3,1},{4,6},{5,7},{6,4},{7,5},{8,10},{9,11},{10,... | collective-permute-start | bytes 786440 | tf_op jit(solution)/shard_map/ppermute | solution.py:15
  76.9 20.7 %collective-permute-done.19 = f16[1024,128]{1,0:T(8,128)(2,1)S(1)} collective-permute-done((f16[1024,128]{1,0:T(8,128)(2,1)S(1)}, f16[1024,128]{1,0:T(8,128)(2,1)S(1)}, u32[]{:S(2)}, u32[]{:S(2)}) %collective-permute-start.19) | collective-permute-done | bytes 262176 | tf_op jit(solution)/shard_map/ppermute | solution.py:15
  97.7 9.9 %collective-permute-done.18 = f16[1024,128]{1,0:T(8,128)(2,1)S(1)} collective-permute-done((f16[1024,128]{1,0:T(8,128)(2,1)S(1)}, f16[1024,128]{1,0:T(8,128)(2,1)S(1)}, u32[]{:S(2)}, u32[]{:S(2)}) %collective-permute-start.18) | collective-permute-done | bytes 262176 | tf_op jit(solution)/shard_map/ppermute | solution.py:15
  107.7 2.3 %shard_map.50.refs_1_ = f32[8192,128]{1,0:T(8,128)} custom-call(s32[4]{0:T(128)S(1)} %pad_add_fusion.flags, f32[8,256]{1,0:T(8,128)S(1)} %get-tuple-element.63.power, f32[1024,128]{1,0:T(8,128)S(1)} %convert_element_type.33.refs_0_, f32[1024,128]{1,0:T(8,128)S(1)} %convert_element_type.34.refs_1_, f32[2048,128]{1,0:T(8,128)S(1)} %slice.61.refs_2_, ...), custom_call_target="tpu_custom_call" | custom-call | flops 1 | bytes 1 | tf_op jit(solution)/shard_map/pallas_call | solution.py:259
  110.0 4.2 %collective-permute-done.17 = f16[2048,128]{1,0:T(8,128)(2,1)S(1)} collective-permute-done((f16[2048,128]{1,0:T(8,128)(2,1)S(1)}, f16[2048,128]{1,0:T(8,128)(2,1)S(1)}, u32[]{:S(2)}, u32[]{:S(2)}) %collective-permute-start.17) | collective-permute-done | bytes 524320 | tf_op jit(solution)/shard_map/ppermute | solution.py:15
  114.2 1.6 %shard_map.51 = f32[8192,128]{1,0:T(8,128)} custom-call(s32[4]{0:T(128)S(1)} %pad_add_fusion.flags, f32[8,256]{1,0:T(8,128)S(1)} %get-tuple-element.63.power, f32[2048,128]{1,0:T(8,128)S(1)} %convert_element_type.32.refs_0_, f32[8192,128]{1,0:T(8,128)} %shard_map.50.refs_1_), custom_call_target="tpu_custom_call", output_to_operand_aliasing={{}: (3, {})} | custom-call | flops 1 | bytes 1 | tf_op jit(solution)/shard_map/pallas_call | solution.py:259
  (62 shorter events, 14.7 us)
Async XLA Ops:
  0.1 17.2 %collective-permute-start.5 = (bf16[1024,2048]{1,0:T(8,128)(2,1)}, bf16[1024,2048]{1,0:T(8,128)(2,1)S(1)}, u32[]{:S(2)}, u32[]{:S(2)}) collective-permute-start(bf16[1024,2048]{1,0:T(8,128)(2,1)} %own), channel_id=1, source_target_pairs={{0,1},{1,0},{2,3},{3,2},{4,5},{5,4},{6,7},{7,6},{8,9},{9,8},{10,11... | collective-permute-start | bytes 12582920 | tf_op jit(solution)/shard_map/ppermute | solution.py:15
  0.8 8.6 %collective-permute-start = (bf16[1,512,128]{2,1,0:T(8,128)(2,1)}, bf16[1,512,128]{2,1,0:T(8,128)(2,1)S(1)}, u32[]{:S(2)}, u32[]{:S(2)}) collective-permute-start(bf16[1,512,128]{2,1,0:T(8,128)(2,1)} %bitcast.5), channel_id=1, source_target_pairs={{0,4},{1,5},{2,6},{3,7},{4,0},{5,1},{6,2},{7,3},{8,12},{9,13},{10,... | collective-permute-start | bytes 393224 | tf_op jit(solution)/shard_map/ppermute | solution.py:15
  5.8 11.1 %collective-permute-start.2 = (bf16[576,512]{1,0:T(8,128)(2,1)S(1)}, bf16[576,512]{1,0:T(8,128)(2,1)S(1)}, u32[]{:S(2)}, u32[]{:S(2)}) collective-permute-start(bf16[576,512]{1,0:T(8,128)(2,1)S(1)} %pad_maximum_fusion.2), channel_id=1, source_target_pairs={{31,7}} | collective-permute-start | bytes 1769480 | tf_op jit(solution)/shard_map/ppermute | solution.py:192
  6.5 3.6 %copy-start.2 = (f32[1024,512]{1,0:T(8,128)S(1)}, f32[1024,512]{1,0:T(8,128)}, u32[]{:S(2)}) copy-start(f32[1024,512]{1,0:T(8,128)} %param.6) | copy-start | bytes 6291460
  6.6 10.4 %collective-permute-start.3 = (bf16[576,512]{1,0:T(8,128)(2,1)S(1)}, bf16[576,512]{1,0:T(8,128)(2,1)S(1)}, u32[]{:S(2)}, u32[]{:S(2)}) collective-permute-start(bf16[576,512]{1,0:T(8,128)(2,1)S(1)} %pad_maximum_fusion.3), channel_id=1, source_target_pairs={{31,15}} | collective-permute-start | bytes 1769480 | tf_op jit(solution)/shard_map/ppermute | solution.py:192
  7.5 9.5 %collective-permute-start.4 = (bf16[576,512]{1,0:T(8,128)(2,1)S(1)}, bf16[576,512]{1,0:T(8,128)(2,1)S(1)}, u32[]{:S(2)}, u32[]{:S(2)}) collective-permute-start(bf16[576,512]{1,0:T(8,128)(2,1)S(1)} %fusion.4), channel_id=1, source_target_pairs={{31,23}} | collective-permute-start | bytes 1769480 | tf_op jit(solution)/shard_map/ppermute | solution.py:192
  9.4 7.5 %collective-permute-start.1 = (bf16[2,512,128]{2,1,0:T(8,128)(2,1)S(1)}, bf16[2,512,128]{2,1,0:T(8,128)(2,1)S(1)}, u32[]{:S(2)}, u32[]{:S(2)}) collective-permute-start(bf16[2,512,128]{2,1,0:T(8,128)(2,1)S(1)} %pad_maximum_fusion.5), channel_id=1, source_target_pairs={{0,2},{1,3},{2,0},{3,1},{4,6},{5,7},{6,4},{7,5},{8,10},{9,11},{10,... | collective-permute-start | bytes 786440 | tf_op jit(solution)/shard_map/ppermute | solution.py:15
  17.3 13.1 %collective-permute-start.9 = (bf16[1024,1024]{1,0:T(8,128)(2,1)S(1)}, bf16[1024,1024]{1,0:T(8,128)(2,1)S(1)}, u32[]{:S(2)}, u32[]{:S(2)}) collective-permute-start(bf16[1024,1024]{1,0:T(8,128)(2,1)S(1)} %pad_maximum_fusion.refs_4_), channel_id=1, source_target_pairs={{0,1},{1,0},{2,3},{3,2},{4,5},{5,4},{6,7},{7,6},{8,9},{9,8},{10,11... | collective-permute-start | bytes 6291464 | tf_op jit(solution)/shard_map/ppermute | solution.py:15
  18.7 11.5 %collective-permute-start.8 = (bf16[576,512]{1,0:T(8,128)(2,1)S(1)}, bf16[576,512]{1,0:T(8,128)(2,1)S(1)}, u32[]{:S(2)}, u32[]{:S(2)}) collective-permute-start(bf16[576,512]{1,0:T(8,128)(2,1)S(1)} %fusion.7), channel_id=1, source_target_pairs={{7,3},{15,11},{23,19},{31,27}} | collective-permute-start | bytes 1769480 | tf_op jit(solution)/shard_map/ppermute | solution.py:211
  20.1 10.3 %collective-permute-start.6 = (bf16[512,256]{1,0:T(8,128)(2,1)S(1)}, bf16[512,256]{1,0:T(8,128)(2,1)S(1)}, u32[]{:S(2)}, u32[]{:S(2)}) collective-permute-start(bf16[512,256]{1,0:T(8,128)(2,1)S(1)} %get-tuple-element.48), channel_id=1, source_target_pairs={{0,16},{8,24},{16,0},{24,8},{1,17},{9,25},{17,1},{25,9},{2,18},{10... | collective-permute-start | bytes 786440 | tf_op jit(solution)/shard_map/ppermute | solution.py:15
  21.4 9.0 %collective-permute-start.7 = (bf16[512,256]{1,0:T(8,128)(2,1)S(1)}, bf16[512,256]{1,0:T(8,128)(2,1)S(1)}, u32[]{:S(2)}, u32[]{:S(2)}) collective-permute-start(bf16[512,256]{1,0:T(8,128)(2,1)S(1)} %get-tuple-element.50), channel_id=1, source_target_pairs={{0,8},{8,0},{16,24},{24,16},{1,9},{9,1},{17,25},{25,17},{2,10},{10... | collective-permute-start | bytes 786440 | tf_op jit(solution)/shard_map/ppermute | solution.py:15
  30.2 15.7 %copy-start = (bf16[1024,2048]{1,0:T(8,128)(2,1)S(1)}, bf16[1024,2048]{1,0:T(8,128)(2,1)}, u32[]{:S(2)}) copy-start(bf16[1024,2048]{1,0:T(8,128)(2,1)} %own) | copy-start | bytes 12582916
  30.4 8.4 %collective-permute-start.10 = (bf16[576,512]{1,0:T(8,128)(2,1)S(1)}, bf16[576,512]{1,0:T(8,128)(2,1)S(1)}, u32[]{:S(2)}, u32[]{:S(2)}) collective-permute-start(bf16[576,512]{1,0:T(8,128)(2,1)S(1)} %add.24), channel_id=1, source_target_pairs={{7,5},{3,1},{15,13},{11,9},{23,21},{19,17},{31,29},{27,25}} | collective-permute-start | bytes 1769480 | tf_op jit(solution)/shard_map/ppermute | solution.py:211
  32.1 13.0 %collective-permute-start.15 = (bf16[1024,256]{1,0:T(8,128)(2,1)S(1)}, bf16[1024,256]{1,0:T(8,128)(2,1)S(1)}, u32[]{:S(2)}, u32[]{:S(2)}) collective-permute-start(bf16[1024,256]{1,0:T(8,128)(2,1)S(1)} %constant_dynamic-update-slice_fusion.2.refs_2_.refs_0_), channel_id=1, source_target_pairs={{0,16},{8,24},{16,0},{24,8},{1,17},{9,25},{17,1},{25,9},{2,18},{10... | collective-permute-start | bytes 1572872 | tf_op jit(solution)/shard_map/ppermute | solution.py:15
  34.9 11.0 %collective-permute-start.14 = (bf16[1024,256]{1,0:T(8,128)(2,1)S(1)}, bf16[1024,256]{1,0:T(8,128)(2,1)S(1)}, u32[]{:S(2)}, u32[]{:S(2)}) collective-permute-start(bf16[1024,256]{1,0:T(8,128)(2,1)S(1)} %constant_dynamic-update-slice_fusion.refs_0_), channel_id=1, source_target_pairs={{0,8},{8,0},{16,24},{24,16},{1,9},{9,1},{17,25},{25,17},{2,10},{10... | collective-permute-start | bytes 1572872 | tf_op jit(solution)/shard_map/ppermute | solution.py:15
  38.9 12.4 %collective-permute-start.13 = (bf16[576,512]{1,0:T(8,128)(2,1)S(1)}, bf16[576,512]{1,0:T(8,128)(2,1)S(1)}, u32[]{:S(2)}, u32[]{:S(2)}) collective-permute-start(bf16[576,512]{1,0:T(8,128)(2,1)S(1)} %add.25), channel_id=1, source_target_pairs={{1,24},{3,26},{5,28},{7,30},{9,16},{11,18},{13,20},{15,22},{17,8},... | collective-permute-start | bytes 1769480 | tf_op jit(solution)/shard_map/ppermute | solution.py:220
  40.3 15.7 %collective-permute-start.12 = (bf16[576,512]{1,0:T(8,128)(2,1)S(1)}, bf16[576,512]{1,0:T(8,128)(2,1)S(1)}, u32[]{:S(2)}, u32[]{:S(2)}) collective-permute-start(bf16[576,512]{1,0:T(8,128)(2,1)S(1)} %add.25), channel_id=1, source_target_pairs={{1,16},{3,18},{5,20},{7,22},{9,24},{11,26},{13,28},{15,30},{17,0},... | collective-permute-start | bytes 1769480 | tf_op jit(solution)/shard_map/ppermute | solution.py:220
  41.6 16.7 %collective-permute-start.11 = (bf16[576,512]{1,0:T(8,128)(2,1)S(1)}, bf16[576,512]{1,0:T(8,128)(2,1)S(1)}, u32[]{:S(2)}, u32[]{:S(2)}) collective-permute-start(bf16[576,512]{1,0:T(8,128)(2,1)S(1)} %add.25), channel_id=1, source_target_pairs={{1,9},{3,11},{5,13},{7,15},{9,1},{11,3},{13,5},{15,7},{17,25},{19,... | collective-permute-start | bytes 1769480 | tf_op jit(solution)/shard_map/ppermute | solution.py:220
  58.7 3.0 %copy-start.1 = (f32[2,256,256]{2,1,0:T(8,128)S(1)}, f32[2,256,256]{2,1,0:T(8,128)}, u32[]{:S(2)}) copy-start(f32[2,256,256]{2,1,0:T(8,128)} %inverse.2) | copy-start | bytes 1572868
  58.8 2.9 %collective-permute-start.16 = (bf16[1152,512]{1,0:T(8,128)(2,1)S(1)}, bf16[1152,512]{1,0:T(8,128)(2,1)S(1)}, u32[]{:S(2)}, u32[]{:S(2)}) collective-permute-start(bf16[1152,512]{1,0:T(8,128)(2,1)S(1)} %pad_maximum_fusion.1.here), channel_id=1, source_target_pairs={{0,1},{1,0},{2,3},{3,2},{4,5},{5,4},{6,7},{7,6},{8,9},{9,8},{10,11... | collective-permute-start | bytes 3538952 | tf_op jit(solution)/shard_map/ppermute | solution.py:15
  66.9 40.7 %collective-permute-start.20 = (f16[2048,128]{1,0:T(8,128)(2,1)S(1)}, f16[2048,128]{1,0:T(8,128)(2,1)S(1)}, u32[]{:S(2)}, u32[]{:S(2)}) collective-permute-start(f16[2048,128]{1,0:T(8,128)(2,1)S(1)} %get-tuple-element.66), channel_id=1, source_target_pairs={{0,4},{1,5},{2,6},{3,7},{4,0},{5,1},{6,2},{7,3},{8,12},{9,13},{10,... | collective-permute-start | bytes 1572872 | tf_op jit(solution)/shard_map/ppermute | solution.py:15
  70.6 43.6 %collective-permute-start.17 = (f16[2048,128]{1,0:T(8,128)(2,1)S(1)}, f16[2048,128]{1,0:T(8,128)(2,1)S(1)}, u32[]{:S(2)}, u32[]{:S(2)}) collective-permute-start(f16[2048,128]{1,0:T(8,128)(2,1)S(1)} %get-tuple-element.64), channel_id=1, source_target_pairs={{0,6},{1,7},{2,4},{3,5},{4,2},{5,3},{6,0},{7,1},{8,14},{9,15},{10,... | collective-permute-start | bytes 1572872 | tf_op jit(solution)/shard_map/ppermute | solution.py:15
  75.3 22.3 %collective-permute-start.19 = (f16[1024,128]{1,0:T(8,128)(2,1)S(1)}, f16[1024,128]{1,0:T(8,128)(2,1)S(1)}, u32[]{:S(2)}, u32[]{:S(2)}) collective-permute-start(f16[1024,128]{1,0:T(8,128)(2,1)S(1)} %get-tuple-element.75), channel_id=1, source_target_pairs={{0,2},{1,3},{2,0},{3,1},{4,6},{5,7},{6,4},{7,5},{8,10},{9,11},{10,... | collective-permute-start | bytes 786440 | tf_op jit(solution)/shard_map/ppermute | solution.py:15
  76.6 30.9 %collective-permute-start.18 = (f16[1024,128]{1,0:T(8,128)(2,1)S(1)}, f16[1024,128]{1,0:T(8,128)(2,1)S(1)}, u32[]{:S(2)}, u32[]{:S(2)}) collective-permute-start(f16[1024,128]{1,0:T(8,128)(2,1)S(1)} %get-tuple-element.76), channel_id=1, source_target_pairs={{0,2},{1,3},{2,0},{3,1},{4,6},{5,7},{6,4},{7,5},{8,10},{9,11},{10,... | collective-permute-start | bytes 786440 | tf_op jit(solution)/shard_map/ppermute | solution.py:15
  (1 other events, 2.8 us)
